TPU v7x, 32 devices: a whole 2x2x4 slice. The times are simulated.
32 devices in a mesh: grp: 4 (over x, core), dev: 8 (over z, y).
Axes of the slice: x: 2, y: 2, z: 4, core: 2. Of those that a mesh axis runs over, the one named last changes fastest.
Arguments:
- tokens: bfloat16 [4096, 2048], P(('grp', 'dev')), may hold values from -6 to 6
- queries: bfloat16 [4096, 2048], P(('grp', 'dev')), may hold values from -7.5 to 7.5
- suffix_keys: bfloat16 [4096, 2048], P(('grp', 'dev')), may hold values from -6 to 6
- suffix_values: bfloat16 [4096, 2048], P(('grp', 'dev')), may hold values from -6 to 6
- prefix_keys: bfloat16 [4, 256, 2048], P('grp', 'dev'), may hold values from -6 to 6
- prefix_values: bfloat16 [4, 256, 2048], P('grp', 'dev'), may hold values from -6 to 6
- out_weight: bfloat16 [2048, 2048], replicated, may hold values from -0.125 to 0.125
- norm_gain: float32 [2048], replicated, may hold values from 0.1 to 1.9
- routes: int32 [4096, 6], P(('grp', 'dev')), may hold values from 0 to 15, all different within a row; in each aligned block of 128 rows (0 to 127, 128 to 255, ...) at most 64 rows name the same one
- route_weights: float32 [4096, 6], P(('grp', 'dev')), may hold values from 0.05 to 0.5
- gate_up_weight: bfloat16 [32, 2048, 1408], P(('grp', 'dev')), may hold values from -0.125 to 0.125
- down_weight: bfloat16 [32, 704, 2048], P(('grp', 'dev')), may hold values from -0.15625 to 0.15625
Outputs:
- attended: bfloat16 [4096, 2048], P(('grp', 'dev'))
- routed: bfloat16 [4096, 2048], P(('grp', 'dev'))
Inputs may be any that keep to these rules, and one draw needn't show every extreme that they name: `routes`: each row names 6 different experts. Within the rows of one request (aligned blocks of 128 rows) no expert is named by more than 64 rows, and in some block one expert is named exactly 64 times.
All inputs are finite; a program needn't handle non-finite values.
Results may differ from a plain program's by a relative error of at most 0.019.
Values may be sent and summed in bfloat16 or wider, within the bound.
No kernel may reach another device: no remote copies, remote signals or barrier semaphores. Data moves between devices by JAX's collectives and lax.ppermute only.
A program may use at most 128 MiB of HBM per device.

v0:
```python
import math

import jax
import jax.numpy as jnp
from jax import lax
from jax.sharding import PartitionSpec as P

HEADS = 16
HEAD_DIM = 128
TOP = 6


def half_expert(rows, gate_up, down_proj):
    hidden_units = down_proj.shape[0]
    projected = jnp.dot(rows, gate_up, preferred_element_type=jnp.float32)
    active = (jax.nn.silu(projected[:, :hidden_units]) * projected[:, hidden_units:]).astype(
        jnp.bfloat16
    )
    return jnp.dot(active, down_proj, preferred_element_type=jnp.float32).astype(jnp.bfloat16)


def on_device(
    tokens,
    queries,
    suffix_keys,
    suffix_values,
    prefix_keys,
    prefix_values,
    out_weight,
    norm_gain,
    routes,
    route_weights,
    gate_up_weight,
    down_weight,
):
    rows_here = tokens.shape[0]
    width = tokens.shape[1]
    divisor = math.sqrt(HEAD_DIM)
    query_heads = queries.reshape(rows_here, HEADS, HEAD_DIM)
    running_max = jnp.full((HEADS, rows_here), -jnp.inf, jnp.float32)
    denominator = jnp.zeros((HEADS, rows_here), jnp.float32)
    weighted = jnp.zeros((HEADS, rows_here, HEAD_DIM), jnp.float32)
    key_piece = lax.all_gather(prefix_keys[0], "dev", axis=0, tiled=True).reshape(
        -1, HEADS, HEAD_DIM
    )
    value_piece = lax.all_gather(prefix_values[0], "dev", axis=0, tiled=True).reshape(
        -1, HEADS, HEAD_DIM
    )
    scores = (
        jnp.einsum("rhd,khd->hrk", query_heads, key_piece, preferred_element_type=jnp.float32)
        / divisor
    )
    new_max = jnp.max(scores, axis=-1)
    shifted = jnp.exp(scores - new_max[..., None])
    factor = jnp.exp(running_max - new_max)
    denominator = denominator * factor + jnp.sum(shifted, axis=-1)
    weighted = weighted * factor[..., None] + jnp.einsum(
        "hrk,khd->hrd",
        shifted.astype(jnp.bfloat16),
        value_piece,
        preferred_element_type=jnp.float32,
    )
    causal = jnp.arange(rows_here)[:, None] >= jnp.arange(rows_here)[None, :]
    suffix_scores = (
        jnp.einsum(
            "rhd,khd->hrk",
            query_heads,
            suffix_keys.reshape(rows_here, HEADS, HEAD_DIM),
            preferred_element_type=jnp.float32,
        )
        / divisor
    )
    suffix_scores = jnp.where(causal[None], suffix_scores, -jnp.inf)
    suffix_max = jnp.max(suffix_scores, axis=-1)
    suffix_exp = jnp.exp(suffix_scores - suffix_max[..., None])
    suffix_sum = jnp.sum(suffix_exp, axis=-1)
    suffix_acc = jnp.einsum(
        "hrk,khd->hrd",
        suffix_exp.astype(jnp.bfloat16),
        suffix_values.reshape(rows_here, HEADS, HEAD_DIM),
        preferred_element_type=jnp.float32,
    )
    merged_max = jnp.maximum(new_max, suffix_max)
    prefix_scale = jnp.exp(new_max - merged_max)
    suffix_scale = jnp.exp(suffix_max - merged_max)
    mixed = (weighted * prefix_scale[..., None] + suffix_acc * suffix_scale[..., None]) / (
        denominator * prefix_scale + suffix_sum * suffix_scale
    )[..., None]
    heads_out = jnp.transpose(mixed, (1, 0, 2)).reshape(rows_here, width).astype(jnp.bfloat16)
    attended = jnp.dot(heads_out, out_weight, preferred_element_type=jnp.float32).astype(
        jnp.bfloat16
    )
    residual = tokens.astype(jnp.float32) + attended.astype(jnp.float32)
    mean_square = jnp.mean(residual * residual, axis=-1, keepdims=True)
    normed = (residual * lax.rsqrt(mean_square + 1e-06) * norm_gain).astype(jnp.bfloat16)
    groups = lax.axis_size("grp")
    members = lax.axis_size("dev")
    experts = groups * members // 2
    capacity = 4 * rows_here * TOP // (3 * experts)
    flat_routes = routes.reshape(-1)
    onehot = (flat_routes[:, None] == jnp.arange(experts, dtype=jnp.int32)[None, :]).astype(
        jnp.int32
    )
    ranking = jnp.sum(jnp.cumsum(onehot, axis=0) * onehot, axis=1) - 1
    slots = flat_routes * capacity + ranking
    owners = jnp.arange(rows_here * TOP, dtype=jnp.int32) // TOP
    outgoing = jnp.zeros((experts * capacity, width), jnp.bfloat16).at[slots].set(normed[owners])
    buffer = jnp.broadcast_to(
        outgoing.reshape(experts, 1, capacity, width), (experts, 2, capacity, width)
    ).reshape(2 * experts, capacity, width)
    received = lax.all_to_all(buffer, ("grp", "dev"), split_axis=0, concat_axis=0, tiled=True)
    partial_rows = half_expert(
        received.reshape(-1, width), gate_up_weight[0], down_weight[0]
    ).reshape(2 * experts, capacity, width)
    returned = lax.all_to_all(partial_rows, ("grp", "dev"), split_axis=0, concat_axis=0, tiled=True)
    halves = returned.reshape(experts, 2, capacity, width)
    expert_table = lax.optimization_barrier(
        (halves[:, 0].astype(jnp.float32) + halves[:, 1].astype(jnp.float32)).astype(jnp.bfloat16)
    ).reshape(experts * capacity, width)
    picked = expert_table[slots].astype(jnp.float32)
    weighted_rows = picked * route_weights.reshape(-1)[:, None]
    routed = jnp.sum(weighted_rows.reshape(rows_here, TOP, width), axis=1).astype(jnp.bfloat16)
    return (attended, routed)


def solution(mesh):
    return jax.shard_map(
        on_device,
        mesh=mesh,
        in_specs=(
            P(("grp", "dev"), None),
            P(("grp", "dev"), None),
            P(("grp", "dev"), None),
            P(("grp", "dev"), None),
            P("grp", "dev", None),
            P("grp", "dev", None),
            P(),
            P(),
            P(("grp", "dev"), None),
            P(("grp", "dev"), None),
            P(("grp", "dev"), None, None),
            P(("grp", "dev"), None, None),
        ),
        out_specs=(P(("grp", "dev"), None), P(("grp", "dev"), None)),
        check_vma=False,
    )
```

profile of v0, /device:TPU:0, one launch (start us, length us, event | category | flops | bytes accessed | tf_op | source)
XLA Modules:
  0.0 585.0 jit_solution(15811611927513484823)
XLA Ops:
  7.2 0.0 copy-start
  7.2 0.0 copy-start.7
  7.2 0.0 all-gather.5.cloned.1.call-start
  7.2 0.7 all-gather.5.cloned.1.call-update
  7.9 0.0 all-gather.7.cloned.1.call-start
  8.0 0.7 all-gather.7.cloned.1.call-update
  8.7 0.8 copy.47
  9.5 0.1 eq.29
  9.6 0.1 eq.25
  9.7 0.7 broadcast_multiply_fusion
  10.5 2.0 copy.55
  12.5 1.7 reduce-window.6
  14.2 0.3 slice_reduce_fusion
  14.5 0.1 copy.46
  14.6 0.1 mul.102
  14.8 0.1 fusion.34
  14.9 1.7 fusion.48
  16.7 0.0 copy-start.5
  16.7 1.0 copy-done.5
  17.6 0.2 fusion.22
  17.8 35.3 %all-gather.5.cloned.1.call-done = bf16[1,256,2048]{2,1,0:T(8,128)(2,1)} async-done(((bf16[1,32,2048]{2,1,0:T(8,128)(2,1)}), bf16[1,256,2048]{2,1,0:T(8,128)(2,1)}) %all-gather.5.cloned.1.call-update) | async-done | bytes 1048592 | tf_op jit(solution)/shard_map/all_gather | solution.py:43
  53.1 2.3 copy.38
  55.4 1.7 multiply_reduce_fusion.1
  57.1 0.0 copy-start.2
  57.1 1.3 copy-done.2
  58.5 0.8 fusion.10
  59.3 34.9 %all-gather.7.cloned.1.call-done = bf16[1,256,2048]{2,1,0:T(8,128)(2,1)} async-done(((bf16[1,32,2048]{2,1,0:T(8,128)(2,1)}), bf16[1,256,2048]{2,1,0:T(8,128)(2,1)}) %all-gather.7.cloned.1.call-update) | async-done | bytes 1048592 | tf_op jit(solution)/shard_map/all_gather | solution.py:46
  94.2 2.3 copy.41
  96.5 2.6 fusion.16
  99.0 0.0 copy-done.8
  99.1 0.3 fusion.18
  99.4 0.0 copy-start.9
  99.4 4.8 multiply_reduce_fusion.2
  104.2 0.0 copy-start.4
  104.2 0.8 copy-done.4
  105.0 0.2 multiply_convert_fusion
  105.2 23.2 %scatter_custom_fusion = bf16[1024,2048]{1,0:T(8,128)(2,1)} fusion(s32[768]{0:T(1024)S(1)} %fusion.42, bf16[128,2048]{1,0:T(8,128)(2,1)S(1)} %multiply_convert_fusion, s32[1024]{0:T(1024)S(1)} %pad_clamp_fusion.1, bf16[]{:T(256)} %constant.17.clone.1), kind=kCustom, calls=%fused_computation.13 | custom fusion | bytes 4194306 | tf_op jit(solution)/shard_map/scatter | solution.py:107
  128.5 6.8 %broadcast_in_dim.28 = bf16[16,2,64,2048]{3,2,1,0:T(8,128)(2,1)} broadcast(bf16[16,64,2048]{2,1,0:T(8,128)(2,1)} %bitcast.118), dimensions={0,2,3} | broadcast | bytes 12582912 | tf_op jit(solution)/shard_map/broadcast_in_dim | solution.py:108
  135.2 188.2 %all_to_all.10 = bf16[32,64,2048]{2,1,0:T(8,128)(2,1)S(1)} all-to-all(bf16[32,64,2048]{2,1,0:T(8,128)(2,1)} %bitcast.117), channel_id=1, replica_groups=mesh['grp'=4,'dev'=8] {'grp','dev'}, dimensions={0} | all-to-all | bytes 16777216 | tf_op jit(solution)/shard_map/all_to_all | solution.py:111
  323.5 17.8 %fusion.1 = f32[2048,1408]{0,1:T(8,128)} fusion(bf16[2048,2048]{1,0:T(8,128)(2,1)S(1)} %bitcast.120, bf16[1,2048,1408]{2,1,0:T(8,128)(2,1)} %param.22), kind=kOutput, calls=%fused_computation.8 | convolution fusion | flops 11811160064 | bytes 25690112 | tf_op jit(solution)/shard_map/dot_general | solution.py:15
  341.3 13.5 %convolution_convert_fusion = bf16[2048,2048]{1,0:T(8,128)(2,1)} fusion(f32[2048,1408]{0,1:T(8,128)} %fusion.1, bf16[1,704,2048]{2,1,0:T(8,128)(2,1)S(1)} %copy-done), kind=kOutput, calls=%fused_computation.5 | convolution fusion | flops 5918425088 | bytes 22806528 | tf_op jit(solution)/shard_map/dot_general | solution.py:19
  354.8 4.1 all-to-all-start.1
  358.9 0.1 copy.52
  359.0 189.1 %all-to-all-done.1 = bf16[32,64,2048]{2,1,0:T(8,128)(2,1)} async-done(((bf16[32,64,2048]{2,1,0:T(8,128)(2,1)}), bf16[32,64,2048]{2,1,0:T(8,128)(2,1)}, u32[]{:S(2)}, u32[]{:S(2)}) %all-to-all-start.1) | async-done | bytes 8388640 | tf_op jit(solution)/shard_map/all_to_all | solution.py:115
  548.1 5.7 fusion.3
  553.8 9.8 %gather_fusion = bf16[768,2048]{1,0:T(8,128)(2,1)} fusion(bf16[1024,2048]{1,0:T(8,128)(2,1)} %bitcast.116, s32[1024]{0:T(1024)S(1)} %pad_clamp_fusion), kind=kCustom, calls=%fused_computation.1 | custom fusion | bytes 6294528 | tf_op jit(solution)/shard_map/gather | solution.py:120
  563.6 6.7 %reshape.210 = f32[128,6,2048]{2,1,0:T(8,128)} reshape(bf16[768,2048]{1,0:T(8,128)(2,1)} %gather_fusion) | data formatting | bytes 9437184 | tf_op jit(solution)/shard_map/convert_element_type | solution.py:120
  570.3 7.4 %multiply_reduce_fusion = bf16[128,2048]{1,0:T(8,128)(2,1)} fusion(f32[128,6,2048]{2,1,0:T(8,128)} %reshape.210, f32[128,6]{1,0:T(8,128)S(1)} %copy.52), kind=kLoop, calls=%fused_computation.3 | loop fusion | flops 2883584 | bytes 6818816 | tf_op jit(solution)/shard_map/reduce_sum | solution.py:122
  (22 shorter events, 0.2 us)
Async XLA Ops:
  7.2 334.1 %copy-start = (bf16[1,704,2048]{2,1,0:T(8,128)(2,1)S(1)}, bf16[1,704,2048]{2,1,0:T(8,128)(2,1)}, u32[]{:S(2)}) copy-start(bf16[1,704,2048]{2,1,0:T(8,128)(2,1)} %param.23) | copy-start | bytes 8650756
  7.2 48.2 %copy-start.7 = (bf16[128,2048]{1,0:T(8,128)(2,1)S(1)}, bf16[128,2048]{1,0:T(8,128)(2,1)}, u32[]{:S(2)}) copy-start(bf16[128,2048]{1,0:T(8,128)(2,1)} %param.13) | copy-start | bytes 1572868
  7.2 45.9 %all-gather.5.cloned.1.call-start = ((), (), s32[]{:S(2)}) async-start(), calls=%async_computation.2 | async-start | bytes 1179648 | tf_op jit(solution)/shard_map/all_gather | solution.py:43
  7.9 86.3 %all-gather.7.cloned.1.call-start = ((), (), s32[]{:S(2)}) async-start(), calls=%async_computation.3 | async-start | bytes 1179648 | tf_op jit(solution)/shard_map/all_gather | solution.py:46
  16.7 1.0 copy-start.5
  57.1 1.4 copy-start.2
  58.5 40.6 %copy-start.8 = (bf16[128,2048]{0,1:T(8,128)(2,1)S(1)}, bf16[128,2048]{0,1:T(8,128)(2,1)}, u32[]{:S(2)}) copy-start(bf16[128,2048]{0,1:T(8,128)(2,1)} %copy.55) | copy-start | bytes 1572868
  96.5 2.6 copy-start.6
  96.5 2.9 copy-start.3
  99.4 5.6 copy-start.9
  104.2 0.8 copy-start.4
  354.8 4.1 copy-start.10
  354.8 193.3 %all-to-all-start.1 = ((bf16[32,64,2048]{2,1,0:T(8,128)(2,1)}), bf16[32,64,2048]{2,1,0:T(8,128)(2,1)}, u32[]{:S(2)}, u32[]{:S(2)}) async-start(bf16[32,64,2048]{2,1,0:T(8,128)(2,1)} %bitcast.119), calls=%async_computation.1 | async-start | bytes 16777216 | tf_op jit(solution)/shard_map/all_to_all | solution.py:115
  563.6 14.1 %copy-start.1 = (bf16[1,704,2048]{2,1,0:T(8,128)(2,1)S(1)}, bf16[1,704,2048]{2,1,0:T(8,128)(2,1)}, u32[]{:S(2)}) copy-start(bf16[1,704,2048]{2,1,0:T(8,128)(2,1)} %param.23) | copy-start | bytes 8650756
Sparse Core Ops, SparseCore 0:
  10.2 42.9 all-gather.4
  55.2 38.8 all-gather.6
where the time goes:
time: 591 us; the launch traced here: 585 us
  waiting for transfers between devices  261 us (44%)
  blocking collectives  188 us (32%)
  local copies, waits for them, and re-layouts  57.9 us (10%)
  matrix products  42.4 us (7%)
  other arithmetic  16.9 us (3%)
  between operations  14.7 us (2%)
    all_to_all x1, waiting for transfers between devices, on_device(): lax.all_to_all(partial_rows, ('grp', 'dev'), split_axis=0, concat_axis=0,...  189 us
    all_to_all x1, blocking collectives, on_device(): lax.all_to_all(buffer, ('grp', 'dev'), split_axis=0, concat_axis=0, tiled...  188 us
    all_gather x1, waiting for transfers between devices, on_device(): lax.all_gather(prefix_keys[0], 'dev', axis=0, tiled=True)  35.3 us
    all_gather x1, waiting for transfers between devices, on_device(): lax.all_gather(prefix_values[0], 'dev', axis=0, tiled=True)  34.9 us
    scatter x1, local copies, waits for them, and re-layouts, on_device(): jnp.zeros((experts * capacity, width), jnp.bfloat16).at[slots]  23.2 us
    dot_general x1, matrix products, half_expert(): projected = jnp.dot(rows, gate_up, preferred_element_type=jnp.float32)  17.8 us
    dot_general x1, matrix products, half_expert(): jnp.dot(active, down_proj, preferred_element_type=jnp.float32)  13.5 us
  transfers between devices with their start and end apart: 3, of which 3 were waited for; matrix products, arithmetic and copies ran while one was open for 2% of the time, Pallas kernels for 0%

commit v1 on v0

v1 whole, which is shorter than its diff:
```python
import math

import jax
import jax.numpy as jnp
from jax import lax
from jax.experimental import pallas as pl
from jax.experimental.pallas import tpu as pltpu
from jax.sharding import PartitionSpec as P

HEADS = 16
HEAD_DIM = 128
TOP = 6
GATHER_BUDGET = 40 * 2**20
VMEM_LIMIT = 52 * 2**20


def attention_kernel(q_ref, kv_ref, sk_ref, sv_ref, out_ref):
    rows = q_ref.shape[0]
    span = q_ref.shape[1]
    scale = 1.0 / math.sqrt(HEAD_DIM)
    causal = lax.broadcasted_iota(jnp.int32, (rows, rows), 0) >= lax.broadcasted_iota(
        jnp.int32, (rows, rows), 1
    )
    contract = (((1,), (1,)), ((), ()))
    for head in range(span // HEAD_DIM):
        cols = slice(head * HEAD_DIM, (head + 1) * HEAD_DIM)
        query = q_ref[:, cols]
        keys = kv_ref[:, 0, :, cols].reshape(-1, HEAD_DIM)
        values = kv_ref[:, 1, :, cols].reshape(-1, HEAD_DIM)
        prefix = (
            lax.dot_general(query, keys, contract, preferred_element_type=jnp.float32) * scale
        )
        suffix = (
            lax.dot_general(query, sk_ref[:, cols], contract, preferred_element_type=jnp.float32)
            * scale
        )
        suffix = jnp.where(causal, suffix, -jnp.inf)
        top = jnp.maximum(
            jnp.max(prefix, axis=1, keepdims=True), jnp.max(suffix, axis=1, keepdims=True)
        )
        prefix = jnp.exp(prefix - top)
        suffix = jnp.exp(suffix - top)
        total = jnp.sum(prefix, axis=1, keepdims=True) + jnp.sum(suffix, axis=1, keepdims=True)
        mixed = jnp.dot(
            prefix.astype(jnp.bfloat16), values, preferred_element_type=jnp.float32
        ) + jnp.dot(
            suffix.astype(jnp.bfloat16), sv_ref[:, cols], preferred_element_type=jnp.float32
        )
        out_ref[:, cols] = (mixed / total).astype(jnp.bfloat16)


def attention(queries, kv, suffix_keys, suffix_values):
    rows, width = queries.shape
    span = 4 * HEAD_DIM
    by_cols = pl.BlockSpec((rows, span), lambda i: (0, i))
    return pl.pallas_call(
        attention_kernel,
        grid=(width // span,),
        in_specs=[
            by_cols,
            pl.BlockSpec(kv.shape[:3] + (span,), lambda i: (0, 0, 0, i)),
            by_cols,
            by_cols,
        ],
        out_specs=by_cols,
        out_shape=jax.ShapeDtypeStruct((rows, width), jnp.bfloat16),
        compiler_params=pltpu.CompilerParams(vmem_limit_bytes=VMEM_LIMIT),
        name="attention",
    )(queries, kv, suffix_keys, suffix_values)


def project_kernel(heads_ref, weight_ref, tokens_ref, gain_ref, attended_ref, normed_ref, held):
    step = pl.program_id(0)
    attended = jnp.dot(
        heads_ref[...], weight_ref[...], preferred_element_type=jnp.float32
    ).astype(jnp.bfloat16)
    attended_ref[...] = attended
    held[step] = tokens_ref[...].astype(jnp.float32) + attended.astype(jnp.float32)

    @pl.when(step == pl.num_programs(0) - 1)
    def finish():
        steps, rows, span = held.shape
        squares = jnp.zeros((rows, 1), jnp.float32)
        for piece in range(steps):
            part = held[piece]
            squares = squares + jnp.sum(part * part, axis=1, keepdims=True)
        factor = lax.rsqrt(squares / (steps * span) + 1e-06)
        for piece in range(steps):
            cols = slice(piece * span, (piece + 1) * span)
            normed_ref[:, cols] = (held[piece] * factor * gain_ref[:, cols]).astype(jnp.bfloat16)


def project(heads_out, out_weight, tokens, norm_gain):
    rows, width = tokens.shape
    span = 512
    steps = width // span
    by_cols = pl.BlockSpec((rows, span), lambda i: (0, i))
    return pl.pallas_call(
        project_kernel,
        grid=(steps,),
        in_specs=[
            pl.BlockSpec((rows, width), lambda i: (0, 0)),
            pl.BlockSpec((width, span), lambda i: (0, i)),
            by_cols,
            pl.BlockSpec((1, width), lambda i: (0, 0)),
        ],
        out_specs=[by_cols, pl.BlockSpec((rows, width), lambda i: (0, 0))],
        out_shape=[
            jax.ShapeDtypeStruct((rows, width), jnp.bfloat16),
            jax.ShapeDtypeStruct((rows, width), jnp.bfloat16),
        ],
        scratch_shapes=[pltpu.VMEM((steps, rows, span), jnp.float32)],
        compiler_params=pltpu.CompilerParams(vmem_limit_bytes=VMEM_LIMIT),
        name="project_and_norm",
    )(heads_out, out_weight, tokens, norm_gain.reshape(1, width))


def expert_kernel(
    capacity, rows_ref, slot_ref, gate_ref, gate_up_ref, down_ref, out_ref, picked, weighted
):
    requests, _, rows = slot_ref.shape
    hidden = down_ref.shape[0]
    levels = lax.broadcasted_iota(jnp.int32, (capacity, rows), 0)
    for one in range(requests):
        chosen = levels == slot_ref[one]
        picked[one * capacity : (one + 1) * capacity, :] = jnp.dot(
            chosen.astype(jnp.bfloat16),
            rows_ref[one * rows : (one + 1) * rows, :],
            preferred_element_type=jnp.float32,
        ).astype(jnp.bfloat16)
    projected = jnp.dot(picked[...], gate_up_ref[...], preferred_element_type=jnp.float32)
    gate = projected[:, :hidden]
    active = (gate / (1.0 + jnp.exp(-gate)) * projected[:, hidden:]).astype(jnp.bfloat16)
    weighted[...] = jnp.dot(active, down_ref[...], preferred_element_type=jnp.float32)
    for one in range(requests):
        chosen = levels == slot_ref[one]
        gates = jnp.sum(jnp.where(chosen, gate_ref[one], 0.0), axis=1, keepdims=True)
        scaled = (weighted[one * capacity : (one + 1) * capacity, :] * gates).astype(jnp.bfloat16)
        out_ref[one * rows : (one + 1) * rows, :] = lax.dot_general(
            chosen.astype(jnp.bfloat16),
            scaled,
            (((0,), (0,)), ((), ())),
            preferred_element_type=jnp.float32,
        ).astype(jnp.bfloat16)


def expert(gathered, slots, gates, gate_up, down, capacity):
    requests, rows = slots.shape
    width = gathered.shape[1]
    step = 4
    table = pl.BlockSpec((step, 1, rows), lambda i: (i, 0, 0))
    by_rows = pl.BlockSpec((step * rows, width), lambda i: (i, 0))
    return pl.pallas_call(
        lambda *refs: expert_kernel(capacity, *refs),
        grid=(requests // step,),
        in_specs=[
            by_rows,
            table,
            table,
            pl.BlockSpec(gate_up.shape, lambda i: (0, 0)),
            pl.BlockSpec(down.shape, lambda i: (0, 0)),
        ],
        out_specs=by_rows,
        out_shape=jax.ShapeDtypeStruct(gathered.shape, jnp.bfloat16),
        scratch_shapes=[
            pltpu.VMEM((step * capacity, width), jnp.bfloat16),
            pltpu.VMEM((step * capacity, width), jnp.float32),
        ],
        compiler_params=pltpu.CompilerParams(vmem_limit_bytes=VMEM_LIMIT),
        name="expert_half",
    )(
        gathered,
        slots.reshape(requests, 1, rows),
        gates.reshape(requests, 1, rows),
        gate_up,
        down,
    )


def half_expert(rows, gate_up, down_proj):
    hidden_units = down_proj.shape[0]
    projected = jnp.dot(rows, gate_up, preferred_element_type=jnp.float32)
    active = (jax.nn.silu(projected[:, :hidden_units]) * projected[:, hidden_units:]).astype(
        jnp.bfloat16
    )
    return jnp.dot(active, down_proj, preferred_element_type=jnp.float32).astype(jnp.bfloat16)


def exchange_plan(normed, routes, route_weights, gate_up, down, experts, capacity):
    rows_here, width = normed.shape
    flat_routes = routes.reshape(-1)
    onehot = (flat_routes[:, None] == jnp.arange(experts, dtype=jnp.int32)[None, :]).astype(
        jnp.int32
    )
    ranking = jnp.sum(jnp.cumsum(onehot, axis=0) * onehot, axis=1) - 1
    slots = flat_routes * capacity + ranking
    owners = jnp.arange(rows_here * TOP, dtype=jnp.int32) // TOP
    outgoing = jnp.zeros((experts * capacity, width), jnp.bfloat16).at[slots].set(normed[owners])
    buffer = jnp.broadcast_to(
        outgoing.reshape(experts, 1, capacity, width), (experts, 2, capacity, width)
    ).reshape(2 * experts, capacity, width)
    received = lax.all_to_all(buffer, ("grp", "dev"), split_axis=0, concat_axis=0, tiled=True)
    partial_rows = half_expert(received.reshape(-1, width), gate_up, down).reshape(
        2 * experts, capacity, width
    )
    returned = lax.all_to_all(partial_rows, ("grp", "dev"), split_axis=0, concat_axis=0, tiled=True)
    halves = returned.reshape(experts, 2, capacity, width)
    expert_table = lax.optimization_barrier(
        (halves[:, 0].astype(jnp.float32) + halves[:, 1].astype(jnp.float32)).astype(jnp.bfloat16)
    ).reshape(experts * capacity, width)
    picked = expert_table[slots].astype(jnp.float32)
    weighted_rows = picked * route_weights.reshape(-1)[:, None]
    return jnp.sum(weighted_rows.reshape(rows_here, TOP, width), axis=1).astype(jnp.bfloat16)


def own_slots(table, mine):
    named = table[:, :TOP] == mine.astype(jnp.float32)
    gates = jnp.sum(jnp.where(named, table[:, TOP:], 0.0), axis=1)
    member = jnp.any(named, axis=1)
    rows = table.shape[-1]
    before = jnp.arange(rows)[:, None] <= jnp.arange(rows)[None, :]
    ranks = jnp.dot(
        member.astype(jnp.bfloat16),
        before.astype(jnp.bfloat16),
        preferred_element_type=jnp.float32,
    ).astype(jnp.int32)
    return jnp.where(member, ranks - 1, -1), gates


def gather_plan(normed, table, gate_up, down, experts, capacity):
    mine = (lax.axis_index("grp") * lax.axis_size("dev") + lax.axis_index("dev")) // 2
    slots, gates = own_slots(table, mine)
    gathered = lax.all_gather(normed, ("grp", "dev"), axis=0, tiled=True)
    partial = expert(gathered, slots, gates, gate_up, down, capacity)
    return lax.psum_scatter(partial, ("grp", "dev"), scatter_dimension=0, tiled=True)


def on_device(
    tokens,
    queries,
    suffix_keys,
    suffix_values,
    prefix_keys,
    prefix_values,
    out_weight,
    norm_gain,
    routes,
    route_weights,
    gate_up_weight,
    down_weight,
):
    rows_here, width = tokens.shape
    groups = lax.axis_size("grp")
    members = lax.axis_size("dev")
    experts = groups * members // 2
    capacity = 4 * rows_here * TOP // (3 * experts)
    gather_fits = groups * members * rows_here * width * 2 <= GATHER_BUDGET
    kv = lax.all_gather(jnp.concatenate([prefix_keys, prefix_values]), "dev", axis=0)
    if gather_fits:
        table = lax.all_gather(
            jnp.concatenate([routes.T.astype(jnp.float32), route_weights.T]),
            ("grp", "dev"),
            axis=0,
        )
    heads_out = attention(queries, kv, suffix_keys, suffix_values)
    attended, normed = project(heads_out, out_weight, tokens, norm_gain)
    if gather_fits:
        routed = gather_plan(normed, table, gate_up_weight[0], down_weight[0], experts, capacity)
    else:
        routed = exchange_plan(
            normed, routes, route_weights, gate_up_weight[0], down_weight[0], experts, capacity
        )
    return (attended, routed)


def solution(mesh):
    return jax.shard_map(
        on_device,
        mesh=mesh,
        in_specs=(
            P(("grp", "dev"), None),
            P(("grp", "dev"), None),
            P(("grp", "dev"), None),
            P(("grp", "dev"), None),
            P("grp", "dev", None),
            P("grp", "dev", None),
            P(),
            P(),
            P(("grp", "dev"), None),
            P(("grp", "dev"), None),
            P(("grp", "dev"), None, None),
            P(("grp", "dev"), None, None),
        ),
        out_specs=(P(("grp", "dev"), None), P(("grp", "dev"), None)),
        check_vma=False,
    )
```

time: 591 us -> 591 us (level)
  waiting for transfers between devices: 261 us -> 456 us
  blocking collectives: 188 us -> 68.2 us
  local copies, waits for them, and re-layouts: 57.9 us -> 3.82 us
  Pallas kernels: 0 us -> 46 us
  matrix products: 42.4 us -> 0.14 us
  other arithmetic: 16.9 us -> 1.83 us
    reduce_scatter x0 -> x1, waiting for transfers between devices: none -> 356 us  [gather_plan(): lax.psum_scatter(partial, ('grp', 'dev'), scatter_dimension=0, tiled=True)]
    all_to_all x1 -> x0, waiting for transfers between devices: 189 us -> none  [on_device(): lax.all_to_all(partial_rows, ('grp', 'dev'), split_axis=0, concat_axis=0,...]
    all_to_all x1 -> x0, blocking collectives: 188 us -> none  [on_device(): lax.all_to_all(buffer, ('grp', 'dev'), split_axis=0, concat_axis=0, tiled...]
    all_gather x0 -> x1, blocking collectives: none -> 68.2 us  [on_device(): lax.all_gather(jnp.concatenate([routes.T.astype(jnp.float32), route_weigh...]
    pallas_call x0 -> x3, Pallas kernels: none -> 46 us  [the longest x1 34.1 us: expert(): pl.pallas_call(lambda *refs: expert_kernel(capacity, *refs), grid=(reques...]
    dot_general x7 -> x1, matrix products: 42.4 us -> 0.14 us  [own_slots(): jnp.dot(member.astype(jnp.bfloat16), before.astype(jnp.bfloat16), preferr...]
    all_gather x2, waiting for transfers between devices: 70.2 us -> 99.6 us  [the longest x1 53.7 us: on_device(): lax.all_gather(jnp.concatenate([prefix_keys, prefix_values]), 'dev', axis=0)]
    scatter x1 -> x0, local copies, waits for them, and re-layouts: 23.2 us -> none  [on_device(): jnp.zeros((experts * capacity, width), jnp.bfloat16).at[slots]]
  transfers between devices with their start and end apart: 3 -> 3, of which waited for: 3 -> 3; matrix products, arithmetic and copies ran while one was open for 2% -> 0% of each run, Pallas kernels for 0% -> 0%
where the time goes in v1:
time: 591 us; the launch traced here: 590 us
  waiting for transfers between devices  456 us (77%)
  blocking collectives  68.2 us (12%)
  Pallas kernels  46 us (8%)
  between operations  13.8 us (2%)
    reduce_scatter x1, waiting for transfers between devices, gather_plan(): lax.psum_scatter(partial, ('grp', 'dev'), scatter_dimension=0, tiled=True)  356 us
    all_gather x1, blocking collectives, on_device(): lax.all_gather(jnp.concatenate([routes.T.astype(jnp.float32), route_weigh...  68.2 us
    all_gather x1, waiting for transfers between devices, on_device(): lax.all_gather(jnp.concatenate([prefix_keys, prefix_values]), 'dev', axis=0)  53.7 us
    all_gather x1, waiting for transfers between devices, gather_plan(): gathered = lax.all_gather(normed, ('grp', 'dev'), axis=0, tiled=True)  45.9 us
    pallas_call x1, Pallas kernels, expert(): pl.pallas_call(lambda *refs: expert_kernel(capacity, *refs), grid=(reques...  34.1 us
  transfers between devices with their start and end apart: 3, of which 3 were waited for; matrix products, arithmetic and copies ran while one was open for 0% of the time, Pallas kernels for 0%

profile of v1, /device:TPU:0, one launch (start us, length us, event | category | flops | bytes accessed | tf_op | source)
XLA Modules:
  0.0 590.1 jit_solution(3436060630857864641)
XLA Ops:
  7.2 0.0 copy-start.4
  7.2 0.0 copy-start.5
  7.2 0.0 all-gather.8.cloned.1.call-start
  7.2 1.7 pad_maximum_fusion
  8.9 0.0 all-gather.8.cloned.1.call-update
  9.0 0.0 all-gather.6.cloned.1.call-start
  9.0 53.7 %all-gather.8.cloned.1.call-done = bf16[16,32,2048]{2,1,0:T(8,128)(2,1)} async-done(((bf16[2,32,2048]{2,1,0:T(8,128)(2,1)}), bf16[16,32,2048]{2,1,0:T(8,128)(2,1)}) %all-gather.8.cloned.1.call-update) | async-done | bytes 2097168 | tf_op jit(solution)/shard_map/all_gather | solution.py:258
  62.7 0.0 copy-start
  62.7 1.0 copy-done
  63.8 0.0 copy-start.1
  63.8 1.0 copy-done.1
  64.8 5.9 %attention.1.heads_ref = bf16[128,2048]{1,0:T(8,128)(2,1)S(1)} custom-call(bf16[128,2048]{1,0:T(8,128)(2,1)S(1)} %copy-done, bf16[8,2,32,2048]{3,2,1,0:T(8,128)(2,1)} %bitcast.17, bf16[128,2048]{1,0:T(8,128)(2,1)S(1)} %copy-done.1, bf16[128,2048]{1,0:T(8,128)(2,1)} %sv_ref.1), custom_call_target="tpu_custom_call" | custom-call | tf_op jit(solution)/shard_map/attention/pallas_call | solution.py:56
  70.8 0.0 copy-start.2
  70.8 1.0 copy-done.2
  71.8 0.0 copy-start.3
  71.8 0.7 copy-done.3
  72.5 6.0 %project_and_norm.1 = (bf16[128,2048]{1,0:T(8,128)(2,1)}, bf16[128,2048]{1,0:T(8,128)(2,1)}) custom-call(bf16[128,2048]{1,0:T(8,128)(2,1)S(1)} %attention.1.heads_ref, bf16[2048,2048]{1,0:T(8,128)(2,1)} %weight_ref.1, bf16[128,2048]{1,0:T(8,128)(2,1)S(1)} %copy-done.2, f32[1,2048]{1,0:T(1,128)S(1)} %bitcast.14), custom_call_target="tpu_custom_call" | custom-call | tf_op jit(solution)/shard_map/project_and_norm/pallas_call | solution.py:98
  78.6 0.0 all-gather.6.cloned.1.call-update
  78.6 0.0 reduce-scatter.2.cloned.1.call-start
  78.6 0.0 copy-done.4
  78.7 0.0 copy-done.5
  78.7 68.2 %all-gather.2 = f32[32,12,128]{2,1,0:T(8,128)S(1)} all-gather(f32[1,12,128]{2,1,0:T(8,128)S(1)} %maximum_bitcast_fusion), channel_id=3, replica_groups=mesh['grp'=4,'dev'=8] {'grp','dev'}, dimensions={0}, use_global_device_ids=true | all-gather | bytes 202752 | tf_op jit(solution)/shard_map/all_gather | solution.py:260
  146.9 0.1 fusion.2
  147.0 0.1 reduce_or.9
  147.0 0.1 fusion.1
  147.2 45.9 %all-gather.6.cloned.1.call-done.refs_0_ = bf16[4096,2048]{1,0:T(8,128)(2,1)} async-done(((bf16[128,2048]{1,0:T(8,128)(2,1)}), bf16[4096,2048]{1,0:T(8,128)(2,1)}) %all-gather.6.cloned.1.call-update) | async-done | bytes 16777232 | tf_op jit(solution)/shard_map/all_gather | solution.py:233
  193.1 34.1 %expert_half.1 = bf16[4096,2048]{1,0:T(8,128)(2,1)} custom-call(bf16[4096,2048]{1,0:T(8,128)(2,1)} %all-gather.6.cloned.1.call-done.refs_0_, s32[32,1,128]{2,1,0:T(1,128)S(1)} %bitcast.13, f32[32,1,128]{2,1,0:T(1,128)S(1)} %bitcast.12, bf16[2048,1408]{1,0:T(8,128)(2,1)} %bitcast.15, bf16[704,2048]{1,0:T(8,128)(2,1)} %bitcast.16), custom_call_target="tpu_custom_call" | custom-call | tf_op jit(solution)/shard_map/expert_half/pallas_call | solution.py:153
  227.1 0.0 reduce-scatter.2.cloned.1.call-update
  227.2 356.4 %reduce-scatter.2.cloned.1.call-done = bf16[128,2048]{1,0:T(8,128)(2,1)} async-done(((bf16[4096,2048]{1,0:T(8,128)(2,1)}), bf16[128,2048]{1,0:T(8,128)(2,1)}) %reduce-scatter.2.cloned.1.call-update) | async-done | bytes 524304 | tf_op jit(solution)/shard_map/reduce_scatter | solution.py:235
  (2 shorter events, 0.0 us)
Async XLA Ops:
  7.2 71.5 %copy-start.4 = (s32[128,6]{0,1:T(8,128)S(1)}, s32[128,6]{0,1:T(8,128)}, u32[]{:S(2)}) copy-start(s32[128,6]{0,1:T(8,128)} %param.20) | copy-start | bytes 9220
  7.2 71.5 %copy-start.5 = (f32[128,6]{0,1:T(8,128)S(1)}, f32[128,6]{0,1:T(8,128)}, u32[]{:S(2)}) copy-start(f32[128,6]{0,1:T(8,128)} %param.21) | copy-start | bytes 9220
  7.2 55.6 %all-gather.8.cloned.1.call-start = ((), (), s32[]{:S(2)}) async-start(), calls=%async_computation.3 | async-start | bytes 2359296 | tf_op jit(solution)/shard_map/all_gather | solution.py:258
  9.0 184.1 %all-gather.6.cloned.1.call-start = ((), (), s32[]{:S(2)}) async-start(), calls=%async_computation.1 | async-start | bytes 17301504 | tf_op jit(solution)/shard_map/all_gather | solution.py:233
  62.7 1.0 copy-start
  63.8 1.0 copy-start.1
  70.8 1.0 copy-start.2
  71.8 0.7 copy-start.3
  78.6 505.0 %reduce-scatter.2.cloned.1.call-start = ((), (), s32[]{:S(2)}) async-start(), calls=%async_computation.2 | async-start | bytes 17301504 | tf_op jit(solution)/shard_map/reduce_scatter | solution.py:235
Sparse Core Ops, SparseCore 0:
  10.7 51.9 all-gather.7
  78.7 114.3 all-gather.5
  227.3 356.2 reduce-scatter.1

commit v2 on v1

v2 whole, which is shorter than its diff:
```python
import math

import jax
import jax.numpy as jnp
from jax import lax
from jax.experimental import pallas as pl
from jax.experimental.pallas import tpu as pltpu
from jax.sharding import Mesh
from jax.sharding import PartitionSpec as P

HEADS = 16
HEAD_DIM = 128
TOP = 6
ALL = ("far", "core", "line", "side")
GATHER_BUDGET = 40 * 2**20
VMEM_LIMIT = 52 * 2**20


def attention_kernel(q_ref, sk_ref, sv_ref, *refs):
    pieces, out_ref = refs[:-1], refs[-1]
    rows = q_ref.shape[0]
    span = q_ref.shape[1]
    scale = 1.0 / math.sqrt(HEAD_DIM)
    causal = lax.broadcasted_iota(jnp.int32, (rows, rows), 0) >= lax.broadcasted_iota(
        jnp.int32, (rows, rows), 1
    )
    contract = (((1,), (1,)), ((), ()))
    for head in range(span // HEAD_DIM):
        cols = slice(head * HEAD_DIM, (head + 1) * HEAD_DIM)
        query = q_ref[:, cols]
        keys = jnp.concatenate([piece[0, :, cols] for piece in pieces])
        values = jnp.concatenate([piece[1, :, cols] for piece in pieces])
        prefix = (
            lax.dot_general(query, keys, contract, preferred_element_type=jnp.float32) * scale
        )
        suffix = (
            lax.dot_general(query, sk_ref[:, cols], contract, preferred_element_type=jnp.float32)
            * scale
        )
        suffix = jnp.where(causal, suffix, -jnp.inf)
        top = jnp.maximum(
            jnp.max(prefix, axis=1, keepdims=True), jnp.max(suffix, axis=1, keepdims=True)
        )
        prefix = jnp.exp(prefix - top)
        suffix = jnp.exp(suffix - top)
        total = jnp.sum(prefix, axis=1, keepdims=True) + jnp.sum(suffix, axis=1, keepdims=True)
        mixed = jnp.dot(
            prefix.astype(jnp.bfloat16), values, preferred_element_type=jnp.float32
        ) + jnp.dot(
            suffix.astype(jnp.bfloat16), sv_ref[:, cols], preferred_element_type=jnp.float32
        )
        out_ref[:, cols] = (mixed / total).astype(jnp.bfloat16)


def attention(queries, suffix_keys, suffix_values, pieces):
    rows, width = queries.shape
    span = 4 * HEAD_DIM
    by_cols = pl.BlockSpec((rows, span), lambda i: (0, i))
    return pl.pallas_call(
        attention_kernel,
        grid=(width // span,),
        in_specs=[by_cols] * 3
        + [pl.BlockSpec(piece.shape[:2] + (span,), lambda i: (0, 0, i)) for piece in pieces],
        out_specs=by_cols,
        out_shape=jax.ShapeDtypeStruct((rows, width), jnp.bfloat16),
        compiler_params=pltpu.CompilerParams(vmem_limit_bytes=VMEM_LIMIT),
        name="attention",
    )(queries, suffix_keys, suffix_values, *pieces)


def project_kernel(heads_ref, weight_ref, tokens_ref, gain_ref, attended_ref, normed_ref, held):
    step = pl.program_id(0)
    attended = jnp.dot(
        heads_ref[...], weight_ref[...], preferred_element_type=jnp.float32
    ).astype(jnp.bfloat16)
    attended_ref[...] = attended
    held[step] = tokens_ref[...].astype(jnp.float32) + attended.astype(jnp.float32)

    @pl.when(step == pl.num_programs(0) - 1)
    def finish():
        steps, rows, span = held.shape
        squares = jnp.zeros((rows, 1), jnp.float32)
        for piece in range(steps):
            part = held[piece]
            squares = squares + jnp.sum(part * part, axis=1, keepdims=True)
        factor = lax.rsqrt(squares / (steps * span) + 1e-06)
        for piece in range(steps):
            cols = slice(piece * span, (piece + 1) * span)
            normed_ref[:, cols] = (held[piece] * factor * gain_ref[:, cols]).astype(jnp.bfloat16)


def project(heads_out, out_weight, tokens, norm_gain):
    rows, width = tokens.shape
    span = 512
    steps = width // span
    by_cols = pl.BlockSpec((rows, span), lambda i: (0, i))
    return pl.pallas_call(
        project_kernel,
        grid=(steps,),
        in_specs=[
            pl.BlockSpec((rows, width), lambda i: (0, 0)),
            pl.BlockSpec((width, span), lambda i: (0, i)),
            by_cols,
            pl.BlockSpec((1, width), lambda i: (0, 0)),
        ],
        out_specs=[by_cols, pl.BlockSpec((rows, width), lambda i: (0, 0))],
        out_shape=[
            jax.ShapeDtypeStruct((rows, width), jnp.bfloat16),
            jax.ShapeDtypeStruct((rows, width), jnp.bfloat16),
        ],
        scratch_shapes=[pltpu.VMEM((steps, rows, span), jnp.float32)],
        compiler_params=pltpu.CompilerParams(vmem_limit_bytes=VMEM_LIMIT),
        name="project_and_norm",
    )(heads_out, out_weight, tokens, norm_gain.reshape(1, width))


def experts_kernel(
    capacity,
    place_ref,
    rows_ref,
    slot_ref,
    gate_ref,
    own_up_ref,
    own_down_ref,
    other_up_ref,
    other_down_ref,
    first_ref,
    second_ref,
    picked,
    scaled,
):
    requests = rows_ref.shape[1]
    rows = rows_ref.shape[3]
    hidden = own_down_ref.shape[0]
    half = first_ref.shape[2]
    levels = lax.broadcasted_iota(jnp.int32, (2 * capacity, rows), 0)
    for one in range(requests):
        chosen = (levels == slot_ref[0, one, 0, 0]) | (levels == slot_ref[0, one, 0, 1])
        taken = jnp.dot(
            chosen.astype(jnp.bfloat16), rows_ref[0, one, 0], preferred_element_type=jnp.float32
        ).astype(jnp.bfloat16)
        picked[0, one * capacity : (one + 1) * capacity, :] = taken[:capacity]
        picked[1, one * capacity : (one + 1) * capacity, :] = taken[capacity:]
    for which, (up_ref, down_ref) in enumerate(
        [(own_up_ref, own_down_ref), (other_up_ref, other_down_ref)]
    ):
        projected = jnp.dot(picked[which], up_ref[...], preferred_element_type=jnp.float32)
        gate = projected[:, :hidden]
        active = (gate / (1.0 + jnp.exp(-gate)) * projected[:, hidden:]).astype(jnp.bfloat16)
        result = jnp.dot(active, down_ref[...], preferred_element_type=jnp.float32)
        for one in range(requests):
            low = which * capacity
            chosen = levels[low : low + capacity] == slot_ref[0, one, 0, which]
            gates = jnp.sum(
                jnp.where(chosen, gate_ref[0, one, 0, which], 0.0), axis=1, keepdims=True
            )
            scaled[one, low : low + capacity, :] = (
                result[one * capacity : (one + 1) * capacity, :] * gates
            ).astype(jnp.bfloat16)
    for one in range(requests):
        chosen = (levels == slot_ref[0, one, 0, 0]) | (levels == slot_ref[0, one, 0, 1])
        summed = lax.dot_general(
            chosen.astype(jnp.bfloat16),
            scaled[one],
            (((0,), (0,)), ((), ())),
            preferred_element_type=jnp.float32,
        ).astype(jnp.bfloat16)
        first_ref[0, one * rows : (one + 1) * rows, :] = summed[:, :half]
        second_ref[0, one * rows : (one + 1) * rows, :] = summed[:, half:]


def run_experts(gathered, slots, gates, weights, offsets, capacity):
    layers, requests, _, rows, width = gathered.shape
    steps = offsets.shape[0]
    half = width // 2
    blocks = lambda i, place: (place[i, 0], 0, place[i, 1], 0, 0)
    table = pl.BlockSpec((1, requests, 1, 2, 1, rows), lambda i, place: blocks(i, place) + (0,))
    whole = [
        pl.BlockSpec(one.shape, lambda i, place: (0, 0), pipeline_mode=pl.Buffered(1))
        for one in weights
    ]
    part = pl.BlockSpec((1, requests * rows, half), lambda i, place: (i, 0, 0))
    slots_in_step = 2 * requests * capacity
    hidden = weights[1].shape[0]
    return pl.pallas_call(
        lambda *refs: experts_kernel(capacity, *refs),
        grid_spec=pltpu.PrefetchScalarGridSpec(
            num_scalar_prefetch=1,
            grid=(steps,),
            in_specs=[pl.BlockSpec((1, requests, 1, rows, width), blocks), table, table] + whole,
            out_specs=[part, part],
            scratch_shapes=[
                pltpu.VMEM((2, requests * capacity, width), jnp.bfloat16),
                pltpu.VMEM((requests, 2 * capacity, width), jnp.bfloat16),
            ],
        ),
        out_shape=[jax.ShapeDtypeStruct((steps, requests * rows, half), jnp.bfloat16)] * 2,
        compiler_params=pltpu.CompilerParams(vmem_limit_bytes=VMEM_LIMIT),
        cost_estimate=pl.CostEstimate(
            flops=steps * slots_in_step * width * hidden * 6,
            bytes_accessed=sum(one.size * 2 for one in weights)
            + steps * requests * rows * width * 4,
            transcendentals=steps * slots_in_step * hidden,
        ),
        name="experts",
    )(offsets, gathered, slots, gates, *weights)


def half_expert(rows, gate_up, down_proj):
    hidden_units = down_proj.shape[0]
    projected = jnp.dot(rows, gate_up, preferred_element_type=jnp.float32)
    active = (jax.nn.silu(projected[:, :hidden_units]) * projected[:, hidden_units:]).astype(
        jnp.bfloat16
    )
    return jnp.dot(active, down_proj, preferred_element_type=jnp.float32).astype(jnp.bfloat16)


def exchange_plan(normed, routes, route_weights, gate_up, down, experts, capacity):
    rows_here, width = normed.shape
    flat_routes = routes.reshape(-1)
    onehot = (flat_routes[:, None] == jnp.arange(experts, dtype=jnp.int32)[None, :]).astype(
        jnp.int32
    )
    ranking = jnp.sum(jnp.cumsum(onehot, axis=0) * onehot, axis=1) - 1
    slots = flat_routes * capacity + ranking
    owners = jnp.arange(rows_here * TOP, dtype=jnp.int32) // TOP
    outgoing = jnp.zeros((experts * capacity, width), jnp.bfloat16).at[slots].set(normed[owners])
    buffer = jnp.broadcast_to(
        outgoing.reshape(experts, 1, capacity, width), (experts, 2, capacity, width)
    ).reshape(2 * experts, capacity, width)
    received = lax.all_to_all(buffer, ALL, split_axis=0, concat_axis=0, tiled=True)
    partial_rows = half_expert(received.reshape(-1, width), gate_up, down).reshape(
        2 * experts, capacity, width
    )
    returned = lax.all_to_all(partial_rows, ALL, split_axis=0, concat_axis=0, tiled=True)
    halves = returned.reshape(experts, 2, capacity, width)
    expert_table = lax.optimization_barrier(
        (halves[:, 0].astype(jnp.float32) + halves[:, 1].astype(jnp.float32)).astype(jnp.bfloat16)
    ).reshape(experts * capacity, width)
    picked = expert_table[slots].astype(jnp.float32)
    weighted_rows = picked * route_weights.reshape(-1)[:, None]
    return jnp.sum(weighted_rows.reshape(rows_here, TOP, width), axis=1).astype(jnp.bfloat16)


def own_slots(table, mine, first_slot):
    named = table[:, :TOP] == mine.astype(jnp.float32)
    gates = jnp.sum(jnp.where(named, table[:, TOP:], 0.0), axis=1)
    member = jnp.any(named, axis=1)
    rows = table.shape[-1]
    before = jnp.arange(rows)[:, None] <= jnp.arange(rows)[None, :]
    ranks = jnp.dot(
        member.astype(jnp.bfloat16),
        before.astype(jnp.bfloat16),
        preferred_element_type=jnp.float32,
    ).astype(jnp.int32)
    return jnp.where(member, ranks - 1 + first_slot, -1), gates


def swap(array, axis):
    return lax.ppermute(array, axis, [(0, 1), (1, 0)])


def shift(array, axis, amount):
    size = lax.axis_size(axis)
    return lax.ppermute(array, axis, [(i, (i + amount) % size) for i in range(size)])


def add(*arrays):
    return sum(one.astype(jnp.float32) for one in arrays).astype(jnp.bfloat16)


def gather_plan(normed, table, weights, capacity):
    rows, width = normed.shape
    layers, columns = lax.axis_size("far"), lax.axis_size("line")
    far, core = lax.axis_index("far"), lax.axis_index("core")
    line, side = lax.axis_index("line"), lax.axis_index("side")
    own = (far * 2 + core) * columns + line
    other = (far * 2 + 1 - core) * columns + line
    own_slot, own_gate = own_slots(table, own, 0)
    other_slot, other_gate = own_slots(table, other, capacity)
    shape = (layers, columns, 2, 2, 1, rows)
    slots = jnp.stack([own_slot, other_slot], axis=1).reshape(shape)
    gates = jnp.stack([own_gate, other_gate], axis=1).reshape(shape)
    gathered = lax.all_gather(normed, ("far", "line", "side"), axis=0).reshape(
        layers, columns, 2, rows, width
    )
    place = lambda a, b: jnp.stack([far ^ a, side ^ b])
    first = run_experts(
        gathered, slots, gates, weights, jnp.stack([place(1, 1)]).astype(jnp.int32), capacity
    )
    rest = run_experts(
        gathered,
        slots,
        gates,
        weights,
        jnp.stack([place(0, 1), place(1, 0), place(0, 0)]).astype(jnp.int32),
        capacity,
    )
    a_corner = swap(first[0][0], "side")
    b_corner = swap(first[1][0], "far")
    a_side = swap(rest[0][0], "side")
    b_far = swap(rest[1][1], "far")
    a_far = swap(add(rest[0][1], a_corner), "far")
    b_side = swap(add(rest[1][0], b_corner), "side")
    total = jnp.concatenate(
        [add(rest[0][2], a_side, a_far), add(rest[1][2], b_far, b_side)], axis=1
    ).reshape(columns, rows, width)
    arrived = [
        shift(lax.dynamic_index_in_dim(total, (line + k) % columns, 0, keepdims=False), "line", k)
        for k in range(1, columns)
    ]
    return add(lax.dynamic_index_in_dim(total, line, 0, keepdims=False), *arrived)


def on_device(
    tokens,
    queries,
    suffix_keys,
    suffix_values,
    prefix_keys,
    prefix_values,
    out_weight,
    norm_gain,
    routes,
    route_weights,
    gate_up_weight,
    down_weight,
):
    rows_here, width = tokens.shape
    devices = lax.axis_size(ALL)
    experts = devices // 2
    capacity = 4 * rows_here * TOP // (3 * experts)
    gather_fits = devices * rows_here * width * 2 <= GATHER_BUDGET
    kv = jnp.concatenate([prefix_keys, prefix_values])
    weights = [gate_up_weight[0], down_weight[0]]
    if gather_fits:
        lines = [kv] + [shift(kv, "line", k) for k in range(1, lax.axis_size("line"))]
        pieces = lines + [swap(piece, "side") for piece in lines]
        weights = weights + [swap(one, "core") for one in weights]
        table = lax.all_gather(
            jnp.concatenate([routes.T.astype(jnp.float32), route_weights.T]),
            ("far", "line", "side"),
            axis=0,
        )
    else:
        pieces = [
            lax.all_gather(kv, ("line", "side"), axis=1, tiled=True)
        ]
    heads_out = attention(queries, suffix_keys, suffix_values, pieces)
    attended, normed = project(heads_out, out_weight, tokens, norm_gain)
    if gather_fits:
        routed = gather_plan(normed, table, weights, capacity)
    else:
        routed = exchange_plan(
            normed, routes, route_weights, weights[0], weights[1], experts, capacity
        )
    return (attended, routed)


def solution(mesh):
    groups, members = mesh.shape["grp"], mesh.shape["dev"]
    fine = Mesh(mesh.devices.reshape(groups // 2, 2, members // 2, 2), ALL)
    rows = P(ALL, None)
    prefix = P(("far", "core"), ("line", "side"), None)
    stacked = P(ALL, None, None)
    return jax.shard_map(
        on_device,
        mesh=fine,
        in_specs=(rows,) * 4
        + (prefix, prefix, P(), P(), rows, rows, stacked, stacked),
        out_specs=(rows, rows),
        check_vma=False,
    )
```

time: 591 us -> 332 us (0.56)
  the two profiles are of different devices: /device:TPU:0 before, /device:TPU:9 now
where the time goes in v2:
time: 332 us; the launch traced here: 331 us
  waiting for transfers between devices  189 us (57%)
  Pallas kernels  55.3 us (17%)
  blocking collectives  31.8 us (10%)
  starting transfers between devices  21 us (6%)
  between operations  14.2 us (4%)
  other arithmetic  11.6 us (3%)
  local copies, waits for them, and re-layouts  7.88 us (2%)
    all_gather x1, waiting for transfers between devices, gather_plan(): lax.all_gather(normed, ('far', 'line', 'side'), axis=0)  79.4 us
    ppermute x6, waiting for transfers between devices, shift(): lax.ppermute(array, axis, [(i, (i + amount) % size) for i in range(size)])  63.4 us
    ppermute x12, waiting for transfers between devices, swap(): return lax.ppermute(array, axis, [(0, 1), (1, 0)])  46.3 us
    pallas_call x2, Pallas kernels, run_experts(): pl.pallas_call(lambda *refs: experts_kernel(capacity, *refs), grid_spec=p...  42.4 us
    all_gather x1, blocking collectives, on_device(): lax.all_gather(jnp.concatenate([routes.T.astype(jnp.float32), route_weigh...  31.8 us
    ppermute x12, starting transfers between devices, swap(): return lax.ppermute(array, axis, [(0, 1), (1, 0)])  11.9 us
    convert_element_type x5, other arithmetic, add(): return sum((one.astype(jnp.float32) for one in arrays)).astype(jnp.bfloat16)  11.1 us
    ppermute x6, starting transfers between devices, shift(): lax.ppermute(array, axis, [(i, (i + amount) % size) for i in range(size)])  9.12 us
  transfers between devices with their start and end apart: 19, of which 12 were waited for; matrix products, arithmetic and copies ran while one was open for 3% of the time, Pallas kernels for 8%

profile of v2, /device:TPU:9, one launch (start us, length us, event | category | flops | bytes accessed | tf_op | source)
XLA Modules:
  0.0 331.1 jit_solution(15708421161330088297)
XLA Ops:
  7.2 0.9 constant_dynamic-update-slice_fusion.1
  8.1 0.9 constant_dynamic-update-slice_fusion.refs_0_
  9.1 1.3 collective-permute-start
  10.4 1.1 collective-permute-start.1
  11.5 1.4 collective-permute-start.2
  12.9 1.2 collective-permute-start.3
  14.1 2.2 collective-permute-done.refs_1_
  16.3 1.2 collective-permute-start.4
  17.5 14.7 %collective-permute-done.1.refs_2_ = bf16[2,32,2048]{2,1,0:T(8,128)(2,1)S(1)} collective-permute-done((bf16[2,32,2048]{2,1,0:T(8,128)(2,1)S(1)}, bf16[2,32,2048]{2,1,0:T(8,128)(2,1)S(1)}, u32[]{:S(2)}, u32[]{:S(2)}) %collective-permute-start.1) | collective-permute-done | bytes 262176 | tf_op jit(solution)/shard_map/ppermute | solution.py:265
  32.2 1.2 collective-permute-start.5
  33.5 1.6 collective-permute-done.2.refs_3_
  35.1 1.2 collective-permute-start.6
  36.3 2.8 collective-permute-done.5.refs_6_
  39.2 5.6 %collective-permute-done.6.refs_7_ = bf16[2,32,2048]{2,1,0:T(8,128)(2,1)S(1)} collective-permute-done((bf16[2,32,2048]{2,1,0:T(8,128)(2,1)S(1)}, bf16[2,32,2048]{2,1,0:T(8,128)(2,1)S(1)}, u32[]{:S(2)}, u32[]{:S(2)}) %collective-permute-start.6) | collective-permute-done | bytes 262176 | tf_op jit(solution)/shard_map/ppermute | solution.py:260
  44.8 0.7 copy-done.5
  45.5 6.6 %attention.1.heads_ref = bf16[128,2048]{1,0:T(8,128)(2,1)} custom-call(bf16[128,2048]{1,0:T(8,128)(2,1)} %q_ref.1, bf16[128,2048]{1,0:T(8,128)(2,1)} %sk_ref.1, bf16[128,2048]{1,0:T(8,128)(2,1)} %sv_ref.1, bf16[2,32,2048]{2,1,0:T(8,128)(2,1)S(1)} %constant_dynamic-update-slice_fusion.refs_0_, bf16[2,32,2048]{2,1,0:T(8,128)(2,1)S(1)} %collective-permute-done.refs_1_, ...), custom_call_target="tpu_custom_call" | custom-call | tf_op jit(solution)/shard_map/attention/pallas_call | solution.py:59
  52.2 1.0 copy-done
  53.2 6.2 %project_and_norm.1 = (bf16[128,2048]{1,0:T(8,128)(2,1)}, bf16[128,2048]{1,0:T(8,128)(2,1)}) custom-call(bf16[128,2048]{1,0:T(8,128)(2,1)S(1)} %copy-done, bf16[2048,2048]{1,0:T(8,128)(2,1)} %weight_ref.1, bf16[128,2048]{1,0:T(8,128)(2,1)S(1)} %copy-done.1, f32[1,2048]{1,0:T(1,128)S(1)} %bitcast.55), custom_call_target="tpu_custom_call" | custom-call | tf_op jit(solution)/shard_map/project_and_norm/pallas_call | solution.py:97
  59.4 2.2 collective-permute-start.7
  61.7 31.8 %all-gather.2 = f32[16,12,128]{2,1,0:T(8,128)S(1)} all-gather(f32[1,12,128]{2,1,0:T(8,128)S(1)} %maximum_bitcast_fusion), channel_id=3, replica_groups=mesh['far'=2,'core'=2,'line'=4,'side'=2] {'far','line','side'}, dimensions={0}, use_global_device_ids=true | all-gather | bytes 104448 | tf_op jit(solution)/shard_map/all_gather | solution.py:340
  94.0 0.1 fusion.7
  94.2 79.4 %all-gather.5.cloned.1.call-done = bf16[2048,2048]{1,0:T(8,128)(2,1)} async-done(((bf16[128,2048]{1,0:T(8,128)(2,1)}), bf16[2048,2048]{1,0:T(8,128)(2,1)}) %all-gather.5.cloned.1.call-update) | async-done | bytes 8388624 | tf_op jit(solution)/shard_map/all_gather | solution.py:284
  173.6 14.5 %experts.3 = (bf16[1,512,1024]{2,1,0:T(8,128)(2,1)S(1)}, bf16[1,512,1024]{2,1,0:T(8,128)(2,1)}) custom-call(s32[1,2]{1,0:T(1,128)S(1)} %get-tuple-element.22.refs_0_, bf16[2,4,2,128,2048]{4,3,2,1,0:T(8,128)(2,1)} %bitcast.59, s32[2,4,2,2,1,128]{5,4,3,2,1,0:T(1,128)S(1)} %pad_add_fusion.refs_2_, f32[2,4,2,2,1,128]{5,4,3,2,1,0:T(1,128)S(1)} %pad_maximum_fusion.1.refs_3_, ...), custom_call_target="tpu_custom_call" | custom-call | flops 4429185024 | bytes 21495808 | tf_op jit(solution)/shard_map/experts/pallas_call | solution.py:185
  188.1 1.2 collective-permute-start.10
  189.3 0.3 collective-permute-start.13
  189.5 28.0 %experts.2 = (bf16[3,512,1024]{2,1,0:T(8,128)(2,1)}, bf16[3,512,1024]{2,1,0:T(8,128)(2,1)}) custom-call(s32[3,2]{1,0:T(4,128)S(1)} %pad_add_fusion.1.refs_0_, bf16[2,4,2,128,2048]{4,3,2,1,0:T(8,128)(2,1)} %bitcast.60, s32[2,4,2,2,1,128]{5,4,3,2,1,0:T(1,128)S(1)} %pad_add_fusion.refs_2_, f32[2,4,2,2,1,128]{5,4,3,2,1,0:T(1,128)S(1)} %pad_maximum_fusion.1.refs_3_, ...), custom_call_target="tpu_custom_call" | custom-call | flops 13287555072 | bytes 29884416 | tf_op jit(solution)/shard_map/experts/pallas_call | solution.py:185
  217.5 2.3 slice_bitcast_fusion.1
  219.8 1.0 collective-permute-start.9
  220.8 2.6 fusion.3
  223.4 0.6 collective-permute-start.11
  224.0 1.1 slice_bitcast_fusion
  225.1 0.8 collective-permute-start.12
  225.9 1.4 fusion
  227.3 0.7 collective-permute-start.14
  228.0 14.5 %collective-permute-done.9 = bf16[512,1024]{1,0:T(8,128)(2,1)} collective-permute-done((bf16[512,1024]{1,0:T(8,128)(2,1)}, bf16[512,1024]{1,0:T(8,128)(2,1)}, u32[]{:S(2)}, u32[]{:S(2)}) %collective-permute-start.9) | collective-permute-done | bytes 1048608 | tf_op jit(solution)/shard_map/ppermute | solution.py:260
  242.5 3.3 %collective-permute-done.11 = bf16[512,1024]{1,0:T(8,128)(2,1)} collective-permute-done((bf16[512,1024]{1,0:T(8,128)(2,1)}, bf16[512,1024]{1,0:T(8,128)(2,1)}, u32[]{:S(2)}, u32[]{:S(2)}) %collective-permute-start.11) | collective-permute-done | bytes 1048608 | tf_op jit(solution)/shard_map/ppermute | solution.py:260
  245.8 2.5 fusion.5
  248.3 20.0 %collective-permute-done.12 = bf16[512,1024]{1,0:T(8,128)(2,1)} collective-permute-done((bf16[512,1024]{1,0:T(8,128)(2,1)}, bf16[512,1024]{1,0:T(8,128)(2,1)}, u32[]{:S(2)}, u32[]{:S(2)}) %collective-permute-start.12) | collective-permute-done | bytes 1048608 | tf_op jit(solution)/shard_map/ppermute | solution.py:260
  268.3 2.2 fusion.2
  270.4 0.2 pad_maximum_fusion
  270.6 1.0 dynamic-slice_bitcast_fusion.2
  271.6 2.7 collective-permute-start.15
  274.3 1.3 collective-permute-start.16
  275.6 1.3 collective-permute-start.17
  276.9 6.8 %collective-permute-done.15 = bf16[128,2048]{1,0:T(8,128)(2,1)} collective-permute-done((bf16[128,2048]{1,0:T(8,128)(2,1)}, bf16[128,2048]{1,0:T(8,128)(2,1)}, u32[]{:S(2)}, u32[]{:S(2)}) %collective-permute-start.15) | collective-permute-done | bytes 524320 | tf_op jit(solution)/shard_map/ppermute | solution.py:265
  283.7 32.9 %collective-permute-done.16 = bf16[128,2048]{1,0:T(8,128)(2,1)} collective-permute-done((bf16[128,2048]{1,0:T(8,128)(2,1)S(1)}, bf16[128,2048]{1,0:T(8,128)(2,1)}, u32[]{:S(2)}, u32[]{:S(2)}) %collective-permute-start.16) | collective-permute-done | bytes 524320 | tf_op jit(solution)/shard_map/ppermute | solution.py:265
  316.6 5.2 %collective-permute-done.17 = bf16[128,2048]{1,0:T(8,128)(2,1)} collective-permute-done((bf16[128,2048]{1,0:T(8,128)(2,1)S(1)}, bf16[128,2048]{1,0:T(8,128)(2,1)}, u32[]{:S(2)}, u32[]{:S(2)}) %collective-permute-start.17) | collective-permute-done | bytes 524320 | tf_op jit(solution)/shard_map/ppermute | solution.py:265
  321.8 2.5 fusion.12
  (35 shorter events, 0.7 us)
Async XLA Ops:
  7.2 166.4 %all-gather.5.cloned.1.call-start = ((), (), s32[]{:S(2)}) async-start(), calls=%async_computation | async-start | bytes 8912896 | tf_op jit(solution)/shard_map/all_gather | solution.py:284
  9.0 43.1 %copy-start.1 = (bf16[128,2048]{1,0:T(8,128)(2,1)S(1)}, bf16[128,2048]{1,0:T(8,128)(2,1)}, u32[]{:S(2)}) copy-start(bf16[128,2048]{1,0:T(8,128)(2,1)} %tokens_ref.1) | copy-start | bytes 1572868
  9.1 43.1 %copy-start.2 = (f32[2048]{0:T(1024)S(1)}, f32[2048]{0:T(1024)}, u32[]{:S(2)}) copy-start(f32[2048]{0:T(1024)} %param.19) | copy-start | bytes 24580
  9.1 7.2 %collective-permute-start = (bf16[2,32,2048]{2,1,0:T(8,128)(2,1)S(1)}, bf16[2,32,2048]{2,1,0:T(8,128)(2,1)S(1)}, u32[]{:S(2)}, u32[]{:S(2)}) collective-permute-start(bf16[2,32,2048]{2,1,0:T(8,128)(2,1)S(1)} %constant_dynamic-update-slice_fusion.refs_0_), channel_id=1, source_target_pairs={{0,2},{2,4},{4,6},{6,0},{1,3},{3,5},{5,7},{7,1},{8,10},{10,12},{12... | collective-permute-start | bytes 786440 | tf_op jit(solution)/shard_map/ppermute | solution.py:265
  10.4 21.8 %collective-permute-start.1 = (bf16[2,32,2048]{2,1,0:T(8,128)(2,1)S(1)}, bf16[2,32,2048]{2,1,0:T(8,128)(2,1)S(1)}, u32[]{:S(2)}, u32[]{:S(2)}) collective-permute-start(bf16[2,32,2048]{2,1,0:T(8,128)(2,1)S(1)} %constant_dynamic-update-slice_fusion.refs_0_), channel_id=1, source_target_pairs={{0,4},{2,6},{4,0},{6,2},{1,5},{3,7},{5,1},{7,3},{8,12},{10,14},{12... | collective-permute-start | bytes 786440 | tf_op jit(solution)/shard_map/ppermute | solution.py:265
  11.5 23.6 %collective-permute-start.2 = (bf16[2,32,2048]{2,1,0:T(8,128)(2,1)S(1)}, bf16[2,32,2048]{2,1,0:T(8,128)(2,1)S(1)}, u32[]{:S(2)}, u32[]{:S(2)}) collective-permute-start(bf16[2,32,2048]{2,1,0:T(8,128)(2,1)S(1)} %constant_dynamic-update-slice_fusion.refs_0_), channel_id=1, source_target_pairs={{0,6},{2,0},{4,2},{6,4},{1,7},{3,1},{5,3},{7,5},{8,14},{10,8},{12,... | collective-permute-start | bytes 786440 | tf_op jit(solution)/shard_map/ppermute | solution.py:265
  12.9 23.4 %collective-permute-start.3 = (bf16[2,32,2048]{2,1,0:T(8,128)(2,1)S(1)}, bf16[2,32,2048]{2,1,0:T(8,128)(2,1)S(1)}, u32[]{:S(2)}, u32[]{:S(2)}) collective-permute-start(bf16[2,32,2048]{2,1,0:T(8,128)(2,1)S(1)} %constant_dynamic-update-slice_fusion.refs_0_), channel_id=1, source_target_pairs={{0,1},{1,0},{2,3},{3,2},{4,5},{5,4},{6,7},{7,6},{8,9},{9,8},{10,11... | collective-permute-start | bytes 786440 | tf_op jit(solution)/shard_map/ppermute | solution.py:260
  16.3 20.0 %collective-permute-start.4 = (bf16[2,32,2048]{2,1,0:T(8,128)(2,1)S(1)}, bf16[2,32,2048]{2,1,0:T(8,128)(2,1)S(1)}, u32[]{:S(2)}, u32[]{:S(2)}) collective-permute-start(bf16[2,32,2048]{2,1,0:T(8,128)(2,1)S(1)} %collective-permute-done.refs_1_), channel_id=1, source_target_pairs={{0,1},{1,0},{2,3},{3,2},{4,5},{5,4},{6,7},{7,6},{8,9},{9,8},{10,11... | collective-permute-start | bytes 786440 | tf_op jit(solution)/shard_map/ppermute | solution.py:260
  32.2 6.9 %collective-permute-start.5 = (bf16[2,32,2048]{2,1,0:T(8,128)(2,1)S(1)}, bf16[2,32,2048]{2,1,0:T(8,128)(2,1)S(1)}, u32[]{:S(2)}, u32[]{:S(2)}) collective-permute-start(bf16[2,32,2048]{2,1,0:T(8,128)(2,1)S(1)} %collective-permute-done.1.refs_2_), channel_id=1, source_target_pairs={{0,1},{1,0},{2,3},{3,2},{4,5},{5,4},{6,7},{7,6},{8,9},{9,8},{10,11... | collective-permute-start | bytes 786440 | tf_op jit(solution)/shard_map/ppermute | solution.py:260
  35.1 9.7 %collective-permute-start.6 = (bf16[2,32,2048]{2,1,0:T(8,128)(2,1)S(1)}, bf16[2,32,2048]{2,1,0:T(8,128)(2,1)S(1)}, u32[]{:S(2)}, u32[]{:S(2)}) collective-permute-start(bf16[2,32,2048]{2,1,0:T(8,128)(2,1)S(1)} %collective-permute-done.2.refs_3_), channel_id=1, source_target_pairs={{0,1},{1,0},{2,3},{3,2},{4,5},{5,4},{6,7},{7,6},{8,9},{9,8},{10,11... | collective-permute-start | bytes 786440 | tf_op jit(solution)/shard_map/ppermute | solution.py:260
  44.8 0.7 copy-start.5
  52.2 1.0 copy-start
  53.2 8.4 %copy-start.4 = (bf16[1,704,2048]{2,1,0:T(8,128)(2,1)S(1)}, bf16[1,704,2048]{2,1,0:T(8,128)(2,1)}, u32[]{:S(2)}) copy-start(bf16[1,704,2048]{2,1,0:T(8,128)(2,1)} %param.23) | copy-start | bytes 8650756
  53.2 8.5 %copy-start.6 = (s32[128,6]{0,1:T(8,128)S(1)}, s32[128,6]{0,1:T(8,128)}, u32[]{:S(2)}) copy-start(s32[128,6]{0,1:T(8,128)} %param.20) | copy-start | bytes 9220
  53.2 8.5 %copy-start.7 = (f32[128,6]{0,1:T(8,128)S(1)}, f32[128,6]{0,1:T(8,128)}, u32[]{:S(2)}) copy-start(f32[128,6]{0,1:T(8,128)} %param.21) | copy-start | bytes 9220
  59.4 34.8 %collective-permute-start.7 = (bf16[2048,1408]{1,0:T(8,128)(2,1)}, bf16[2048,1408]{1,0:T(8,128)(2,1)}, u32[]{:S(2)}, u32[]{:S(2)}) collective-permute-start(bf16[2048,1408]{1,0:T(8,128)(2,1)} %bitcast.61), channel_id=1, source_target_pairs={{0,8},{8,0},{1,9},{9,1},{2,10},{10,2},{3,11},{11,3},{4,12},{12,4},... | collective-permute-start | bytes 17301512 | tf_op jit(solution)/shard_map/ppermute | solution.py:260
  61.6 32.6 %collective-permute-start.8 = (bf16[704,2048]{1,0:T(8,128)(2,1)S(1)}, bf16[704,2048]{1,0:T(8,128)(2,1)}, u32[]{:S(2)}, u32[]{:S(2)}) collective-permute-start(bf16[704,2048]{1,0:T(8,128)(2,1)S(1)} %bitcast.66), channel_id=1, source_target_pairs={{0,8},{8,0},{1,9},{9,1},{2,10},{10,2},{3,11},{11,3},{4,12},{12,4},... | collective-permute-start | bytes 8650760 | tf_op jit(solution)/shard_map/ppermute | solution.py:260
  188.1 32.7 %collective-permute-start.10 = (bf16[512,1024]{1,0:T(8,128)(2,1)S(1)}, bf16[512,1024]{1,0:T(8,128)(2,1)S(1)}, u32[]{:S(2)}, u32[]{:S(2)}) collective-permute-start(bf16[512,1024]{1,0:T(8,128)(2,1)S(1)} %bitcast.56), channel_id=1, source_target_pairs={{0,1},{1,0},{2,3},{3,2},{4,5},{5,4},{6,7},{7,6},{8,9},{9,8},{10,11... | collective-permute-start | bytes 3145736 | tf_op jit(solution)/shard_map/ppermute | solution.py:260
  189.3 36.7 %collective-permute-start.13 = (bf16[512,1024]{1,0:T(8,128)(2,1)}, bf16[512,1024]{1,0:T(8,128)(2,1)S(1)}, u32[]{:S(2)}, u32[]{:S(2)}) collective-permute-start(bf16[512,1024]{1,0:T(8,128)(2,1)} %bitcast.72), channel_id=1, source_target_pairs={{0,16},{16,0},{1,17},{17,1},{2,18},{18,2},{3,19},{19,3},{4,20},{20... | collective-permute-start | bytes 3145736 | tf_op jit(solution)/shard_map/ppermute | solution.py:260
  219.8 4.2 %copy-start.3 = (bf16[3,512,1024]{2,1,0:T(8,128)(2,1)S(1)}, bf16[3,512,1024]{2,1,0:T(8,128)(2,1)}, u32[]{:S(2)}) copy-start(bf16[3,512,1024]{2,1,0:T(8,128)(2,1)} %get-tuple-element.12) | copy-start | bytes 9437188
  219.8 22.7 %collective-permute-start.9 = (bf16[512,1024]{1,0:T(8,128)(2,1)}, bf16[512,1024]{1,0:T(8,128)(2,1)}, u32[]{:S(2)}, u32[]{:S(2)}) collective-permute-start(bf16[512,1024]{1,0:T(8,128)(2,1)} %slice_bitcast_fusion.1), channel_id=1, source_target_pairs={{0,1},{1,0},{2,3},{3,2},{4,5},{5,4},{6,7},{7,6},{8,9},{9,8},{10,11... | collective-permute-start | bytes 3145736 | tf_op jit(solution)/shard_map/ppermute | solution.py:260
  223.4 22.4 %collective-permute-start.11 = (bf16[512,1024]{1,0:T(8,128)(2,1)}, bf16[512,1024]{1,0:T(8,128)(2,1)}, u32[]{:S(2)}, u32[]{:S(2)}) collective-permute-start(bf16[512,1024]{1,0:T(8,128)(2,1)} %fusion.3), channel_id=1, source_target_pairs={{0,16},{16,0},{1,17},{17,1},{2,18},{18,2},{3,19},{19,3},{4,20},{20... | collective-permute-start | bytes 3145736 | tf_op jit(solution)/shard_map/ppermute | solution.py:260
  225.1 43.2 %collective-permute-start.12 = (bf16[512,1024]{1,0:T(8,128)(2,1)}, bf16[512,1024]{1,0:T(8,128)(2,1)}, u32[]{:S(2)}, u32[]{:S(2)}) collective-permute-start(bf16[512,1024]{1,0:T(8,128)(2,1)} %slice_bitcast_fusion), channel_id=1, source_target_pairs={{0,16},{16,0},{1,17},{17,1},{2,18},{18,2},{3,19},{19,3},{4,20},{20... | collective-permute-start | bytes 3145736 | tf_op jit(solution)/shard_map/ppermute | solution.py:260
  227.3 41.0 %collective-permute-start.14 = (bf16[512,1024]{1,0:T(8,128)(2,1)}, bf16[512,1024]{1,0:T(8,128)(2,1)}, u32[]{:S(2)}, u32[]{:S(2)}) collective-permute-start(bf16[512,1024]{1,0:T(8,128)(2,1)} %fusion), channel_id=1, source_target_pairs={{0,1},{1,0},{2,3},{3,2},{4,5},{5,4},{6,7},{7,6},{8,9},{9,8},{10,11... | collective-permute-start | bytes 3145736 | tf_op jit(solution)/shard_map/ppermute | solution.py:260
  271.6 12.1 %collective-permute-start.15 = (bf16[128,2048]{1,0:T(8,128)(2,1)}, bf16[128,2048]{1,0:T(8,128)(2,1)}, u32[]{:S(2)}, u32[]{:S(2)}) collective-permute-start(bf16[128,2048]{1,0:T(8,128)(2,1)} %get-tuple-element.18), channel_id=1, source_target_pairs={{0,2},{2,4},{4,6},{6,0},{1,3},{3,5},{5,7},{7,1},{8,10},{10,12},{12... | collective-permute-start | bytes 1572872 | tf_op jit(solution)/shard_map/ppermute | solution.py:265
  274.3 42.3 %collective-permute-start.16 = (bf16[128,2048]{1,0:T(8,128)(2,1)S(1)}, bf16[128,2048]{1,0:T(8,128)(2,1)}, u32[]{:S(2)}, u32[]{:S(2)}) collective-permute-start(bf16[128,2048]{1,0:T(8,128)(2,1)S(1)} %get-tuple-element.20), channel_id=1, source_target_pairs={{0,4},{2,6},{4,0},{6,2},{1,5},{3,7},{5,1},{7,3},{8,12},{10,14},{12... | collective-permute-start | bytes 1572872 | tf_op jit(solution)/shard_map/ppermute | solution.py:265
  275.6 46.2 %collective-permute-start.17 = (bf16[128,2048]{1,0:T(8,128)(2,1)S(1)}, bf16[128,2048]{1,0:T(8,128)(2,1)}, u32[]{:S(2)}, u32[]{:S(2)}) collective-permute-start(bf16[128,2048]{1,0:T(8,128)(2,1)S(1)} %get-tuple-element.19), channel_id=1, source_target_pairs={{0,6},{2,0},{4,2},{6,4},{1,7},{3,1},{5,3},{7,5},{8,14},{10,8},{12,... | collective-permute-start | bytes 1572872 | tf_op jit(solution)/shard_map/ppermute | solution.py:265
Sparse Core Ops, SparseCore 0:
  59.6 113.9 all-gather.4

commit v3 on v2

--- a/solution.py
+++ b/solution.py
@@ -14,6 +14,7 @@
 ALL = ("far", "core", "line", "side")
 GATHER_BUDGET = 40 * 2**20
 VMEM_LIMIT = 52 * 2**20
+EXPERT_VMEM = 36 * 2**20
 
 
 def attention_kernel(q_ref, sk_ref, sv_ref, *refs):
@@ -114,96 +115,80 @@
     )(heads_out, out_weight, tokens, norm_gain.reshape(1, width))
 
 
-def experts_kernel(
-    capacity,
-    place_ref,
-    rows_ref,
-    slot_ref,
-    gate_ref,
-    own_up_ref,
-    own_down_ref,
-    other_up_ref,
-    other_down_ref,
-    first_ref,
-    second_ref,
-    picked,
-    scaled,
-):
-    requests = rows_ref.shape[1]
-    rows = rows_ref.shape[3]
-    hidden = own_down_ref.shape[0]
-    half = first_ref.shape[2]
+def experts_kernel(capacity, count, slot_ref, gate_ref, *refs):
+    rows_refs, refs = refs[:count], refs[count:]
+    weight_refs, refs = refs[:4], refs[4:]
+    out_refs, refs = refs[:count], refs[count:]
+    picked, scaled, held, arrived = refs[0], refs[1], refs[2:6], refs[6]
+    copies = [
+        pltpu.make_async_copy(source, target, arrived.at[i])
+        for i, (source, target) in enumerate(zip(weight_refs, held))
+    ]
+    for copy in copies:
+        copy.start()
+    rows = rows_refs[0].shape[0]
+    hidden = held[1].shape[0]
     levels = lax.broadcasted_iota(jnp.int32, (2 * capacity, rows), 0)
-    for one in range(requests):
-        chosen = (levels == slot_ref[0, one, 0, 0]) | (levels == slot_ref[0, one, 0, 1])
+    for one in range(count):
+        chosen = (levels == slot_ref[one, 0]) | (levels == slot_ref[one, 1])
         taken = jnp.dot(
-            chosen.astype(jnp.bfloat16), rows_ref[0, one, 0], preferred_element_type=jnp.float32
+            chosen.astype(jnp.bfloat16), rows_refs[one][...], preferred_element_type=jnp.float32
         ).astype(jnp.bfloat16)
         picked[0, one * capacity : (one + 1) * capacity, :] = taken[:capacity]
         picked[1, one * capacity : (one + 1) * capacity, :] = taken[capacity:]
-    for which, (up_ref, down_ref) in enumerate(
-        [(own_up_ref, own_down_ref), (other_up_ref, other_down_ref)]
-    ):
-        projected = jnp.dot(picked[which], up_ref[...], preferred_element_type=jnp.float32)
+    for which in range(2):
+        low = which * capacity
+        copies[2 * which].wait()
+        projected = jnp.dot(
+            picked[which], held[2 * which][...], preferred_element_type=jnp.float32
+        )
         gate = projected[:, :hidden]
         active = (gate / (1.0 + jnp.exp(-gate)) * projected[:, hidden:]).astype(jnp.bfloat16)
-        result = jnp.dot(active, down_ref[...], preferred_element_type=jnp.float32)
-        for one in range(requests):
-            low = which * capacity
-            chosen = levels[low : low + capacity] == slot_ref[0, one, 0, which]
+        copies[2 * which + 1].wait()
+        result = jnp.dot(active, held[2 * which + 1][...], preferred_element_type=jnp.float32)
+        for one in range(count):
+            chosen = levels[low : low + capacity] == slot_ref[one, which]
             gates = jnp.sum(
-                jnp.where(chosen, gate_ref[0, one, 0, which], 0.0), axis=1, keepdims=True
+                jnp.where(chosen, gate_ref[one, which], 0.0), axis=1, keepdims=True
             )
             scaled[one, low : low + capacity, :] = (
                 result[one * capacity : (one + 1) * capacity, :] * gates
             ).astype(jnp.bfloat16)
-    for one in range(requests):
-        chosen = (levels == slot_ref[0, one, 0, 0]) | (levels == slot_ref[0, one, 0, 1])
-        summed = lax.dot_general(
+    for one in range(count):
+        chosen = (levels == slot_ref[one, 0]) | (levels == slot_ref[one, 1])
+        out_refs[one][...] = lax.dot_general(
             chosen.astype(jnp.bfloat16),
             scaled[one],
             (((0,), (0,)), ((), ())),
             preferred_element_type=jnp.float32,
         ).astype(jnp.bfloat16)
-        first_ref[0, one * rows : (one + 1) * rows, :] = summed[:, :half]
-        second_ref[0, one * rows : (one + 1) * rows, :] = summed[:, half:]
-
-
-def run_experts(gathered, slots, gates, weights, offsets, capacity):
-    layers, requests, _, rows, width = gathered.shape
-    steps = offsets.shape[0]
-    half = width // 2
-    blocks = lambda i, place: (place[i, 0], 0, place[i, 1], 0, 0)
-    table = pl.BlockSpec((1, requests, 1, 2, 1, rows), lambda i, place: blocks(i, place) + (0,))
-    whole = [
-        pl.BlockSpec(one.shape, lambda i, place: (0, 0), pipeline_mode=pl.Buffered(1))
-        for one in weights
-    ]
-    part = pl.BlockSpec((1, requests * rows, half), lambda i, place: (i, 0, 0))
-    slots_in_step = 2 * requests * capacity
+
+
+def run_experts(blocks, slots, gates, weights, capacity):
+    count = len(blocks)
+    rows, width = blocks[0].shape
     hidden = weights[1].shape[0]
+    total = 2 * count * capacity
+    local = pl.BlockSpec(memory_space=pltpu.VMEM)
     return pl.pallas_call(
-        lambda *refs: experts_kernel(capacity, *refs),
-        grid_spec=pltpu.PrefetchScalarGridSpec(
-            num_scalar_prefetch=1,
-            grid=(steps,),
-            in_specs=[pl.BlockSpec((1, requests, 1, rows, width), blocks), table, table] + whole,
-            out_specs=[part, part],
-            scratch_shapes=[
-                pltpu.VMEM((2, requests * capacity, width), jnp.bfloat16),
-                pltpu.VMEM((requests, 2 * capacity, width), jnp.bfloat16),
-            ],
-        ),
-        out_shape=[jax.ShapeDtypeStruct((steps, requests * rows, half), jnp.bfloat16)] * 2,
-        compiler_params=pltpu.CompilerParams(vmem_limit_bytes=VMEM_LIMIT),
+        lambda *refs: experts_kernel(capacity, count, *refs),
+        in_specs=[local] * (2 + count) + [pl.BlockSpec(memory_space=pl.ANY)] * 4,
+        out_specs=[local] * count,
+        out_shape=[jax.ShapeDtypeStruct((rows, width), jnp.bfloat16)] * count,
+        scratch_shapes=[
+            pltpu.VMEM((2, count * capacity, width), jnp.bfloat16),
+            pltpu.VMEM((count, 2 * capacity, width), jnp.bfloat16),
+        ]
+        + [pltpu.VMEM(one.shape, jnp.bfloat16) for one in weights]
+        + [pltpu.SemaphoreType.DMA((4,))],
+        compiler_params=pltpu.CompilerParams(vmem_limit_bytes=EXPERT_VMEM),
         cost_estimate=pl.CostEstimate(
-            flops=steps * slots_in_step * width * hidden * 6,
-            bytes_accessed=sum(one.size * 2 for one in weights)
-            + steps * requests * rows * width * 4,
-            transcendentals=steps * slots_in_step * hidden,
+            flops=total * width * hidden * 6,
+            bytes_accessed=sum(one.size * 2 for one in weights) + count * rows * width * 4,
+            transcendentals=total * hidden,
         ),
         name="experts",
-    )(offsets, gathered, slots, gates, *weights)
+    )(slots, gates, *blocks, *weights)
 
 
 def half_expert(rows, gate_up, down_proj):
@@ -269,47 +254,49 @@
     return sum(one.astype(jnp.float32) for one in arrays).astype(jnp.bfloat16)
 
 
-def gather_plan(normed, table, weights, capacity):
-    rows, width = normed.shape
-    layers, columns = lax.axis_size("far"), lax.axis_size("line")
+def relative_slots(table, capacity):
+    columns = lax.axis_size("line")
     far, core = lax.axis_index("far"), lax.axis_index("core")
     line, side = lax.axis_index("line"), lax.axis_index("side")
+    places = jnp.arange(4 * columns)
+    back, across, beside = places // 4, places // 2 % 2, places % 2
+    source = ((far ^ across) * columns + (line - back + columns) % columns) * 2 + (side ^ beside)
+    table = table[source]
     own = (far * 2 + core) * columns + line
     other = (far * 2 + 1 - core) * columns + line
     own_slot, own_gate = own_slots(table, own, 0)
     other_slot, other_gate = own_slots(table, other, capacity)
-    shape = (layers, columns, 2, 2, 1, rows)
+    shape = (columns, 4, 2, 1, -1)
     slots = jnp.stack([own_slot, other_slot], axis=1).reshape(shape)
     gates = jnp.stack([own_gate, other_gate], axis=1).reshape(shape)
-    gathered = lax.all_gather(normed, ("far", "line", "side"), axis=0).reshape(
-        layers, columns, 2, rows, width
-    )
-    place = lambda a, b: jnp.stack([far ^ a, side ^ b])
-    first = run_experts(
-        gathered, slots, gates, weights, jnp.stack([place(1, 1)]).astype(jnp.int32), capacity
-    )
-    rest = run_experts(
-        gathered,
-        slots,
-        gates,
-        weights,
-        jnp.stack([place(0, 1), place(1, 0), place(0, 0)]).astype(jnp.int32),
-        capacity,
-    )
-    a_corner = swap(first[0][0], "side")
-    b_corner = swap(first[1][0], "far")
-    a_side = swap(rest[0][0], "side")
-    b_far = swap(rest[1][1], "far")
-    a_far = swap(add(rest[0][1], a_corner), "far")
-    b_side = swap(add(rest[1][0], b_corner), "side")
-    total = jnp.concatenate(
-        [add(rest[0][2], a_side, a_far), add(rest[1][2], b_far, b_side)], axis=1
-    ).reshape(columns, rows, width)
-    arrived = [
-        shift(lax.dynamic_index_in_dim(total, (line + k) % columns, 0, keepdims=False), "line", k)
-        for k in range(1, columns)
-    ]
-    return add(lax.dynamic_index_in_dim(total, line, 0, keepdims=False), *arrived)
+    return slots, gates
+
+
+def gather_plan(normed, slots, gates, weights, capacity):
+    columns = lax.axis_size("line")
+    arrived = []
+    for back in range(columns):
+        block = shift(normed, "line", back) if back else normed
+        if back % 2 == 0:
+            beside = swap(block, "side")
+            across = swap(block, "far")
+            corner = swap(beside, "far")
+        else:
+            across = swap(block, "far")
+            beside = swap(block, "side")
+            corner = swap(across, "side")
+        results = run_experts(
+            [block, beside, across, corner], slots[back], gates[back], weights, capacity
+        )
+        here, beside, across, corner = results
+        if back % 2 == 0:
+            across = add(across, swap(corner, "side"))
+            total = add(here, swap(beside, "side"), swap(across, "far"))
+        else:
+            beside = add(beside, swap(corner, "far"))
+            total = add(here, swap(across, "far"), swap(beside, "side"))
+        arrived.append(shift(total, "line", -back) if back else total)
+    return add(*arrived)
 
 
 def on_device(
@@ -342,6 +329,8 @@
             ("far", "line", "side"),
             axis=0,
         )
+        slots, gates = relative_slots(table, capacity)
+        queries, slots, gates = lax.optimization_barrier((queries, slots, gates))
     else:
         pieces = [
             lax.all_gather(kv, ("line", "side"), axis=1, tiled=True)
@@ -349,7 +338,7 @@
     heads_out = attention(queries, suffix_keys, suffix_values, pieces)
     attended, normed = project(heads_out, out_weight, tokens, norm_gain)
     if gather_fits:
-        routed = gather_plan(normed, table, weights, capacity)
+        routed = gather_plan(normed, slots, gates, weights, capacity)
     else:
         routed = exchange_plan(
             normed, routes, route_weights, weights[0], weights[1], experts, capacity

time: 332 us -> 297 us (0.89)
  the two profiles are of different devices: /device:TPU:9 before, /device:TPU:26 now
where the time goes in v3:
time: 297 us
  waiting for transfers between devices  151 us (51%)
  starting transfers between devices  46.6 us (16%)
  blocking collectives  44.4 us (15%)
  Pallas kernels  44.1 us (15%)
  local copies, waits for them, and re-layouts  5.05 us (2%)
  other arithmetic  4.1 us (1%)
    ppermute x30, waiting for transfers between devices, swap(): return lax.ppermute(array, axis, [(0, 1), (1, 0)])  91.4 us
    ppermute x9, waiting for transfers between devices, shift(): lax.ppermute(array, axis, [(i, (i + amount) % size) for i in range(size)])  59.9 us
    all_gather x1, blocking collectives, on_device(): lax.all_gather(jnp.concatenate([routes.T.astype(jnp.float32), route_weigh...  44.4 us
    pallas_call x4, Pallas kernels, run_experts(): pl.pallas_call(lambda *refs: experts_kernel(capacity, count, *refs), in_s...  31.2 us
    ppermute x30, starting transfers between devices, swap(): return lax.ppermute(array, axis, [(0, 1), (1, 0)])  27.4 us
    ppermute x9, starting transfers between devices, shift(): lax.ppermute(array, axis, [(i, (i + amount) % size) for i in range(size)])  19.3 us
    pallas_call x1, Pallas kernels, attention(): pl.pallas_call(attention_kernel, grid=(width // span,), in_specs=[by_cols...  6.76 us
    pallas_call x1, Pallas kernels, project(): pl.pallas_call(project_kernel, grid=(steps,), in_specs=[pl.BlockSpec((row...  6.13 us
  transfers between devices with their start and end apart: 39, of which 19 were waited for; matrix products, arithmetic and copies ran while one was open for 2% of the time, Pallas kernels for 15%

profile of v3, /device:TPU:26, one launch (start us, length us, event | category | flops | bytes accessed | tf_op | source)
XLA Modules:
  0.0 296.8 jit_solution(11897202449536843123)
XLA Ops:
  0.7 1.0 constant_dynamic-update-slice_fusion.1
  1.7 0.9 constant_dynamic-update-slice_fusion.refs_0_
  2.9 1.7 collective-permute-start.1
  6.4 44.4 %all-gather.1 = f32[16,12,128]{2,1,0:T(8,128)S(1)} all-gather(f32[1,12,128]{2,1,0:T(8,128)S(1)} %maximum_bitcast_fusion), channel_id=2, replica_groups=mesh['far'=2,'core'=2,'line'=4,'side'=2] {'far','line','side'}, dimensions={0}, use_global_device_ids=true | all-gather | bytes 104448 | tf_op jit(solution)/shard_map/all_gather | solution.py:327
  51.4 2.5 collective-permute-start.3
  54.2 2.0 collective-permute-start.5
  56.3 4.9 %collective-permute-done.3.refs_4_ = bf16[2,32,2048]{2,1,0:T(8,128)(2,1)S(1)} collective-permute-done((bf16[2,32,2048]{2,1,0:T(8,128)(2,1)S(1)}, bf16[2,32,2048]{2,1,0:T(8,128)(2,1)S(1)}, u32[]{:S(2)}, u32[]{:S(2)}) %collective-permute-start.3) | collective-permute-done | bytes 262176 | tf_op jit(solution)/shard_map/ppermute | solution.py:245
  61.2 2.0 collective-permute-start.6
  63.4 2.1 collective-permute-done.4.refs_5_
  65.5 2.8 collective-permute-done.5.refs_6_
  68.3 2.8 collective-permute-done.6.refs_7_
  71.8 6.8 %attention.1.heads_ref = bf16[128,2048]{1,0:T(8,128)(2,1)} custom-call(bf16[128,2048]{1,0:T(8,128)(2,1)} %q_ref, bf16[128,2048]{1,0:T(8,128)(2,1)} %sk_ref.1, bf16[128,2048]{1,0:T(8,128)(2,1)} %sv_ref.1, bf16[2,32,2048]{2,1,0:T(8,128)(2,1)S(1)} %constant_dynamic-update-slice_fusion.refs_0_, bf16[2,32,2048]{2,1,0:T(8,128)(2,1)S(1)} %collective-permute-done.refs_1_, ...), custom_call_target="tpu_custom_call" | custom-call | tf_op jit(solution)/shard_map/attention/pallas_call | solution.py:60
  78.6 1.2 copy-done.1
  80.5 6.1 %project_and_norm.1 = (bf16[128,2048]{1,0:T(8,128)(2,1)}, bf16[128,2048]{1,0:T(8,128)(2,1)S(1)}) custom-call(bf16[128,2048]{1,0:T(8,128)(2,1)S(1)} %copy-done.1, bf16[2048,2048]{1,0:T(8,128)(2,1)} %weight_ref.1, bf16[128,2048]{1,0:T(8,128)(2,1)S(1)} %copy-done.2, f32[1,2048]{1,0:T(1,128)S(1)} %bitcast.56), custom_call_target="tpu_custom_call" | custom-call | tf_op jit(solution)/shard_map/project_and_norm/pallas_call | solution.py:98
  86.6 6.2 %collective-permute-start.23 = (bf16[128,2048]{1,0:T(8,128)(2,1)S(1)}, bf16[128,2048]{1,0:T(8,128)(2,1)S(1)}, u32[]{:S(2)}, u32[]{:S(2)}) collective-permute-start(bf16[128,2048]{1,0:T(8,128)(2,1)S(1)} %get-tuple-element.27.refs_2_), channel_id=1, source_target_pairs={{0,4},{2,6},{4,0},{6,2},{1,5},{3,7},{5,1},{7,3},{8,12},{10,14},{12... | collective-permute-start | bytes 1572872 | tf_op jit(solution)/shard_map/ppermute | solution.py:250
  92.8 12.3 %collective-permute-done.31.refs_2_ = bf16[128,2048]{1,0:T(8,128)(2,1)S(1)} collective-permute-done((bf16[128,2048]{1,0:T(8,128)(2,1)S(1)}, bf16[128,2048]{1,0:T(8,128)(2,1)S(1)}, u32[]{:S(2)}, u32[]{:S(2)}) %collective-permute-start.31) | collective-permute-done | bytes 524320 | tf_op jit(solution)/shard_map/ppermute | solution.py:250
  105.4 14.7 %collective-permute-done.23.refs_2_ = bf16[128,2048]{1,0:T(8,128)(2,1)S(1)} collective-permute-done((bf16[128,2048]{1,0:T(8,128)(2,1)S(1)}, bf16[128,2048]{1,0:T(8,128)(2,1)S(1)}, u32[]{:S(2)}, u32[]{:S(2)}) %collective-permute-start.23) | collective-permute-done | bytes 524320 | tf_op jit(solution)/shard_map/ppermute | solution.py:250
  120.2 0.8 collective-permute-start.33
  121.6 1.2 collective-permute-start.17
  122.8 12.2 %collective-permute-done.33.refs_4_ = bf16[128,2048]{1,0:T(8,128)(2,1)S(1)} collective-permute-done((bf16[128,2048]{1,0:T(8,128)(2,1)S(1)}, bf16[128,2048]{1,0:T(8,128)(2,1)S(1)}, u32[]{:S(2)}, u32[]{:S(2)}) %collective-permute-start.33) | collective-permute-done | bytes 524320 | tf_op jit(solution)/shard_map/ppermute | solution.py:245
  135.6 1.5 collective-permute-start.7
  137.0 8.2 %collective-permute-done.17.refs_4_ = bf16[128,2048]{1,0:T(8,128)(2,1)S(1)} collective-permute-done((bf16[128,2048]{1,0:T(8,128)(2,1)S(1)}, bf16[128,2048]{1,0:T(8,128)(2,1)S(1)}, u32[]{:S(2)}, u32[]{:S(2)}) %collective-permute-start.17) | collective-permute-done | bytes 524320 | tf_op jit(solution)/shard_map/ppermute | solution.py:245
  145.2 0.8 collective-permute-start.25
  146.0 3.9 %collective-permute-done.34.refs_5_ = bf16[128,2048]{1,0:T(8,128)(2,1)S(1)} collective-permute-done((bf16[128,2048]{1,0:T(8,128)(2,1)S(1)}, bf16[128,2048]{1,0:T(8,128)(2,1)S(1)}, u32[]{:S(2)}, u32[]{:S(2)}) %collective-permute-start.34) | collective-permute-done | bytes 524320 | tf_op jit(solution)/shard_map/ppermute | solution.py:245
  149.8 0.8 collective-permute-start.26
  151.3 1.4 collective-permute-start.18
  152.7 7.7 %experts.7 = (bf16[128,2048]{1,0:T(8,128)(2,1)S(1)}, bf16[128,2048]{1,0:T(8,128)(2,1)S(1)}, bf16[128,2048]{1,0:T(8,128)(2,1)S(1)}, bf16[128,2048]{1,0:T(8,128)(2,1)S(1)}) custom-call(s32[4,2,1,128]{3,2,1,0:T(1,128)S(1)} %bitcast.54, f32[4,2,1,128]{3,2,1,0:T(1,128)S(1)} %bitcast.55, bf16[128,2048]{1,0:T(8,128)(2,1)S(1)} %collective-permute-done.31.refs_2_, ...), custom_call_target="tpu_custom_call" | custom-call | flops 4429185024 | bytes 21495808 | tf_op jit(solution)/shard_map/experts/pallas_call | solution.py:173
  161.1 0.8 collective-permute-start.8
  161.9 1.2 collective-permute-start.9
  163.1 8.2 %collective-permute-done.26.refs_5_ = bf16[128,2048]{1,0:T(8,128)(2,1)S(1)} collective-permute-done((bf16[128,2048]{1,0:T(8,128)(2,1)S(1)}, bf16[128,2048]{1,0:T(8,128)(2,1)S(1)}, u32[]{:S(2)}, u32[]{:S(2)}) %collective-permute-start.26) | collective-permute-done | bytes 524320 | tf_op jit(solution)/shard_map/ppermute | solution.py:245
  172.1 7.9 %experts.6 = (bf16[128,2048]{1,0:T(8,128)(2,1)S(1)}, bf16[128,2048]{1,0:T(8,128)(2,1)S(1)}, bf16[128,2048]{1,0:T(8,128)(2,1)S(1)}, bf16[128,2048]{1,0:T(8,128)(2,1)S(1)}) custom-call(s32[4,2,1,128]{3,2,1,0:T(1,128)S(1)} %bitcast.51, f32[4,2,1,128]{3,2,1,0:T(1,128)S(1)} %bitcast.53, bf16[128,2048]{1,0:T(8,128)(2,1)S(1)} %collective-permute-done.23.refs_2_, ...), custom_call_target="tpu_custom_call" | custom-call | flops 4429185024 | bytes 21495808 | tf_op jit(solution)/shard_map/experts/pallas_call | solution.py:173
  180.0 1.3 collective-permute-start.35
  181.8 7.7 %experts.5 = (bf16[128,2048]{1,0:T(8,128)(2,1)S(1)}, bf16[128,2048]{1,0:T(8,128)(2,1)S(1)}, bf16[128,2048]{1,0:T(8,128)(2,1)S(1)}, bf16[128,2048]{1,0:T(8,128)(2,1)S(1)}) custom-call(s32[4,2,1,128]{3,2,1,0:T(1,128)S(1)} %bitcast.50, f32[4,2,1,128]{3,2,1,0:T(1,128)S(1)} %bitcast.52, bf16[128,2048]{1,0:T(8,128)(2,1)S(1)} %collective-permute-done.15.refs_2_, ...), custom_call_target="tpu_custom_call" | custom-call | flops 4429185024 | bytes 21495808 | tf_op jit(solution)/shard_map/experts/pallas_call | solution.py:173
  189.5 1.5 collective-permute-start.27
  191.1 2.7 collective-permute-done.9.refs_5_
  193.7 0.8 collective-permute-start.20
  194.5 7.9 %experts.4 = (bf16[128,2048]{1,0:T(8,128)(2,1)S(1)}, bf16[128,2048]{1,0:T(8,128)(2,1)S(1)}, bf16[128,2048]{1,0:T(8,128)(2,1)S(1)}, bf16[128,2048]{1,0:T(8,128)(2,1)S(1)}) custom-call(s32[4,2,1,128]{3,2,1,0:T(1,128)S(1)} %bitcast.48, f32[4,2,1,128]{3,2,1,0:T(1,128)S(1)} %bitcast.49, bf16[128,2048]{1,0:T(8,128)(2,1)S(1)} %get-tuple-element.27.refs_2_, ...), custom_call_target="tpu_custom_call" | custom-call | flops 4429185024 | bytes 21495808 | tf_op jit(solution)/shard_map/experts/pallas_call | solution.py:173
  202.5 2.5 collective-permute-done.36
  206.3 21.1 %collective-permute-done.20 = bf16[128,2048]{1,0:T(8,128)(2,1)S(1)} collective-permute-done((bf16[128,2048]{1,0:T(8,128)(2,1)S(1)}, bf16[128,2048]{1,0:T(8,128)(2,1)S(1)}, u32[]{:S(2)}, u32[]{:S(2)}) %collective-permute-start.20) | collective-permute-done | bytes 524320 | tf_op jit(solution)/shard_map/ppermute | solution.py:245
  228.8 1.9 collective-permute-start.12
  230.7 11.6 %collective-permute-done.37 = bf16[128,2048]{1,0:T(8,128)(2,1)S(1)} collective-permute-done((bf16[128,2048]{1,0:T(8,128)(2,1)S(1)}, bf16[128,2048]{1,0:T(8,128)(2,1)S(1)}, u32[]{:S(2)}, u32[]{:S(2)}) %collective-permute-start.37) | collective-permute-done | bytes 524320 | tf_op jit(solution)/shard_map/ppermute | solution.py:245
  243.7 6.3 %collective-permute-done.29 = bf16[128,2048]{1,0:T(8,128)(2,1)S(1)} collective-permute-done((bf16[128,2048]{1,0:T(8,128)(2,1)S(1)}, bf16[128,2048]{1,0:T(8,128)(2,1)S(1)}, u32[]{:S(2)}, u32[]{:S(2)}) %collective-permute-start.29) | collective-permute-done | bytes 524320 | tf_op jit(solution)/shard_map/ppermute | solution.py:245
  249.9 8.1 %collective-permute-start.38 = (bf16[128,2048]{1,0:T(8,128)(2,1)S(1)}, bf16[128,2048]{1,0:T(8,128)(2,1)S(1)}, u32[]{:S(2)}, u32[]{:S(2)}) collective-permute-start(bf16[128,2048]{1,0:T(8,128)(2,1)S(1)} %add_convert_fusion.1), channel_id=1, source_target_pairs={{0,2},{2,4},{4,6},{6,0},{1,3},{3,5},{5,7},{7,1},{8,10},{10,12},{12... | collective-permute-start | bytes 1572872 | tf_op jit(solution)/shard_map/ppermute | solution.py:250
  258.3 1.6 collective-permute-done.21
  260.2 2.5 collective-permute-start.22
  262.7 7.5 %collective-permute-done.38 = bf16[128,2048]{1,0:T(8,128)(2,1)S(1)} collective-permute-done((bf16[128,2048]{1,0:T(8,128)(2,1)S(1)}, bf16[128,2048]{1,0:T(8,128)(2,1)S(1)}, u32[]{:S(2)}, u32[]{:S(2)}) %collective-permute-start.38) | collective-permute-done | bytes 524320 | tf_op jit(solution)/shard_map/ppermute | solution.py:250
  270.1 25.4 %collective-permute-done.30 = bf16[128,2048]{1,0:T(8,128)(2,1)S(1)} collective-permute-done((bf16[128,2048]{1,0:T(8,128)(2,1)S(1)}, bf16[128,2048]{1,0:T(8,128)(2,1)S(1)}, u32[]{:S(2)}, u32[]{:S(2)}) %collective-permute-start.30) | collective-permute-done | bytes 524320 | tf_op jit(solution)/shard_map/ppermute | solution.py:250
  295.5 1.3 add_convert_fusion
  (76 shorter events, 13.5 us)
Async XLA Ops:
  0.6 77.9 %copy-start.2 = (bf16[128,2048]{1,0:T(8,128)(2,1)S(1)}, bf16[128,2048]{1,0:T(8,128)(2,1)}, u32[]{:S(2)}) copy-start(bf16[128,2048]{1,0:T(8,128)(2,1)} %tokens_ref.1) | copy-start | bytes 1572868
  0.6 150.7 %collective-permute-start.10 = (bf16[2048,1408]{1,0:T(8,128)(2,1)}, bf16[2048,1408]{1,0:T(8,128)(2,1)}, u32[]{:S(2)}, u32[]{:S(2)}) collective-permute-start(bf16[2048,1408]{1,0:T(8,128)(2,1)} %bitcast.36), channel_id=1, source_target_pairs={{0,8},{8,0},{1,9},{9,1},{2,10},{10,2},{3,11},{11,3},{4,12},{12,4},... | collective-permute-start | bytes 17301512 | tf_op jit(solution)/shard_map/ppermute | solution.py:245
  2.6 48.8 %collective-permute-start = (bf16[2,32,2048]{2,1,0:T(8,128)(2,1)S(1)}, bf16[2,32,2048]{2,1,0:T(8,128)(2,1)S(1)}, u32[]{:S(2)}, u32[]{:S(2)}) collective-permute-start(bf16[2,32,2048]{2,1,0:T(8,128)(2,1)S(1)} %constant_dynamic-update-slice_fusion.refs_0_), channel_id=1, source_target_pairs={{0,2},{2,4},{4,6},{6,0},{1,3},{3,5},{5,7},{7,1},{8,10},{10,12},{12... | collective-permute-start | bytes 786440 | tf_op jit(solution)/shard_map/ppermute | solution.py:250
  2.9 51.3 %collective-permute-start.1 = (bf16[2,32,2048]{2,1,0:T(8,128)(2,1)S(1)}, bf16[2,32,2048]{2,1,0:T(8,128)(2,1)S(1)}, u32[]{:S(2)}, u32[]{:S(2)}) collective-permute-start(bf16[2,32,2048]{2,1,0:T(8,128)(2,1)S(1)} %constant_dynamic-update-slice_fusion.refs_0_), channel_id=1, source_target_pairs={{0,4},{2,6},{4,0},{6,2},{1,5},{3,7},{5,1},{7,3},{8,12},{10,14},{12... | collective-permute-start | bytes 786440 | tf_op jit(solution)/shard_map/ppermute | solution.py:250
  4.6 49.7 %collective-permute-start.2 = (bf16[2,32,2048]{2,1,0:T(8,128)(2,1)S(1)}, bf16[2,32,2048]{2,1,0:T(8,128)(2,1)S(1)}, u32[]{:S(2)}, u32[]{:S(2)}) collective-permute-start(bf16[2,32,2048]{2,1,0:T(8,128)(2,1)S(1)} %constant_dynamic-update-slice_fusion.refs_0_), channel_id=1, source_target_pairs={{0,6},{2,0},{4,2},{6,4},{1,7},{3,1},{5,3},{7,5},{8,14},{10,8},{12,... | collective-permute-start | bytes 786440 | tf_op jit(solution)/shard_map/ppermute | solution.py:250
  5.0 145.6 %collective-permute-start.11 = (bf16[704,2048]{1,0:T(8,128)(2,1)}, bf16[704,2048]{1,0:T(8,128)(2,1)}, u32[]{:S(2)}, u32[]{:S(2)}) collective-permute-start(bf16[704,2048]{1,0:T(8,128)(2,1)} %bitcast.43), channel_id=1, source_target_pairs={{0,8},{8,0},{1,9},{9,1},{2,10},{10,2},{3,11},{11,3},{4,12},{12,4},... | collective-permute-start | bytes 8650760 | tf_op jit(solution)/shard_map/ppermute | solution.py:245
  51.4 9.7 %collective-permute-start.3 = (bf16[2,32,2048]{2,1,0:T(8,128)(2,1)S(1)}, bf16[2,32,2048]{2,1,0:T(8,128)(2,1)S(1)}, u32[]{:S(2)}, u32[]{:S(2)}) collective-permute-start(bf16[2,32,2048]{2,1,0:T(8,128)(2,1)S(1)} %constant_dynamic-update-slice_fusion.refs_0_), channel_id=1, source_target_pairs={{0,1},{1,0},{2,3},{3,2},{4,5},{5,4},{6,7},{7,6},{8,9},{9,8},{10,11... | collective-permute-start | bytes 786440 | tf_op jit(solution)/shard_map/ppermute | solution.py:245
  54.2 11.3 %collective-permute-start.4 = (bf16[2,32,2048]{2,1,0:T(8,128)(2,1)S(1)}, bf16[2,32,2048]{2,1,0:T(8,128)(2,1)S(1)}, u32[]{:S(2)}, u32[]{:S(2)}) collective-permute-start(bf16[2,32,2048]{2,1,0:T(8,128)(2,1)S(1)} %collective-permute-done.refs_1_), channel_id=1, source_target_pairs={{0,1},{1,0},{2,3},{3,2},{4,5},{5,4},{6,7},{7,6},{8,9},{9,8},{10,11... | collective-permute-start | bytes 786440 | tf_op jit(solution)/shard_map/ppermute | solution.py:245
  54.2 14.0 %collective-permute-start.5 = (bf16[2,32,2048]{2,1,0:T(8,128)(2,1)S(1)}, bf16[2,32,2048]{2,1,0:T(8,128)(2,1)S(1)}, u32[]{:S(2)}, u32[]{:S(2)}) collective-permute-start(bf16[2,32,2048]{2,1,0:T(8,128)(2,1)S(1)} %collective-permute-done.1.refs_2_), channel_id=1, source_target_pairs={{0,1},{1,0},{2,3},{3,2},{4,5},{5,4},{6,7},{7,6},{8,9},{9,8},{10,11... | collective-permute-start | bytes 786440 | tf_op jit(solution)/shard_map/ppermute | solution.py:245
  61.2 10.0 %collective-permute-start.6 = (bf16[2,32,2048]{2,1,0:T(8,128)(2,1)S(1)}, bf16[2,32,2048]{2,1,0:T(8,128)(2,1)S(1)}, u32[]{:S(2)}, u32[]{:S(2)}) collective-permute-start(bf16[2,32,2048]{2,1,0:T(8,128)(2,1)S(1)} %collective-permute-done.2.refs_3_), channel_id=1, source_target_pairs={{0,1},{1,0},{2,3},{3,2},{4,5},{5,4},{6,7},{7,6},{8,9},{9,8},{10,11... | collective-permute-start | bytes 786440 | tf_op jit(solution)/shard_map/ppermute | solution.py:245
  71.1 0.7 copy-start.4
  71.8 80.9 %slice-start = ((s8[5767168]{0:T(1024)(128)(4,1)}), s8[1572864]{0:T(1024)(128)(4,1)S(1)}, s32[]{:S(2)}) async-start(s8[5767168]{0:T(1024)(128)(4,1)} %bitcast.37), calls=%async_computation | async-start | bytes 3145728
  78.6 74.1 %copy-start = (bf16[1,704,2048]{2,1,0:T(8,128)(2,1)S(1)}, bf16[1,704,2048]{2,1,0:T(8,128)(2,1)}, u32[]{:S(2)}) copy-start(bf16[1,704,2048]{2,1,0:T(8,128)(2,1)} %param.23) | copy-start | bytes 8650756
  78.6 1.2 copy-start.1
  79.8 0.7 copy-start.3
  80.5 72.2 %slice-start.1 = ((s8[5767168]{0:T(1024)(128)(4,1)}), s8[4194304]{0:T(1024)(128)(4,1)S(1)}, s32[]{:S(2)}) async-start(s8[5767168]{0:T(1024)(128)(4,1)} %bitcast.37), calls=%async_computation.1 | async-start | bytes 8388608
  86.6 18.6 %collective-permute-start.31 = (bf16[128,2048]{1,0:T(8,128)(2,1)S(1)}, bf16[128,2048]{1,0:T(8,128)(2,1)S(1)}, u32[]{:S(2)}, u32[]{:S(2)}) collective-permute-start(bf16[128,2048]{1,0:T(8,128)(2,1)S(1)} %get-tuple-element.27.refs_2_), channel_id=1, source_target_pairs={{0,6},{2,0},{4,2},{6,4},{1,7},{3,1},{5,3},{7,5},{8,14},{10,8},{12,... | collective-permute-start | bytes 1572872 | tf_op jit(solution)/shard_map/ppermute | solution.py:250
  86.6 33.6 %collective-permute-start.23 = (bf16[128,2048]{1,0:T(8,128)(2,1)S(1)}, bf16[128,2048]{1,0:T(8,128)(2,1)S(1)}, u32[]{:S(2)}, u32[]{:S(2)}) collective-permute-start(bf16[128,2048]{1,0:T(8,128)(2,1)S(1)} %get-tuple-element.27.refs_2_), channel_id=1, source_target_pairs={{0,4},{2,6},{4,0},{6,2},{1,5},{3,7},{5,1},{7,3},{8,12},{10,14},{12... | collective-permute-start | bytes 1572872 | tf_op jit(solution)/shard_map/ppermute | solution.py:250
  92.8 28.2 %collective-permute-start.15 = (bf16[128,2048]{1,0:T(8,128)(2,1)S(1)}, bf16[128,2048]{1,0:T(8,128)(2,1)S(1)}, u32[]{:S(2)}, u32[]{:S(2)}) collective-permute-start(bf16[128,2048]{1,0:T(8,128)(2,1)S(1)} %get-tuple-element.27.refs_2_), channel_id=1, source_target_pairs={{0,2},{2,4},{4,6},{6,0},{1,3},{3,5},{5,7},{7,1},{8,10},{10,12},{12... | collective-permute-start | bytes 1572872 | tf_op jit(solution)/shard_map/ppermute | solution.py:250
  105.2 16.4 %collective-permute-start.32 = (bf16[128,2048]{1,0:T(8,128)(2,1)S(1)}, bf16[128,2048]{1,0:T(8,128)(2,1)S(1)}, u32[]{:S(2)}, u32[]{:S(2)}) collective-permute-start(bf16[128,2048]{1,0:T(8,128)(2,1)S(1)} %collective-permute-done.31.refs_2_), channel_id=1, source_target_pairs={{0,1},{1,0},{2,3},{3,2},{4,5},{5,4},{6,7},{7,6},{8,9},{9,8},{10,11... | collective-permute-start | bytes 1572872 | tf_op jit(solution)/shard_map/ppermute | solution.py:245
  120.2 14.8 %collective-permute-start.33 = (bf16[128,2048]{1,0:T(8,128)(2,1)S(1)}, bf16[128,2048]{1,0:T(8,128)(2,1)S(1)}, u32[]{:S(2)}, u32[]{:S(2)}) collective-permute-start(bf16[128,2048]{1,0:T(8,128)(2,1)S(1)} %collective-permute-done.31.refs_2_), channel_id=1, source_target_pairs={{0,16},{16,0},{1,17},{17,1},{2,18},{18,2},{3,19},{19,3},{4,20},{20... | collective-permute-start | bytes 1572872 | tf_op jit(solution)/shard_map/ppermute | solution.py:245
  121.0 14.6 %collective-permute-start.24 = (bf16[128,2048]{1,0:T(8,128)(2,1)S(1)}, bf16[128,2048]{1,0:T(8,128)(2,1)S(1)}, u32[]{:S(2)}, u32[]{:S(2)}) collective-permute-start(bf16[128,2048]{1,0:T(8,128)(2,1)S(1)} %collective-permute-done.23.refs_2_), channel_id=1, source_target_pairs={{0,1},{1,0},{2,3},{3,2},{4,5},{5,4},{6,7},{7,6},{8,9},{9,8},{10,11... | collective-permute-start | bytes 1572872 | tf_op jit(solution)/shard_map/ppermute | solution.py:245
  121.6 23.6 %collective-permute-start.17 = (bf16[128,2048]{1,0:T(8,128)(2,1)S(1)}, bf16[128,2048]{1,0:T(8,128)(2,1)S(1)}, u32[]{:S(2)}, u32[]{:S(2)}) collective-permute-start(bf16[128,2048]{1,0:T(8,128)(2,1)S(1)} %collective-permute-done.15.refs_2_), channel_id=1, source_target_pairs={{0,16},{16,0},{1,17},{17,1},{2,18},{18,2},{3,19},{19,3},{4,20},{20... | collective-permute-start | bytes 1572872 | tf_op jit(solution)/shard_map/ppermute | solution.py:245
  135.0 14.9 %collective-permute-start.34 = (bf16[128,2048]{1,0:T(8,128)(2,1)S(1)}, bf16[128,2048]{1,0:T(8,128)(2,1)S(1)}, u32[]{:S(2)}, u32[]{:S(2)}) collective-permute-start(bf16[128,2048]{1,0:T(8,128)(2,1)S(1)} %collective-permute-done.33.refs_4_), channel_id=1, source_target_pairs={{0,1},{1,0},{2,3},{3,2},{4,5},{5,4},{6,7},{7,6},{8,9},{9,8},{10,11... | collective-permute-start | bytes 1572872 | tf_op jit(solution)/shard_map/ppermute | solution.py:245
  135.6 25.5 %collective-permute-start.7 = (bf16[128,2048]{1,0:T(8,128)(2,1)S(1)}, bf16[128,2048]{1,0:T(8,128)(2,1)S(1)}, u32[]{:S(2)}, u32[]{:S(2)}) collective-permute-start(bf16[128,2048]{1,0:T(8,128)(2,1)S(1)} %get-tuple-element.27.refs_2_), channel_id=1, source_target_pairs={{0,1},{1,0},{2,3},{3,2},{4,5},{5,4},{6,7},{7,6},{8,9},{9,8},{10,11... | collective-permute-start | bytes 1572872 | tf_op jit(solution)/shard_map/ppermute | solution.py:245
  145.2 16.7 %collective-permute-start.25 = (bf16[128,2048]{1,0:T(8,128)(2,1)S(1)}, bf16[128,2048]{1,0:T(8,128)(2,1)S(1)}, u32[]{:S(2)}, u32[]{:S(2)}) collective-permute-start(bf16[128,2048]{1,0:T(8,128)(2,1)S(1)} %collective-permute-done.23.refs_2_), channel_id=1, source_target_pairs={{0,16},{16,0},{1,17},{17,1},{2,18},{18,2},{3,19},{19,3},{4,20},{20... | collective-permute-start | bytes 1572872 | tf_op jit(solution)/shard_map/ppermute | solution.py:245
  149.8 21.4 %collective-permute-start.26 = (bf16[128,2048]{1,0:T(8,128)(2,1)S(1)}, bf16[128,2048]{1,0:T(8,128)(2,1)S(1)}, u32[]{:S(2)}, u32[]{:S(2)}) collective-permute-start(bf16[128,2048]{1,0:T(8,128)(2,1)S(1)} %collective-permute-done.24.refs_3_), channel_id=1, source_target_pairs={{0,16},{16,0},{1,17},{17,1},{2,18},{18,2},{3,19},{19,3},{4,20},{20... | collective-permute-start | bytes 1572872 | tf_op jit(solution)/shard_map/ppermute | solution.py:245
  150.7 29.3 %collective-permute-start.16 = (bf16[128,2048]{1,0:T(8,128)(2,1)S(1)}, bf16[128,2048]{1,0:T(8,128)(2,1)S(1)}, u32[]{:S(2)}, u32[]{:S(2)}) collective-permute-start(bf16[128,2048]{1,0:T(8,128)(2,1)S(1)} %collective-permute-done.15.refs_2_), channel_id=1, source_target_pairs={{0,1},{1,0},{2,3},{3,2},{4,5},{5,4},{6,7},{7,6},{8,9},{9,8},{10,11... | collective-permute-start | bytes 1572872 | tf_op jit(solution)/shard_map/ppermute | solution.py:245
  151.3 29.9 %collective-permute-start.18 = (bf16[128,2048]{1,0:T(8,128)(2,1)S(1)}, bf16[128,2048]{1,0:T(8,128)(2,1)S(1)}, u32[]{:S(2)}, u32[]{:S(2)}) collective-permute-start(bf16[128,2048]{1,0:T(8,128)(2,1)S(1)} %collective-permute-done.17.refs_4_), channel_id=1, source_target_pairs={{0,1},{1,0},{2,3},{3,2},{4,5},{5,4},{6,7},{7,6},{8,9},{9,8},{10,11... | collective-permute-start | bytes 1572872 | tf_op jit(solution)/shard_map/ppermute | solution.py:245
  161.1 28.5 %collective-permute-start.8 = (bf16[128,2048]{1,0:T(8,128)(2,1)S(1)}, bf16[128,2048]{1,0:T(8,128)(2,1)S(1)}, u32[]{:S(2)}, u32[]{:S(2)}) collective-permute-start(bf16[128,2048]{1,0:T(8,128)(2,1)S(1)} %get-tuple-element.27.refs_2_), channel_id=1, source_target_pairs={{0,16},{16,0},{1,17},{17,1},{2,18},{18,2},{3,19},{19,3},{4,20},{20... | collective-permute-start | bytes 1572872 | tf_op jit(solution)/shard_map/ppermute | solution.py:245
  161.9 31.8 %collective-permute-start.9 = (bf16[128,2048]{1,0:T(8,128)(2,1)S(1)}, bf16[128,2048]{1,0:T(8,128)(2,1)S(1)}, u32[]{:S(2)}, u32[]{:S(2)}) collective-permute-start(bf16[128,2048]{1,0:T(8,128)(2,1)S(1)} %collective-permute-done.7.refs_3_), channel_id=1, source_target_pairs={{0,16},{16,0},{1,17},{17,1},{2,18},{18,2},{3,19},{19,3},{4,20},{20... | collective-permute-start | bytes 1572872 | tf_op jit(solution)/shard_map/ppermute | solution.py:245
  171.3 33.7 %collective-permute-start.36 = (bf16[128,2048]{1,0:T(8,128)(2,1)S(1)}, bf16[128,2048]{1,0:T(8,128)(2,1)S(1)}, u32[]{:S(2)}, u32[]{:S(2)}) collective-permute-start(bf16[128,2048]{1,0:T(8,128)(2,1)S(1)} %get-tuple-element.43), channel_id=1, source_target_pairs={{0,16},{16,0},{1,17},{17,1},{2,18},{18,2},{3,19},{19,3},{4,20},{20... | collective-permute-start | bytes 1572872 | tf_op jit(solution)/shard_map/ppermute | solution.py:245
  180.0 48.8 %collective-permute-start.35 = (bf16[128,2048]{1,0:T(8,128)(2,1)S(1)}, bf16[128,2048]{1,0:T(8,128)(2,1)S(1)}, u32[]{:S(2)}, u32[]{:S(2)}) collective-permute-start(bf16[128,2048]{1,0:T(8,128)(2,1)S(1)} %get-tuple-element.41), channel_id=1, source_target_pairs={{0,16},{16,0},{1,17},{17,1},{2,18},{18,2},{3,19},{19,3},{4,20},{20... | collective-permute-start | bytes 1572872 | tf_op jit(solution)/shard_map/ppermute | solution.py:245
  181.3 24.7 %collective-permute-start.28 = (bf16[128,2048]{1,0:T(8,128)(2,1)S(1)}, bf16[128,2048]{1,0:T(8,128)(2,1)S(1)}, u32[]{:S(2)}, u32[]{:S(2)}) collective-permute-start(bf16[128,2048]{1,0:T(8,128)(2,1)S(1)} %get-tuple-element.39), channel_id=1, source_target_pairs={{0,1},{1,0},{2,3},{3,2},{4,5},{5,4},{6,7},{7,6},{8,9},{9,8},{10,11... | collective-permute-start | bytes 1572872 | tf_op jit(solution)/shard_map/ppermute | solution.py:245
  189.5 53.6 %collective-permute-start.27 = (bf16[128,2048]{1,0:T(8,128)(2,1)S(1)}, bf16[128,2048]{1,0:T(8,128)(2,1)S(1)}, u32[]{:S(2)}, u32[]{:S(2)}) collective-permute-start(bf16[128,2048]{1,0:T(8,128)(2,1)S(1)} %get-tuple-element.37), channel_id=1, source_target_pairs={{0,1},{1,0},{2,3},{3,2},{4,5},{5,4},{6,7},{7,6},{8,9},{9,8},{10,11... | collective-permute-start | bytes 1572872 | tf_op jit(solution)/shard_map/ppermute | solution.py:245
  193.7 33.7 %collective-permute-start.20 = (bf16[128,2048]{1,0:T(8,128)(2,1)S(1)}, bf16[128,2048]{1,0:T(8,128)(2,1)S(1)}, u32[]{:S(2)}, u32[]{:S(2)}) collective-permute-start(bf16[128,2048]{1,0:T(8,128)(2,1)S(1)} %get-tuple-element.35), channel_id=1, source_target_pairs={{0,16},{16,0},{1,17},{17,1},{2,18},{18,2},{3,19},{19,3},{4,20},{20... | collective-permute-start | bytes 1572872 | tf_op jit(solution)/shard_map/ppermute | solution.py:245
  205.0 53.3 %collective-permute-start.19 = (bf16[128,2048]{1,0:T(8,128)(2,1)S(1)}, bf16[128,2048]{1,0:T(8,128)(2,1)S(1)}, u32[]{:S(2)}, u32[]{:S(2)}) collective-permute-start(bf16[128,2048]{1,0:T(8,128)(2,1)S(1)} %get-tuple-element.33), channel_id=1, source_target_pairs={{0,16},{16,0},{1,17},{17,1},{2,18},{18,2},{3,19},{19,3},{4,20},{20... | collective-permute-start | bytes 1572872 | tf_op jit(solution)/shard_map/ppermute | solution.py:245
  205.9 22.2 %collective-permute-start.13 = (bf16[128,2048]{1,0:T(8,128)(2,1)S(1)}, bf16[128,2048]{1,0:T(8,128)(2,1)S(1)}, u32[]{:S(2)}, u32[]{:S(2)}) collective-permute-start(bf16[128,2048]{1,0:T(8,128)(2,1)S(1)} %get-tuple-element.31), channel_id=1, source_target_pairs={{0,1},{1,0},{2,3},{3,2},{4,5},{5,4},{6,7},{7,6},{8,9},{9,8},{10,11... | collective-permute-start | bytes 1572872 | tf_op jit(solution)/shard_map/ppermute | solution.py:245
  227.4 14.9 %collective-permute-start.37 = (bf16[128,2048]{1,0:T(8,128)(2,1)S(1)}, bf16[128,2048]{1,0:T(8,128)(2,1)S(1)}, u32[]{:S(2)}, u32[]{:S(2)}) collective-permute-start(bf16[128,2048]{1,0:T(8,128)(2,1)S(1)} %add_convert_fusion.2), channel_id=1, source_target_pairs={{0,1},{1,0},{2,3},{3,2},{4,5},{5,4},{6,7},{7,6},{8,9},{9,8},{10,11... | collective-permute-start | bytes 1572872 | tf_op jit(solution)/shard_map/ppermute | solution.py:245
  228.2 21.8 %collective-permute-start.29 = (bf16[128,2048]{1,0:T(8,128)(2,1)S(1)}, bf16[128,2048]{1,0:T(8,128)(2,1)S(1)}, u32[]{:S(2)}, u32[]{:S(2)}) collective-permute-start(bf16[128,2048]{1,0:T(8,128)(2,1)S(1)} %add_convert_fusion.4), channel_id=1, source_target_pairs={{0,16},{16,0},{1,17},{17,1},{2,18},{18,2},{3,19},{19,3},{4,20},{20... | collective-permute-start | bytes 1572872 | tf_op jit(solution)/shard_map/ppermute | solution.py:245
  228.8 33.8 %collective-permute-start.12 = (bf16[128,2048]{1,0:T(8,128)(2,1)S(1)}, bf16[128,2048]{1,0:T(8,128)(2,1)S(1)}, u32[]{:S(2)}, u32[]{:S(2)}) collective-permute-start(bf16[128,2048]{1,0:T(8,128)(2,1)S(1)} %get-tuple-element.29), channel_id=1, source_target_pairs={{0,1},{1,0},{2,3},{3,2},{4,5},{5,4},{6,7},{7,6},{8,9},{9,8},{10,11... | collective-permute-start | bytes 1572872 | tf_op jit(solution)/shard_map/ppermute | solution.py:245
  242.3 17.6 %collective-permute-start.21 = (bf16[128,2048]{1,0:T(8,128)(2,1)S(1)}, bf16[128,2048]{1,0:T(8,128)(2,1)S(1)}, u32[]{:S(2)}, u32[]{:S(2)}) collective-permute-start(bf16[128,2048]{1,0:T(8,128)(2,1)S(1)} %add_convert_fusion.6), channel_id=1, source_target_pairs={{0,1},{1,0},{2,3},{3,2},{4,5},{5,4},{6,7},{7,6},{8,9},{9,8},{10,11... | collective-permute-start | bytes 1572872 | tf_op jit(solution)/shard_map/ppermute | solution.py:245
  243.1 19.5 %collective-permute-start.14 = (bf16[128,2048]{1,0:T(8,128)(2,1)S(1)}, bf16[128,2048]{1,0:T(8,128)(2,1)S(1)}, u32[]{:S(2)}, u32[]{:S(2)}) collective-permute-start(bf16[128,2048]{1,0:T(8,128)(2,1)S(1)} %add_convert_fusion.8), channel_id=1, source_target_pairs={{0,16},{16,0},{1,17},{17,1},{2,18},{18,2},{3,19},{19,3},{4,20},{20... | collective-permute-start | bytes 1572872 | tf_op jit(solution)/shard_map/ppermute | solution.py:245
  249.9 20.2 %collective-permute-start.38 = (bf16[128,2048]{1,0:T(8,128)(2,1)S(1)}, bf16[128,2048]{1,0:T(8,128)(2,1)S(1)}, u32[]{:S(2)}, u32[]{:S(2)}) collective-permute-start(bf16[128,2048]{1,0:T(8,128)(2,1)S(1)} %add_convert_fusion.1), channel_id=1, source_target_pairs={{0,2},{2,4},{4,6},{6,0},{1,3},{3,5},{5,7},{7,1},{8,10},{10,12},{12... | collective-permute-start | bytes 1572872 | tf_op jit(solution)/shard_map/ppermute | solution.py:250
  258.3 37.2 %collective-permute-start.30 = (bf16[128,2048]{1,0:T(8,128)(2,1)S(1)}, bf16[128,2048]{1,0:T(8,128)(2,1)S(1)}, u32[]{:S(2)}, u32[]{:S(2)}) collective-permute-start(bf16[128,2048]{1,0:T(8,128)(2,1)S(1)} %add_convert_fusion.3), channel_id=1, source_target_pairs={{0,4},{2,6},{4,0},{6,2},{1,5},{3,7},{5,1},{7,3},{8,12},{10,14},{12... | collective-permute-start | bytes 1572872 | tf_op jit(solution)/shard_map/ppermute | solution.py:250
  260.2 35.3 %collective-permute-start.22 = (bf16[128,2048]{1,0:T(8,128)(2,1)S(1)}, bf16[128,2048]{1,0:T(8,128)(2,1)S(1)}, u32[]{:S(2)}, u32[]{:S(2)}) collective-permute-start(bf16[128,2048]{1,0:T(8,128)(2,1)S(1)} %add_convert_fusion.5), channel_id=1, source_target_pairs={{0,6},{2,0},{4,2},{6,4},{1,7},{3,1},{5,3},{7,5},{8,14},{10,8},{12,... | collective-permute-start | bytes 1572872 | tf_op jit(solution)/shard_map/ppermute | solution.py:250

commit v4 on v3

--- a/solution.py
+++ b/solution.py
@@ -254,27 +254,39 @@
     return sum(one.astype(jnp.float32) for one in arrays).astype(jnp.bfloat16)
 
 
-def relative_slots(table, capacity):
+def relative_slots(routes, route_weights, capacity):
     columns = lax.axis_size("line")
-    far, core = lax.axis_index("far"), lax.axis_index("core")
-    line, side = lax.axis_index("line"), lax.axis_index("side")
-    places = jnp.arange(4 * columns)
-    back, across, beside = places // 4, places // 2 % 2, places % 2
-    source = ((far ^ across) * columns + (line - back + columns) % columns) * 2 + (side ^ beside)
-    table = table[source]
+    far, core, line = lax.axis_index("far"), lax.axis_index("core"), lax.axis_index("line")
+    table = jnp.concatenate([routes.T.astype(jnp.float32), route_weights.T])
+    table = jnp.stack([table] + [shift(table, "line", back) for back in range(1, columns)])
+    table = jnp.stack([table, swap(table, "side")])
+    table = jnp.stack([table, swap(table, "far")])
+    table = table.reshape((4 * columns,) + table.shape[3:])
     own = (far * 2 + core) * columns + line
     other = (far * 2 + 1 - core) * columns + line
     own_slot, own_gate = own_slots(table, own, 0)
     other_slot, other_gate = own_slots(table, other, capacity)
-    shape = (columns, 4, 2, 1, -1)
+    shape = (4, columns, 2, 1, -1)
     slots = jnp.stack([own_slot, other_slot], axis=1).reshape(shape)
     gates = jnp.stack([own_gate, other_gate], axis=1).reshape(shape)
     return slots, gates
 
 
+def go_home(results, back):
+    here, beside, across, corner = results
+    if back % 2 == 0:
+        across = add(across, swap(corner, "side"))
+        total = add(here, swap(beside, "side"), swap(across, "far"))
+    else:
+        beside = add(beside, swap(corner, "far"))
+        total = add(here, swap(across, "far"), swap(beside, "side"))
+    return shift(total, "line", -back) if back else total
+
+
 def gather_plan(normed, slots, gates, weights, capacity):
     columns = lax.axis_size("line")
-    arrived = []
+    normed, weights = lax.optimization_barrier((normed, weights))
+    results = []
     for back in range(columns):
         block = shift(normed, "line", back) if back else normed
         if back % 2 == 0:
@@ -285,18 +297,18 @@
             across = swap(block, "far")
             beside = swap(block, "side")
             corner = swap(across, "side")
-        results = run_experts(
-            [block, beside, across, corner], slots[back], gates[back], weights, capacity
-        )
-        here, beside, across, corner = results
-        if back % 2 == 0:
-            across = add(across, swap(corner, "side"))
-            total = add(here, swap(beside, "side"), swap(across, "far"))
-        else:
-            beside = add(beside, swap(corner, "far"))
-            total = add(here, swap(across, "far"), swap(beside, "side"))
-        arrived.append(shift(total, "line", -back) if back else total)
-    return add(*arrived)
+        mine = slots[:, back]
+        if back:
+            mine, results[-1][0] = lax.optimization_barrier((mine, results[-1][0]))
+        results.append(
+            list(
+                run_experts(
+                    [block, beside, across, corner], mine, gates[:, back], weights, capacity
+                )
+            )
+        )
+    results[0], results[-1] = lax.optimization_barrier((results[0], results[-1]))
+    return add(*[go_home(results[back], back) for back in range(columns)])
 
 
 def on_device(
@@ -324,12 +336,7 @@
         lines = [kv] + [shift(kv, "line", k) for k in range(1, lax.axis_size("line"))]
         pieces = lines + [swap(piece, "side") for piece in lines]
         weights = weights + [swap(one, "core") for one in weights]
-        table = lax.all_gather(
-            jnp.concatenate([routes.T.astype(jnp.float32), route_weights.T]),
-            ("far", "line", "side"),
-            axis=0,
-        )
-        slots, gates = relative_slots(table, capacity)
+        slots, gates = relative_slots(routes, route_weights, capacity)
         queries, slots, gates = lax.optimization_barrier((queries, slots, gates))
     else:
         pieces = [

time: 297 us -> 280 us (0.943)
  the two profiles are of different devices: /device:TPU:26 before, /device:TPU:9 now
where the time goes in v4:
time: 280 us; the launch traced here: 279 us
  waiting for transfers between devices  189 us (68%)
  Pallas kernels  44.1 us (16%)
  starting transfers between devices  37.6 us (13%)
  other arithmetic  4.11 us (1%)
  local copies, waits for them, and re-layouts  3.78 us (1%)
    ppermute x12, waiting for transfers between devices, shift(): lax.ppermute(array, axis, [(i, (i + amount) % size) for i in range(size)])  101 us
    ppermute x32, waiting for transfers between devices, swap(): return lax.ppermute(array, axis, [(0, 1), (1, 0)])  88 us
    pallas_call x4, Pallas kernels, run_experts(): pl.pallas_call(lambda *refs: experts_kernel(capacity, count, *refs), in_s...  31.2 us
    ppermute x32, starting transfers between devices, swap(): return lax.ppermute(array, axis, [(0, 1), (1, 0)])  21.5 us
    ppermute x12, starting transfers between devices, shift(): lax.ppermute(array, axis, [(i, (i + amount) % size) for i in range(size)])  16.1 us
    pallas_call x1, Pallas kernels, attention(): pl.pallas_call(attention_kernel, grid=(width // span,), in_specs=[by_cols...  6.76 us
    pallas_call x1, Pallas kernels, project(): pl.pallas_call(project_kernel, grid=(steps,), in_specs=[pl.BlockSpec((row...  6.13 us
  transfers between devices with their start and end apart: 44, of which 22 were waited for; matrix products, arithmetic and copies ran while one was open for 2% of the time, Pallas kernels for 13%

profile of v4, /device:TPU:9, one launch (start us, length us, event | category | flops | bytes accessed | tf_op | source)
XLA Modules:
  0.0 279.3 jit_solution(9259709664407410112)
XLA Ops:
  2.9 2.5 collective-permute-start.1
  5.3 2.2 collective-permute-start
  7.5 0.9 constant_dynamic-update-slice_fusion.1
  8.5 1.3 collective-permute-start.3
  9.8 0.9 constant_dynamic-update-slice_fusion.refs_0_
  10.7 1.6 collective-permute-start.5
  12.3 1.3 collective-permute-start.4
  13.6 2.7 collective-permute-start.6
  18.3 15.2 %collective-permute-done.6.refs_2_ = bf16[2,32,2048]{2,1,0:T(8,128)(2,1)S(1)} collective-permute-done((bf16[2,32,2048]{2,1,0:T(8,128)(2,1)S(1)}, bf16[2,32,2048]{2,1,0:T(8,128)(2,1)S(1)}, u32[]{:S(2)}, u32[]{:S(2)}) %collective-permute-start.6) | collective-permute-done | bytes 262176 | tf_op jit(solution)/shard_map/ppermute | solution.py:250
  33.8 4.8 %collective-permute-done.7.refs_3_ = bf16[2,32,2048]{2,1,0:T(8,128)(2,1)S(1)} collective-permute-done((bf16[2,32,2048]{2,1,0:T(8,128)(2,1)S(1)}, bf16[2,32,2048]{2,1,0:T(8,128)(2,1)S(1)}, u32[]{:S(2)}, u32[]{:S(2)}) %collective-permute-start.7) | collective-permute-done | bytes 262176 | tf_op jit(solution)/shard_map/ppermute | solution.py:250
  38.9 1.2 collective-permute-start.11
  40.4 1.4 collective-permute-done.9.refs_5_
  41.8 5.6 %collective-permute-done.10.refs_6_ = bf16[2,32,2048]{2,1,0:T(8,128)(2,1)S(1)} collective-permute-done((bf16[2,32,2048]{2,1,0:T(8,128)(2,1)S(1)}, bf16[2,32,2048]{2,1,0:T(8,128)(2,1)S(1)}, u32[]{:S(2)}, u32[]{:S(2)}) %collective-permute-start.10) | collective-permute-done | bytes 262176 | tf_op jit(solution)/shard_map/ppermute | solution.py:245
  47.4 5.6 %collective-permute-done.11.refs_7_ = bf16[2,32,2048]{2,1,0:T(8,128)(2,1)S(1)} collective-permute-done((bf16[2,32,2048]{2,1,0:T(8,128)(2,1)S(1)}, bf16[2,32,2048]{2,1,0:T(8,128)(2,1)S(1)}, u32[]{:S(2)}, u32[]{:S(2)}) %collective-permute-start.11) | collective-permute-done | bytes 262176 | tf_op jit(solution)/shard_map/ppermute | solution.py:245
  53.7 6.8 %attention.1.heads_ref = bf16[128,2048]{1,0:T(8,128)(2,1)} custom-call(bf16[128,2048]{1,0:T(8,128)(2,1)} %q_ref, bf16[128,2048]{1,0:T(8,128)(2,1)} %sk_ref.1, bf16[128,2048]{1,0:T(8,128)(2,1)} %sv_ref.1, bf16[2,32,2048]{2,1,0:T(8,128)(2,1)S(1)} %constant_dynamic-update-slice_fusion.refs_0_, bf16[2,32,2048]{2,1,0:T(8,128)(2,1)S(1)} %collective-permute-done.5.refs_1_, ...), custom_call_target="tpu_custom_call" | custom-call | tf_op jit(solution)/shard_map/attention/pallas_call | solution.py:60
  60.5 1.2 copy-done.1
  61.7 6.1 %project_and_norm.1 = (bf16[128,2048]{1,0:T(8,128)(2,1)}, bf16[128,2048]{1,0:T(8,128)(2,1)S(1)}) custom-call(bf16[128,2048]{1,0:T(8,128)(2,1)S(1)} %copy-done.1, bf16[2048,2048]{1,0:T(8,128)(2,1)} %weight_ref.1, bf16[128,2048]{1,0:T(8,128)(2,1)S(1)} %copy-done.2, f32[1,2048]{1,0:T(1,128)S(1)} %bitcast.64), custom_call_target="tpu_custom_call" | custom-call | tf_op jit(solution)/shard_map/project_and_norm/pallas_call | solution.py:98
  68.3 1.5 collective-permute-start.21
  69.9 1.2 collective-permute-start.15
  71.1 8.0 %collective-permute-done.17.refs_2_ = bf16[128,2048]{1,0:T(8,128)(2,1)S(1)} collective-permute-done((bf16[128,2048]{1,0:T(8,128)(2,1)S(1)}, bf16[128,2048]{1,0:T(8,128)(2,1)S(1)}, u32[]{:S(2)}, u32[]{:S(2)}) %collective-permute-start.17) | collective-permute-done | bytes 524320 | tf_op jit(solution)/shard_map/ppermute | solution.py:250
  79.2 1.3 collective-permute-start.16
  80.6 30.2 %collective-permute-done.21.refs_2_ = bf16[128,2048]{1,0:T(8,128)(2,1)S(1)} collective-permute-done((bf16[128,2048]{1,0:T(8,128)(2,1)S(1)}, bf16[128,2048]{1,0:T(8,128)(2,1)S(1)}, u32[]{:S(2)}, u32[]{:S(2)}) %collective-permute-start.21) | collective-permute-done | bytes 524320 | tf_op jit(solution)/shard_map/ppermute | solution.py:250
  111.3 1.0 collective-permute-start.18
  112.3 3.5 %collective-permute-done.25.refs_2_ = bf16[128,2048]{1,0:T(8,128)(2,1)S(1)} collective-permute-done((bf16[128,2048]{1,0:T(8,128)(2,1)S(1)}, bf16[128,2048]{1,0:T(8,128)(2,1)S(1)}, u32[]{:S(2)}, u32[]{:S(2)}) %collective-permute-start.25) | collective-permute-done | bytes 524320 | tf_op jit(solution)/shard_map/ppermute | solution.py:250
  115.8 1.2 collective-permute-start.27
  117.5 3.8 %collective-permute-done.22.refs_3_ = bf16[128,2048]{1,0:T(8,128)(2,1)S(1)} collective-permute-done((bf16[128,2048]{1,0:T(8,128)(2,1)S(1)}, bf16[128,2048]{1,0:T(8,128)(2,1)S(1)}, u32[]{:S(2)}, u32[]{:S(2)}) %collective-permute-start.22) | collective-permute-done | bytes 524320 | tf_op jit(solution)/shard_map/ppermute | solution.py:245
  121.3 7.7 %experts.4 = (bf16[128,2048]{1,0:T(8,128)(2,1)S(1)}, bf16[128,2048]{1,0:T(8,128)(2,1)S(1)}, bf16[128,2048]{1,0:T(8,128)(2,1)S(1)}, bf16[128,2048]{1,0:T(8,128)(2,1)S(1)}) custom-call(s32[4,2,1,128]{3,2,1,0:T(1,128)S(1)} %bitcast.63, f32[4,2,1,128]{3,2,1,0:T(1,128)S(1)} %bitcast.62, bf16[128,2048]{1,0:T(8,128)(2,1)S(1)} %get-tuple-element.47.refs_2_, ...), custom_call_target="tpu_custom_call" | custom-call | flops 4429185024 | bytes 21495808 | tf_op jit(solution)/shard_map/experts/pallas_call | solution.py:173
  129.1 3.5 %collective-permute-done.18.refs_3_ = bf16[128,2048]{1,0:T(8,128)(2,1)S(1)} collective-permute-done((bf16[128,2048]{1,0:T(8,128)(2,1)S(1)}, bf16[128,2048]{1,0:T(8,128)(2,1)S(1)}, u32[]{:S(2)}, u32[]{:S(2)}) %collective-permute-start.18) | collective-permute-done | bytes 524320 | tf_op jit(solution)/shard_map/ppermute | solution.py:245
  133.2 0.9 collective-permute-start.28
  134.0 9.8 %collective-permute-done.20.refs_5_ = bf16[128,2048]{1,0:T(8,128)(2,1)S(1)} collective-permute-done((bf16[128,2048]{1,0:T(8,128)(2,1)S(1)}, bf16[128,2048]{1,0:T(8,128)(2,1)S(1)}, u32[]{:S(2)}, u32[]{:S(2)}) %collective-permute-start.20) | collective-permute-done | bytes 524320 | tf_op jit(solution)/shard_map/ppermute | solution.py:245
  143.8 7.9 %experts.5 = (bf16[128,2048]{1,0:T(8,128)(2,1)S(1)}, bf16[128,2048]{1,0:T(8,128)(2,1)S(1)}, bf16[128,2048]{1,0:T(8,128)(2,1)S(1)}, bf16[128,2048]{1,0:T(8,128)(2,1)S(1)}) custom-call(s32[4,2,1,128]{3,2,1,0:T(1,128)S(1)} %bitcast.61, f32[4,2,1,128]{3,2,1,0:T(1,128)S(1)} %bitcast.59, bf16[128,2048]{1,0:T(8,128)(2,1)S(1)} %collective-permute-done.17.refs_2_, ...), custom_call_target="tpu_custom_call" | custom-call | flops 4429185024 | bytes 21495808 | tf_op jit(solution)/shard_map/experts/pallas_call | solution.py:173
  152.3 7.7 %experts.6 = (bf16[128,2048]{1,0:T(8,128)(2,1)S(1)}, bf16[128,2048]{1,0:T(8,128)(2,1)S(1)}, bf16[128,2048]{1,0:T(8,128)(2,1)S(1)}, bf16[128,2048]{1,0:T(8,128)(2,1)S(1)}) custom-call(s32[4,2,1,128]{3,2,1,0:T(1,128)S(1)} %bitcast.60, f32[4,2,1,128]{3,2,1,0:T(1,128)S(1)} %bitcast.57, bf16[128,2048]{1,0:T(8,128)(2,1)S(1)} %collective-permute-done.21.refs_2_, ...), custom_call_target="tpu_custom_call" | custom-call | flops 4429185024 | bytes 21495808 | tf_op jit(solution)/shard_map/experts/pallas_call | solution.py:173
  160.0 6.3 %collective-permute-done.28.refs_5_ = bf16[128,2048]{1,0:T(8,128)(2,1)S(1)} collective-permute-done((bf16[128,2048]{1,0:T(8,128)(2,1)S(1)}, bf16[128,2048]{1,0:T(8,128)(2,1)S(1)}, u32[]{:S(2)}, u32[]{:S(2)}) %collective-permute-start.28) | collective-permute-done | bytes 524320 | tf_op jit(solution)/shard_map/ppermute | solution.py:245
  166.2 7.9 %experts.7 = (bf16[128,2048]{1,0:T(8,128)(2,1)S(1)}, bf16[128,2048]{1,0:T(8,128)(2,1)S(1)}, bf16[128,2048]{1,0:T(8,128)(2,1)S(1)}, bf16[128,2048]{1,0:T(8,128)(2,1)S(1)}) custom-call(s32[4,2,1,128]{3,2,1,0:T(1,128)S(1)} %bitcast.58, f32[4,2,1,128]{3,2,1,0:T(1,128)S(1)} %bitcast.56, bf16[128,2048]{1,0:T(8,128)(2,1)S(1)} %collective-permute-done.25.refs_2_, ...), custom_call_target="tpu_custom_call" | custom-call | flops 4429185024 | bytes 21495808 | tf_op jit(solution)/shard_map/experts/pallas_call | solution.py:173
  174.9 1.4 collective-permute-start.40
  177.2 6.6 %collective-permute-done.41 = bf16[128,2048]{1,0:T(8,128)(2,1)S(1)} collective-permute-done((bf16[128,2048]{1,0:T(8,128)(2,1)S(1)}, bf16[128,2048]{1,0:T(8,128)(2,1)S(1)}, u32[]{:S(2)}, u32[]{:S(2)}) %collective-permute-start.41) | collective-permute-done | bytes 524320 | tf_op jit(solution)/shard_map/ppermute | solution.py:245
  183.9 1.0 collective-permute-start.30
  185.1 21.2 %collective-permute-done.33 = bf16[128,2048]{1,0:T(8,128)(2,1)S(1)} collective-permute-done((bf16[128,2048]{1,0:T(8,128)(2,1)S(1)}, bf16[128,2048]{1,0:T(8,128)(2,1)S(1)}, u32[]{:S(2)}, u32[]{:S(2)}) %collective-permute-start.33) | collective-permute-done | bytes 524320 | tf_op jit(solution)/shard_map/ppermute | solution.py:245
  208.4 7.9 %collective-permute-done.42 = bf16[128,2048]{1,0:T(8,128)(2,1)S(1)} collective-permute-done((bf16[128,2048]{1,0:T(8,128)(2,1)S(1)}, bf16[128,2048]{1,0:T(8,128)(2,1)S(1)}, u32[]{:S(2)}, u32[]{:S(2)}) %collective-permute-start.42) | collective-permute-done | bytes 524320 | tf_op jit(solution)/shard_map/ppermute | solution.py:245
  217.2 1.5 collective-permute-start.31
  218.7 10.1 %collective-permute-done.38 = bf16[128,2048]{1,0:T(8,128)(2,1)S(1)} collective-permute-done((bf16[128,2048]{1,0:T(8,128)(2,1)S(1)}, bf16[128,2048]{1,0:T(8,128)(2,1)S(1)}, u32[]{:S(2)}, u32[]{:S(2)}) %collective-permute-start.38) | collective-permute-done | bytes 524320 | tf_op jit(solution)/shard_map/ppermute | solution.py:245
  229.0 3.2 %collective-permute-start.39 = (bf16[128,2048]{1,0:T(8,128)(2,1)S(1)}, bf16[128,2048]{1,0:T(8,128)(2,1)S(1)}, u32[]{:S(2)}, u32[]{:S(2)}) collective-permute-start(bf16[128,2048]{1,0:T(8,128)(2,1)S(1)} %add_convert_fusion.3), channel_id=1, source_target_pairs={{0,4},{2,6},{4,0},{6,2},{1,5},{3,7},{5,1},{7,3},{8,12},{10,14},{12... | collective-permute-start | bytes 1572872 | tf_op jit(solution)/shard_map/ppermute | solution.py:250
  232.2 4.3 %collective-permute-done.34 = bf16[128,2048]{1,0:T(8,128)(2,1)S(1)} collective-permute-done((bf16[128,2048]{1,0:T(8,128)(2,1)S(1)}, bf16[128,2048]{1,0:T(8,128)(2,1)S(1)}, u32[]{:S(2)}, u32[]{:S(2)}) %collective-permute-start.34) | collective-permute-done | bytes 524320 | tf_op jit(solution)/shard_map/ppermute | solution.py:245
  236.8 2.0 collective-permute-start.35
  238.7 1.3 collective-permute-done.31
  240.0 27.3 %collective-permute-done.39 = bf16[128,2048]{1,0:T(8,128)(2,1)S(1)} collective-permute-done((bf16[128,2048]{1,0:T(8,128)(2,1)S(1)}, bf16[128,2048]{1,0:T(8,128)(2,1)S(1)}, u32[]{:S(2)}, u32[]{:S(2)}) %collective-permute-start.39) | collective-permute-done | bytes 524320 | tf_op jit(solution)/shard_map/ppermute | solution.py:250
  267.3 10.7 %collective-permute-done.35 = bf16[128,2048]{1,0:T(8,128)(2,1)S(1)} collective-permute-done((bf16[128,2048]{1,0:T(8,128)(2,1)S(1)}, bf16[128,2048]{1,0:T(8,128)(2,1)S(1)}, u32[]{:S(2)}, u32[]{:S(2)}) %collective-permute-start.35) | collective-permute-done | bytes 524320 | tf_op jit(solution)/shard_map/ppermute | solution.py:250
  278.0 1.3 add_convert_fusion
  (89 shorter events, 13.9 us)
Async XLA Ops:
  0.6 59.9 %copy-start.2 = (bf16[128,2048]{1,0:T(8,128)(2,1)S(1)}, bf16[128,2048]{1,0:T(8,128)(2,1)}, u32[]{:S(2)}) copy-start(bf16[128,2048]{1,0:T(8,128)(2,1)} %tokens_ref.1) | copy-start | bytes 1572868
  0.6 59.9 %copy-start.3 = (f32[2048]{0:T(1024)S(1)}, f32[2048]{0:T(1024)}, u32[]{:S(2)}) copy-start(f32[2048]{0:T(1024)} %param.19) | copy-start | bytes 24580
  0.6 67.2 %collective-permute-start.12 = (bf16[2048,1408]{1,0:T(8,128)(2,1)}, bf16[2048,1408]{1,0:T(8,128)(2,1)}, u32[]{:S(2)}, u32[]{:S(2)}) collective-permute-start(bf16[2048,1408]{1,0:T(8,128)(2,1)} %bitcast.44), channel_id=1, source_target_pairs={{0,8},{8,0},{1,9},{9,1},{2,10},{10,2},{3,11},{11,3},{4,12},{12,4},... | collective-permute-start | bytes 17301512 | tf_op jit(solution)/shard_map/ppermute | solution.py:245
  1.4 66.5 %collective-permute-start.13 = (bf16[704,2048]{1,0:T(8,128)(2,1)}, bf16[704,2048]{1,0:T(8,128)(2,1)}, u32[]{:S(2)}, u32[]{:S(2)}) collective-permute-start(bf16[704,2048]{1,0:T(8,128)(2,1)} %bitcast.51), channel_id=1, source_target_pairs={{0,8},{8,0},{1,9},{9,1},{2,10},{10,2},{3,11},{11,3},{4,12},{12,4},... | collective-permute-start | bytes 8650760 | tf_op jit(solution)/shard_map/ppermute | solution.py:245
  2.9 5.6 %collective-permute-start.2 = (f32[12,128]{1,0:T(8,128)S(1)}, f32[12,128]{1,0:T(8,128)S(1)}, u32[]{:S(2)}, u32[]{:S(2)}) collective-permute-start(f32[12,128]{1,0:T(8,128)S(1)} %get-tuple-element.99), channel_id=1, source_target_pairs={{0,6},{2,0},{4,2},{6,4},{1,7},{3,1},{5,3},{7,5},{8,14},{10,8},{12,... | collective-permute-start | bytes 18440 | tf_op jit(solution)/shard_map/ppermute | solution.py:250
  2.9 5.6 %collective-permute-start.1 = (f32[12,128]{1,0:T(8,128)S(1)}, f32[12,128]{1,0:T(8,128)S(1)}, u32[]{:S(2)}, u32[]{:S(2)}) collective-permute-start(f32[12,128]{1,0:T(8,128)S(1)} %get-tuple-element.99), channel_id=1, source_target_pairs={{0,4},{2,6},{4,0},{6,2},{1,5},{3,7},{5,1},{7,3},{8,12},{10,14},{12... | collective-permute-start | bytes 18440 | tf_op jit(solution)/shard_map/ppermute | solution.py:250
  5.3 3.1 %collective-permute-start = (f32[12,128]{1,0:T(8,128)S(1)}, f32[12,128]{1,0:T(8,128)S(1)}, u32[]{:S(2)}, u32[]{:S(2)}) collective-permute-start(f32[12,128]{1,0:T(8,128)S(1)} %get-tuple-element.99), channel_id=1, source_target_pairs={{0,2},{2,4},{4,6},{6,0},{1,3},{3,5},{5,7},{7,1},{8,10},{10,12},{12... | collective-permute-start | bytes 18440 | tf_op jit(solution)/shard_map/ppermute | solution.py:250
  8.5 3.8 %collective-permute-start.3 = (f32[4,12,128]{2,1,0:T(8,128)S(1)}, f32[4,12,128]{2,1,0:T(8,128)S(1)}, u32[]{:S(2)}, u32[]{:S(2)}) collective-permute-start(f32[4,12,128]{2,1,0:T(8,128)S(1)} %get-tuple-element.89), channel_id=1, source_target_pairs={{0,1},{1,0},{2,3},{3,2},{4,5},{5,4},{6,7},{7,6},{8,9},{9,8},{10,11... | collective-permute-start | bytes 73736 | tf_op jit(solution)/shard_map/ppermute | solution.py:245
  10.7 6.7 %collective-permute-start.5 = (bf16[2,32,2048]{2,1,0:T(8,128)(2,1)S(1)}, bf16[2,32,2048]{2,1,0:T(8,128)(2,1)S(1)}, u32[]{:S(2)}, u32[]{:S(2)}) collective-permute-start(bf16[2,32,2048]{2,1,0:T(8,128)(2,1)S(1)} %constant_dynamic-update-slice_fusion.refs_0_), channel_id=1, source_target_pairs={{0,2},{2,4},{4,6},{6,0},{1,3},{3,5},{5,7},{7,1},{8,10},{10,12},{12... | collective-permute-start | bytes 786440 | tf_op jit(solution)/shard_map/ppermute | solution.py:250
  12.3 4.0 %collective-permute-start.4 = (f32[2,4,12,128]{3,2,1,0:T(8,128)S(1)}, f32[2,4,12,128]{3,2,1,0:T(8,128)S(1)}, u32[]{:S(2)}, u32[]{:S(2)}) collective-permute-start(f32[2,4,12,128]{3,2,1,0:T(8,128)S(1)} %get-tuple-element.87), channel_id=1, source_target_pairs={{0,16},{16,0},{1,17},{17,1},{2,18},{18,2},{3,19},{19,3},{4,20},{20... | collective-permute-start | bytes 147464 | tf_op jit(solution)/shard_map/ppermute | solution.py:245
  13.6 19.9 %collective-permute-start.6 = (bf16[2,32,2048]{2,1,0:T(8,128)(2,1)S(1)}, bf16[2,32,2048]{2,1,0:T(8,128)(2,1)S(1)}, u32[]{:S(2)}, u32[]{:S(2)}) collective-permute-start(bf16[2,32,2048]{2,1,0:T(8,128)(2,1)S(1)} %constant_dynamic-update-slice_fusion.refs_0_), channel_id=1, source_target_pairs={{0,4},{2,6},{4,0},{6,2},{1,5},{3,7},{5,1},{7,3},{8,12},{10,14},{12... | collective-permute-start | bytes 786440 | tf_op jit(solution)/shard_map/ppermute | solution.py:250
  16.3 22.3 %collective-permute-start.7 = (bf16[2,32,2048]{2,1,0:T(8,128)(2,1)S(1)}, bf16[2,32,2048]{2,1,0:T(8,128)(2,1)S(1)}, u32[]{:S(2)}, u32[]{:S(2)}) collective-permute-start(bf16[2,32,2048]{2,1,0:T(8,128)(2,1)S(1)} %constant_dynamic-update-slice_fusion.refs_0_), channel_id=1, source_target_pairs={{0,6},{2,0},{4,2},{6,4},{1,7},{3,1},{5,3},{7,5},{8,14},{10,8},{12,... | collective-permute-start | bytes 786440 | tf_op jit(solution)/shard_map/ppermute | solution.py:250
  17.4 21.4 %collective-permute-start.8 = (bf16[2,32,2048]{2,1,0:T(8,128)(2,1)S(1)}, bf16[2,32,2048]{2,1,0:T(8,128)(2,1)S(1)}, u32[]{:S(2)}, u32[]{:S(2)}) collective-permute-start(bf16[2,32,2048]{2,1,0:T(8,128)(2,1)S(1)} %constant_dynamic-update-slice_fusion.refs_0_), channel_id=1, source_target_pairs={{0,1},{1,0},{2,3},{3,2},{4,5},{5,4},{6,7},{7,6},{8,9},{9,8},{10,11... | collective-permute-start | bytes 786440 | tf_op jit(solution)/shard_map/ppermute | solution.py:245
  33.5 8.3 %collective-permute-start.9 = (bf16[2,32,2048]{2,1,0:T(8,128)(2,1)S(1)}, bf16[2,32,2048]{2,1,0:T(8,128)(2,1)S(1)}, u32[]{:S(2)}, u32[]{:S(2)}) collective-permute-start(bf16[2,32,2048]{2,1,0:T(8,128)(2,1)S(1)} %collective-permute-done.5.refs_1_), channel_id=1, source_target_pairs={{0,1},{1,0},{2,3},{3,2},{4,5},{5,4},{6,7},{7,6},{8,9},{9,8},{10,11... | collective-permute-start | bytes 786440 | tf_op jit(solution)/shard_map/ppermute | solution.py:245
  38.6 8.8 %collective-permute-start.10 = (bf16[2,32,2048]{2,1,0:T(8,128)(2,1)S(1)}, bf16[2,32,2048]{2,1,0:T(8,128)(2,1)S(1)}, u32[]{:S(2)}, u32[]{:S(2)}) collective-permute-start(bf16[2,32,2048]{2,1,0:T(8,128)(2,1)S(1)} %collective-permute-done.6.refs_2_), channel_id=1, source_target_pairs={{0,1},{1,0},{2,3},{3,2},{4,5},{5,4},{6,7},{7,6},{8,9},{9,8},{10,11... | collective-permute-start | bytes 786440 | tf_op jit(solution)/shard_map/ppermute | solution.py:245
  38.9 14.2 %collective-permute-start.11 = (bf16[2,32,2048]{2,1,0:T(8,128)(2,1)S(1)}, bf16[2,32,2048]{2,1,0:T(8,128)(2,1)S(1)}, u32[]{:S(2)}, u32[]{:S(2)}) collective-permute-start(bf16[2,32,2048]{2,1,0:T(8,128)(2,1)S(1)} %collective-permute-done.7.refs_3_), channel_id=1, source_target_pairs={{0,1},{1,0},{2,3},{3,2},{4,5},{5,4},{6,7},{7,6},{8,9},{9,8},{10,11... | collective-permute-start | bytes 786440 | tf_op jit(solution)/shard_map/ppermute | solution.py:245
  53.7 67.6 %slice-start = ((s8[5767168]{0:T(1024)(128)(4,1)}), s8[1572864]{0:T(1024)(128)(4,1)S(1)}, s32[]{:S(2)}) async-start(s8[5767168]{0:T(1024)(128)(4,1)} %bitcast.45), calls=%async_computation | async-start | bytes 3145728
  60.5 60.8 %copy-start = (bf16[1,704,2048]{2,1,0:T(8,128)(2,1)S(1)}, bf16[1,704,2048]{2,1,0:T(8,128)(2,1)}, u32[]{:S(2)}) copy-start(bf16[1,704,2048]{2,1,0:T(8,128)(2,1)} %param.23) | copy-start | bytes 8650756
  67.8 11.2 %collective-permute-start.17 = (bf16[128,2048]{1,0:T(8,128)(2,1)S(1)}, bf16[128,2048]{1,0:T(8,128)(2,1)S(1)}, u32[]{:S(2)}, u32[]{:S(2)}) collective-permute-start(bf16[128,2048]{1,0:T(8,128)(2,1)S(1)} %get-tuple-element.47.refs_2_), channel_id=1, source_target_pairs={{0,2},{2,4},{4,6},{6,0},{1,3},{3,5},{5,7},{7,1},{8,10},{10,12},{12... | collective-permute-start | bytes 1572872 | tf_op jit(solution)/shard_map/ppermute | solution.py:250
  67.9 11.3 %collective-permute-start.14 = (bf16[128,2048]{1,0:T(8,128)(2,1)S(1)}, bf16[128,2048]{1,0:T(8,128)(2,1)S(1)}, u32[]{:S(2)}, u32[]{:S(2)}) collective-permute-start(bf16[128,2048]{1,0:T(8,128)(2,1)S(1)} %get-tuple-element.47.refs_2_), channel_id=1, source_target_pairs={{0,1},{1,0},{2,3},{3,2},{4,5},{5,4},{6,7},{7,6},{8,9},{9,8},{10,11... | collective-permute-start | bytes 1572872 | tf_op jit(solution)/shard_map/ppermute | solution.py:245
  68.3 42.5 %collective-permute-start.21 = (bf16[128,2048]{1,0:T(8,128)(2,1)S(1)}, bf16[128,2048]{1,0:T(8,128)(2,1)S(1)}, u32[]{:S(2)}, u32[]{:S(2)}) collective-permute-start(bf16[128,2048]{1,0:T(8,128)(2,1)S(1)} %get-tuple-element.47.refs_2_), channel_id=1, source_target_pairs={{0,4},{2,6},{4,0},{6,2},{1,5},{3,7},{5,1},{7,3},{8,12},{10,14},{12... | collective-permute-start | bytes 1572872 | tf_op jit(solution)/shard_map/ppermute | solution.py:250
  69.9 41.4 %collective-permute-start.15 = (bf16[128,2048]{1,0:T(8,128)(2,1)S(1)}, bf16[128,2048]{1,0:T(8,128)(2,1)S(1)}, u32[]{:S(2)}, u32[]{:S(2)}) collective-permute-start(bf16[128,2048]{1,0:T(8,128)(2,1)S(1)} %get-tuple-element.47.refs_2_), channel_id=1, source_target_pairs={{0,16},{16,0},{1,17},{17,1},{2,18},{18,2},{3,19},{19,3},{4,20},{20... | collective-permute-start | bytes 1572872 | tf_op jit(solution)/shard_map/ppermute | solution.py:245
  71.1 44.7 %collective-permute-start.25 = (bf16[128,2048]{1,0:T(8,128)(2,1)S(1)}, bf16[128,2048]{1,0:T(8,128)(2,1)S(1)}, u32[]{:S(2)}, u32[]{:S(2)}) collective-permute-start(bf16[128,2048]{1,0:T(8,128)(2,1)S(1)} %get-tuple-element.47.refs_2_), channel_id=1, source_target_pairs={{0,6},{2,0},{4,2},{6,4},{1,7},{3,1},{5,3},{7,5},{8,14},{10,8},{12,... | collective-permute-start | bytes 1572872 | tf_op jit(solution)/shard_map/ppermute | solution.py:250
  79.1 37.9 %collective-permute-start.19 = (bf16[128,2048]{1,0:T(8,128)(2,1)S(1)}, bf16[128,2048]{1,0:T(8,128)(2,1)S(1)}, u32[]{:S(2)}, u32[]{:S(2)}) collective-permute-start(bf16[128,2048]{1,0:T(8,128)(2,1)S(1)} %collective-permute-done.17.refs_2_), channel_id=1, source_target_pairs={{0,16},{16,0},{1,17},{17,1},{2,18},{18,2},{3,19},{19,3},{4,20},{20... | collective-permute-start | bytes 1572872 | tf_op jit(solution)/shard_map/ppermute | solution.py:245
  79.2 38.0 %collective-permute-start.16 = (bf16[128,2048]{1,0:T(8,128)(2,1)S(1)}, bf16[128,2048]{1,0:T(8,128)(2,1)S(1)}, u32[]{:S(2)}, u32[]{:S(2)}) collective-permute-start(bf16[128,2048]{1,0:T(8,128)(2,1)S(1)} %collective-permute-done.14.refs_3_), channel_id=1, source_target_pairs={{0,16},{16,0},{1,17},{17,1},{2,18},{18,2},{3,19},{19,3},{4,20},{20... | collective-permute-start | bytes 1572872 | tf_op jit(solution)/shard_map/ppermute | solution.py:245
  110.8 10.5 %collective-permute-start.22 = (bf16[128,2048]{1,0:T(8,128)(2,1)S(1)}, bf16[128,2048]{1,0:T(8,128)(2,1)S(1)}, u32[]{:S(2)}, u32[]{:S(2)}) collective-permute-start(bf16[128,2048]{1,0:T(8,128)(2,1)S(1)} %collective-permute-done.21.refs_2_), channel_id=1, source_target_pairs={{0,1},{1,0},{2,3},{3,2},{4,5},{5,4},{6,7},{7,6},{8,9},{9,8},{10,11... | collective-permute-start | bytes 1572872 | tf_op jit(solution)/shard_map/ppermute | solution.py:245
  111.3 21.2 %collective-permute-start.18 = (bf16[128,2048]{1,0:T(8,128)(2,1)S(1)}, bf16[128,2048]{1,0:T(8,128)(2,1)S(1)}, u32[]{:S(2)}, u32[]{:S(2)}) collective-permute-start(bf16[128,2048]{1,0:T(8,128)(2,1)S(1)} %collective-permute-done.17.refs_2_), channel_id=1, source_target_pairs={{0,1},{1,0},{2,3},{3,2},{4,5},{5,4},{6,7},{7,6},{8,9},{9,8},{10,11... | collective-permute-start | bytes 1572872 | tf_op jit(solution)/shard_map/ppermute | solution.py:245
  115.8 17.4 %collective-permute-start.27 = (bf16[128,2048]{1,0:T(8,128)(2,1)S(1)}, bf16[128,2048]{1,0:T(8,128)(2,1)S(1)}, u32[]{:S(2)}, u32[]{:S(2)}) collective-permute-start(bf16[128,2048]{1,0:T(8,128)(2,1)S(1)} %collective-permute-done.25.refs_2_), channel_id=1, source_target_pairs={{0,16},{16,0},{1,17},{17,1},{2,18},{18,2},{3,19},{19,3},{4,20},{20... | collective-permute-start | bytes 1572872 | tf_op jit(solution)/shard_map/ppermute | solution.py:245
  116.9 26.8 %collective-permute-start.20 = (bf16[128,2048]{1,0:T(8,128)(2,1)S(1)}, bf16[128,2048]{1,0:T(8,128)(2,1)S(1)}, u32[]{:S(2)}, u32[]{:S(2)}) collective-permute-start(bf16[128,2048]{1,0:T(8,128)(2,1)S(1)} %collective-permute-done.19.refs_4_), channel_id=1, source_target_pairs={{0,1},{1,0},{2,3},{3,2},{4,5},{5,4},{6,7},{7,6},{8,9},{9,8},{10,11... | collective-permute-start | bytes 1572872 | tf_op jit(solution)/shard_map/ppermute | solution.py:245
  117.2 34.4 %collective-permute-start.23 = (bf16[128,2048]{1,0:T(8,128)(2,1)S(1)}, bf16[128,2048]{1,0:T(8,128)(2,1)S(1)}, u32[]{:S(2)}, u32[]{:S(2)}) collective-permute-start(bf16[128,2048]{1,0:T(8,128)(2,1)S(1)} %collective-permute-done.21.refs_2_), channel_id=1, source_target_pairs={{0,16},{16,0},{1,17},{17,1},{2,18},{18,2},{3,19},{19,3},{4,20},{20... | collective-permute-start | bytes 1572872 | tf_op jit(solution)/shard_map/ppermute | solution.py:245
  121.3 30.9 %collective-permute-start.24 = (bf16[128,2048]{1,0:T(8,128)(2,1)S(1)}, bf16[128,2048]{1,0:T(8,128)(2,1)S(1)}, u32[]{:S(2)}, u32[]{:S(2)}) collective-permute-start(bf16[128,2048]{1,0:T(8,128)(2,1)S(1)} %collective-permute-done.22.refs_3_), channel_id=1, source_target_pairs={{0,16},{16,0},{1,17},{17,1},{2,18},{18,2},{3,19},{19,3},{4,20},{20... | collective-permute-start | bytes 1572872 | tf_op jit(solution)/shard_map/ppermute | solution.py:245
  132.5 27.4 %collective-permute-start.26 = (bf16[128,2048]{1,0:T(8,128)(2,1)S(1)}, bf16[128,2048]{1,0:T(8,128)(2,1)S(1)}, u32[]{:S(2)}, u32[]{:S(2)}) collective-permute-start(bf16[128,2048]{1,0:T(8,128)(2,1)S(1)} %collective-permute-done.25.refs_2_), channel_id=1, source_target_pairs={{0,1},{1,0},{2,3},{3,2},{4,5},{5,4},{6,7},{7,6},{8,9},{9,8},{10,11... | collective-permute-start | bytes 1572872 | tf_op jit(solution)/shard_map/ppermute | solution.py:245
  133.2 33.1 %collective-permute-start.28 = (bf16[128,2048]{1,0:T(8,128)(2,1)S(1)}, bf16[128,2048]{1,0:T(8,128)(2,1)S(1)}, u32[]{:S(2)}, u32[]{:S(2)}) collective-permute-start(bf16[128,2048]{1,0:T(8,128)(2,1)S(1)} %collective-permute-done.27.refs_4_), channel_id=1, source_target_pairs={{0,1},{1,0},{2,3},{3,2},{4,5},{5,4},{6,7},{7,6},{8,9},{9,8},{10,11... | collective-permute-start | bytes 1572872 | tf_op jit(solution)/shard_map/ppermute | solution.py:245
  174.2 9.6 %collective-permute-start.41 = (bf16[128,2048]{1,0:T(8,128)(2,1)S(1)}, bf16[128,2048]{1,0:T(8,128)(2,1)S(1)}, u32[]{:S(2)}, u32[]{:S(2)}) collective-permute-start(bf16[128,2048]{1,0:T(8,128)(2,1)S(1)} %get-tuple-element.81), channel_id=1, source_target_pairs={{0,16},{16,0},{1,17},{17,1},{2,18},{18,2},{3,19},{19,3},{4,20},{20... | collective-permute-start | bytes 1572872 | tf_op jit(solution)/shard_map/ppermute | solution.py:245
  174.2 9.7 %collective-permute-start.37 = (bf16[128,2048]{1,0:T(8,128)(2,1)S(1)}, bf16[128,2048]{1,0:T(8,128)(2,1)S(1)}, u32[]{:S(2)}, u32[]{:S(2)}) collective-permute-start(bf16[128,2048]{1,0:T(8,128)(2,1)S(1)} %get-tuple-element.77), channel_id=1, source_target_pairs={{0,1},{1,0},{2,3},{3,2},{4,5},{5,4},{6,7},{7,6},{8,9},{9,8},{10,11... | collective-permute-start | bytes 1572872 | tf_op jit(solution)/shard_map/ppermute | solution.py:245
  174.9 32.7 %collective-permute-start.40 = (bf16[128,2048]{1,0:T(8,128)(2,1)S(1)}, bf16[128,2048]{1,0:T(8,128)(2,1)S(1)}, u32[]{:S(2)}, u32[]{:S(2)}) collective-permute-start(bf16[128,2048]{1,0:T(8,128)(2,1)S(1)} %get-tuple-element.79), channel_id=1, source_target_pairs={{0,16},{16,0},{1,17},{17,1},{2,18},{18,2},{3,19},{19,3},{4,20},{20... | collective-permute-start | bytes 1572872 | tf_op jit(solution)/shard_map/ppermute | solution.py:245
  176.3 40.9 %collective-permute-start.36 = (bf16[128,2048]{1,0:T(8,128)(2,1)S(1)}, bf16[128,2048]{1,0:T(8,128)(2,1)S(1)}, u32[]{:S(2)}, u32[]{:S(2)}) collective-permute-start(bf16[128,2048]{1,0:T(8,128)(2,1)S(1)} %get-tuple-element.75), channel_id=1, source_target_pairs={{0,1},{1,0},{2,3},{3,2},{4,5},{5,4},{6,7},{7,6},{8,9},{9,8},{10,11... | collective-permute-start | bytes 1572872 | tf_op jit(solution)/shard_map/ppermute | solution.py:245
  177.2 29.1 %collective-permute-start.33 = (bf16[128,2048]{1,0:T(8,128)(2,1)S(1)}, bf16[128,2048]{1,0:T(8,128)(2,1)S(1)}, u32[]{:S(2)}, u32[]{:S(2)}) collective-permute-start(bf16[128,2048]{1,0:T(8,128)(2,1)S(1)} %get-tuple-element.73), channel_id=1, source_target_pairs={{0,16},{16,0},{1,17},{17,1},{2,18},{18,2},{3,19},{19,3},{4,20},{20... | collective-permute-start | bytes 1572872 | tf_op jit(solution)/shard_map/ppermute | solution.py:245
  183.8 45.2 %collective-permute-start.32 = (bf16[128,2048]{1,0:T(8,128)(2,1)S(1)}, bf16[128,2048]{1,0:T(8,128)(2,1)S(1)}, u32[]{:S(2)}, u32[]{:S(2)}) collective-permute-start(bf16[128,2048]{1,0:T(8,128)(2,1)S(1)} %get-tuple-element.71), channel_id=1, source_target_pairs={{0,16},{16,0},{1,17},{17,1},{2,18},{18,2},{3,19},{19,3},{4,20},{20... | collective-permute-start | bytes 1572872 | tf_op jit(solution)/shard_map/ppermute | solution.py:245
  183.9 23.2 %collective-permute-start.30 = (bf16[128,2048]{1,0:T(8,128)(2,1)S(1)}, bf16[128,2048]{1,0:T(8,128)(2,1)S(1)}, u32[]{:S(2)}, u32[]{:S(2)}) collective-permute-start(bf16[128,2048]{1,0:T(8,128)(2,1)S(1)} %get-tuple-element.69), channel_id=1, source_target_pairs={{0,1},{1,0},{2,3},{3,2},{4,5},{5,4},{6,7},{7,6},{8,9},{9,8},{10,11... | collective-permute-start | bytes 1572872 | tf_op jit(solution)/shard_map/ppermute | solution.py:245
  206.3 10.1 %collective-permute-start.42 = (bf16[128,2048]{1,0:T(8,128)(2,1)S(1)}, bf16[128,2048]{1,0:T(8,128)(2,1)S(1)}, u32[]{:S(2)}, u32[]{:S(2)}) collective-permute-start(bf16[128,2048]{1,0:T(8,128)(2,1)S(1)} %add_convert_fusion.2), channel_id=1, source_target_pairs={{0,1},{1,0},{2,3},{3,2},{4,5},{5,4},{6,7},{7,6},{8,9},{9,8},{10,11... | collective-permute-start | bytes 1572872 | tf_op jit(solution)/shard_map/ppermute | solution.py:245
  207.1 21.6 %collective-permute-start.38 = (bf16[128,2048]{1,0:T(8,128)(2,1)S(1)}, bf16[128,2048]{1,0:T(8,128)(2,1)S(1)}, u32[]{:S(2)}, u32[]{:S(2)}) collective-permute-start(bf16[128,2048]{1,0:T(8,128)(2,1)S(1)} %add_convert_fusion.4), channel_id=1, source_target_pairs={{0,16},{16,0},{1,17},{17,1},{2,18},{18,2},{3,19},{19,3},{4,20},{20... | collective-permute-start | bytes 1572872 | tf_op jit(solution)/shard_map/ppermute | solution.py:245
  207.6 31.1 %collective-permute-start.29 = (bf16[128,2048]{1,0:T(8,128)(2,1)S(1)}, bf16[128,2048]{1,0:T(8,128)(2,1)S(1)}, u32[]{:S(2)}, u32[]{:S(2)}) collective-permute-start(bf16[128,2048]{1,0:T(8,128)(2,1)S(1)} %get-tuple-element.67), channel_id=1, source_target_pairs={{0,1},{1,0},{2,3},{3,2},{4,5},{5,4},{6,7},{7,6},{8,9},{9,8},{10,11... | collective-permute-start | bytes 1572872 | tf_op jit(solution)/shard_map/ppermute | solution.py:245
  216.3 20.2 %collective-permute-start.34 = (bf16[128,2048]{1,0:T(8,128)(2,1)S(1)}, bf16[128,2048]{1,0:T(8,128)(2,1)S(1)}, u32[]{:S(2)}, u32[]{:S(2)}) collective-permute-start(bf16[128,2048]{1,0:T(8,128)(2,1)S(1)} %add_convert_fusion.6), channel_id=1, source_target_pairs={{0,1},{1,0},{2,3},{3,2},{4,5},{5,4},{6,7},{7,6},{8,9},{9,8},{10,11... | collective-permute-start | bytes 1572872 | tf_op jit(solution)/shard_map/ppermute | solution.py:245
  217.2 22.8 %collective-permute-start.31 = (bf16[128,2048]{1,0:T(8,128)(2,1)S(1)}, bf16[128,2048]{1,0:T(8,128)(2,1)S(1)}, u32[]{:S(2)}, u32[]{:S(2)}) collective-permute-start(bf16[128,2048]{1,0:T(8,128)(2,1)S(1)} %add_convert_fusion.8), channel_id=1, source_target_pairs={{0,16},{16,0},{1,17},{17,1},{2,18},{18,2},{3,19},{19,3},{4,20},{20... | collective-permute-start | bytes 1572872 | tf_op jit(solution)/shard_map/ppermute | solution.py:245
  228.7 11.2 %collective-permute-start.43 = (bf16[128,2048]{1,0:T(8,128)(2,1)S(1)}, bf16[128,2048]{1,0:T(8,128)(2,1)S(1)}, u32[]{:S(2)}, u32[]{:S(2)}) collective-permute-start(bf16[128,2048]{1,0:T(8,128)(2,1)S(1)} %add_convert_fusion.1), channel_id=1, source_target_pairs={{0,2},{2,4},{4,6},{6,0},{1,3},{3,5},{5,7},{7,1},{8,10},{10,12},{12... | collective-permute-start | bytes 1572872 | tf_op jit(solution)/shard_map/ppermute | solution.py:250
  229.0 38.3 %collective-permute-start.39 = (bf16[128,2048]{1,0:T(8,128)(2,1)S(1)}, bf16[128,2048]{1,0:T(8,128)(2,1)S(1)}, u32[]{:S(2)}, u32[]{:S(2)}) collective-permute-start(bf16[128,2048]{1,0:T(8,128)(2,1)S(1)} %add_convert_fusion.3), channel_id=1, source_target_pairs={{0,4},{2,6},{4,0},{6,2},{1,5},{3,7},{5,1},{7,3},{8,12},{10,14},{12... | collective-permute-start | bytes 1572872 | tf_op jit(solution)/shard_map/ppermute | solution.py:250
  236.8 41.3 %collective-permute-start.35 = (bf16[128,2048]{1,0:T(8,128)(2,1)S(1)}, bf16[128,2048]{1,0:T(8,128)(2,1)S(1)}, u32[]{:S(2)}, u32[]{:S(2)}) collective-permute-start(bf16[128,2048]{1,0:T(8,128)(2,1)S(1)} %add_convert_fusion.5), channel_id=1, source_target_pairs={{0,6},{2,0},{4,2},{6,4},{1,7},{3,1},{5,3},{7,5},{8,14},{10,8},{12,... | collective-permute-start | bytes 1572872 | tf_op jit(solution)/shard_map/ppermute | solution.py:250
  (3 other events, 61.5 us)

commit v5 on v4

--- a/solution.py
+++ b/solution.py
@@ -65,6 +65,9 @@
         out_specs=by_cols,
         out_shape=jax.ShapeDtypeStruct((rows, width), jnp.bfloat16),
         compiler_params=pltpu.CompilerParams(vmem_limit_bytes=VMEM_LIMIT),
+        cost_estimate=pl.CostEstimate(
+            flops=12 * rows * rows * width, bytes_accessed=12 * rows * width, transcendentals=0
+        ),
         name="attention",
     )(queries, suffix_keys, suffix_values, *pieces)
 
@@ -111,6 +114,9 @@
         ],
         scratch_shapes=[pltpu.VMEM((steps, rows, span), jnp.float32)],
         compiler_params=pltpu.CompilerParams(vmem_limit_bytes=VMEM_LIMIT),
+        cost_estimate=pl.CostEstimate(
+            flops=2 * rows * width * width, bytes_accessed=2 * width * width, transcendentals=0
+        ),
         name="project_and_norm",
     )(heads_out, out_weight, tokens, norm_gain.reshape(1, width))
 
@@ -254,13 +260,52 @@
     return sum(one.astype(jnp.float32) for one in arrays).astype(jnp.bfloat16)
 
 
-def relative_slots(routes, route_weights, capacity):
+def along_line(block):
+    columns = lax.axis_size("line")
+    blocks = {0: block}
+    for back in nearest_first()[1:]:
+        if back <= columns // 2:
+            blocks[back] = shift(blocks[back - 1], "line", 1)
+        else:
+            blocks[back] = shift(blocks[(back + 1) % columns], "line", -1)
+    return [blocks[back] for back in range(columns)]
+
+
+def nearest_first():
+    columns = lax.axis_size("line")
+    return sorted(range(columns), key=lambda back: (min(back, columns - back), back))
+
+
+def prefix_pieces(kv, table, weights):
+    order = nearest_first()
+    held, swapped = {0: kv}, {}
+    ready = [0]
+    for i in range(1, len(order), 2):
+        fresh = order[i : i + 2]
+        for back in fresh:
+            step = 1 if back <= len(order) // 2 else -1
+            held[back] = shift(held[(back - step) % len(order)], "line", step)
+        for back in ready:
+            swapped[back] = swap(held[back], "side")
+        moved, crossed, table, weights = lax.optimization_barrier(
+            ([held[back] for back in fresh], [swapped[back] for back in ready], table, weights)
+        )
+        if i == 1:
+            others = [swap(one, "core") for one in weights]
+        held.update(zip(fresh, moved))
+        swapped.update(zip(ready, crossed))
+        ready = fresh
+    for back in ready:
+        swapped[back] = swap(held[back], "side")
+    tables = [table] + [shift(table, "line", back) for back in range(1, len(order))]
+    tables, crossed = lax.optimization_barrier((tables, [swapped[back] for back in ready]))
+    swapped.update(zip(ready, crossed))
+    return list(held.values()) + list(swapped.values()), jnp.stack(tables), others
+
+
+def relative_slots(table, capacity):
     columns = lax.axis_size("line")
     far, core, line = lax.axis_index("far"), lax.axis_index("core"), lax.axis_index("line")
-    table = jnp.concatenate([routes.T.astype(jnp.float32), route_weights.T])
-    table = jnp.stack([table] + [shift(table, "line", back) for back in range(1, columns)])
-    table = jnp.stack([table, swap(table, "side")])
-    table = jnp.stack([table, swap(table, "far")])
     table = table.reshape((4 * columns,) + table.shape[3:])
     own = (far * 2 + core) * columns + line
     other = (far * 2 + 1 - core) * columns + line
@@ -272,43 +317,48 @@
     return slots, gates
 
 
-def go_home(results, back):
+def over_plane(block, axes):
+    first = swap(block, axes[0])
+    second = swap(block, axes[1])
+    corner = swap(first, axes[1])
+    if axes[0] == "side":
+        return [block, first, second, corner]
+    return [block, second, first, corner]
+
+
+def first_sums(results, axes):
     here, beside, across, corner = results
-    if back % 2 == 0:
-        across = add(across, swap(corner, "side"))
-        total = add(here, swap(beside, "side"), swap(across, "far"))
-    else:
-        beside = add(beside, swap(corner, "far"))
-        total = add(here, swap(across, "far"), swap(beside, "side"))
+    near, rest = (beside, across) if axes[0] == "side" else (across, beside)
+    return here, rest, swap(corner, axes[0]), swap(near, axes[0])
+
+
+def last_sums(here, rest, corner, near, axes, back):
+    total = add(here, near, swap(add(rest, corner), axes[1]))
     return shift(total, "line", -back) if back else total
 
 
 def gather_plan(normed, slots, gates, weights, capacity):
-    columns = lax.axis_size("line")
-    normed, weights = lax.optimization_barrier((normed, weights))
-    results = []
-    for back in range(columns):
-        block = shift(normed, "line", back) if back else normed
-        if back % 2 == 0:
-            beside = swap(block, "side")
-            across = swap(block, "far")
-            corner = swap(beside, "far")
-        else:
-            across = swap(block, "far")
-            beside = swap(block, "side")
-            corner = swap(across, "side")
+    order = nearest_first()
+    blocks = along_line(normed)
+    axes = [("side", "far") if i % 2 == 0 else ("far", "side") for i in range(len(order))]
+    sums, previous, own = {}, None, None
+    for i, back in enumerate(order):
+        plane = over_plane(blocks[back], axes[i])
         mine = slots[:, back]
-        if back:
-            mine, results[-1][0] = lax.optimization_barrier((mine, results[-1][0]))
-        results.append(
-            list(
-                run_experts(
-                    [block, beside, across, corner], mine, gates[:, back], weights, capacity
-                )
-            )
-        )
-    results[0], results[-1] = lax.optimization_barrier((results[0], results[-1]))
-    return add(*[go_home(results[back], back) for back in range(columns)])
+        if i >= 3:
+            mine, sums[i - 2] = lax.optimization_barrier((mine, sums[i - 2]))
+        if i > 0:
+            mine, previous = lax.optimization_barrier((mine, previous))
+            if i == 1:
+                own = previous
+            else:
+                sums[i - 1] = first_sums(previous, axes[i - 1])
+        previous = run_experts(plane, mine, gates[:, back], weights, capacity)
+    last = len(order) - 1
+    sums[last] = first_sums(previous, axes[last])
+    own, sums[last] = lax.optimization_barrier((own, sums[last]))
+    sums[0] = first_sums(own, axes[0])
+    return add(*[last_sums(*sums[i], axes[i], back) for i, back in enumerate(order)])
 
 
 def on_device(
@@ -333,19 +383,21 @@
     kv = jnp.concatenate([prefix_keys, prefix_values])
     weights = [gate_up_weight[0], down_weight[0]]
     if gather_fits:
-        lines = [kv] + [shift(kv, "line", k) for k in range(1, lax.axis_size("line"))]
-        pieces = lines + [swap(piece, "side") for piece in lines]
-        weights = weights + [swap(one, "core") for one in weights]
-        slots, gates = relative_slots(routes, route_weights, capacity)
-        queries, slots, gates = lax.optimization_barrier((queries, slots, gates))
+        table = jnp.concatenate([routes.T.astype(jnp.float32), route_weights.T])
+        pieces, table, others = prefix_pieces(kv, table, weights)
+        beside = swap(table, "side")
     else:
-        pieces = [
-            lax.all_gather(kv, ("line", "side"), axis=1, tiled=True)
-        ]
+        pieces = [lax.all_gather(kv, ("line", "side"), axis=1, tiled=True)]
     heads_out = attention(queries, suffix_keys, suffix_values, pieces)
+    if gather_fits:
+        heads_out, beside = lax.optimization_barrier((heads_out, beside))
+        table = jnp.stack([table, beside])
+        across = swap(table, "far")
     attended, normed = project(heads_out, out_weight, tokens, norm_gain)
     if gather_fits:
-        routed = gather_plan(normed, slots, gates, weights, capacity)
+        normed, others, across = lax.optimization_barrier((normed, others, across))
+        slots, gates = relative_slots(jnp.stack([table, across]), capacity)
+        routed = gather_plan(normed, slots, gates, weights + others, capacity)
     else:
         routed = exchange_plan(
             normed, routes, route_weights, weights[0], weights[1], experts, capacity

time: 280 us -> 244 us (0.87)
  the two profiles are of different devices: /device:TPU:9 before, /device:TPU:0 now
where the time goes in v5:
time: 244 us; the launch traced here: 243 us
  waiting for transfers between devices  98.1 us (40%)
  starting transfers between devices  68.4 us (28%)
  Pallas kernels  49.5 us (20%)
  local copies, waits for them, and re-layouts  21.7 us (9%)
  other arithmetic  4.11 us (2%)
    ppermute x32, waiting for transfers between devices, swap(): return lax.ppermute(array, axis, [(0, 1), (1, 0)])  55.7 us
    ppermute x12, waiting for transfers between devices, shift(): lax.ppermute(array, axis, [(i, (i + amount) % size) for i in range(size)])  42.4 us
    pallas_call x4, Pallas kernels, run_experts(): pl.pallas_call(lambda *refs: experts_kernel(capacity, count, *refs), in_s...  36.9 us
    ppermute x12, starting transfers between devices, shift(): lax.ppermute(array, axis, [(i, (i + amount) % size) for i in range(size)])  35.3 us
    ppermute x32, starting transfers between devices, swap(): return lax.ppermute(array, axis, [(0, 1), (1, 0)])  33.1 us
    unnamed x49, local copies, waits for them, and re-layouts  20.7 us
    pallas_call x1, Pallas kernels, attention(): pl.pallas_call(attention_kernel, grid=(width // span,), in_specs=[by_cols...  6.64 us
    pallas_call x1, Pallas kernels, project(): pl.pallas_call(project_kernel, grid=(steps,), in_specs=[pl.BlockSpec((row...  5.97 us
  transfers between devices with their start and end apart: 44, of which 20 were waited for; matrix products, arithmetic and copies ran while one was open for 1% of the time, Pallas kernels for 17%

profile of v5, /device:TPU:0, one launch (start us, length us, event | category | flops | bytes accessed | tf_op | source)
XLA Modules:
  0.0 243.0 jit_solution(9128302220031861096)
XLA Ops:
  2.5 3.1 %collective-permute-start = (bf16[2,32,2048]{2,1,0:T(8,128)(2,1)S(1)}, bf16[2,32,2048]{2,1,0:T(8,128)(2,1)S(1)}, u32[]{:S(2)}, u32[]{:S(2)}) collective-permute-start(bf16[2,32,2048]{2,1,0:T(8,128)(2,1)S(1)} %constant_dynamic-update-slice_fusion.refs_0_), channel_id=1, source_target_pairs={{0,2},{2,4},{4,6},{6,0},{1,3},{3,5},{5,7},{7,1},{8,10},{10,12},{12... | collective-permute-start | bytes 786440 | tf_op jit(solution)/shard_map/ppermute | solution.py:256
  5.5 2.1 collective-permute-start.1
  7.6 1.7 collective-permute-start.2
  10.7 4.1 %collective-permute-done.refs_1_ = bf16[2,32,2048]{2,1,0:T(8,128)(2,1)S(1)} collective-permute-done((bf16[2,32,2048]{2,1,0:T(8,128)(2,1)S(1)}, bf16[2,32,2048]{2,1,0:T(8,128)(2,1)S(1)}, u32[]{:S(2)}, u32[]{:S(2)}) %collective-permute-start) | collective-permute-done | bytes 262176 | tf_op jit(solution)/shard_map/ppermute | solution.py:256
  14.7 4.2 %collective-permute-done.1.refs_2_ = bf16[2,32,2048]{2,1,0:T(8,128)(2,1)S(1)} collective-permute-done((bf16[2,32,2048]{2,1,0:T(8,128)(2,1)S(1)}, bf16[2,32,2048]{2,1,0:T(8,128)(2,1)S(1)}, u32[]{:S(2)}, u32[]{:S(2)}) %collective-permute-start.1) | collective-permute-done | bytes 262176 | tf_op jit(solution)/shard_map/ppermute | solution.py:256
  19.4 1.1 collective-permute-start.3
  20.6 1.5 collective-permute-start.4
  22.6 6.9 %collective-permute-done.3.refs_3_ = bf16[2,32,2048]{2,1,0:T(8,128)(2,1)S(1)} collective-permute-done((bf16[2,32,2048]{2,1,0:T(8,128)(2,1)S(1)}, bf16[2,32,2048]{2,1,0:T(8,128)(2,1)S(1)}, u32[]{:S(2)}, u32[]{:S(2)}) %collective-permute-start.3) | collective-permute-done | bytes 262176 | tf_op jit(solution)/shard_map/ppermute | solution.py:256
  29.8 4.4 %collective-permute-done.5.refs_6_ = bf16[2,32,2048]{2,1,0:T(8,128)(2,1)S(1)} collective-permute-done((bf16[2,32,2048]{2,1,0:T(8,128)(2,1)S(1)}, bf16[2,32,2048]{2,1,0:T(8,128)(2,1)S(1)}, u32[]{:S(2)}, u32[]{:S(2)}) %collective-permute-start.5) | collective-permute-done | bytes 262176 | tf_op jit(solution)/shard_map/ppermute | solution.py:251
  34.1 1.5 collective-permute-start.9
  36.4 2.5 %collective-permute-start.7 = (f32[12,128]{1,0:T(8,128)S(1)}, f32[12,128]{1,0:T(8,128)S(1)}, u32[]{:S(2)}, u32[]{:S(2)}) collective-permute-start(f32[12,128]{1,0:T(8,128)S(1)} %pad_maximum_fusion.3), channel_id=1, source_target_pairs={{0,4},{2,6},{4,0},{6,2},{1,5},{3,7},{5,1},{7,3},{8,12},{10,14},{12... | collective-permute-start | bytes 18440 | tf_op jit(solution)/shard_map/ppermute | solution.py:256
  38.9 2.2 collective-permute-done.6
  42.0 2.8 %collective-permute-done.8 = f32[12,128]{1,0:T(8,128)S(1)} collective-permute-done((f32[12,128]{1,0:T(8,128)S(1)}, f32[12,128]{1,0:T(8,128)S(1)}, u32[]{:S(2)}, u32[]{:S(2)}) %collective-permute-start.8) | collective-permute-done | bytes 6176 | tf_op jit(solution)/shard_map/ppermute | solution.py:256
  45.5 6.6 %attention.1.heads_ref = bf16[128,2048]{1,0:T(8,128)(2,1)} custom-call(bf16[128,2048]{1,0:T(8,128)(2,1)} %q_ref.1, bf16[128,2048]{1,0:T(8,128)(2,1)} %sk_ref.1, bf16[128,2048]{1,0:T(8,128)(2,1)} %sv_ref.1, bf16[2,32,2048]{2,1,0:T(8,128)(2,1)S(1)} %constant_dynamic-update-slice_fusion.refs_0_, bf16[2,32,2048]{2,1,0:T(8,128)(2,1)S(1)} %collective-permute-done.refs_1_, ...), custom_call_target="tpu_custom_call" | custom-call | flops 402653184 | bytes 3145728 | tf_op jit(solution)/shard_map/attention/pallas_call | solution.py:60
  52.1 1.6 collective-permute-start.13
  56.5 6.0 %project_and_norm.1 = (bf16[128,2048]{1,0:T(8,128)(2,1)}, bf16[128,2048]{1,0:T(8,128)(2,1)S(1)}) custom-call(bf16[128,2048]{1,0:T(8,128)(2,1)S(1)} %copy-done.6, bf16[2048,2048]{1,0:T(8,128)(2,1)} %weight_ref.1, bf16[128,2048]{1,0:T(8,128)(2,1)S(1)} %copy-done.15, f32[1,2048]{1,0:T(1,128)S(1)} %bitcast.63), custom_call_target="tpu_custom_call" | custom-call | flops 1073741824 | bytes 8388608 | tf_op jit(solution)/shard_map/project_and_norm/pallas_call | solution.py:101
  62.5 1.6 copy-done.3
  64.1 1.4 collective-permute-start.14
  66.0 3.8 %collective-permute-start.23 = (bf16[128,2048]{1,0:T(8,128)(2,1)S(1)}, bf16[128,2048]{1,0:T(8,128)(2,1)}, u32[]{:S(2)}, u32[]{:S(2)}) collective-permute-start(bf16[128,2048]{1,0:T(8,128)(2,1)S(1)} %get-tuple-element.89.refs_2_), channel_id=1, source_target_pairs={{0,6},{2,0},{4,2},{6,4},{1,7},{3,1},{5,3},{7,5},{8,14},{10,8},{12,... | collective-permute-start | bytes 1572872 | tf_op jit(solution)/shard_map/ppermute | solution.py:256
  70.8 10.0 %collective-permute-done.17.refs_2_ = bf16[128,2048]{1,0:T(8,128)(2,1)S(1)} collective-permute-done((bf16[128,2048]{1,0:T(8,128)(2,1)S(1)}, bf16[128,2048]{1,0:T(8,128)(2,1)S(1)}, u32[]{:S(2)}, u32[]{:S(2)}) %collective-permute-start.17) | collective-permute-done | bytes 524320 | tf_op jit(solution)/shard_map/ppermute | solution.py:256
  81.3 1.7 collective-permute-start.27
  83.0 2.0 collective-permute-start.16
  87.2 3.4 %collective-permute-done.23.refs_2_ = bf16[128,2048]{1,0:T(8,128)(2,1)} collective-permute-done((bf16[128,2048]{1,0:T(8,128)(2,1)S(1)}, bf16[128,2048]{1,0:T(8,128)(2,1)}, u32[]{:S(2)}, u32[]{:S(2)}) %collective-permute-start.23) | collective-permute-done | bytes 524320 | tf_op jit(solution)/shard_map/ppermute | solution.py:256
  92.9 7.2 %collective-permute-done.16.refs_5_ = bf16[128,2048]{1,0:T(8,128)(2,1)} collective-permute-done((bf16[128,2048]{1,0:T(8,128)(2,1)S(1)}, bf16[128,2048]{1,0:T(8,128)(2,1)}, u32[]{:S(2)}, u32[]{:S(2)}) %collective-permute-start.16) | collective-permute-done | bytes 524320 | tf_op jit(solution)/shard_map/ppermute | solution.py:251
  100.1 2.0 collective-permute-start.29
  102.1 2.6 %copy-done = bf16[1,2048,1408]{2,1,0:T(8,128)(2,1)S(1)} copy-done((bf16[1,2048,1408]{2,1,0:T(8,128)(2,1)S(1)}, bf16[1,2048,1408]{2,1,0:T(8,128)(2,1)}, u32[]{:S(2)}) %copy-start) | copy-done | bytes 5767192
  104.8 1.8 copy-done.1
  106.6 1.8 copy-done.4
  110.5 9.2 %experts.4 = (bf16[128,2048]{1,0:T(8,128)(2,1)S(1)}, bf16[128,2048]{1,0:T(8,128)(2,1)S(1)}, bf16[128,2048]{1,0:T(8,128)(2,1)S(1)}, bf16[128,2048]{1,0:T(8,128)(2,1)S(1)}) custom-call(s32[4,2,1,128]{3,2,1,0:T(1,128)S(1)} %bitcast.62, f32[4,2,1,128]{3,2,1,0:T(1,128)S(1)} %bitcast.60, bf16[128,2048]{1,0:T(8,128)(2,1)S(1)} %copy-done.8, ...), custom_call_target="tpu_custom_call" | custom-call | flops 4429185024 | bytes 21495808 | tf_op jit(solution)/shard_map/experts/pallas_call | solution.py:179
  125.1 9.1 %experts.5 = (bf16[128,2048]{1,0:T(8,128)(2,1)S(1)}, bf16[128,2048]{1,0:T(8,128)(2,1)S(1)}, bf16[128,2048]{1,0:T(8,128)(2,1)S(1)}, bf16[128,2048]{1,0:T(8,128)(2,1)S(1)}) custom-call(s32[4,2,1,128]{3,2,1,0:T(1,128)S(1)} %bitcast.61, f32[4,2,1,128]{3,2,1,0:T(1,128)S(1)} %bitcast.59, bf16[128,2048]{1,0:T(8,128)(2,1)S(1)} %collective-permute-done.17.refs_2_, ...), custom_call_target="tpu_custom_call" | custom-call | flops 4429185024 | bytes 21495808 | tf_op jit(solution)/shard_map/experts/pallas_call | solution.py:179
  134.2 2.1 collective-permute-start.21
  136.8 1.6 collective-permute-start.30
  138.4 9.3 %experts.6 = (bf16[128,2048]{1,0:T(8,128)(2,1)S(1)}, bf16[128,2048]{1,0:T(8,128)(2,1)S(1)}, bf16[128,2048]{1,0:T(8,128)(2,1)S(1)}, bf16[128,2048]{1,0:T(8,128)(2,1)S(1)}) custom-call(s32[4,2,1,128]{3,2,1,0:T(1,128)S(1)} %bitcast.58, f32[4,2,1,128]{3,2,1,0:T(1,128)S(1)} %bitcast.57, bf16[128,2048]{1,0:T(8,128)(2,1)} %collective-permute-done.23.refs_2_, ...), custom_call_target="tpu_custom_call" | custom-call | flops 4429185024 | bytes 21495808 | tf_op jit(solution)/shard_map/experts/pallas_call | solution.py:179
  148.1 5.6 %collective-permute-done.22 = bf16[128,2048]{1,0:T(8,128)(2,1)S(1)} collective-permute-done((bf16[128,2048]{1,0:T(8,128)(2,1)S(1)}, bf16[128,2048]{1,0:T(8,128)(2,1)S(1)}, u32[]{:S(2)}, u32[]{:S(2)}) %collective-permute-start.22) | collective-permute-done | bytes 524320 | tf_op jit(solution)/shard_map/ppermute | solution.py:251
  154.5 9.3 %experts.7 = (bf16[128,2048]{1,0:T(8,128)(2,1)S(1)}, bf16[128,2048]{1,0:T(8,128)(2,1)S(1)}, bf16[128,2048]{1,0:T(8,128)(2,1)S(1)}, bf16[128,2048]{1,0:T(8,128)(2,1)S(1)}) custom-call(s32[4,2,1,128]{3,2,1,0:T(1,128)S(1)} %bitcast.56, f32[4,2,1,128]{3,2,1,0:T(1,128)S(1)} %bitcast.55, bf16[128,2048]{1,0:T(8,128)(2,1)} %collective-permute-done.27.refs_2_, ...), custom_call_target="tpu_custom_call" | custom-call | flops 4429185024 | bytes 21495808 | tf_op jit(solution)/shard_map/experts/pallas_call | solution.py:179
  163.9 1.7 collective-permute-start.31
  166.8 1.1 collective-permute-start.38
  169.1 6.9 %collective-permute-done.31 = bf16[128,2048]{1,0:T(8,128)(2,1)S(1)} collective-permute-done((bf16[128,2048]{1,0:T(8,128)(2,1)S(1)}, bf16[128,2048]{1,0:T(8,128)(2,1)S(1)}, u32[]{:S(2)}, u32[]{:S(2)}) %collective-permute-start.31) | collective-permute-done | bytes 524320 | tf_op jit(solution)/shard_map/ppermute | solution.py:251
  175.9 9.3 %collective-permute-done.32 = bf16[128,2048]{1,0:T(8,128)(2,1)S(1)} collective-permute-done((bf16[128,2048]{1,0:T(8,128)(2,1)S(1)}, bf16[128,2048]{1,0:T(8,128)(2,1)S(1)}, u32[]{:S(2)}, u32[]{:S(2)}) %collective-permute-start.32) | collective-permute-done | bytes 524320 | tf_op jit(solution)/shard_map/ppermute | solution.py:251
  185.3 2.6 %collective-permute-start.42 = (bf16[128,2048]{1,0:T(8,128)(2,1)S(1)}, bf16[128,2048]{1,0:T(8,128)(2,1)S(1)}, u32[]{:S(2)}, u32[]{:S(2)}) collective-permute-start(bf16[128,2048]{1,0:T(8,128)(2,1)S(1)} %add_convert_fusion.2), channel_id=1, source_target_pairs={{0,1},{1,0},{2,3},{3,2},{4,5},{5,4},{6,7},{7,6},{8,9},{9,8},{10,11... | collective-permute-start | bytes 1572872 | tf_op jit(solution)/shard_map/ppermute | solution.py:251
  188.6 14.7 %collective-permute-done.36 = bf16[128,2048]{1,0:T(8,128)(2,1)S(1)} collective-permute-done((bf16[128,2048]{1,0:T(8,128)(2,1)S(1)}, bf16[128,2048]{1,0:T(8,128)(2,1)S(1)}, u32[]{:S(2)}, u32[]{:S(2)}) %collective-permute-start.36) | collective-permute-done | bytes 524320 | tf_op jit(solution)/shard_map/ppermute | solution.py:251
  203.5 14.5 %collective-permute-start.37 = (bf16[128,2048]{1,0:T(8,128)(2,1)S(1)}, bf16[128,2048]{1,0:T(8,128)(2,1)S(1)}, u32[]{:S(2)}, u32[]{:S(2)}) collective-permute-start(bf16[128,2048]{1,0:T(8,128)(2,1)S(1)} %add_convert_fusion.5), channel_id=1, source_target_pairs={{0,6},{2,0},{4,2},{6,4},{1,7},{3,1},{5,3},{7,5},{8,14},{10,8},{12,... | collective-permute-start | bytes 1572872 | tf_op jit(solution)/shard_map/ppermute | solution.py:256
  220.7 4.8 %collective-permute-start.41 = (bf16[128,2048]{1,0:T(8,128)(2,1)S(1)}, bf16[128,2048]{1,0:T(8,128)(2,1)S(1)}, u32[]{:S(2)}, u32[]{:S(2)}) collective-permute-start(bf16[128,2048]{1,0:T(8,128)(2,1)S(1)} %add_convert_fusion.3), channel_id=1, source_target_pairs={{0,2},{2,4},{4,6},{6,0},{1,3},{3,5},{5,7},{7,1},{8,10},{10,12},{12... | collective-permute-start | bytes 1572872 | tf_op jit(solution)/shard_map/ppermute | solution.py:256
  225.5 1.8 collective-permute-done.34
  227.4 1.6 collective-permute-start.35
  228.9 3.9 %collective-permute-done.33 = bf16[128,2048]{1,0:T(8,128)(2,1)S(1)} collective-permute-done((bf16[128,2048]{1,0:T(8,128)(2,1)S(1)}, bf16[128,2048]{1,0:T(8,128)(2,1)S(1)}, u32[]{:S(2)}, u32[]{:S(2)}) %collective-permute-start.33) | collective-permute-done | bytes 524320 | tf_op jit(solution)/shard_map/ppermute | solution.py:251
  232.8 8.9 %collective-permute-done.43 = bf16[128,2048]{1,0:T(8,128)(2,1)S(1)} collective-permute-done((bf16[128,2048]{1,0:T(8,128)(2,1)S(1)}, bf16[128,2048]{1,0:T(8,128)(2,1)S(1)}, u32[]{:S(2)}, u32[]{:S(2)}) %collective-permute-start.43) | collective-permute-done | bytes 524320 | tf_op jit(solution)/shard_map/ppermute | solution.py:256
  241.7 1.3 add_convert_fusion
  (121 shorter events, 31.4 us)
Async XLA Ops:
  2.5 12.3 %collective-permute-start = (bf16[2,32,2048]{2,1,0:T(8,128)(2,1)S(1)}, bf16[2,32,2048]{2,1,0:T(8,128)(2,1)S(1)}, u32[]{:S(2)}, u32[]{:S(2)}) collective-permute-start(bf16[2,32,2048]{2,1,0:T(8,128)(2,1)S(1)} %constant_dynamic-update-slice_fusion.refs_0_), channel_id=1, source_target_pairs={{0,2},{2,4},{4,6},{6,0},{1,3},{3,5},{5,7},{7,1},{8,10},{10,12},{12... | collective-permute-start | bytes 786440 | tf_op jit(solution)/shard_map/ppermute | solution.py:256
  5.5 13.4 %collective-permute-start.1 = (bf16[2,32,2048]{2,1,0:T(8,128)(2,1)S(1)}, bf16[2,32,2048]{2,1,0:T(8,128)(2,1)S(1)}, u32[]{:S(2)}, u32[]{:S(2)}) collective-permute-start(bf16[2,32,2048]{2,1,0:T(8,128)(2,1)S(1)} %constant_dynamic-update-slice_fusion.refs_0_), channel_id=1, source_target_pairs={{0,6},{2,0},{4,2},{6,4},{1,7},{3,1},{5,3},{7,5},{8,14},{10,8},{12,... | collective-permute-start | bytes 786440 | tf_op jit(solution)/shard_map/ppermute | solution.py:256
  7.6 11.3 %collective-permute-start.2 = (bf16[2,32,2048]{2,1,0:T(8,128)(2,1)S(1)}, bf16[2,32,2048]{2,1,0:T(8,128)(2,1)S(1)}, u32[]{:S(2)}, u32[]{:S(2)}) collective-permute-start(bf16[2,32,2048]{2,1,0:T(8,128)(2,1)S(1)} %constant_dynamic-update-slice_fusion.refs_0_), channel_id=1, source_target_pairs={{0,1},{1,0},{2,3},{3,2},{4,5},{5,4},{6,7},{7,6},{8,9},{9,8},{10,11... | collective-permute-start | bytes 786440 | tf_op jit(solution)/shard_map/ppermute | solution.py:251
  18.9 45.2 %collective-permute-start.11 = (bf16[2048,1408]{1,0:T(8,128)(2,1)}, bf16[2048,1408]{1,0:T(8,128)(2,1)}, u32[]{:S(2)}, u32[]{:S(2)}) collective-permute-start(bf16[2048,1408]{1,0:T(8,128)(2,1)} %bitcast.43), channel_id=1, source_target_pairs={{0,8},{8,0},{1,9},{9,1},{2,10},{10,2},{3,11},{11,3},{4,12},{12,4},... | collective-permute-start | bytes 17301512 | tf_op jit(solution)/shard_map/ppermute | solution.py:251
  18.9 43.5 %collective-permute-start.12 = (bf16[704,2048]{1,0:T(8,128)(2,1)}, bf16[704,2048]{1,0:T(8,128)(2,1)S(1)}, u32[]{:S(2)}, u32[]{:S(2)}) collective-permute-start(bf16[704,2048]{1,0:T(8,128)(2,1)} %bitcast.50), channel_id=1, source_target_pairs={{0,8},{8,0},{1,9},{9,1},{2,10},{10,2},{3,11},{11,3},{4,12},{12,4},... | collective-permute-start | bytes 8650760 | tf_op jit(solution)/shard_map/ppermute | solution.py:251
  19.4 10.0 %collective-permute-start.3 = (bf16[2,32,2048]{2,1,0:T(8,128)(2,1)S(1)}, bf16[2,32,2048]{2,1,0:T(8,128)(2,1)S(1)}, u32[]{:S(2)}, u32[]{:S(2)}) collective-permute-start(bf16[2,32,2048]{2,1,0:T(8,128)(2,1)S(1)} %collective-permute-done.refs_1_), channel_id=1, source_target_pairs={{0,2},{2,4},{4,6},{6,0},{1,3},{3,5},{5,7},{7,1},{8,10},{10,12},{12... | collective-permute-start | bytes 786440 | tf_op jit(solution)/shard_map/ppermute | solution.py:256
  20.6 9.2 %collective-permute-start.4 = (bf16[2,32,2048]{2,1,0:T(8,128)(2,1)S(1)}, bf16[2,32,2048]{2,1,0:T(8,128)(2,1)S(1)}, u32[]{:S(2)}, u32[]{:S(2)}) collective-permute-start(bf16[2,32,2048]{2,1,0:T(8,128)(2,1)S(1)} %collective-permute-done.refs_1_), channel_id=1, source_target_pairs={{0,1},{1,0},{2,3},{3,2},{4,5},{5,4},{6,7},{7,6},{8,9},{9,8},{10,11... | collective-permute-start | bytes 786440 | tf_op jit(solution)/shard_map/ppermute | solution.py:251
  22.1 12.0 %collective-permute-start.5 = (bf16[2,32,2048]{2,1,0:T(8,128)(2,1)S(1)}, bf16[2,32,2048]{2,1,0:T(8,128)(2,1)S(1)}, u32[]{:S(2)}, u32[]{:S(2)}) collective-permute-start(bf16[2,32,2048]{2,1,0:T(8,128)(2,1)S(1)} %collective-permute-done.1.refs_2_), channel_id=1, source_target_pairs={{0,1},{1,0},{2,3},{3,2},{4,5},{5,4},{6,7},{7,6},{8,9},{9,8},{10,11... | collective-permute-start | bytes 786440 | tf_op jit(solution)/shard_map/ppermute | solution.py:251
  34.1 10.6 %collective-permute-start.9 = (bf16[2,32,2048]{2,1,0:T(8,128)(2,1)S(1)}, bf16[2,32,2048]{2,1,0:T(8,128)(2,1)S(1)}, u32[]{:S(2)}, u32[]{:S(2)}) collective-permute-start(bf16[2,32,2048]{2,1,0:T(8,128)(2,1)S(1)} %collective-permute-done.3.refs_3_), channel_id=1, source_target_pairs={{0,1},{1,0},{2,3},{3,2},{4,5},{5,4},{6,7},{7,6},{8,9},{9,8},{10,11... | collective-permute-start | bytes 786440 | tf_op jit(solution)/shard_map/ppermute | solution.py:251
  35.7 5.4 %collective-permute-start.6 = (f32[12,128]{1,0:T(8,128)S(1)}, f32[12,128]{1,0:T(8,128)S(1)}, u32[]{:S(2)}, u32[]{:S(2)}) collective-permute-start(f32[12,128]{1,0:T(8,128)S(1)} %pad_maximum_fusion.3), channel_id=1, source_target_pairs={{0,2},{2,4},{4,6},{6,0},{1,3},{3,5},{5,7},{7,1},{8,10},{10,12},{12... | collective-permute-start | bytes 18440 | tf_op jit(solution)/shard_map/ppermute | solution.py:256
  36.4 5.5 %collective-permute-start.7 = (f32[12,128]{1,0:T(8,128)S(1)}, f32[12,128]{1,0:T(8,128)S(1)}, u32[]{:S(2)}, u32[]{:S(2)}) collective-permute-start(f32[12,128]{1,0:T(8,128)S(1)} %pad_maximum_fusion.3), channel_id=1, source_target_pairs={{0,4},{2,6},{4,0},{6,2},{1,5},{3,7},{5,1},{7,3},{8,12},{10,14},{12... | collective-permute-start | bytes 18440 | tf_op jit(solution)/shard_map/ppermute | solution.py:256
  41.1 3.7 %collective-permute-start.8 = (f32[12,128]{1,0:T(8,128)S(1)}, f32[12,128]{1,0:T(8,128)S(1)}, u32[]{:S(2)}, u32[]{:S(2)}) collective-permute-start(f32[12,128]{1,0:T(8,128)S(1)} %pad_maximum_fusion.3), channel_id=1, source_target_pairs={{0,6},{2,0},{4,2},{6,4},{1,7},{3,1},{5,3},{7,5},{8,14},{10,8},{12,... | collective-permute-start | bytes 18440 | tf_op jit(solution)/shard_map/ppermute | solution.py:256
  44.8 7.3 %collective-permute-start.10 = (f32[4,12,128]{2,1,0:T(8,128)S(1)}, f32[4,12,128]{2,1,0:T(8,128)S(1)}, u32[]{:S(2)}, u32[]{:S(2)}) collective-permute-start(f32[4,12,128]{2,1,0:T(8,128)S(1)} %get-tuple-element.143), channel_id=1, source_target_pairs={{0,1},{1,0},{2,3},{3,2},{4,5},{5,4},{6,7},{7,6},{8,9},{9,8},{10,11... | collective-permute-start | bytes 73736 | tf_op jit(solution)/shard_map/ppermute | solution.py:251
  52.1 10.3 %collective-permute-start.13 = (f32[2,4,12,128]{3,2,1,0:T(8,128)S(1)}, f32[2,4,12,128]{3,2,1,0:T(8,128)S(1)}, u32[]{:S(2)}, u32[]{:S(2)}) collective-permute-start(f32[2,4,12,128]{3,2,1,0:T(8,128)S(1)} %get-tuple-element.141), channel_id=1, source_target_pairs={{0,16},{16,0},{1,17},{17,1},{2,18},{18,2},{3,19},{19,3},{4,20},{20... | collective-permute-start | bytes 147464 | tf_op jit(solution)/shard_map/ppermute | solution.py:251
  56.5 66.6 %slice-start = ((s8[5767168]{0:T(1024)(128)(4,1)}), s8[1572864]{0:T(1024)(128)(4,1)S(1)}, s32[]{:S(2)}) async-start(s8[5767168]{0:T(1024)(128)(4,1)} %bitcast.45), calls=%async_computation | async-start | bytes 3145728
  64.1 16.7 %collective-permute-start.17 = (bf16[128,2048]{1,0:T(8,128)(2,1)S(1)}, bf16[128,2048]{1,0:T(8,128)(2,1)S(1)}, u32[]{:S(2)}, u32[]{:S(2)}) collective-permute-start(bf16[128,2048]{1,0:T(8,128)(2,1)S(1)} %get-tuple-element.89.refs_2_), channel_id=1, source_target_pairs={{0,2},{2,4},{4,6},{6,0},{1,3},{3,5},{5,7},{7,1},{8,10},{10,12},{12... | collective-permute-start | bytes 1572872 | tf_op jit(solution)/shard_map/ppermute | solution.py:256
  64.1 18.9 %collective-permute-start.14 = (bf16[128,2048]{1,0:T(8,128)(2,1)S(1)}, bf16[128,2048]{1,0:T(8,128)(2,1)S(1)}, u32[]{:S(2)}, u32[]{:S(2)}) collective-permute-start(bf16[128,2048]{1,0:T(8,128)(2,1)S(1)} %get-tuple-element.89.refs_2_), channel_id=1, source_target_pairs={{0,1},{1,0},{2,3},{3,2},{4,5},{5,4},{6,7},{7,6},{8,9},{9,8},{10,11... | collective-permute-start | bytes 1572872 | tf_op jit(solution)/shard_map/ppermute | solution.py:251
  65.5 20.7 %collective-permute-start.15 = (bf16[128,2048]{1,0:T(8,128)(2,1)S(1)}, bf16[128,2048]{1,0:T(8,128)(2,1)}, u32[]{:S(2)}, u32[]{:S(2)}) collective-permute-start(bf16[128,2048]{1,0:T(8,128)(2,1)S(1)} %get-tuple-element.89.refs_2_), channel_id=1, source_target_pairs={{0,16},{16,0},{1,17},{17,1},{2,18},{18,2},{3,19},{19,3},{4,20},{20... | collective-permute-start | bytes 1572872 | tf_op jit(solution)/shard_map/ppermute | solution.py:251
  66.0 24.6 %collective-permute-start.23 = (bf16[128,2048]{1,0:T(8,128)(2,1)S(1)}, bf16[128,2048]{1,0:T(8,128)(2,1)}, u32[]{:S(2)}, u32[]{:S(2)}) collective-permute-start(bf16[128,2048]{1,0:T(8,128)(2,1)S(1)} %get-tuple-element.89.refs_2_), channel_id=1, source_target_pairs={{0,6},{2,0},{4,2},{6,4},{1,7},{3,1},{5,3},{7,5},{8,14},{10,8},{12,... | collective-permute-start | bytes 1572872 | tf_op jit(solution)/shard_map/ppermute | solution.py:256
  80.8 11.2 %collective-permute-start.19 = (bf16[128,2048]{1,0:T(8,128)(2,1)S(1)}, bf16[128,2048]{1,0:T(8,128)(2,1)}, u32[]{:S(2)}, u32[]{:S(2)}) collective-permute-start(bf16[128,2048]{1,0:T(8,128)(2,1)S(1)} %collective-permute-done.17.refs_2_), channel_id=1, source_target_pairs={{0,16},{16,0},{1,17},{17,1},{2,18},{18,2},{3,19},{19,3},{4,20},{20... | collective-permute-start | bytes 1572872 | tf_op jit(solution)/shard_map/ppermute | solution.py:251
  81.3 18.8 %collective-permute-start.27 = (bf16[128,2048]{1,0:T(8,128)(2,1)S(1)}, bf16[128,2048]{1,0:T(8,128)(2,1)}, u32[]{:S(2)}, u32[]{:S(2)}) collective-permute-start(bf16[128,2048]{1,0:T(8,128)(2,1)S(1)} %collective-permute-done.17.refs_2_), channel_id=1, source_target_pairs={{0,2},{2,4},{4,6},{6,0},{1,3},{3,5},{5,7},{7,1},{8,10},{10,12},{12... | collective-permute-start | bytes 1572872 | tf_op jit(solution)/shard_map/ppermute | solution.py:256
  83.0 17.1 %collective-permute-start.16 = (bf16[128,2048]{1,0:T(8,128)(2,1)S(1)}, bf16[128,2048]{1,0:T(8,128)(2,1)}, u32[]{:S(2)}, u32[]{:S(2)}) collective-permute-start(bf16[128,2048]{1,0:T(8,128)(2,1)S(1)} %collective-permute-done.14.refs_3_), channel_id=1, source_target_pairs={{0,16},{16,0},{1,17},{17,1},{2,18},{18,2},{3,19},{19,3},{4,20},{20... | collective-permute-start | bytes 1572872 | tf_op jit(solution)/shard_map/ppermute | solution.py:251
  86.3 35.2 %collective-permute-start.18 = (bf16[128,2048]{1,0:T(8,128)(2,1)S(1)}, bf16[128,2048]{1,0:T(8,128)(2,1)S(1)}, u32[]{:S(2)}, u32[]{:S(2)}) collective-permute-start(bf16[128,2048]{1,0:T(8,128)(2,1)S(1)} %collective-permute-done.17.refs_2_), channel_id=1, source_target_pairs={{0,1},{1,0},{2,3},{3,2},{4,5},{5,4},{6,7},{7,6},{8,9},{9,8},{10,11... | collective-permute-start | bytes 1572872 | tf_op jit(solution)/shard_map/ppermute | solution.py:251
  90.6 30.8 %collective-permute-start.24 = (bf16[128,2048]{1,0:T(8,128)(2,1)}, bf16[128,2048]{1,0:T(8,128)(2,1)}, u32[]{:S(2)}, u32[]{:S(2)}) collective-permute-start(bf16[128,2048]{1,0:T(8,128)(2,1)} %collective-permute-done.23.refs_2_), channel_id=1, source_target_pairs={{0,1},{1,0},{2,3},{3,2},{4,5},{5,4},{6,7},{7,6},{8,9},{9,8},{10,11... | collective-permute-start | bytes 1572872 | tf_op jit(solution)/shard_map/ppermute | solution.py:251
  92.0 30.2 %collective-permute-start.20 = (bf16[128,2048]{1,0:T(8,128)(2,1)}, bf16[128,2048]{1,0:T(8,128)(2,1)S(1)}, u32[]{:S(2)}, u32[]{:S(2)}) collective-permute-start(bf16[128,2048]{1,0:T(8,128)(2,1)} %collective-permute-done.19.refs_4_), channel_id=1, source_target_pairs={{0,1},{1,0},{2,3},{3,2},{4,5},{5,4},{6,7},{7,6},{8,9},{9,8},{10,11... | collective-permute-start | bytes 1572872 | tf_op jit(solution)/shard_map/ppermute | solution.py:251
  100.1 36.3 %collective-permute-start.25 = (bf16[128,2048]{1,0:T(8,128)(2,1)}, bf16[128,2048]{1,0:T(8,128)(2,1)}, u32[]{:S(2)}, u32[]{:S(2)}) collective-permute-start(bf16[128,2048]{1,0:T(8,128)(2,1)} %collective-permute-done.23.refs_2_), channel_id=1, source_target_pairs={{0,16},{16,0},{1,17},{17,1},{2,18},{18,2},{3,19},{19,3},{4,20},{20... | collective-permute-start | bytes 1572872 | tf_op jit(solution)/shard_map/ppermute | solution.py:251
  100.1 36.7 %collective-permute-start.29 = (bf16[128,2048]{1,0:T(8,128)(2,1)}, bf16[128,2048]{1,0:T(8,128)(2,1)}, u32[]{:S(2)}, u32[]{:S(2)}) collective-permute-start(bf16[128,2048]{1,0:T(8,128)(2,1)} %collective-permute-done.27.refs_2_), channel_id=1, source_target_pairs={{0,16},{16,0},{1,17},{17,1},{2,18},{18,2},{3,19},{19,3},{4,20},{20... | collective-permute-start | bytes 1572872 | tf_op jit(solution)/shard_map/ppermute | solution.py:251
  110.5 12.6 %copy-start.5 = (bf16[704,2048]{1,0:T(8,128)(2,1)S(1)}, bf16[704,2048]{1,0:T(8,128)(2,1)}, u32[]{:S(2)}) copy-start(bf16[704,2048]{1,0:T(8,128)(2,1)} %copy-done.3) | copy-start | bytes 8650756
  121.4 17.0 %collective-permute-start.26 = (bf16[128,2048]{1,0:T(8,128)(2,1)}, bf16[128,2048]{1,0:T(8,128)(2,1)S(1)}, u32[]{:S(2)}, u32[]{:S(2)}) collective-permute-start(bf16[128,2048]{1,0:T(8,128)(2,1)} %collective-permute-done.24.refs_3_), channel_id=1, source_target_pairs={{0,16},{16,0},{1,17},{17,1},{2,18},{18,2},{3,19},{19,3},{4,20},{20... | collective-permute-start | bytes 1572872 | tf_op jit(solution)/shard_map/ppermute | solution.py:251
  134.2 13.8 %collective-permute-start.21 = (bf16[128,2048]{1,0:T(8,128)(2,1)S(1)}, bf16[128,2048]{1,0:T(8,128)(2,1)S(1)}, u32[]{:S(2)}, u32[]{:S(2)}) collective-permute-start(bf16[128,2048]{1,0:T(8,128)(2,1)S(1)} %get-tuple-element.107), channel_id=1, source_target_pairs={{0,16},{16,0},{1,17},{17,1},{2,18},{18,2},{3,19},{19,3},{4,20},{20... | collective-permute-start | bytes 1572872 | tf_op jit(solution)/shard_map/ppermute | solution.py:251
  136.3 17.4 %collective-permute-start.22 = (bf16[128,2048]{1,0:T(8,128)(2,1)S(1)}, bf16[128,2048]{1,0:T(8,128)(2,1)S(1)}, u32[]{:S(2)}, u32[]{:S(2)}) collective-permute-start(bf16[128,2048]{1,0:T(8,128)(2,1)S(1)} %get-tuple-element.108), channel_id=1, source_target_pairs={{0,16},{16,0},{1,17},{17,1},{2,18},{18,2},{3,19},{19,3},{4,20},{20... | collective-permute-start | bytes 1572872 | tf_op jit(solution)/shard_map/ppermute | solution.py:251
  136.4 17.3 %collective-permute-start.28 = (bf16[128,2048]{1,0:T(8,128)(2,1)}, bf16[128,2048]{1,0:T(8,128)(2,1)S(1)}, u32[]{:S(2)}, u32[]{:S(2)}) collective-permute-start(bf16[128,2048]{1,0:T(8,128)(2,1)} %collective-permute-done.27.refs_2_), channel_id=1, source_target_pairs={{0,1},{1,0},{2,3},{3,2},{4,5},{5,4},{6,7},{7,6},{8,9},{9,8},{10,11... | collective-permute-start | bytes 1572872 | tf_op jit(solution)/shard_map/ppermute | solution.py:251
  136.8 17.7 %collective-permute-start.30 = (bf16[128,2048]{1,0:T(8,128)(2,1)}, bf16[128,2048]{1,0:T(8,128)(2,1)S(1)}, u32[]{:S(2)}, u32[]{:S(2)}) collective-permute-start(bf16[128,2048]{1,0:T(8,128)(2,1)} %collective-permute-done.29.refs_4_), channel_id=1, source_target_pairs={{0,1},{1,0},{2,3},{3,2},{4,5},{5,4},{6,7},{7,6},{8,9},{9,8},{10,11... | collective-permute-start | bytes 1572872 | tf_op jit(solution)/shard_map/ppermute | solution.py:251
  163.8 54.2 %copy-start.20 = (bf16[128,2048]{1,0:T(8,128)(2,1)S(1)}, bf16[128,2048]{1,0:T(8,128)(2,1)}, u32[]{:S(2)}) copy-start(bf16[128,2048]{1,0:T(8,128)(2,1)} %copy-done.19) | copy-start | bytes 1572868
  163.8 55.1 %copy-start.18 = (bf16[128,2048]{1,0:T(8,128)(2,1)S(1)}, bf16[128,2048]{1,0:T(8,128)(2,1)}, u32[]{:S(2)}) copy-start(bf16[128,2048]{1,0:T(8,128)(2,1)} %copy-done.17) | copy-start | bytes 1572868
  163.9 12.1 %collective-permute-start.31 = (bf16[128,2048]{1,0:T(8,128)(2,1)S(1)}, bf16[128,2048]{1,0:T(8,128)(2,1)S(1)}, u32[]{:S(2)}, u32[]{:S(2)}) collective-permute-start(bf16[128,2048]{1,0:T(8,128)(2,1)S(1)} %get-tuple-element.118), channel_id=1, source_target_pairs={{0,16},{16,0},{1,17},{17,1},{2,18},{18,2},{3,19},{19,3},{4,20},{20... | collective-permute-start | bytes 1572872 | tf_op jit(solution)/shard_map/ppermute | solution.py:251
  165.6 19.6 %collective-permute-start.32 = (bf16[128,2048]{1,0:T(8,128)(2,1)S(1)}, bf16[128,2048]{1,0:T(8,128)(2,1)S(1)}, u32[]{:S(2)}, u32[]{:S(2)}) collective-permute-start(bf16[128,2048]{1,0:T(8,128)(2,1)S(1)} %get-tuple-element.119), channel_id=1, source_target_pairs={{0,16},{16,0},{1,17},{17,1},{2,18},{18,2},{3,19},{19,3},{4,20},{20... | collective-permute-start | bytes 1572872 | tf_op jit(solution)/shard_map/ppermute | solution.py:251
  165.9 22.0 %collective-permute-start.39 = (bf16[128,2048]{1,0:T(8,128)(2,1)S(1)}, bf16[128,2048]{1,0:T(8,128)(2,1)S(1)}, u32[]{:S(2)}, u32[]{:S(2)}) collective-permute-start(bf16[128,2048]{1,0:T(8,128)(2,1)S(1)} %get-tuple-element.131), channel_id=1, source_target_pairs={{0,1},{1,0},{2,3},{3,2},{4,5},{5,4},{6,7},{7,6},{8,9},{9,8},{10,11... | collective-permute-start | bytes 1572872 | tf_op jit(solution)/shard_map/ppermute | solution.py:251
  166.8 53.5 %collective-permute-start.38 = (bf16[128,2048]{1,0:T(8,128)(2,1)S(1)}, bf16[128,2048]{1,0:T(8,128)(2,1)S(1)}, u32[]{:S(2)}, u32[]{:S(2)}) collective-permute-start(bf16[128,2048]{1,0:T(8,128)(2,1)S(1)} %get-tuple-element.129), channel_id=1, source_target_pairs={{0,1},{1,0},{2,3},{3,2},{4,5},{5,4},{6,7},{7,6},{8,9},{9,8},{10,11... | collective-permute-start | bytes 1572872 | tf_op jit(solution)/shard_map/ppermute | solution.py:251
  168.1 35.2 %collective-permute-start.36 = (bf16[128,2048]{1,0:T(8,128)(2,1)S(1)}, bf16[128,2048]{1,0:T(8,128)(2,1)S(1)}, u32[]{:S(2)}, u32[]{:S(2)}) collective-permute-start(bf16[128,2048]{1,0:T(8,128)(2,1)S(1)} %add_convert_fusion.6), channel_id=1, source_target_pairs={{0,1},{1,0},{2,3},{3,2},{4,5},{5,4},{6,7},{7,6},{8,9},{9,8},{10,11... | collective-permute-start | bytes 1572872 | tf_op jit(solution)/shard_map/ppermute | solution.py:251
  185.3 33.6 %collective-permute-start.42 = (bf16[128,2048]{1,0:T(8,128)(2,1)S(1)}, bf16[128,2048]{1,0:T(8,128)(2,1)S(1)}, u32[]{:S(2)}, u32[]{:S(2)}) collective-permute-start(bf16[128,2048]{1,0:T(8,128)(2,1)S(1)} %add_convert_fusion.2), channel_id=1, source_target_pairs={{0,1},{1,0},{2,3},{3,2},{4,5},{5,4},{6,7},{7,6},{8,9},{9,8},{10,11... | collective-permute-start | bytes 1572872 | tf_op jit(solution)/shard_map/ppermute | solution.py:251
  188.1 32.4 %collective-permute-start.40 = (bf16[128,2048]{1,0:T(8,128)(2,1)S(1)}, bf16[128,2048]{1,0:T(8,128)(2,1)S(1)}, u32[]{:S(2)}, u32[]{:S(2)}) collective-permute-start(bf16[128,2048]{1,0:T(8,128)(2,1)S(1)} %add_convert_fusion.4), channel_id=1, source_target_pairs={{0,16},{16,0},{1,17},{17,1},{2,18},{18,2},{3,19},{19,3},{4,20},{20... | collective-permute-start | bytes 1572872 | tf_op jit(solution)/shard_map/ppermute | solution.py:251
  203.5 25.4 %collective-permute-start.37 = (bf16[128,2048]{1,0:T(8,128)(2,1)S(1)}, bf16[128,2048]{1,0:T(8,128)(2,1)S(1)}, u32[]{:S(2)}, u32[]{:S(2)}) collective-permute-start(bf16[128,2048]{1,0:T(8,128)(2,1)S(1)} %add_convert_fusion.5), channel_id=1, source_target_pairs={{0,6},{2,0},{4,2},{6,4},{1,7},{3,1},{5,3},{7,5},{8,14},{10,8},{12,... | collective-permute-start | bytes 1572872 | tf_op jit(solution)/shard_map/ppermute | solution.py:256
  218.0 9.2 %collective-permute-start.34 = (bf16[128,2048]{1,0:T(8,128)(2,1)S(1)}, bf16[128,2048]{1,0:T(8,128)(2,1)S(1)}, u32[]{:S(2)}, u32[]{:S(2)}) collective-permute-start(bf16[128,2048]{1,0:T(8,128)(2,1)S(1)} %copy-done.20), channel_id=1, source_target_pairs={{0,1},{1,0},{2,3},{3,2},{4,5},{5,4},{6,7},{7,6},{8,9},{9,8},{10,11... | collective-permute-start | bytes 1572872 | tf_op jit(solution)/shard_map/ppermute | solution.py:251
  218.9 13.9 %collective-permute-start.33 = (bf16[128,2048]{1,0:T(8,128)(2,1)S(1)}, bf16[128,2048]{1,0:T(8,128)(2,1)S(1)}, u32[]{:S(2)}, u32[]{:S(2)}) collective-permute-start(bf16[128,2048]{1,0:T(8,128)(2,1)S(1)} %copy-done.18), channel_id=1, source_target_pairs={{0,1},{1,0},{2,3},{3,2},{4,5},{5,4},{6,7},{7,6},{8,9},{9,8},{10,11... | collective-permute-start | bytes 1572872 | tf_op jit(solution)/shard_map/ppermute | solution.py:251
  220.3 21.4 %collective-permute-start.43 = (bf16[128,2048]{1,0:T(8,128)(2,1)S(1)}, bf16[128,2048]{1,0:T(8,128)(2,1)S(1)}, u32[]{:S(2)}, u32[]{:S(2)}) collective-permute-start(bf16[128,2048]{1,0:T(8,128)(2,1)S(1)} %add_convert_fusion.1), channel_id=1, source_target_pairs={{0,4},{2,6},{4,0},{6,2},{1,5},{3,7},{5,1},{7,3},{8,12},{10,14},{12... | collective-permute-start | bytes 1572872 | tf_op jit(solution)/shard_map/ppermute | solution.py:256
  220.7 21.0 %collective-permute-start.41 = (bf16[128,2048]{1,0:T(8,128)(2,1)S(1)}, bf16[128,2048]{1,0:T(8,128)(2,1)S(1)}, u32[]{:S(2)}, u32[]{:S(2)}) collective-permute-start(bf16[128,2048]{1,0:T(8,128)(2,1)S(1)} %add_convert_fusion.3), channel_id=1, source_target_pairs={{0,2},{2,4},{4,6},{6,0},{1,3},{3,5},{5,7},{7,1},{8,10},{10,12},{12... | collective-permute-start | bytes 1572872 | tf_op jit(solution)/shard_map/ppermute | solution.py:256
  227.4 14.4 %collective-permute-start.35 = (bf16[128,2048]{1,0:T(8,128)(2,1)S(1)}, bf16[128,2048]{1,0:T(8,128)(2,1)S(1)}, u32[]{:S(2)}, u32[]{:S(2)}) collective-permute-start(bf16[128,2048]{1,0:T(8,128)(2,1)S(1)} %add_convert_fusion.8), channel_id=1, source_target_pairs={{0,16},{16,0},{1,17},{17,1},{2,18},{18,2},{3,19},{19,3},{4,20},{20... | collective-permute-start | bytes 1572872 | tf_op jit(solution)/shard_map/ppermute | solution.py:251
  (20 other events, 45.5 us)

commit v6 on v5

--- a/solution.py
+++ b/solution.py
@@ -13,8 +13,8 @@
 TOP = 6
 ALL = ("far", "core", "line", "side")
 GATHER_BUDGET = 40 * 2**20
-VMEM_LIMIT = 52 * 2**20
-EXPERT_VMEM = 36 * 2**20
+VMEM_LIMIT = 20 * 2**20
+EXPERT_VMEM = 32 * 2**20
 
 
 def attention_kernel(q_ref, sk_ref, sv_ref, *refs):
@@ -178,7 +178,7 @@
     local = pl.BlockSpec(memory_space=pltpu.VMEM)
     return pl.pallas_call(
         lambda *refs: experts_kernel(capacity, count, *refs),
-        in_specs=[local] * (2 + count) + [pl.BlockSpec(memory_space=pl.ANY)] * 4,
+        in_specs=[local] * (2 + count) + [pl.BlockSpec(memory_space=pltpu.HBM)] * 4,
         out_specs=[local] * count,
         out_shape=[jax.ShapeDtypeStruct((rows, width), jnp.bfloat16)] * count,
         scratch_shapes=[
@@ -317,48 +317,61 @@
     return slots, gates
 
 
-def over_plane(block, axes):
-    first = swap(block, axes[0])
-    second = swap(block, axes[1])
-    corner = swap(first, axes[1])
-    if axes[0] == "side":
-        return [block, first, second, corner]
-    return [block, second, first, corner]
-
-
-def first_sums(results, axes):
-    here, beside, across, corner = results
-    near, rest = (beside, across) if axes[0] == "side" else (across, beside)
-    return here, rest, swap(corner, axes[0]), swap(near, axes[0])
-
-
-def last_sums(here, rest, corner, near, axes, back):
-    total = add(here, near, swap(add(rest, corner), axes[1]))
-    return shift(total, "line", -back) if back else total
+def spread(normed):
+    columns = lax.axis_size("line")
+    beside, across = swap(normed, "side"), swap(normed, "far")
+    planes = {0: [normed, beside, across, swap(beside, "far")]}
+    up, down = shift(normed, "line", 1), shift(normed, "line", -1)
+    lines = {1: up, columns - 1: down}
+    for back in nearest_first()[3:]:
+        step = 1 if back <= columns // 2 else -1
+        lines[back] = shift(lines[back - step], "line", step)
+        far_block = swap(lines[back], "far")
+        planes[back] = [
+            lines[back],
+            swap(lines[back], "side"),
+            far_block,
+            swap(far_block, "side"),
+        ]
+    across_up, beside_down = shift(across, "line", 1), shift(beside, "line", -1)
+    planes[1] = [up, swap(up, "side"), across_up, swap(across_up, "side")]
+    planes[columns - 1] = [down, beside_down, swap(down, "far"), swap(beside_down, "far")]
+    return planes
 
 
 def gather_plan(normed, slots, gates, weights, capacity):
+    columns = lax.axis_size("line")
     order = nearest_first()
-    blocks = along_line(normed)
-    axes = [("side", "far") if i % 2 == 0 else ("far", "side") for i in range(len(order))]
-    sums, previous, own = {}, None, None
+    planes = spread(normed)
+    results, first_corner, previous = {}, None, None
     for i, back in enumerate(order):
-        plane = over_plane(blocks[back], axes[i])
         mine = slots[:, back]
-        if i >= 3:
-            mine, sums[i - 2] = lax.optimization_barrier((mine, sums[i - 2]))
         if i > 0:
             mine, previous = lax.optimization_barrier((mine, previous))
-            if i == 1:
-                own = previous
-            else:
-                sums[i - 1] = first_sums(previous, axes[i - 1])
-        previous = run_experts(plane, mine, gates[:, back], weights, capacity)
-    last = len(order) - 1
-    sums[last] = first_sums(previous, axes[last])
-    own, sums[last] = lax.optimization_barrier((own, sums[last]))
-    sums[0] = first_sums(own, axes[0])
-    return add(*[last_sums(*sums[i], axes[i], back) for i, back in enumerate(order)])
+            results[order[i - 1]] = previous
+        if i == 2:
+            first_corner = swap(results[1][3], "side")
+        if i == len(order) - 1 and i > 2:
+            mine, first_corner = lax.optimization_barrier((mine, first_corner))
+        previous = run_experts(planes[back], mine, gates[:, back], weights, capacity)
+    results[order[-1]] = previous
+    here, beside, across, corner = results[1]
+    up = add(here, swap(beside, "side"))
+    across_up = add(across, first_corner)
+    here, beside, across, corner = results[columns - 1]
+    beside_down = add(beside, swap(corner, "far"))
+    down = add(here, swap(across, "far"))
+    parts = []
+    for back in order[3:]:
+        here, beside, across, corner = results[back]
+        far_sum = add(across, swap(corner, "side"))
+        total = add(here, swap(beside, "side"), swap(far_sum, "far"))
+        parts.append(shift(total, "line", -back))
+    here, beside, across, corner = results[0]
+    across = add(across, shift(across_up, "line", -1))
+    beside = add(beside, swap(corner, "far"), shift(beside_down, "line", 1))
+    parts = parts + [shift(up, "line", -1), shift(down, "line", 1)]
+    return add(here, swap(across, "far"), swap(beside, "side"), *parts)
 
 
 def on_device(
@@ -379,7 +392,9 @@
     devices = lax.axis_size(ALL)
     experts = devices // 2
     capacity = 4 * rows_here * TOP // (3 * experts)
-    gather_fits = devices * rows_here * width * 2 <= GATHER_BUDGET
+    gather_fits = (
+        devices * rows_here * width * 2 <= GATHER_BUDGET and lax.axis_size("line") > 2
+    )
     kv = jnp.concatenate([prefix_keys, prefix_values])
     weights = [gate_up_weight[0], down_weight[0]]
     if gather_fits:

time: 244 us -> 264 us (1.082)
  waiting for transfers between devices: 98.1 us -> 116 us
  local copies, waits for them, and re-layouts: 21.7 us -> 38.2 us
  starting transfers between devices: 68.4 us -> 56.3 us
    ppermute x12 -> x16, waiting for transfers between devices: 42.4 us -> 66.9 us  [shift(): lax.ppermute(array, axis, [(i, (i + amount) % size) for i in range(size)])]
    unnamed x49 -> x55, local copies, waits for them, and re-layouts: 20.7 us -> 37.2 us
    ppermute x32 -> x28, waiting for transfers between devices: 55.7 us -> 49.1 us  [swap(): return lax.ppermute(array, axis, [(0, 1), (1, 0)])]
    ppermute x12 -> x16, starting transfers between devices: 35.3 us -> 28.9 us  [shift(): lax.ppermute(array, axis, [(i, (i + amount) % size) for i in range(size)])]
    ppermute x32 -> x28, starting transfers between devices: 33.1 us -> 27.4 us  [swap(): return lax.ppermute(array, axis, [(0, 1), (1, 0)])]
  transfers between devices with their start and end apart: 44 -> 44, of which waited for: 20 -> 20; matrix products, arithmetic and copies ran while one was open for 1% -> 1% of each run, Pallas kernels for 17% -> 18%
where the time goes in v6:
time: 264 us; the launch traced here: 263 us
  waiting for transfers between devices  116 us (44%)
  starting transfers between devices  56.3 us (21%)
  Pallas kernels  46.9 us (18%)
  local copies, waits for them, and re-layouts  38.2 us (14%)
  other arithmetic  4.13 us (2%)
    ppermute x16, waiting for transfers between devices, shift(): lax.ppermute(array, axis, [(i, (i + amount) % size) for i in range(size)])  66.9 us
    ppermute x28, waiting for transfers between devices, swap(): return lax.ppermute(array, axis, [(0, 1), (1, 0)])  49.1 us
    pallas_call x4, Pallas kernels, run_experts(): pl.pallas_call(lambda *refs: experts_kernel(capacity, count, *refs), in_s...  38.3 us
    unnamed x55, local copies, waits for them, and re-layouts  37.2 us
    ppermute x16, starting transfers between devices, shift(): lax.ppermute(array, axis, [(i, (i + amount) % size) for i in range(size)])  28.9 us
    ppermute x28, starting transfers between devices, swap(): return lax.ppermute(array, axis, [(0, 1), (1, 0)])  27.4 us
  transfers between devices with their start and end apart: 44, of which 20 were waited for; matrix products, arithmetic and copies ran while one was open for 1% of the time, Pallas kernels for 18%

profile of v6, /device:TPU:0, one launch (start us, length us, event | category | flops | bytes accessed | tf_op | source)
XLA Modules:
  0.0 262.8 jit_solution(12522991131253107155)
XLA Ops:
  2.5 3.1 %collective-permute-start = (bf16[2,32,2048]{2,1,0:T(8,128)(2,1)S(1)}, bf16[2,32,2048]{2,1,0:T(8,128)(2,1)S(1)}, u32[]{:S(2)}, u32[]{:S(2)}) collective-permute-start(bf16[2,32,2048]{2,1,0:T(8,128)(2,1)S(1)} %constant_dynamic-update-slice_fusion.refs_0_), channel_id=1, source_target_pairs={{0,2},{2,4},{4,6},{6,0},{1,3},{3,5},{5,7},{7,1},{8,10},{10,12},{12... | collective-permute-start | bytes 786440 | tf_op jit(solution)/shard_map/ppermute | solution.py:256
  5.5 2.1 collective-permute-start.1
  7.6 1.7 collective-permute-start.2
  10.7 4.1 %collective-permute-done.refs_1_ = bf16[2,32,2048]{2,1,0:T(8,128)(2,1)S(1)} collective-permute-done((bf16[2,32,2048]{2,1,0:T(8,128)(2,1)S(1)}, bf16[2,32,2048]{2,1,0:T(8,128)(2,1)S(1)}, u32[]{:S(2)}, u32[]{:S(2)}) %collective-permute-start) | collective-permute-done | bytes 262176 | tf_op jit(solution)/shard_map/ppermute | solution.py:256
  14.7 4.2 %collective-permute-done.1.refs_2_ = bf16[2,32,2048]{2,1,0:T(8,128)(2,1)S(1)} collective-permute-done((bf16[2,32,2048]{2,1,0:T(8,128)(2,1)S(1)}, bf16[2,32,2048]{2,1,0:T(8,128)(2,1)S(1)}, u32[]{:S(2)}, u32[]{:S(2)}) %collective-permute-start.1) | collective-permute-done | bytes 262176 | tf_op jit(solution)/shard_map/ppermute | solution.py:256
  22.6 6.9 %collective-permute-done.3.refs_3_ = bf16[2,32,2048]{2,1,0:T(8,128)(2,1)S(1)} collective-permute-done((bf16[2,32,2048]{2,1,0:T(8,128)(2,1)S(1)}, bf16[2,32,2048]{2,1,0:T(8,128)(2,1)S(1)}, u32[]{:S(2)}, u32[]{:S(2)}) %collective-permute-start.3) | collective-permute-done | bytes 262176 | tf_op jit(solution)/shard_map/ppermute | solution.py:256
  29.8 4.4 %collective-permute-done.5.refs_6_ = bf16[2,32,2048]{2,1,0:T(8,128)(2,1)S(1)} collective-permute-done((bf16[2,32,2048]{2,1,0:T(8,128)(2,1)S(1)}, bf16[2,32,2048]{2,1,0:T(8,128)(2,1)S(1)}, u32[]{:S(2)}, u32[]{:S(2)}) %collective-permute-start.5) | collective-permute-done | bytes 262176 | tf_op jit(solution)/shard_map/ppermute | solution.py:251
  36.4 2.5 collective-permute-start.7
  38.9 2.2 collective-permute-done.6
  42.0 2.8 %collective-permute-done.8 = f32[12,128]{1,0:T(8,128)S(1)} collective-permute-done((f32[12,128]{1,0:T(8,128)S(1)}, f32[12,128]{1,0:T(8,128)S(1)}, u32[]{:S(2)}, u32[]{:S(2)}) %collective-permute-start.8) | collective-permute-done | bytes 6176 | tf_op jit(solution)/shard_map/ppermute | solution.py:256
  48.5 5.1 %attention.1.heads_ref = bf16[128,2048]{1,0:T(8,128)(2,1)S(1)} custom-call(bf16[128,2048]{1,0:T(8,128)(2,1)S(1)} %copy-done.18, bf16[128,2048]{1,0:T(8,128)(2,1)S(1)} %copy-done.19, bf16[128,2048]{1,0:T(8,128)(2,1)S(1)} %copy-done.20, bf16[2,32,2048]{2,1,0:T(8,128)(2,1)S(1)} %constant_dynamic-update-slice_fusion.refs_0_, ...), custom_call_target="tpu_custom_call" | custom-call | flops 402653184 | bytes 3145728 | tf_op jit(solution)/shard_map/attention/pallas_call | solution.py:60
  53.7 1.6 collective-permute-start.13
  55.2 3.4 %copy-done.11 = bf16[2048,2048]{1,0:T(8,128)(2,1)S(1)} copy-done((bf16[2048,2048]{1,0:T(8,128)(2,1)S(1)}, bf16[2048,2048]{1,0:T(8,128)(2,1)}, u32[]{:S(2)}) %copy-start.11) | copy-done | bytes 8388632
  60.3 3.5 %project_and_norm.1 = (bf16[128,2048]{1,0:T(8,128)(2,1)}, bf16[128,2048]{1,0:T(8,128)(2,1)S(1)}) custom-call(bf16[128,2048]{1,0:T(8,128)(2,1)S(1)} %attention.1.heads_ref, bf16[2048,2048]{1,0:T(8,128)(2,1)S(1)} %copy-done.11, bf16[128,2048]{1,0:T(8,128)(2,1)S(1)} %copy-done.21, f32[1,2048]{1,0:T(1,128)S(1)} %bitcast.63), custom_call_target="tpu_custom_call" | custom-call | flops 1073741824 | bytes 8388608 | tf_op jit(solution)/shard_map/project_and_norm/pallas_call | solution.py:101
  63.8 1.6 copy-done.8
  65.5 2.5 copy-done.1
  70.0 3.8 %collective-permute-start.21 = (bf16[128,2048]{1,0:T(8,128)(2,1)S(1)}, bf16[128,2048]{1,0:T(8,128)(2,1)}, u32[]{:S(2)}, u32[]{:S(2)}) collective-permute-start(bf16[128,2048]{1,0:T(8,128)(2,1)S(1)} %get-tuple-element.78.refs_2_), channel_id=1, source_target_pairs={{0,6},{2,0},{4,2},{6,4},{1,7},{3,1},{5,3},{7,5},{8,14},{10,8},{12,... | collective-permute-start | bytes 1572872 | tf_op jit(solution)/shard_map/ppermute | solution.py:256
  73.9 3.8 %collective-permute-done.14.refs_3_ = bf16[128,2048]{1,0:T(8,128)(2,1)S(1)} collective-permute-done((bf16[128,2048]{1,0:T(8,128)(2,1)S(1)}, bf16[128,2048]{1,0:T(8,128)(2,1)S(1)}, u32[]{:S(2)}, u32[]{:S(2)}) %collective-permute-start.14) | collective-permute-done | bytes 524320 | tf_op jit(solution)/shard_map/ppermute | solution.py:251
  78.3 2.4 collective-permute-start.22
  80.7 1.8 collective-permute-done.15.refs_4_
  82.9 3.8 %collective-permute-done.17.refs_2_ = bf16[128,2048]{1,0:T(8,128)(2,1)} collective-permute-done((bf16[128,2048]{1,0:T(8,128)(2,1)S(1)}, bf16[128,2048]{1,0:T(8,128)(2,1)}, u32[]{:S(2)}, u32[]{:S(2)}) %collective-permute-start.17) | collective-permute-done | bytes 524320 | tf_op jit(solution)/shard_map/ppermute | solution.py:256
  87.3 6.4 %collective-permute-done.21.refs_2_ = bf16[128,2048]{1,0:T(8,128)(2,1)} collective-permute-done((bf16[128,2048]{1,0:T(8,128)(2,1)S(1)}, bf16[128,2048]{1,0:T(8,128)(2,1)}, u32[]{:S(2)}, u32[]{:S(2)}) %collective-permute-start.21) | collective-permute-done | bytes 524320 | tf_op jit(solution)/shard_map/ppermute | solution.py:256
  93.6 7.7 %collective-permute-start.32 = (bf16[128,2048]{1,0:T(8,128)(2,1)}, bf16[128,2048]{1,0:T(8,128)(2,1)}, u32[]{:S(2)}, u32[]{:S(2)}) collective-permute-start(bf16[128,2048]{1,0:T(8,128)(2,1)} %collective-permute-done.17.refs_2_), channel_id=1, source_target_pairs={{0,2},{2,4},{4,6},{6,0},{1,3},{3,5},{5,7},{7,1},{8,10},{10,12},{12... | collective-permute-start | bytes 1572872 | tf_op jit(solution)/shard_map/ppermute | solution.py:256
  101.3 19.1 %collective-permute-done.19.refs_4_ = bf16[128,2048]{1,0:T(8,128)(2,1)} collective-permute-done((bf16[128,2048]{1,0:T(8,128)(2,1)S(1)}, bf16[128,2048]{1,0:T(8,128)(2,1)}, u32[]{:S(2)}, u32[]{:S(2)}) %collective-permute-start.19) | collective-permute-done | bytes 524320 | tf_op jit(solution)/shard_map/ppermute | solution.py:256
  121.0 1.6 collective-permute-start.23
  123.1 2.6 %copy-done = bf16[1,2048,1408]{2,1,0:T(8,128)(2,1)S(1)} copy-done((bf16[1,2048,1408]{2,1,0:T(8,128)(2,1)S(1)}, bf16[1,2048,1408]{2,1,0:T(8,128)(2,1)}, u32[]{:S(2)}) %copy-start) | copy-done | bytes 5767192
  125.7 2.6 %copy-done.2 = bf16[2048,1408]{1,0:T(8,128)(2,1)S(1)} copy-done((bf16[2048,1408]{1,0:T(8,128)(2,1)S(1)}, bf16[2048,1408]{1,0:T(8,128)(2,1)}, u32[]{:S(2)}) %copy-start.2) | copy-done | bytes 5767192
  128.4 1.8 copy-done.6
  130.2 1.8 copy-done.9
  132.0 9.5 %experts.4 = (bf16[128,2048]{1,0:T(8,128)(2,1)S(1)}, bf16[128,2048]{1,0:T(8,128)(2,1)S(1)}, bf16[128,2048]{1,0:T(8,128)(2,1)S(1)}, bf16[128,2048]{1,0:T(8,128)(2,1)S(1)}) custom-call(s32[4,2,1,128]{3,2,1,0:T(1,128)S(1)} %bitcast.62, f32[4,2,1,128]{3,2,1,0:T(1,128)S(1)} %bitcast.60, bf16[128,2048]{1,0:T(8,128)(2,1)S(1)} %get-tuple-element.78.refs_2_, ...), custom_call_target="tpu_custom_call" | custom-call | flops 4429185024 | bytes 21495808 | tf_op jit(solution)/shard_map/experts/pallas_call | solution.py:179
  145.4 2.6 %copy-done.3 = bf16[2048,1408]{1,0:T(8,128)(2,1)S(1)} copy-done((bf16[2048,1408]{1,0:T(8,128)(2,1)S(1)}, bf16[2048,1408]{1,0:T(8,128)(2,1)}, u32[]{:S(2)}) %copy-start.3) | copy-done | bytes 5767192
  148.0 1.8 copy-done.10
  150.9 9.8 %experts.5 = (bf16[128,2048]{1,0:T(8,128)(2,1)S(1)}, bf16[128,2048]{1,0:T(8,128)(2,1)S(1)}, bf16[128,2048]{1,0:T(8,128)(2,1)S(1)}, bf16[128,2048]{1,0:T(8,128)(2,1)S(1)}) custom-call(s32[4,2,1,128]{3,2,1,0:T(1,128)S(1)} %bitcast.61, f32[4,2,1,128]{3,2,1,0:T(1,128)S(1)} %bitcast.58, bf16[128,2048]{1,0:T(8,128)(2,1)} %collective-permute-done.17.refs_2_, ...), custom_call_target="tpu_custom_call" | custom-call | flops 4429185024 | bytes 21495808 | tf_op jit(solution)/shard_map/experts/pallas_call | solution.py:179
  160.7 1.6 collective-permute-start.25
  163.1 2.6 %copy-done.4 = bf16[2048,1408]{1,0:T(8,128)(2,1)S(1)} copy-done((bf16[2048,1408]{1,0:T(8,128)(2,1)S(1)}, bf16[2048,1408]{1,0:T(8,128)(2,1)}, u32[]{:S(2)}) %copy-start.4) | copy-done | bytes 5767192
  166.8 9.8 %experts.6 = (bf16[128,2048]{1,0:T(8,128)(2,1)S(1)}, bf16[128,2048]{1,0:T(8,128)(2,1)S(1)}, bf16[128,2048]{1,0:T(8,128)(2,1)S(1)}, bf16[128,2048]{1,0:T(8,128)(2,1)S(1)}) custom-call(s32[4,2,1,128]{3,2,1,0:T(1,128)S(1)} %bitcast.59, f32[4,2,1,128]{3,2,1,0:T(1,128)S(1)} %bitcast.57, bf16[128,2048]{1,0:T(8,128)(2,1)} %collective-permute-done.21.refs_2_, ...), custom_call_target="tpu_custom_call" | custom-call | flops 4429185024 | bytes 21495808 | tf_op jit(solution)/shard_map/experts/pallas_call | solution.py:179
  181.3 8.0 %collective-permute-done.29 = bf16[128,2048]{1,0:T(8,128)(2,1)S(1)} collective-permute-done((bf16[128,2048]{1,0:T(8,128)(2,1)S(1)}, bf16[128,2048]{1,0:T(8,128)(2,1)S(1)}, u32[]{:S(2)}, u32[]{:S(2)}) %collective-permute-start.29) | collective-permute-done | bytes 524320 | tf_op jit(solution)/shard_map/ppermute | solution.py:251
  189.9 2.5 collective-permute-done.33.refs_3_
  192.7 10.9 %collective-permute-done.35.refs_5_ = bf16[128,2048]{1,0:T(8,128)(2,1)S(1)} collective-permute-done((bf16[128,2048]{1,0:T(8,128)(2,1)S(1)}, bf16[128,2048]{1,0:T(8,128)(2,1)S(1)}, u32[]{:S(2)}, u32[]{:S(2)}) %collective-permute-start.35) | collective-permute-done | bytes 524320 | tf_op jit(solution)/shard_map/ppermute | solution.py:251
  203.7 2.6 %copy-done.5 = bf16[2048,1408]{1,0:T(8,128)(2,1)S(1)} copy-done((bf16[2048,1408]{1,0:T(8,128)(2,1)S(1)}, bf16[2048,1408]{1,0:T(8,128)(2,1)}, u32[]{:S(2)}) %copy-start.5) | copy-done | bytes 5767192
  206.3 9.3 %experts.7 = (bf16[128,2048]{1,0:T(8,128)(2,1)S(1)}, bf16[128,2048]{1,0:T(8,128)(2,1)S(1)}, bf16[128,2048]{1,0:T(8,128)(2,1)S(1)}, bf16[128,2048]{1,0:T(8,128)(2,1)S(1)}) custom-call(s32[4,2,1,128]{3,2,1,0:T(1,128)S(1)} %bitcast.56, f32[4,2,1,128]{3,2,1,0:T(1,128)S(1)} %bitcast.55, bf16[128,2048]{1,0:T(8,128)(2,1)} %collective-permute-done.32.refs_2_, ...), custom_call_target="tpu_custom_call" | custom-call | flops 4429185024 | bytes 21495808 | tf_op jit(solution)/shard_map/experts/pallas_call | solution.py:179
  215.6 1.6 collective-permute-start.37
  218.1 11.4 %collective-permute-done.37 = bf16[128,2048]{1,0:T(8,128)(2,1)S(1)} collective-permute-done((bf16[128,2048]{1,0:T(8,128)(2,1)S(1)}, bf16[128,2048]{1,0:T(8,128)(2,1)S(1)}, u32[]{:S(2)}, u32[]{:S(2)}) %collective-permute-start.37) | collective-permute-done | bytes 524320 | tf_op jit(solution)/shard_map/ppermute | solution.py:251
  229.4 4.1 %collective-permute-start.41 = (bf16[128,2048]{1,0:T(8,128)(2,1)S(1)}, bf16[128,2048]{1,0:T(8,128)(2,1)S(1)}, u32[]{:S(2)}, u32[]{:S(2)}) collective-permute-start(bf16[128,2048]{1,0:T(8,128)(2,1)S(1)} %add_convert_fusion.2), channel_id=1, source_target_pairs={{0,6},{2,0},{4,2},{6,4},{1,7},{3,1},{5,3},{7,5},{8,14},{10,8},{12,... | collective-permute-start | bytes 1572872 | tf_op jit(solution)/shard_map/ppermute | solution.py:256
  234.5 1.6 collective-permute-start.27
  237.7 5.3 %collective-permute-done.38 = bf16[128,2048]{1,0:T(8,128)(2,1)S(1)} collective-permute-done((bf16[128,2048]{1,0:T(8,128)(2,1)S(1)}, bf16[128,2048]{1,0:T(8,128)(2,1)S(1)}, u32[]{:S(2)}, u32[]{:S(2)}) %collective-permute-start.38) | collective-permute-done | bytes 524320 | tf_op jit(solution)/shard_map/ppermute | solution.py:251
  243.3 4.6 %collective-permute-done.41 = bf16[128,2048]{1,0:T(8,128)(2,1)S(1)} collective-permute-done((bf16[128,2048]{1,0:T(8,128)(2,1)S(1)}, bf16[128,2048]{1,0:T(8,128)(2,1)S(1)}, u32[]{:S(2)}, u32[]{:S(2)}) %collective-permute-start.41) | collective-permute-done | bytes 524320 | tf_op jit(solution)/shard_map/ppermute | solution.py:256
  248.6 12.9 %collective-permute-done.39 = bf16[128,2048]{1,0:T(8,128)(2,1)S(1)} collective-permute-done((bf16[128,2048]{1,0:T(8,128)(2,1)S(1)}, bf16[128,2048]{1,0:T(8,128)(2,1)S(1)}, u32[]{:S(2)}, u32[]{:S(2)}) %collective-permute-start.39) | collective-permute-done | bytes 524320 | tf_op jit(solution)/shard_map/ppermute | solution.py:256
  (128 shorter events, 38.6 us)
Async XLA Ops:
  2.5 12.3 %collective-permute-start = (bf16[2,32,2048]{2,1,0:T(8,128)(2,1)S(1)}, bf16[2,32,2048]{2,1,0:T(8,128)(2,1)S(1)}, u32[]{:S(2)}, u32[]{:S(2)}) collective-permute-start(bf16[2,32,2048]{2,1,0:T(8,128)(2,1)S(1)} %constant_dynamic-update-slice_fusion.refs_0_), channel_id=1, source_target_pairs={{0,2},{2,4},{4,6},{6,0},{1,3},{3,5},{5,7},{7,1},{8,10},{10,12},{12... | collective-permute-start | bytes 786440 | tf_op jit(solution)/shard_map/ppermute | solution.py:256
  5.5 13.4 %collective-permute-start.1 = (bf16[2,32,2048]{2,1,0:T(8,128)(2,1)S(1)}, bf16[2,32,2048]{2,1,0:T(8,128)(2,1)S(1)}, u32[]{:S(2)}, u32[]{:S(2)}) collective-permute-start(bf16[2,32,2048]{2,1,0:T(8,128)(2,1)S(1)} %constant_dynamic-update-slice_fusion.refs_0_), channel_id=1, source_target_pairs={{0,6},{2,0},{4,2},{6,4},{1,7},{3,1},{5,3},{7,5},{8,14},{10,8},{12,... | collective-permute-start | bytes 786440 | tf_op jit(solution)/shard_map/ppermute | solution.py:256
  7.6 11.3 %collective-permute-start.2 = (bf16[2,32,2048]{2,1,0:T(8,128)(2,1)S(1)}, bf16[2,32,2048]{2,1,0:T(8,128)(2,1)S(1)}, u32[]{:S(2)}, u32[]{:S(2)}) collective-permute-start(bf16[2,32,2048]{2,1,0:T(8,128)(2,1)S(1)} %constant_dynamic-update-slice_fusion.refs_0_), channel_id=1, source_target_pairs={{0,1},{1,0},{2,3},{3,2},{4,5},{5,4},{6,7},{7,6},{8,9},{9,8},{10,11... | collective-permute-start | bytes 786440 | tf_op jit(solution)/shard_map/ppermute | solution.py:251
  18.9 46.5 %collective-permute-start.11 = (bf16[2048,1408]{1,0:T(8,128)(2,1)}, bf16[2048,1408]{1,0:T(8,128)(2,1)S(1)}, u32[]{:S(2)}, u32[]{:S(2)}) collective-permute-start(bf16[2048,1408]{1,0:T(8,128)(2,1)} %bitcast.43), channel_id=1, source_target_pairs={{0,8},{8,0},{1,9},{9,1},{2,10},{10,2},{3,11},{11,3},{4,12},{12,4},... | collective-permute-start | bytes 17301512 | tf_op jit(solution)/shard_map/ppermute | solution.py:251
  18.9 44.9 %collective-permute-start.12 = (bf16[704,2048]{1,0:T(8,128)(2,1)}, bf16[704,2048]{1,0:T(8,128)(2,1)S(1)}, u32[]{:S(2)}, u32[]{:S(2)}) collective-permute-start(bf16[704,2048]{1,0:T(8,128)(2,1)} %bitcast.50), channel_id=1, source_target_pairs={{0,8},{8,0},{1,9},{9,1},{2,10},{10,2},{3,11},{11,3},{4,12},{12,4},... | collective-permute-start | bytes 8650760 | tf_op jit(solution)/shard_map/ppermute | solution.py:251
  19.4 10.0 %collective-permute-start.3 = (bf16[2,32,2048]{2,1,0:T(8,128)(2,1)S(1)}, bf16[2,32,2048]{2,1,0:T(8,128)(2,1)S(1)}, u32[]{:S(2)}, u32[]{:S(2)}) collective-permute-start(bf16[2,32,2048]{2,1,0:T(8,128)(2,1)S(1)} %collective-permute-done.refs_1_), channel_id=1, source_target_pairs={{0,2},{2,4},{4,6},{6,0},{1,3},{3,5},{5,7},{7,1},{8,10},{10,12},{12... | collective-permute-start | bytes 786440 | tf_op jit(solution)/shard_map/ppermute | solution.py:256
  20.6 9.2 %collective-permute-start.4 = (bf16[2,32,2048]{2,1,0:T(8,128)(2,1)S(1)}, bf16[2,32,2048]{2,1,0:T(8,128)(2,1)S(1)}, u32[]{:S(2)}, u32[]{:S(2)}) collective-permute-start(bf16[2,32,2048]{2,1,0:T(8,128)(2,1)S(1)} %collective-permute-done.refs_1_), channel_id=1, source_target_pairs={{0,1},{1,0},{2,3},{3,2},{4,5},{5,4},{6,7},{7,6},{8,9},{9,8},{10,11... | collective-permute-start | bytes 786440 | tf_op jit(solution)/shard_map/ppermute | solution.py:251
  22.1 12.0 %collective-permute-start.5 = (bf16[2,32,2048]{2,1,0:T(8,128)(2,1)S(1)}, bf16[2,32,2048]{2,1,0:T(8,128)(2,1)S(1)}, u32[]{:S(2)}, u32[]{:S(2)}) collective-permute-start(bf16[2,32,2048]{2,1,0:T(8,128)(2,1)S(1)} %collective-permute-done.1.refs_2_), channel_id=1, source_target_pairs={{0,1},{1,0},{2,3},{3,2},{4,5},{5,4},{6,7},{7,6},{8,9},{9,8},{10,11... | collective-permute-start | bytes 786440 | tf_op jit(solution)/shard_map/ppermute | solution.py:251
  34.1 10.6 %collective-permute-start.9 = (bf16[2,32,2048]{2,1,0:T(8,128)(2,1)S(1)}, bf16[2,32,2048]{2,1,0:T(8,128)(2,1)S(1)}, u32[]{:S(2)}, u32[]{:S(2)}) collective-permute-start(bf16[2,32,2048]{2,1,0:T(8,128)(2,1)S(1)} %collective-permute-done.3.refs_3_), channel_id=1, source_target_pairs={{0,1},{1,0},{2,3},{3,2},{4,5},{5,4},{6,7},{7,6},{8,9},{9,8},{10,11... | collective-permute-start | bytes 786440 | tf_op jit(solution)/shard_map/ppermute | solution.py:251
  35.7 5.4 %collective-permute-start.6 = (f32[12,128]{1,0:T(8,128)S(1)}, f32[12,128]{1,0:T(8,128)S(1)}, u32[]{:S(2)}, u32[]{:S(2)}) collective-permute-start(f32[12,128]{1,0:T(8,128)S(1)} %pad_maximum_fusion.3), channel_id=1, source_target_pairs={{0,2},{2,4},{4,6},{6,0},{1,3},{3,5},{5,7},{7,1},{8,10},{10,12},{12... | collective-permute-start | bytes 18440 | tf_op jit(solution)/shard_map/ppermute | solution.py:256
  36.4 5.5 %collective-permute-start.7 = (f32[12,128]{1,0:T(8,128)S(1)}, f32[12,128]{1,0:T(8,128)S(1)}, u32[]{:S(2)}, u32[]{:S(2)}) collective-permute-start(f32[12,128]{1,0:T(8,128)S(1)} %pad_maximum_fusion.3), channel_id=1, source_target_pairs={{0,4},{2,6},{4,0},{6,2},{1,5},{3,7},{5,1},{7,3},{8,12},{10,14},{12... | collective-permute-start | bytes 18440 | tf_op jit(solution)/shard_map/ppermute | solution.py:256
  41.1 3.7 %collective-permute-start.8 = (f32[12,128]{1,0:T(8,128)S(1)}, f32[12,128]{1,0:T(8,128)S(1)}, u32[]{:S(2)}, u32[]{:S(2)}) collective-permute-start(f32[12,128]{1,0:T(8,128)S(1)} %pad_maximum_fusion.3), channel_id=1, source_target_pairs={{0,6},{2,0},{4,2},{6,4},{1,7},{3,1},{5,3},{7,5},{8,14},{10,8},{12,... | collective-permute-start | bytes 18440 | tf_op jit(solution)/shard_map/ppermute | solution.py:256
  44.8 8.9 %collective-permute-start.10 = (f32[4,12,128]{2,1,0:T(8,128)S(1)}, f32[4,12,128]{2,1,0:T(8,128)S(1)}, u32[]{:S(2)}, u32[]{:S(2)}) collective-permute-start(f32[4,12,128]{2,1,0:T(8,128)S(1)} %get-tuple-element.121), channel_id=1, source_target_pairs={{0,1},{1,0},{2,3},{3,2},{4,5},{5,4},{6,7},{7,6},{8,9},{9,8},{10,11... | collective-permute-start | bytes 73736 | tf_op jit(solution)/shard_map/ppermute | solution.py:251
  53.7 10.2 %collective-permute-start.13 = (f32[2,4,12,128]{3,2,1,0:T(8,128)S(1)}, f32[2,4,12,128]{3,2,1,0:T(8,128)S(1)}, u32[]{:S(2)}, u32[]{:S(2)}) collective-permute-start(f32[2,4,12,128]{3,2,1,0:T(8,128)S(1)} %get-tuple-element.119), channel_id=1, source_target_pairs={{0,16},{16,0},{1,17},{17,1},{2,18},{18,2},{3,19},{19,3},{4,20},{20... | collective-permute-start | bytes 147464 | tf_op jit(solution)/shard_map/ppermute | solution.py:251
  60.3 85.1 %slice-start = ((s8[5767168]{0:T(1024)(128)(4,1)}), s8[1572864]{0:T(1024)(128)(4,1)S(1)}, s32[]{:S(2)}) async-start(s8[5767168]{0:T(1024)(128)(4,1)} %bitcast.45), calls=%async_computation | async-start | bytes 3145728
  67.9 9.8 %collective-permute-start.14 = (bf16[128,2048]{1,0:T(8,128)(2,1)S(1)}, bf16[128,2048]{1,0:T(8,128)(2,1)S(1)}, u32[]{:S(2)}, u32[]{:S(2)}) collective-permute-start(bf16[128,2048]{1,0:T(8,128)(2,1)S(1)} %get-tuple-element.78.refs_2_), channel_id=1, source_target_pairs={{0,1},{1,0},{2,3},{3,2},{4,5},{5,4},{6,7},{7,6},{8,9},{9,8},{10,11... | collective-permute-start | bytes 1572872 | tf_op jit(solution)/shard_map/ppermute | solution.py:251
  69.5 13.0 %collective-permute-start.15 = (bf16[128,2048]{1,0:T(8,128)(2,1)S(1)}, bf16[128,2048]{1,0:T(8,128)(2,1)S(1)}, u32[]{:S(2)}, u32[]{:S(2)}) collective-permute-start(bf16[128,2048]{1,0:T(8,128)(2,1)S(1)} %get-tuple-element.78.refs_2_), channel_id=1, source_target_pairs={{0,16},{16,0},{1,17},{17,1},{2,18},{18,2},{3,19},{19,3},{4,20},{20... | collective-permute-start | bytes 1572872 | tf_op jit(solution)/shard_map/ppermute | solution.py:251
  70.0 16.8 %collective-permute-start.17 = (bf16[128,2048]{1,0:T(8,128)(2,1)S(1)}, bf16[128,2048]{1,0:T(8,128)(2,1)}, u32[]{:S(2)}, u32[]{:S(2)}) collective-permute-start(bf16[128,2048]{1,0:T(8,128)(2,1)S(1)} %get-tuple-element.78.refs_2_), channel_id=1, source_target_pairs={{0,2},{2,4},{4,6},{6,0},{1,3},{3,5},{5,7},{7,1},{8,10},{10,12},{12... | collective-permute-start | bytes 1572872 | tf_op jit(solution)/shard_map/ppermute | solution.py:256
  70.0 23.7 %collective-permute-start.21 = (bf16[128,2048]{1,0:T(8,128)(2,1)S(1)}, bf16[128,2048]{1,0:T(8,128)(2,1)}, u32[]{:S(2)}, u32[]{:S(2)}) collective-permute-start(bf16[128,2048]{1,0:T(8,128)(2,1)S(1)} %get-tuple-element.78.refs_2_), channel_id=1, source_target_pairs={{0,6},{2,0},{4,2},{6,4},{1,7},{3,1},{5,3},{7,5},{8,14},{10,8},{12,... | collective-permute-start | bytes 1572872 | tf_op jit(solution)/shard_map/ppermute | solution.py:256
  77.8 43.2 %collective-permute-start.16 = (bf16[128,2048]{1,0:T(8,128)(2,1)S(1)}, bf16[128,2048]{1,0:T(8,128)(2,1)}, u32[]{:S(2)}, u32[]{:S(2)}) collective-permute-start(bf16[128,2048]{1,0:T(8,128)(2,1)S(1)} %collective-permute-done.14.refs_3_), channel_id=1, source_target_pairs={{0,16},{16,0},{1,17},{17,1},{2,18},{18,2},{3,19},{19,3},{4,20},{20... | collective-permute-start | bytes 1572872 | tf_op jit(solution)/shard_map/ppermute | solution.py:251
  78.3 44.3 %collective-permute-start.22 = (bf16[128,2048]{1,0:T(8,128)(2,1)S(1)}, bf16[128,2048]{1,0:T(8,128)(2,1)}, u32[]{:S(2)}, u32[]{:S(2)}) collective-permute-start(bf16[128,2048]{1,0:T(8,128)(2,1)S(1)} %collective-permute-done.14.refs_3_), channel_id=1, source_target_pairs={{0,6},{2,0},{4,2},{6,4},{1,7},{3,1},{5,3},{7,5},{8,14},{10,8},{12,... | collective-permute-start | bytes 1572872 | tf_op jit(solution)/shard_map/ppermute | solution.py:256
  82.5 38.0 %collective-permute-start.19 = (bf16[128,2048]{1,0:T(8,128)(2,1)S(1)}, bf16[128,2048]{1,0:T(8,128)(2,1)}, u32[]{:S(2)}, u32[]{:S(2)}) collective-permute-start(bf16[128,2048]{1,0:T(8,128)(2,1)S(1)} %collective-permute-done.15.refs_4_), channel_id=1, source_target_pairs={{0,2},{2,4},{4,6},{6,0},{1,3},{3,5},{5,7},{7,1},{8,10},{10,12},{12... | collective-permute-start | bytes 1572872 | tf_op jit(solution)/shard_map/ppermute | solution.py:256
  86.7 57.8 %collective-permute-start.18 = (bf16[128,2048]{1,0:T(8,128)(2,1)}, bf16[128,2048]{1,0:T(8,128)(2,1)S(1)}, u32[]{:S(2)}, u32[]{:S(2)}) collective-permute-start(bf16[128,2048]{1,0:T(8,128)(2,1)} %collective-permute-done.17.refs_2_), channel_id=1, source_target_pairs={{0,1},{1,0},{2,3},{3,2},{4,5},{5,4},{6,7},{7,6},{8,9},{9,8},{10,11... | collective-permute-start | bytes 1572872 | tf_op jit(solution)/shard_map/ppermute | solution.py:251
  93.6 49.4 %collective-permute-start.32 = (bf16[128,2048]{1,0:T(8,128)(2,1)}, bf16[128,2048]{1,0:T(8,128)(2,1)}, u32[]{:S(2)}, u32[]{:S(2)}) collective-permute-start(bf16[128,2048]{1,0:T(8,128)(2,1)} %collective-permute-done.17.refs_2_), channel_id=1, source_target_pairs={{0,2},{2,4},{4,6},{6,0},{1,3},{3,5},{5,7},{7,1},{8,10},{10,12},{12... | collective-permute-start | bytes 1572872 | tf_op jit(solution)/shard_map/ppermute | solution.py:256
  120.5 24.1 %collective-permute-start.20 = (bf16[128,2048]{1,0:T(8,128)(2,1)}, bf16[128,2048]{1,0:T(8,128)(2,1)S(1)}, u32[]{:S(2)}, u32[]{:S(2)}) collective-permute-start(bf16[128,2048]{1,0:T(8,128)(2,1)} %collective-permute-done.19.refs_4_), channel_id=1, source_target_pairs={{0,1},{1,0},{2,3},{3,2},{4,5},{5,4},{6,7},{7,6},{8,9},{9,8},{10,11... | collective-permute-start | bytes 1572872 | tf_op jit(solution)/shard_map/ppermute | solution.py:251
  121.0 41.3 %collective-permute-start.23 = (bf16[128,2048]{1,0:T(8,128)(2,1)}, bf16[128,2048]{1,0:T(8,128)(2,1)S(1)}, u32[]{:S(2)}, u32[]{:S(2)}) collective-permute-start(bf16[128,2048]{1,0:T(8,128)(2,1)} %collective-permute-done.21.refs_2_), channel_id=1, source_target_pairs={{0,16},{16,0},{1,17},{17,1},{2,18},{18,2},{3,19},{19,3},{4,20},{20... | collective-permute-start | bytes 1572872 | tf_op jit(solution)/shard_map/ppermute | solution.py:251
  122.6 39.7 %collective-permute-start.24 = (bf16[128,2048]{1,0:T(8,128)(2,1)}, bf16[128,2048]{1,0:T(8,128)(2,1)S(1)}, u32[]{:S(2)}, u32[]{:S(2)}) collective-permute-start(bf16[128,2048]{1,0:T(8,128)(2,1)} %collective-permute-done.22.refs_3_), channel_id=1, source_target_pairs={{0,16},{16,0},{1,17},{17,1},{2,18},{18,2},{3,19},{19,3},{4,20},{20... | collective-permute-start | bytes 1572872 | tf_op jit(solution)/shard_map/ppermute | solution.py:251
  132.0 13.4 %slice-start.1 = ((s8[5767168]{0:T(1024)(128)(4,1)}), s8[4194304]{0:T(1024)(128)(4,1)S(1)}, s32[]{:S(2)}) async-start(s8[5767168]{0:T(1024)(128)(4,1)} %bitcast.45), calls=%async_computation.1 | async-start | bytes 8388608
  143.1 36.0 %collective-permute-start.34 = (bf16[128,2048]{1,0:T(8,128)(2,1)}, bf16[128,2048]{1,0:T(8,128)(2,1)S(1)}, u32[]{:S(2)}, u32[]{:S(2)}) collective-permute-start(bf16[128,2048]{1,0:T(8,128)(2,1)} %collective-permute-done.32.refs_2_), channel_id=1, source_target_pairs={{0,16},{16,0},{1,17},{17,1},{2,18},{18,2},{3,19},{19,3},{4,20},{20... | collective-permute-start | bytes 1572872 | tf_op jit(solution)/shard_map/ppermute | solution.py:251
  150.9 12.2 %copy-start.7 = (bf16[1,704,2048]{2,1,0:T(8,128)(2,1)S(1)}, bf16[1,704,2048]{2,1,0:T(8,128)(2,1)}, u32[]{:S(2)}) copy-start(bf16[1,704,2048]{2,1,0:T(8,128)(2,1)} %param.23) | copy-start | bytes 8650756
  160.7 20.0 %collective-permute-start.25 = (bf16[128,2048]{1,0:T(8,128)(2,1)S(1)}, bf16[128,2048]{1,0:T(8,128)(2,1)S(1)}, u32[]{:S(2)}, u32[]{:S(2)}) collective-permute-start(bf16[128,2048]{1,0:T(8,128)(2,1)S(1)} %get-tuple-element.99), channel_id=1, source_target_pairs={{0,1},{1,0},{2,3},{3,2},{4,5},{5,4},{6,7},{7,6},{8,9},{9,8},{10,11... | collective-permute-start | bytes 1572872 | tf_op jit(solution)/shard_map/ppermute | solution.py:251
  176.5 12.7 %collective-permute-start.29 = (bf16[128,2048]{1,0:T(8,128)(2,1)S(1)}, bf16[128,2048]{1,0:T(8,128)(2,1)S(1)}, u32[]{:S(2)}, u32[]{:S(2)}) collective-permute-start(bf16[128,2048]{1,0:T(8,128)(2,1)S(1)} %get-tuple-element.104), channel_id=1, source_target_pairs={{0,16},{16,0},{1,17},{17,1},{2,18},{18,2},{3,19},{19,3},{4,20},{20... | collective-permute-start | bytes 1572872 | tf_op jit(solution)/shard_map/ppermute | solution.py:251
  177.1 57.3 %collective-permute-start.28 = (bf16[128,2048]{1,0:T(8,128)(2,1)S(1)}, bf16[128,2048]{1,0:T(8,128)(2,1)S(1)}, u32[]{:S(2)}, u32[]{:S(2)}) collective-permute-start(bf16[128,2048]{1,0:T(8,128)(2,1)S(1)} %copy-done.24), channel_id=1, source_target_pairs={{0,16},{16,0},{1,17},{17,1},{2,18},{18,2},{3,19},{19,3},{4,20},{20... | collective-permute-start | bytes 1572872 | tf_op jit(solution)/shard_map/ppermute | solution.py:251
  178.6 13.8 %collective-permute-start.33 = (bf16[128,2048]{1,0:T(8,128)(2,1)}, bf16[128,2048]{1,0:T(8,128)(2,1)S(1)}, u32[]{:S(2)}, u32[]{:S(2)}) collective-permute-start(bf16[128,2048]{1,0:T(8,128)(2,1)} %collective-permute-done.32.refs_2_), channel_id=1, source_target_pairs={{0,1},{1,0},{2,3},{3,2},{4,5},{5,4},{6,7},{7,6},{8,9},{9,8},{10,11... | collective-permute-start | bytes 1572872 | tf_op jit(solution)/shard_map/ppermute | solution.py:251
  179.1 36.5 %collective-permute-start.40 = (bf16[128,2048]{1,0:T(8,128)(2,1)S(1)}, bf16[128,2048]{1,0:T(8,128)(2,1)S(1)}, u32[]{:S(2)}, u32[]{:S(2)}) collective-permute-start(bf16[128,2048]{1,0:T(8,128)(2,1)S(1)} %get-tuple-element.111), channel_id=1, source_target_pairs={{0,1},{1,0},{2,3},{3,2},{4,5},{5,4},{6,7},{7,6},{8,9},{9,8},{10,11... | collective-permute-start | bytes 1572872 | tf_op jit(solution)/shard_map/ppermute | solution.py:251
  180.7 23.0 %collective-permute-start.35 = (bf16[128,2048]{1,0:T(8,128)(2,1)S(1)}, bf16[128,2048]{1,0:T(8,128)(2,1)S(1)}, u32[]{:S(2)}, u32[]{:S(2)}) collective-permute-start(bf16[128,2048]{1,0:T(8,128)(2,1)S(1)} %collective-permute-done.34.refs_4_), channel_id=1, source_target_pairs={{0,1},{1,0},{2,3},{3,2},{4,5},{5,4},{6,7},{7,6},{8,9},{9,8},{10,11... | collective-permute-start | bytes 1572872 | tf_op jit(solution)/shard_map/ppermute | solution.py:251
  189.3 28.1 %collective-permute-start.42 = (bf16[128,2048]{1,0:T(8,128)(2,1)S(1)}, bf16[128,2048]{1,0:T(8,128)(2,1)S(1)}, u32[]{:S(2)}, u32[]{:S(2)}) collective-permute-start(bf16[128,2048]{1,0:T(8,128)(2,1)S(1)} %get-tuple-element.113), channel_id=1, source_target_pairs={{0,16},{16,0},{1,17},{17,1},{2,18},{18,2},{3,19},{19,3},{4,20},{20... | collective-permute-start | bytes 1572872 | tf_op jit(solution)/shard_map/ppermute | solution.py:251
  192.4 41.3 %collective-permute-start.26 = (bf16[128,2048]{1,0:T(8,128)(2,1)S(1)}, bf16[128,2048]{1,0:T(8,128)(2,1)S(1)}, u32[]{:S(2)}, u32[]{:S(2)}) collective-permute-start(bf16[128,2048]{1,0:T(8,128)(2,1)S(1)} %add_convert_fusion.8), channel_id=1, source_target_pairs={{0,6},{2,0},{4,2},{6,4},{1,7},{3,1},{5,3},{7,5},{8,14},{10,8},{12,... | collective-permute-start | bytes 1572872 | tf_op jit(solution)/shard_map/ppermute | solution.py:256
  203.7 30.9 %collective-permute-start.30 = (bf16[128,2048]{1,0:T(8,128)(2,1)S(1)}, bf16[128,2048]{1,0:T(8,128)(2,1)S(1)}, u32[]{:S(2)}, u32[]{:S(2)}) collective-permute-start(bf16[128,2048]{1,0:T(8,128)(2,1)S(1)} %add_convert_fusion.6), channel_id=1, source_target_pairs={{0,2},{2,4},{4,6},{6,0},{1,3},{3,5},{5,7},{7,1},{8,10},{10,12},{12... | collective-permute-start | bytes 1572872 | tf_op jit(solution)/shard_map/ppermute | solution.py:256
  215.6 20.5 %copy-start.17 = (bf16[128,2048]{1,0:T(8,128)(2,1)S(1)}, bf16[128,2048]{1,0:T(8,128)(2,1)}, u32[]{:S(2)}) copy-start(bf16[128,2048]{1,0:T(8,128)(2,1)} %copy-done.16) | copy-start | bytes 1572868
  215.6 13.8 %collective-permute-start.37 = (bf16[128,2048]{1,0:T(8,128)(2,1)S(1)}, bf16[128,2048]{1,0:T(8,128)(2,1)S(1)}, u32[]{:S(2)}, u32[]{:S(2)}) collective-permute-start(bf16[128,2048]{1,0:T(8,128)(2,1)S(1)} %get-tuple-element.109), channel_id=1, source_target_pairs={{0,1},{1,0},{2,3},{3,2},{4,5},{5,4},{6,7},{7,6},{8,9},{9,8},{10,11... | collective-permute-start | bytes 1572872 | tf_op jit(solution)/shard_map/ppermute | solution.py:251
  217.4 19.0 %collective-permute-start.36 = (bf16[128,2048]{1,0:T(8,128)(2,1)S(1)}, bf16[128,2048]{1,0:T(8,128)(2,1)S(1)}, u32[]{:S(2)}, u32[]{:S(2)}) collective-permute-start(bf16[128,2048]{1,0:T(8,128)(2,1)S(1)} %get-tuple-element.107), channel_id=1, source_target_pairs={{0,1},{1,0},{2,3},{3,2},{4,5},{5,4},{6,7},{7,6},{8,9},{9,8},{10,11... | collective-permute-start | bytes 1572872 | tf_op jit(solution)/shard_map/ppermute | solution.py:251
  229.4 18.5 %collective-permute-start.41 = (bf16[128,2048]{1,0:T(8,128)(2,1)S(1)}, bf16[128,2048]{1,0:T(8,128)(2,1)S(1)}, u32[]{:S(2)}, u32[]{:S(2)}) collective-permute-start(bf16[128,2048]{1,0:T(8,128)(2,1)S(1)} %add_convert_fusion.2), channel_id=1, source_target_pairs={{0,6},{2,0},{4,2},{6,4},{1,7},{3,1},{5,3},{7,5},{8,14},{10,8},{12,... | collective-permute-start | bytes 1572872 | tf_op jit(solution)/shard_map/ppermute | solution.py:256
  233.7 9.2 %collective-permute-start.38 = (bf16[128,2048]{1,0:T(8,128)(2,1)S(1)}, bf16[128,2048]{1,0:T(8,128)(2,1)S(1)}, u32[]{:S(2)}, u32[]{:S(2)}) collective-permute-start(bf16[128,2048]{1,0:T(8,128)(2,1)S(1)} %add_convert_fusion.4), channel_id=1, source_target_pairs={{0,16},{16,0},{1,17},{17,1},{2,18},{18,2},{3,19},{19,3},{4,20},{20... | collective-permute-start | bytes 1572872 | tf_op jit(solution)/shard_map/ppermute | solution.py:251
  234.4 13.5 %collective-permute-start.43 = (bf16[128,2048]{1,0:T(8,128)(2,1)S(1)}, bf16[128,2048]{1,0:T(8,128)(2,1)S(1)}, u32[]{:S(2)}, u32[]{:S(2)}) collective-permute-start(bf16[128,2048]{1,0:T(8,128)(2,1)S(1)} %add_convert_fusion.1), channel_id=1, source_target_pairs={{0,2},{2,4},{4,6},{6,0},{1,3},{3,5},{5,7},{7,1},{8,10},{10,12},{12... | collective-permute-start | bytes 1572872 | tf_op jit(solution)/shard_map/ppermute | solution.py:256
  234.5 14.1 %collective-permute-start.27 = (bf16[128,2048]{1,0:T(8,128)(2,1)S(1)}, bf16[128,2048]{1,0:T(8,128)(2,1)S(1)}, u32[]{:S(2)}, u32[]{:S(2)}) collective-permute-start(bf16[128,2048]{1,0:T(8,128)(2,1)S(1)} %add_convert_fusion.7), channel_id=1, source_target_pairs={{0,16},{16,0},{1,17},{17,1},{2,18},{18,2},{3,19},{19,3},{4,20},{20... | collective-permute-start | bytes 1572872 | tf_op jit(solution)/shard_map/ppermute | solution.py:251
  236.3 12.2 %collective-permute-start.31 = (bf16[128,2048]{1,0:T(8,128)(2,1)S(1)}, bf16[128,2048]{1,0:T(8,128)(2,1)S(1)}, u32[]{:S(2)}, u32[]{:S(2)}) collective-permute-start(bf16[128,2048]{1,0:T(8,128)(2,1)S(1)} %add_convert_fusion.5), channel_id=1, source_target_pairs={{0,1},{1,0},{2,3},{3,2},{4,5},{5,4},{6,7},{7,6},{8,9},{9,8},{10,11... | collective-permute-start | bytes 1572872 | tf_op jit(solution)/shard_map/ppermute | solution.py:251
  243.2 18.2 %collective-permute-start.39 = (bf16[128,2048]{1,0:T(8,128)(2,1)S(1)}, bf16[128,2048]{1,0:T(8,128)(2,1)S(1)}, u32[]{:S(2)}, u32[]{:S(2)}) collective-permute-start(bf16[128,2048]{1,0:T(8,128)(2,1)S(1)} %add_convert_fusion.3), channel_id=1, source_target_pairs={{0,4},{2,6},{4,0},{6,2},{1,5},{3,7},{5,1},{7,3},{8,12},{10,14},{12... | collective-permute-start | bytes 1572872 | tf_op jit(solution)/shard_map/ppermute | solution.py:256
  (23 other events, 46.6 us)

commit v7 on v6

--- a/solution.py
+++ b/solution.py
@@ -13,20 +13,31 @@
 TOP = 6
 ALL = ("far", "core", "line", "side")
 GATHER_BUDGET = 40 * 2**20
-VMEM_LIMIT = 20 * 2**20
-EXPERT_VMEM = 32 * 2**20
-
-
-def attention_kernel(q_ref, sk_ref, sv_ref, *refs):
-    pieces, out_ref = refs[:-1], refs[-1]
-    rows = q_ref.shape[0]
-    span = q_ref.shape[1]
+ATTEND_VMEM = 24 * 2**20
+EXPERT_VMEM = 36 * 2**20
+
+
+def attend_kernel(count, gain_ref, *refs):
+    pieces, refs = refs[:count], refs[count:]
+    sources, refs = refs[:5], refs[5:]
+    attended_ref, normed_ref, heads, residual = refs[:4]
+    held, arrived = refs[4:9], refs[9]
+    copies = [
+        pltpu.make_async_copy(source, target, arrived.at[i])
+        for i, (source, target) in enumerate(zip(sources, held))
+    ]
+    for copy in copies:
+        copy.start()
+    q_ref, sk_ref, sv_ref, tokens_ref, weight_ref = held
+    rows, width = heads.shape
     scale = 1.0 / math.sqrt(HEAD_DIM)
     causal = lax.broadcasted_iota(jnp.int32, (rows, rows), 0) >= lax.broadcasted_iota(
         jnp.int32, (rows, rows), 1
     )
     contract = (((1,), (1,)), ((), ()))
-    for head in range(span // HEAD_DIM):
+    for copy in copies[:3]:
+        copy.wait()
+    for head in range(width // HEAD_DIM):
         cols = slice(head * HEAD_DIM, (head + 1) * HEAD_DIM)
         query = q_ref[:, cols]
         keys = jnp.concatenate([piece[0, :, cols] for piece in pieces])
@@ -50,75 +61,49 @@
         ) + jnp.dot(
             suffix.astype(jnp.bfloat16), sv_ref[:, cols], preferred_element_type=jnp.float32
         )
-        out_ref[:, cols] = (mixed / total).astype(jnp.bfloat16)
-
-
-def attention(queries, suffix_keys, suffix_values, pieces):
-    rows, width = queries.shape
-    span = 4 * HEAD_DIM
-    by_cols = pl.BlockSpec((rows, span), lambda i: (0, i))
+        heads[:, cols] = (mixed / total).astype(jnp.bfloat16)
+    for copy in copies[3:]:
+        copy.wait()
+    span = 512
+    squares = jnp.zeros((rows, 1), jnp.float32)
+    for low in range(0, width, span):
+        cols = slice(low, low + span)
+        attended = jnp.dot(
+            heads[...], weight_ref[:, cols], preferred_element_type=jnp.float32
+        ).astype(jnp.bfloat16)
+        attended_ref[:, cols] = attended
+        part = tokens_ref[:, cols].astype(jnp.float32) + attended.astype(jnp.float32)
+        residual[:, cols] = part
+        squares = squares + jnp.sum(part * part, axis=1, keepdims=True)
+    factor = lax.rsqrt(squares / width + 1e-06)
+    for low in range(0, width, span):
+        cols = slice(low, low + span)
+        normed_ref[:, cols] = (residual[:, cols] * factor * gain_ref[:, cols]).astype(
+            jnp.bfloat16
+        )
+
+
+def attend(queries, suffix_keys, suffix_values, pieces, tokens, out_weight, norm_gain):
+    rows, width = tokens.shape
+    sources = [queries, suffix_keys, suffix_values, tokens, out_weight]
+    local = pl.BlockSpec(memory_space=pltpu.VMEM)
     return pl.pallas_call(
-        attention_kernel,
-        grid=(width // span,),
-        in_specs=[by_cols] * 3
-        + [pl.BlockSpec(piece.shape[:2] + (span,), lambda i: (0, 0, i)) for piece in pieces],
-        out_specs=by_cols,
-        out_shape=jax.ShapeDtypeStruct((rows, width), jnp.bfloat16),
-        compiler_params=pltpu.CompilerParams(vmem_limit_bytes=VMEM_LIMIT),
+        lambda *refs: attend_kernel(len(pieces), *refs),
+        in_specs=[local] * (1 + len(pieces)) + [pl.BlockSpec(memory_space=pltpu.HBM)] * 5,
+        out_specs=[local] * 2,
+        out_shape=[jax.ShapeDtypeStruct((rows, width), jnp.bfloat16)] * 2,
+        scratch_shapes=[
+            pltpu.VMEM((rows, width), jnp.bfloat16),
+            pltpu.VMEM((rows, width), jnp.float32),
+        ]
+        + [pltpu.VMEM(one.shape, jnp.bfloat16) for one in sources]
+        + [pltpu.SemaphoreType.DMA((5,))],
+        compiler_params=pltpu.CompilerParams(vmem_limit_bytes=ATTEND_VMEM),
         cost_estimate=pl.CostEstimate(
-            flops=12 * rows * rows * width, bytes_accessed=12 * rows * width, transcendentals=0
+            flops=12 * rows * width * width, bytes_accessed=4 * rows * width, transcendentals=0
         ),
-        name="attention",
-    )(queries, suffix_keys, suffix_values, *pieces)
-
-
-def project_kernel(heads_ref, weight_ref, tokens_ref, gain_ref, attended_ref, normed_ref, held):
-    step = pl.program_id(0)
-    attended = jnp.dot(
-        heads_ref[...], weight_ref[...], preferred_element_type=jnp.float32
-    ).astype(jnp.bfloat16)
-    attended_ref[...] = attended
-    held[step] = tokens_ref[...].astype(jnp.float32) + attended.astype(jnp.float32)
-
-    @pl.when(step == pl.num_programs(0) - 1)
-    def finish():
-        steps, rows, span = held.shape
-        squares = jnp.zeros((rows, 1), jnp.float32)
-        for piece in range(steps):
-            part = held[piece]
-            squares = squares + jnp.sum(part * part, axis=1, keepdims=True)
-        factor = lax.rsqrt(squares / (steps * span) + 1e-06)
-        for piece in range(steps):
-            cols = slice(piece * span, (piece + 1) * span)
-            normed_ref[:, cols] = (held[piece] * factor * gain_ref[:, cols]).astype(jnp.bfloat16)
-
-
-def project(heads_out, out_weight, tokens, norm_gain):
-    rows, width = tokens.shape
-    span = 512
-    steps = width // span
-    by_cols = pl.BlockSpec((rows, span), lambda i: (0, i))
-    return pl.pallas_call(
-        project_kernel,
-        grid=(steps,),
-        in_specs=[
-            pl.BlockSpec((rows, width), lambda i: (0, 0)),
-            pl.BlockSpec((width, span), lambda i: (0, i)),
-            by_cols,
-            pl.BlockSpec((1, width), lambda i: (0, 0)),
-        ],
-        out_specs=[by_cols, pl.BlockSpec((rows, width), lambda i: (0, 0))],
-        out_shape=[
-            jax.ShapeDtypeStruct((rows, width), jnp.bfloat16),
-            jax.ShapeDtypeStruct((rows, width), jnp.bfloat16),
-        ],
-        scratch_shapes=[pltpu.VMEM((steps, rows, span), jnp.float32)],
-        compiler_params=pltpu.CompilerParams(vmem_limit_bytes=VMEM_LIMIT),
-        cost_estimate=pl.CostEstimate(
-            flops=2 * rows * width * width, bytes_accessed=2 * width * width, transcendentals=0
-        ),
-        name="project_and_norm",
-    )(heads_out, out_weight, tokens, norm_gain.reshape(1, width))
+        name="attend_project_norm",
+    )(norm_gain.reshape(1, width), *pieces, *sources)
 
 
 def experts_kernel(capacity, count, slot_ref, gate_ref, *refs):
@@ -189,8 +174,8 @@
         + [pltpu.SemaphoreType.DMA((4,))],
         compiler_params=pltpu.CompilerParams(vmem_limit_bytes=EXPERT_VMEM),
         cost_estimate=pl.CostEstimate(
-            flops=total * width * hidden * 6,
-            bytes_accessed=sum(one.size * 2 for one in weights) + count * rows * width * 4,
+            flops=total * width * hidden * 12,
+            bytes_accessed=count * rows * width,
             transcendentals=total * hidden,
         ),
         name="experts",
@@ -287,8 +272,10 @@
             held[back] = shift(held[(back - step) % len(order)], "line", step)
         for back in ready:
             swapped[back] = swap(held[back], "side")
-        moved, crossed, table, weights = lax.optimization_barrier(
-            ([held[back] for back in fresh], [swapped[back] for back in ready], table, weights)
+        if i == 1:
+            tables = [table] + [shift(table, "line", back) for back in range(1, len(order))]
+        moved, crossed, tables, weights = lax.optimization_barrier(
+            ([held[back] for back in fresh], [swapped[back] for back in ready], tables, weights)
         )
         if i == 1:
             others = [swap(one, "core") for one in weights]
@@ -297,10 +284,13 @@
         ready = fresh
     for back in ready:
         swapped[back] = swap(held[back], "side")
-    tables = [table] + [shift(table, "line", back) for back in range(1, len(order))]
-    tables, crossed = lax.optimization_barrier((tables, [swapped[back] for back in ready]))
+    table = jnp.stack(tables)
+    beside, crossed = lax.optimization_barrier(
+        (swap(table, "side"), [swapped[back] for back in ready])
+    )
     swapped.update(zip(ready, crossed))
-    return list(held.values()) + list(swapped.values()), jnp.stack(tables), others
+    table = jnp.stack([table, beside])
+    return list(held.values()) + list(swapped.values()), table, others
 
 
 def relative_slots(table, capacity):
@@ -320,8 +310,9 @@
 def spread(normed):
     columns = lax.axis_size("line")
     beside, across = swap(normed, "side"), swap(normed, "far")
+    up, down = shift(normed, "line", 1), shift(normed, "line", -1)
     planes = {0: [normed, beside, across, swap(beside, "far")]}
-    up, down = shift(normed, "line", 1), shift(normed, "line", -1)
+    up, down, beside, across = lax.optimization_barrier((up, down, beside, across))
     lines = {1: up, columns - 1: down}
     for back in nearest_first()[3:]:
         step = 1 if back <= columns // 2 else -1
@@ -341,35 +332,43 @@
 
 def gather_plan(normed, slots, gates, weights, capacity):
     columns = lax.axis_size("line")
-    order = nearest_first()
+    distant = nearest_first()[3:]
+    order = [0, 1] + distant + [columns - 1]
     planes = spread(normed)
-    results, first_corner, previous = {}, None, None
+    results, corner_up, previous = {}, None, None
     for i, back in enumerate(order):
         mine = slots[:, back]
         if i > 0:
             mine, previous = lax.optimization_barrier((mine, previous))
             results[order[i - 1]] = previous
+        if back == 1:
+            mine, planes[columns - 1][:3] = lax.optimization_barrier(
+                (mine, planes[columns - 1][:3])
+            )
         if i == 2:
-            first_corner = swap(results[1][3], "side")
-        if i == len(order) - 1 and i > 2:
-            mine, first_corner = lax.optimization_barrier((mine, first_corner))
+            corner_up = swap(results[1][3], "side")
+            results[0], planes[back][3] = lax.optimization_barrier(
+                (results[0], planes[back][3])
+            )
+        if i == 3:
+            mine, corner_up = lax.optimization_barrier((mine, corner_up))
         previous = run_experts(planes[back], mine, gates[:, back], weights, capacity)
     results[order[-1]] = previous
+    parts = []
+    for back in distant:
+        here, beside, across, corner = results[back]
+        side_sum = add(beside, swap(corner, "far"))
+        total = add(here, swap(across, "far"), swap(side_sum, "side"))
+        parts.append(shift(total, "line", -back))
     here, beside, across, corner = results[1]
     up = add(here, swap(beside, "side"))
-    across_up = add(across, first_corner)
+    across_up = add(across, corner_up)
     here, beside, across, corner = results[columns - 1]
     beside_down = add(beside, swap(corner, "far"))
     down = add(here, swap(across, "far"))
-    parts = []
-    for back in order[3:]:
-        here, beside, across, corner = results[back]
-        far_sum = add(across, swap(corner, "side"))
-        total = add(here, swap(beside, "side"), swap(far_sum, "far"))
-        parts.append(shift(total, "line", -back))
     here, beside, across, corner = results[0]
-    across = add(across, shift(across_up, "line", -1))
-    beside = add(beside, swap(corner, "far"), shift(beside_down, "line", 1))
+    across = add(across, swap(corner, "side"), shift(across_up, "line", -1))
+    beside = add(beside, shift(beside_down, "line", 1))
     parts = parts + [shift(up, "line", -1), shift(down, "line", 1)]
     return add(here, swap(across, "far"), swap(beside, "side"), *parts)
 
@@ -400,15 +399,12 @@
     if gather_fits:
         table = jnp.concatenate([routes.T.astype(jnp.float32), route_weights.T])
         pieces, table, others = prefix_pieces(kv, table, weights)
-        beside = swap(table, "side")
+        across = swap(table, "far")
     else:
         pieces = [lax.all_gather(kv, ("line", "side"), axis=1, tiled=True)]
-    heads_out = attention(queries, suffix_keys, suffix_values, pieces)
-    if gather_fits:
-        heads_out, beside = lax.optimization_barrier((heads_out, beside))
-        table = jnp.stack([table, beside])
-        across = swap(table, "far")
-    attended, normed = project(heads_out, out_weight, tokens, norm_gain)
+    attended, normed = attend(
+        queries, suffix_keys, suffix_values, pieces, tokens, out_weight, norm_gain
+    )
     if gather_fits:
         normed, others, across = lax.optimization_barrier((normed, others, across))
         slots, gates = relative_slots(jnp.stack([table, across]), capacity)

time: 264 us -> 257 us (0.973)
  waiting for transfers between devices: 116 us -> 135 us
  local copies, waits for them, and re-layouts: 38.2 us -> 22.1 us
  starting transfers between devices: 56.3 us -> 51.2 us
  Pallas kernels: 46.9 us -> 43.1 us
    ppermute x28, waiting for transfers between devices: 49.1 us -> 71.8 us  [swap(): return lax.ppermute(array, axis, [(0, 1), (1, 0)])]
    unnamed x55 -> x35, local copies, waits for them, and re-layouts: 37.2 us -> 21.1 us
    ppermute x16, starting transfers between devices: 28.9 us -> 24.6 us  [shift(): lax.ppermute(array, axis, [(i, (i + amount) % size) for i in range(size)])]
    ppermute x16, waiting for transfers between devices: 66.9 us -> 62.8 us  [shift(): lax.ppermute(array, axis, [(i, (i + amount) % size) for i in range(size)])]
    pallas_call x2 -> x1, Pallas kernels: 8.62 us -> 7.17 us  [attend(): pl.pallas_call(lambda *refs: attend_kernel(len(pieces), *refs), in_specs=...]
  transfers between devices with their start and end apart: 44 -> 44, of which waited for: 20 -> 23; matrix products, arithmetic and copies ran while one was open for 1% -> 1% of each run, Pallas kernels for 18% -> 17%
where the time goes in v7:
time: 257 us; the launch traced here: 256 us
  waiting for transfers between devices  135 us (53%)
  starting transfers between devices  51.2 us (20%)
  Pallas kernels  43.1 us (17%)
  local copies, waits for them, and re-layouts  22.1 us (9%)
  other arithmetic  4.12 us (2%)
    ppermute x28, waiting for transfers between devices, swap(): return lax.ppermute(array, axis, [(0, 1), (1, 0)])  71.8 us
    ppermute x16, waiting for transfers between devices, shift(): lax.ppermute(array, axis, [(i, (i + amount) % size) for i in range(size)])  62.8 us
    pallas_call x4, Pallas kernels, run_experts(): pl.pallas_call(lambda *refs: experts_kernel(capacity, count, *refs), in_s...  35.9 us
    ppermute x28, starting transfers between devices, swap(): return lax.ppermute(array, axis, [(0, 1), (1, 0)])  26.7 us
    ppermute x16, starting transfers between devices, shift(): lax.ppermute(array, axis, [(i, (i + amount) % size) for i in range(size)])  24.6 us
    unnamed x35, local copies, waits for them, and re-layouts  21.1 us
    pallas_call x1, Pallas kernels, attend(): pl.pallas_call(lambda *refs: attend_kernel(len(pieces), *refs), in_specs=...  7.17 us
  transfers between devices with their start and end apart: 44, of which 23 were waited for; matrix products, arithmetic and copies ran while one was open for 1% of the time, Pallas kernels for 17%

profile of v7, /device:TPU:0, one launch (start us, length us, event | category | flops | bytes accessed | tf_op | source)
XLA Modules:
  0.0 256.4 jit_solution(9413152859857661899)
XLA Ops:
  2.5 3.1 %collective-permute-start = (bf16[2,32,2048]{2,1,0:T(8,128)(2,1)S(1)}, bf16[2,32,2048]{2,1,0:T(8,128)(2,1)S(1)}, u32[]{:S(2)}, u32[]{:S(2)}) collective-permute-start(bf16[2,32,2048]{2,1,0:T(8,128)(2,1)S(1)} %constant_dynamic-update-slice_fusion.refs_1_), channel_id=1, source_target_pairs={{0,2},{2,4},{4,6},{6,0},{1,3},{3,5},{5,7},{7,1},{8,10},{10,12},{12... | collective-permute-start | bytes 786440 | tf_op jit(solution)/shard_map/ppermute | solution.py:241
  5.5 2.1 collective-permute-start.1
  7.6 1.7 collective-permute-start.2
  10.7 2.4 collective-permute-start.4
  13.1 6.9 %collective-permute-done.3 = f32[12,128]{1,0:T(8,128)S(1)} collective-permute-done((f32[12,128]{1,0:T(8,128)S(1)}, f32[12,128]{1,0:T(8,128)S(1)}, u32[]{:S(2)}, u32[]{:S(2)}) %collective-permute-start.3) | collective-permute-done | bytes 6176 | tf_op jit(solution)/shard_map/ppermute | solution.py:241
  19.9 1.5 collective-permute-start.5
  21.5 2.1 collective-permute-done.5
  24.2 1.5 collective-permute-start.7
  26.2 8.1 %collective-permute-done.6.refs_4_ = bf16[2,32,2048]{2,1,0:T(8,128)(2,1)S(1)} collective-permute-done((bf16[2,32,2048]{2,1,0:T(8,128)(2,1)S(1)}, bf16[2,32,2048]{2,1,0:T(8,128)(2,1)S(1)}, u32[]{:S(2)}, u32[]{:S(2)}) %collective-permute-start.6) | collective-permute-done | bytes 262176 | tf_op jit(solution)/shard_map/ppermute | solution.py:241
  34.3 3.8 %collective-permute-done.8.refs_7_ = bf16[2,32,2048]{2,1,0:T(8,128)(2,1)S(1)} collective-permute-done((bf16[2,32,2048]{2,1,0:T(8,128)(2,1)S(1)}, bf16[2,32,2048]{2,1,0:T(8,128)(2,1)S(1)}, u32[]{:S(2)}, u32[]{:S(2)}) %collective-permute-start.8) | collective-permute-done | bytes 262176 | tf_op jit(solution)/shard_map/ppermute | solution.py:236
  40.1 6.1 %collective-permute-done.9 = f32[4,12,128]{2,1,0:T(8,128)S(1)} collective-permute-done((f32[4,12,128]{2,1,0:T(8,128)S(1)}, f32[4,12,128]{2,1,0:T(8,128)S(1)}, u32[]{:S(2)}, u32[]{:S(2)}) %collective-permute-start.9) | collective-permute-done | bytes 24608 | tf_op jit(solution)/shard_map/ppermute | solution.py:236
  46.3 1.6 collective-permute-start.13
  47.8 3.4 %copy-done = bf16[2048,2048]{1,0:T(8,128)(2,1)S(1)} copy-done((bf16[2048,2048]{1,0:T(8,128)(2,1)S(1)}, bf16[2048,2048]{1,0:T(8,128)(2,1)}, u32[]{:S(2)}) %copy-start) | copy-done | bytes 8388632
  56.1 7.2 %attend_project_norm.1 = (bf16[128,2048]{1,0:T(8,128)(2,1)}, bf16[128,2048]{1,0:T(8,128)(2,1)S(1)}) custom-call(f32[1,2048]{1,0:T(1,128)S(1)} %bitcast.63, bf16[2,32,2048]{2,1,0:T(8,128)(2,1)S(1)} %constant_dynamic-update-slice_fusion.refs_1_, bf16[2,32,2048]{2,1,0:T(8,128)(2,1)S(1)} %collective-permute-done.refs_2_, ...), custom_call_target="tpu_custom_call" | custom-call | flops 6442450944 | bytes 1048576 | tf_op jit(solution)/shard_map/attend_project_norm/pallas_call | solution.py:90
  63.3 1.6 copy-done.5
  64.9 1.5 collective-permute-start.14
  68.1 3.1 %collective-permute-start.18 = (bf16[128,2048]{1,0:T(8,128)(2,1)S(1)}, bf16[128,2048]{1,0:T(8,128)(2,1)S(1)}, u32[]{:S(2)}, u32[]{:S(2)}) collective-permute-start(bf16[128,2048]{1,0:T(8,128)(2,1)S(1)} %get-tuple-element.93.refs_2_), channel_id=1, source_target_pairs={{0,6},{2,0},{4,2},{6,4},{1,7},{3,1},{5,3},{7,5},{8,14},{10,8},{12,... | collective-permute-start | bytes 1572872 | tf_op jit(solution)/shard_map/ppermute | solution.py:241
  71.3 5.5 %collective-permute-done.14.refs_3_ = bf16[128,2048]{1,0:T(8,128)(2,1)} collective-permute-done((bf16[128,2048]{1,0:T(8,128)(2,1)S(1)}, bf16[128,2048]{1,0:T(8,128)(2,1)}, u32[]{:S(2)}, u32[]{:S(2)}) %collective-permute-start.14) | collective-permute-done | bytes 524320 | tf_op jit(solution)/shard_map/ppermute | solution.py:236
  78.1 5.9 %collective-permute-done.17.refs_2_ = bf16[128,2048]{1,0:T(8,128)(2,1)S(1)} collective-permute-done((bf16[128,2048]{1,0:T(8,128)(2,1)S(1)}, bf16[128,2048]{1,0:T(8,128)(2,1)S(1)}, u32[]{:S(2)}, u32[]{:S(2)}) %collective-permute-start.17) | collective-permute-done | bytes 524320 | tf_op jit(solution)/shard_map/ppermute | solution.py:241
  84.1 8.0 %collective-permute-done.18.refs_2_ = bf16[128,2048]{1,0:T(8,128)(2,1)S(1)} collective-permute-done((bf16[128,2048]{1,0:T(8,128)(2,1)S(1)}, bf16[128,2048]{1,0:T(8,128)(2,1)S(1)}, u32[]{:S(2)}, u32[]{:S(2)}) %collective-permute-start.18) | collective-permute-done | bytes 524320 | tf_op jit(solution)/shard_map/ppermute | solution.py:241
  95.0 1.6 collective-permute-start.25
  96.6 2.6 %collective-permute-start.23 = (bf16[128,2048]{1,0:T(8,128)(2,1)}, bf16[128,2048]{1,0:T(8,128)(2,1)S(1)}, u32[]{:S(2)}, u32[]{:S(2)}) collective-permute-start(bf16[128,2048]{1,0:T(8,128)(2,1)} %collective-permute-done.14.refs_3_), channel_id=1, source_target_pairs={{0,6},{2,0},{4,2},{6,4},{1,7},{3,1},{5,3},{7,5},{8,14},{10,8},{12,... | collective-permute-start | bytes 1572872 | tf_op jit(solution)/shard_map/ppermute | solution.py:241
  99.2 9.7 %collective-permute-done.19.refs_2_ = bf16[128,2048]{1,0:T(8,128)(2,1)} collective-permute-done((bf16[128,2048]{1,0:T(8,128)(2,1)S(1)}, bf16[128,2048]{1,0:T(8,128)(2,1)}, u32[]{:S(2)}, u32[]{:S(2)}) %collective-permute-start.19) | collective-permute-done | bytes 524320 | tf_op jit(solution)/shard_map/ppermute | solution.py:241
  110.9 9.1 %collective-permute-done.26.refs_4_ = bf16[128,2048]{1,0:T(8,128)(2,1)} collective-permute-done((bf16[128,2048]{1,0:T(8,128)(2,1)}, bf16[128,2048]{1,0:T(8,128)(2,1)}, u32[]{:S(2)}, u32[]{:S(2)}) %collective-permute-start.26) | collective-permute-done | bytes 524320 | tf_op jit(solution)/shard_map/ppermute | solution.py:241
  120.0 1.5 collective-permute-start.27
  121.6 2.6 %copy-done.1 = bf16[1,2048,1408]{2,1,0:T(8,128)(2,1)S(1)} copy-done((bf16[1,2048,1408]{2,1,0:T(8,128)(2,1)S(1)}, bf16[1,2048,1408]{2,1,0:T(8,128)(2,1)}, u32[]{:S(2)}) %copy-start.1) | copy-done | bytes 5767192
  124.2 1.8 copy-done.2
  126.0 1.8 copy-done.6
  127.9 9.4 %experts.4 = (bf16[128,2048]{1,0:T(8,128)(2,1)S(1)}, bf16[128,2048]{1,0:T(8,128)(2,1)S(1)}, bf16[128,2048]{1,0:T(8,128)(2,1)S(1)}, bf16[128,2048]{1,0:T(8,128)(2,1)S(1)}) custom-call(s32[4,2,1,128]{3,2,1,0:T(1,128)S(1)} %bitcast.49, f32[4,2,1,128]{3,2,1,0:T(1,128)S(1)} %bitcast.50, bf16[128,2048]{1,0:T(8,128)(2,1)S(1)} %get-tuple-element.93.refs_2_, ...), custom_call_target="tpu_custom_call" | custom-call | flops 8858370048 | bytes 1048576 | tf_op jit(solution)/shard_map/experts/pallas_call | solution.py:164
  138.4 1.5 collective-permute-start.21
  139.9 1.8 copy-done.3
  141.7 1.8 copy-done.7
  143.6 9.3 %experts.5 = (bf16[128,2048]{1,0:T(8,128)(2,1)S(1)}, bf16[128,2048]{1,0:T(8,128)(2,1)S(1)}, bf16[128,2048]{1,0:T(8,128)(2,1)S(1)}, bf16[128,2048]{1,0:T(8,128)(2,1)S(1)}) custom-call(s32[4,2,1,128]{3,2,1,0:T(1,128)S(1)} %bitcast.47, f32[4,2,1,128]{3,2,1,0:T(1,128)S(1)} %bitcast.48, bf16[128,2048]{1,0:T(8,128)(2,1)S(1)} %collective-permute-done.17.refs_2_, ...), custom_call_target="tpu_custom_call" | custom-call | flops 8858370048 | bytes 1048576 | tf_op jit(solution)/shard_map/experts/pallas_call | solution.py:164
  153.4 1.5 collective-permute-start.40
  155.0 8.7 %collective-permute-done.21.refs_5_ = bf16[128,2048]{1,0:T(8,128)(2,1)S(1)} collective-permute-done((bf16[128,2048]{1,0:T(8,128)(2,1)S(1)}, bf16[128,2048]{1,0:T(8,128)(2,1)S(1)}, u32[]{:S(2)}, u32[]{:S(2)}) %collective-permute-start.21) | collective-permute-done | bytes 524320 | tf_op jit(solution)/shard_map/ppermute | solution.py:236
  163.7 9.3 %experts.6 = (bf16[128,2048]{1,0:T(8,128)(2,1)S(1)}, bf16[128,2048]{1,0:T(8,128)(2,1)S(1)}, bf16[128,2048]{1,0:T(8,128)(2,1)S(1)}, bf16[128,2048]{1,0:T(8,128)(2,1)S(1)}) custom-call(s32[4,2,1,128]{3,2,1,0:T(1,128)S(1)} %bitcast.45, f32[4,2,1,128]{3,2,1,0:T(1,128)S(1)} %bitcast.46, bf16[128,2048]{1,0:T(8,128)(2,1)} %collective-permute-done.19.refs_2_, ...), custom_call_target="tpu_custom_call" | custom-call | flops 8858370048 | bytes 1048576 | tf_op jit(solution)/shard_map/experts/pallas_call | solution.py:164
  173.0 1.9 collective-permute-done.29
  175.6 7.9 %experts.7 = (bf16[128,2048]{1,0:T(8,128)(2,1)S(1)}, bf16[128,2048]{1,0:T(8,128)(2,1)S(1)}, bf16[128,2048]{1,0:T(8,128)(2,1)S(1)}, bf16[128,2048]{1,0:T(8,128)(2,1)S(1)}) custom-call(s32[4,2,1,128]{3,2,1,0:T(1,128)S(1)} %bitcast.43, f32[4,2,1,128]{3,2,1,0:T(1,128)S(1)} %bitcast.44, bf16[128,2048]{1,0:T(8,128)(2,1)S(1)} %collective-permute-done.18.refs_2_, ...), custom_call_target="tpu_custom_call" | custom-call | flops 8858370048 | bytes 1048576 | tf_op jit(solution)/shard_map/experts/pallas_call | solution.py:164
  188.5 4.9 %collective-permute-done.22 = bf16[128,2048]{1,0:T(8,128)(2,1)S(1)} collective-permute-done((bf16[128,2048]{1,0:T(8,128)(2,1)S(1)}, bf16[128,2048]{1,0:T(8,128)(2,1)S(1)}, u32[]{:S(2)}, u32[]{:S(2)}) %collective-permute-start.22) | collective-permute-done | bytes 524320 | tf_op jit(solution)/shard_map/ppermute | solution.py:236
  194.2 4.2 %collective-permute-done.33 = bf16[128,2048]{1,0:T(8,128)(2,1)S(1)} collective-permute-done((bf16[128,2048]{1,0:T(8,128)(2,1)S(1)}, bf16[128,2048]{1,0:T(8,128)(2,1)S(1)}, u32[]{:S(2)}, u32[]{:S(2)}) %collective-permute-start.33) | collective-permute-done | bytes 524320 | tf_op jit(solution)/shard_map/ppermute | solution.py:236
  199.1 10.6 %collective-permute-done.37 = bf16[128,2048]{1,0:T(8,128)(2,1)S(1)} collective-permute-done((bf16[128,2048]{1,0:T(8,128)(2,1)S(1)}, bf16[128,2048]{1,0:T(8,128)(2,1)S(1)}, u32[]{:S(2)}, u32[]{:S(2)}) %collective-permute-start.37) | collective-permute-done | bytes 524320 | tf_op jit(solution)/shard_map/ppermute | solution.py:236
  209.7 1.9 collective-permute-start.34
  211.8 17.1 %collective-permute-done.42 = bf16[128,2048]{1,0:T(8,128)(2,1)S(1)} collective-permute-done((bf16[128,2048]{1,0:T(8,128)(2,1)S(1)}, bf16[128,2048]{1,0:T(8,128)(2,1)S(1)}, u32[]{:S(2)}, u32[]{:S(2)}) %collective-permute-start.42) | collective-permute-done | bytes 524320 | tf_op jit(solution)/shard_map/ppermute | solution.py:236
  230.4 1.7 collective-permute-start.43
  232.9 5.1 %collective-permute-done.38 = bf16[128,2048]{1,0:T(8,128)(2,1)S(1)} collective-permute-done((bf16[128,2048]{1,0:T(8,128)(2,1)S(1)}, bf16[128,2048]{1,0:T(8,128)(2,1)S(1)}, u32[]{:S(2)}, u32[]{:S(2)}) %collective-permute-start.38) | collective-permute-done | bytes 524320 | tf_op jit(solution)/shard_map/ppermute | solution.py:236
  238.3 1.8 collective-permute-start.39
  241.5 2.1 collective-permute-done.35
  243.6 11.4 %collective-permute-done.39 = bf16[128,2048]{1,0:T(8,128)(2,1)S(1)} collective-permute-done((bf16[128,2048]{1,0:T(8,128)(2,1)S(1)}, bf16[128,2048]{1,0:T(8,128)(2,1)S(1)}, u32[]{:S(2)}, u32[]{:S(2)}) %collective-permute-start.39) | collective-permute-done | bytes 524320 | tf_op jit(solution)/shard_map/ppermute | solution.py:241
  (107 shorter events, 33.5 us)
Async XLA Ops:
  2.5 21.1 %collective-permute-start = (bf16[2,32,2048]{2,1,0:T(8,128)(2,1)S(1)}, bf16[2,32,2048]{2,1,0:T(8,128)(2,1)S(1)}, u32[]{:S(2)}, u32[]{:S(2)}) collective-permute-start(bf16[2,32,2048]{2,1,0:T(8,128)(2,1)S(1)} %constant_dynamic-update-slice_fusion.refs_1_), channel_id=1, source_target_pairs={{0,2},{2,4},{4,6},{6,0},{1,3},{3,5},{5,7},{7,1},{8,10},{10,12},{12... | collective-permute-start | bytes 786440 | tf_op jit(solution)/shard_map/ppermute | solution.py:241
  5.5 18.0 %collective-permute-start.1 = (bf16[2,32,2048]{2,1,0:T(8,128)(2,1)S(1)}, bf16[2,32,2048]{2,1,0:T(8,128)(2,1)S(1)}, u32[]{:S(2)}, u32[]{:S(2)}) collective-permute-start(bf16[2,32,2048]{2,1,0:T(8,128)(2,1)S(1)} %constant_dynamic-update-slice_fusion.refs_1_), channel_id=1, source_target_pairs={{0,6},{2,0},{4,2},{6,4},{1,7},{3,1},{5,3},{7,5},{8,14},{10,8},{12,... | collective-permute-start | bytes 786440 | tf_op jit(solution)/shard_map/ppermute | solution.py:241
  7.6 16.0 %collective-permute-start.2 = (bf16[2,32,2048]{2,1,0:T(8,128)(2,1)S(1)}, bf16[2,32,2048]{2,1,0:T(8,128)(2,1)S(1)}, u32[]{:S(2)}, u32[]{:S(2)}) collective-permute-start(bf16[2,32,2048]{2,1,0:T(8,128)(2,1)S(1)} %constant_dynamic-update-slice_fusion.refs_1_), channel_id=1, source_target_pairs={{0,1},{1,0},{2,3},{3,2},{4,5},{5,4},{6,7},{7,6},{8,9},{9,8},{10,11... | collective-permute-start | bytes 786440 | tf_op jit(solution)/shard_map/ppermute | solution.py:236
  10.7 9.2 %collective-permute-start.3 = (f32[12,128]{1,0:T(8,128)S(1)}, f32[12,128]{1,0:T(8,128)S(1)}, u32[]{:S(2)}, u32[]{:S(2)}) collective-permute-start(f32[12,128]{1,0:T(8,128)S(1)} %pad_maximum_fusion.3), channel_id=1, source_target_pairs={{0,2},{2,4},{4,6},{6,0},{1,3},{3,5},{5,7},{7,1},{8,10},{10,12},{12... | collective-permute-start | bytes 18440 | tf_op jit(solution)/shard_map/ppermute | solution.py:241
  10.7 10.8 %collective-permute-start.4 = (f32[12,128]{1,0:T(8,128)S(1)}, f32[12,128]{1,0:T(8,128)S(1)}, u32[]{:S(2)}, u32[]{:S(2)}) collective-permute-start(f32[12,128]{1,0:T(8,128)S(1)} %pad_maximum_fusion.3), channel_id=1, source_target_pairs={{0,4},{2,6},{4,0},{6,2},{1,5},{3,7},{5,1},{7,3},{8,12},{10,14},{12... | collective-permute-start | bytes 18440 | tf_op jit(solution)/shard_map/ppermute | solution.py:241
  19.9 3.7 %collective-permute-start.5 = (f32[12,128]{1,0:T(8,128)S(1)}, f32[12,128]{1,0:T(8,128)S(1)}, u32[]{:S(2)}, u32[]{:S(2)}) collective-permute-start(f32[12,128]{1,0:T(8,128)S(1)} %pad_maximum_fusion.3), channel_id=1, source_target_pairs={{0,6},{2,0},{4,2},{6,4},{1,7},{3,1},{5,3},{7,5},{8,14},{10,8},{12,... | collective-permute-start | bytes 18440 | tf_op jit(solution)/shard_map/ppermute | solution.py:241
  23.6 41.3 %collective-permute-start.11 = (bf16[2048,1408]{1,0:T(8,128)(2,1)}, bf16[2048,1408]{1,0:T(8,128)(2,1)S(1)}, u32[]{:S(2)}, u32[]{:S(2)}) collective-permute-start(bf16[2048,1408]{1,0:T(8,128)(2,1)} %bitcast.51), channel_id=1, source_target_pairs={{0,8},{8,0},{1,9},{9,1},{2,10},{10,2},{3,11},{11,3},{4,12},{12,4},... | collective-permute-start | bytes 17301512 | tf_op jit(solution)/shard_map/ppermute | solution.py:236
  23.7 39.6 %collective-permute-start.12 = (bf16[704,2048]{1,0:T(8,128)(2,1)}, bf16[704,2048]{1,0:T(8,128)(2,1)S(1)}, u32[]{:S(2)}, u32[]{:S(2)}) collective-permute-start(bf16[704,2048]{1,0:T(8,128)(2,1)} %bitcast.58), channel_id=1, source_target_pairs={{0,8},{8,0},{1,9},{9,1},{2,10},{10,2},{3,11},{11,3},{4,12},{12,4},... | collective-permute-start | bytes 8650760 | tf_op jit(solution)/shard_map/ppermute | solution.py:236
  24.2 10.1 %collective-permute-start.6 = (bf16[2,32,2048]{2,1,0:T(8,128)(2,1)S(1)}, bf16[2,32,2048]{2,1,0:T(8,128)(2,1)S(1)}, u32[]{:S(2)}, u32[]{:S(2)}) collective-permute-start(bf16[2,32,2048]{2,1,0:T(8,128)(2,1)S(1)} %collective-permute-done.refs_2_), channel_id=1, source_target_pairs={{0,2},{2,4},{4,6},{6,0},{1,3},{3,5},{5,7},{7,1},{8,10},{10,12},{12... | collective-permute-start | bytes 786440 | tf_op jit(solution)/shard_map/ppermute | solution.py:241
  24.2 10.1 %collective-permute-start.7 = (bf16[2,32,2048]{2,1,0:T(8,128)(2,1)S(1)}, bf16[2,32,2048]{2,1,0:T(8,128)(2,1)S(1)}, u32[]{:S(2)}, u32[]{:S(2)}) collective-permute-start(bf16[2,32,2048]{2,1,0:T(8,128)(2,1)S(1)} %collective-permute-done.refs_2_), channel_id=1, source_target_pairs={{0,1},{1,0},{2,3},{3,2},{4,5},{5,4},{6,7},{7,6},{8,9},{9,8},{10,11... | collective-permute-start | bytes 786440 | tf_op jit(solution)/shard_map/ppermute | solution.py:236
  25.7 12.4 %collective-permute-start.8 = (bf16[2,32,2048]{2,1,0:T(8,128)(2,1)S(1)}, bf16[2,32,2048]{2,1,0:T(8,128)(2,1)S(1)}, u32[]{:S(2)}, u32[]{:S(2)}) collective-permute-start(bf16[2,32,2048]{2,1,0:T(8,128)(2,1)S(1)} %collective-permute-done.1.refs_3_), channel_id=1, source_target_pairs={{0,1},{1,0},{2,3},{3,2},{4,5},{5,4},{6,7},{7,6},{8,9},{9,8},{10,11... | collective-permute-start | bytes 786440 | tf_op jit(solution)/shard_map/ppermute | solution.py:236
  38.1 8.2 %collective-permute-start.10 = (bf16[2,32,2048]{2,1,0:T(8,128)(2,1)S(1)}, bf16[2,32,2048]{2,1,0:T(8,128)(2,1)S(1)}, u32[]{:S(2)}, u32[]{:S(2)}) collective-permute-start(bf16[2,32,2048]{2,1,0:T(8,128)(2,1)S(1)} %collective-permute-done.6.refs_4_), channel_id=1, source_target_pairs={{0,1},{1,0},{2,3},{3,2},{4,5},{5,4},{6,7},{7,6},{8,9},{9,8},{10,11... | collective-permute-start | bytes 786440 | tf_op jit(solution)/shard_map/ppermute | solution.py:236
  39.6 6.6 %collective-permute-start.9 = (f32[4,12,128]{2,1,0:T(8,128)S(1)}, f32[4,12,128]{2,1,0:T(8,128)S(1)}, u32[]{:S(2)}, u32[]{:S(2)}) collective-permute-start(f32[4,12,128]{2,1,0:T(8,128)S(1)} %get-tuple-element.149), channel_id=1, source_target_pairs={{0,1},{1,0},{2,3},{3,2},{4,5},{5,4},{6,7},{7,6},{8,9},{9,8},{10,11... | collective-permute-start | bytes 73736 | tf_op jit(solution)/shard_map/ppermute | solution.py:236
  46.3 17.0 %collective-permute-start.13 = (f32[2,4,12,128]{3,2,1,0:T(8,128)S(1)}, f32[2,4,12,128]{3,2,1,0:T(8,128)S(1)}, u32[]{:S(2)}, u32[]{:S(2)}) collective-permute-start(f32[2,4,12,128]{3,2,1,0:T(8,128)S(1)} %get-tuple-element.147), channel_id=1, source_target_pairs={{0,16},{16,0},{1,17},{17,1},{2,18},{18,2},{3,19},{19,3},{4,20},{20... | collective-permute-start | bytes 147464 | tf_op jit(solution)/shard_map/ppermute | solution.py:236
  56.1 83.9 %slice-start = ((s8[5767168]{0:T(1024)(128)(4,1)}), s8[1572864]{0:T(1024)(128)(4,1)S(1)}, s32[]{:S(2)}) async-start(s8[5767168]{0:T(1024)(128)(4,1)} %bitcast.53), calls=%async_computation | async-start | bytes 3145728
  64.9 12.0 %collective-permute-start.14 = (bf16[128,2048]{1,0:T(8,128)(2,1)S(1)}, bf16[128,2048]{1,0:T(8,128)(2,1)}, u32[]{:S(2)}, u32[]{:S(2)}) collective-permute-start(bf16[128,2048]{1,0:T(8,128)(2,1)S(1)} %get-tuple-element.93.refs_2_), channel_id=1, source_target_pairs={{0,1},{1,0},{2,3},{3,2},{4,5},{5,4},{6,7},{7,6},{8,9},{9,8},{10,11... | collective-permute-start | bytes 1572872 | tf_op jit(solution)/shard_map/ppermute | solution.py:236
  66.4 11.7 %collective-permute-start.15 = (bf16[128,2048]{1,0:T(8,128)(2,1)S(1)}, bf16[128,2048]{1,0:T(8,128)(2,1)}, u32[]{:S(2)}, u32[]{:S(2)}) collective-permute-start(bf16[128,2048]{1,0:T(8,128)(2,1)S(1)} %get-tuple-element.93.refs_2_), channel_id=1, source_target_pairs={{0,16},{16,0},{1,17},{17,1},{2,18},{18,2},{3,19},{19,3},{4,20},{20... | collective-permute-start | bytes 1572872 | tf_op jit(solution)/shard_map/ppermute | solution.py:236
  67.4 16.7 %collective-permute-start.17 = (bf16[128,2048]{1,0:T(8,128)(2,1)S(1)}, bf16[128,2048]{1,0:T(8,128)(2,1)S(1)}, u32[]{:S(2)}, u32[]{:S(2)}) collective-permute-start(bf16[128,2048]{1,0:T(8,128)(2,1)S(1)} %get-tuple-element.93.refs_2_), channel_id=1, source_target_pairs={{0,2},{2,4},{4,6},{6,0},{1,3},{3,5},{5,7},{7,1},{8,10},{10,12},{12... | collective-permute-start | bytes 1572872 | tf_op jit(solution)/shard_map/ppermute | solution.py:241
  68.1 23.9 %collective-permute-start.18 = (bf16[128,2048]{1,0:T(8,128)(2,1)S(1)}, bf16[128,2048]{1,0:T(8,128)(2,1)S(1)}, u32[]{:S(2)}, u32[]{:S(2)}) collective-permute-start(bf16[128,2048]{1,0:T(8,128)(2,1)S(1)} %get-tuple-element.93.refs_2_), channel_id=1, source_target_pairs={{0,6},{2,0},{4,2},{6,4},{1,7},{3,1},{5,3},{7,5},{8,14},{10,8},{12,... | collective-permute-start | bytes 1572872 | tf_op jit(solution)/shard_map/ppermute | solution.py:241
  92.0 16.9 %collective-permute-start.19 = (bf16[128,2048]{1,0:T(8,128)(2,1)S(1)}, bf16[128,2048]{1,0:T(8,128)(2,1)}, u32[]{:S(2)}, u32[]{:S(2)}) collective-permute-start(bf16[128,2048]{1,0:T(8,128)(2,1)S(1)} %collective-permute-done.17.refs_2_), channel_id=1, source_target_pairs={{0,2},{2,4},{4,6},{6,0},{1,3},{3,5},{5,7},{7,1},{8,10},{10,12},{12... | collective-permute-start | bytes 1572872 | tf_op jit(solution)/shard_map/ppermute | solution.py:241
  92.9 27.2 %collective-permute-start.26 = (bf16[128,2048]{1,0:T(8,128)(2,1)}, bf16[128,2048]{1,0:T(8,128)(2,1)}, u32[]{:S(2)}, u32[]{:S(2)}) collective-permute-start(bf16[128,2048]{1,0:T(8,128)(2,1)} %collective-permute-done.15.refs_4_), channel_id=1, source_target_pairs={{0,2},{2,4},{4,6},{6,0},{1,3},{3,5},{5,7},{7,1},{8,10},{10,12},{12... | collective-permute-start | bytes 1572872 | tf_op jit(solution)/shard_map/ppermute | solution.py:241
  94.0 15.4 %collective-permute-start.16 = (bf16[128,2048]{1,0:T(8,128)(2,1)}, bf16[128,2048]{1,0:T(8,128)(2,1)}, u32[]{:S(2)}, u32[]{:S(2)}) collective-permute-start(bf16[128,2048]{1,0:T(8,128)(2,1)} %collective-permute-done.14.refs_3_), channel_id=1, source_target_pairs={{0,16},{16,0},{1,17},{17,1},{2,18},{18,2},{3,19},{19,3},{4,20},{20... | collective-permute-start | bytes 1572872 | tf_op jit(solution)/shard_map/ppermute | solution.py:236
  95.0 44.9 %collective-permute-start.25 = (bf16[128,2048]{1,0:T(8,128)(2,1)S(1)}, bf16[128,2048]{1,0:T(8,128)(2,1)S(1)}, u32[]{:S(2)}, u32[]{:S(2)}) collective-permute-start(bf16[128,2048]{1,0:T(8,128)(2,1)S(1)} %collective-permute-done.17.refs_2_), channel_id=1, source_target_pairs={{0,1},{1,0},{2,3},{3,2},{4,5},{5,4},{6,7},{7,6},{8,9},{9,8},{10,11... | collective-permute-start | bytes 1572872 | tf_op jit(solution)/shard_map/ppermute | solution.py:236
  96.6 40.6 %collective-permute-start.23 = (bf16[128,2048]{1,0:T(8,128)(2,1)}, bf16[128,2048]{1,0:T(8,128)(2,1)S(1)}, u32[]{:S(2)}, u32[]{:S(2)}) collective-permute-start(bf16[128,2048]{1,0:T(8,128)(2,1)} %collective-permute-done.14.refs_3_), channel_id=1, source_target_pairs={{0,6},{2,0},{4,2},{6,4},{1,7},{3,1},{5,3},{7,5},{8,14},{10,8},{12,... | collective-permute-start | bytes 1572872 | tf_op jit(solution)/shard_map/ppermute | solution.py:241
  108.9 28.4 %collective-permute-start.24 = (bf16[128,2048]{1,0:T(8,128)(2,1)S(1)}, bf16[128,2048]{1,0:T(8,128)(2,1)S(1)}, u32[]{:S(2)}, u32[]{:S(2)}) collective-permute-start(bf16[128,2048]{1,0:T(8,128)(2,1)S(1)} %collective-permute-done.18.refs_2_), channel_id=1, source_target_pairs={{0,16},{16,0},{1,17},{17,1},{2,18},{18,2},{3,19},{19,3},{4,20},{20... | collective-permute-start | bytes 1572872 | tf_op jit(solution)/shard_map/ppermute | solution.py:236
  109.5 28.9 %collective-permute-start.20 = (bf16[128,2048]{1,0:T(8,128)(2,1)}, bf16[128,2048]{1,0:T(8,128)(2,1)S(1)}, u32[]{:S(2)}, u32[]{:S(2)}) collective-permute-start(bf16[128,2048]{1,0:T(8,128)(2,1)} %collective-permute-done.19.refs_2_), channel_id=1, source_target_pairs={{0,16},{16,0},{1,17},{17,1},{2,18},{18,2},{3,19},{19,3},{4,20},{20... | collective-permute-start | bytes 1572872 | tf_op jit(solution)/shard_map/ppermute | solution.py:236
  120.0 19.9 %collective-permute-start.27 = (bf16[128,2048]{1,0:T(8,128)(2,1)}, bf16[128,2048]{1,0:T(8,128)(2,1)S(1)}, u32[]{:S(2)}, u32[]{:S(2)}) collective-permute-start(bf16[128,2048]{1,0:T(8,128)(2,1)} %collective-permute-done.26.refs_4_), channel_id=1, source_target_pairs={{0,1},{1,0},{2,3},{3,2},{4,5},{5,4},{6,7},{7,6},{8,9},{9,8},{10,11... | collective-permute-start | bytes 1572872 | tf_op jit(solution)/shard_map/ppermute | solution.py:236
  127.8 12.1 %slice-start.1 = ((s8[5767168]{0:T(1024)(128)(4,1)}), s8[4194304]{0:T(1024)(128)(4,1)S(1)}, s32[]{:S(2)}) async-start(s8[5767168]{0:T(1024)(128)(4,1)} %bitcast.53), calls=%async_computation.1 | async-start | bytes 8388608
  137.3 26.4 %collective-permute-start.28 = (bf16[128,2048]{1,0:T(8,128)(2,1)}, bf16[128,2048]{1,0:T(8,128)(2,1)S(1)}, u32[]{:S(2)}, u32[]{:S(2)}) collective-permute-start(bf16[128,2048]{1,0:T(8,128)(2,1)} %collective-permute-done.19.refs_2_), channel_id=1, source_target_pairs={{0,1},{1,0},{2,3},{3,2},{4,5},{5,4},{6,7},{7,6},{8,9},{9,8},{10,11... | collective-permute-start | bytes 1572872 | tf_op jit(solution)/shard_map/ppermute | solution.py:236
  137.8 37.8 %collective-permute-start.32 = (bf16[128,2048]{1,0:T(8,128)(2,1)S(1)}, bf16[128,2048]{1,0:T(8,128)(2,1)S(1)}, u32[]{:S(2)}, u32[]{:S(2)}) collective-permute-start(bf16[128,2048]{1,0:T(8,128)(2,1)S(1)} %collective-permute-done.23.refs_3_), channel_id=1, source_target_pairs={{0,16},{16,0},{1,17},{17,1},{2,18},{18,2},{3,19},{19,3},{4,20},{20... | collective-permute-start | bytes 1572872 | tf_op jit(solution)/shard_map/ppermute | solution.py:236
  138.4 25.3 %collective-permute-start.21 = (bf16[128,2048]{1,0:T(8,128)(2,1)S(1)}, bf16[128,2048]{1,0:T(8,128)(2,1)S(1)}, u32[]{:S(2)}, u32[]{:S(2)}) collective-permute-start(bf16[128,2048]{1,0:T(8,128)(2,1)S(1)} %collective-permute-done.20.refs_4_), channel_id=1, source_target_pairs={{0,1},{1,0},{2,3},{3,2},{4,5},{5,4},{6,7},{7,6},{8,9},{9,8},{10,11... | collective-permute-start | bytes 1572872 | tf_op jit(solution)/shard_map/ppermute | solution.py:236
  143.6 20.1 %copy-start.8 = (bf16[704,2048]{1,0:T(8,128)(2,1)S(1)}, bf16[704,2048]{1,0:T(8,128)(2,1)}, u32[]{:S(2)}) copy-start(bf16[704,2048]{1,0:T(8,128)(2,1)} %copy-done.5) | copy-start | bytes 8650756
  152.9 22.0 %collective-permute-start.29 = (bf16[128,2048]{1,0:T(8,128)(2,1)S(1)}, bf16[128,2048]{1,0:T(8,128)(2,1)S(1)}, u32[]{:S(2)}, u32[]{:S(2)}) collective-permute-start(bf16[128,2048]{1,0:T(8,128)(2,1)S(1)} %get-tuple-element.125), channel_id=1, source_target_pairs={{0,1},{1,0},{2,3},{3,2},{4,5},{5,4},{6,7},{7,6},{8,9},{9,8},{10,11... | collective-permute-start | bytes 1572872 | tf_op jit(solution)/shard_map/ppermute | solution.py:236
  153.4 32.7 %collective-permute-start.40 = (bf16[128,2048]{1,0:T(8,128)(2,1)S(1)}, bf16[128,2048]{1,0:T(8,128)(2,1)S(1)}, u32[]{:S(2)}, u32[]{:S(2)}) collective-permute-start(bf16[128,2048]{1,0:T(8,128)(2,1)S(1)} %get-tuple-element.139), channel_id=1, source_target_pairs={{0,1},{1,0},{2,3},{3,2},{4,5},{5,4},{6,7},{7,6},{8,9},{9,8},{10,11... | collective-permute-start | bytes 1572872 | tf_op jit(solution)/shard_map/ppermute | solution.py:236
  163.7 12.0 %copy-start.4 = (bf16[1,704,2048]{2,1,0:T(8,128)(2,1)S(1)}, bf16[1,704,2048]{2,1,0:T(8,128)(2,1)}, u32[]{:S(2)}) copy-start(bf16[1,704,2048]{2,1,0:T(8,128)(2,1)} %param.23) | copy-start | bytes 8650756
  175.0 12.0 %collective-permute-start.30 = (bf16[128,2048]{1,0:T(8,128)(2,1)S(1)}, bf16[128,2048]{1,0:T(8,128)(2,1)S(1)}, u32[]{:S(2)}, u32[]{:S(2)}) collective-permute-start(bf16[128,2048]{1,0:T(8,128)(2,1)S(1)} %add_convert_fusion.8), channel_id=1, source_target_pairs={{0,6},{2,0},{4,2},{6,4},{1,7},{3,1},{5,3},{7,5},{8,14},{10,8},{12,... | collective-permute-start | bytes 1572872 | tf_op jit(solution)/shard_map/ppermute | solution.py:241
  175.1 18.3 %collective-permute-start.22 = (bf16[128,2048]{1,0:T(8,128)(2,1)S(1)}, bf16[128,2048]{1,0:T(8,128)(2,1)S(1)}, u32[]{:S(2)}, u32[]{:S(2)}) collective-permute-start(bf16[128,2048]{1,0:T(8,128)(2,1)S(1)} %get-tuple-element.107), channel_id=1, source_target_pairs={{0,1},{1,0},{2,3},{3,2},{4,5},{5,4},{6,7},{7,6},{8,9},{9,8},{10,11... | collective-permute-start | bytes 1572872 | tf_op jit(solution)/shard_map/ppermute | solution.py:236
  183.5 14.9 %collective-permute-start.33 = (bf16[128,2048]{1,0:T(8,128)(2,1)S(1)}, bf16[128,2048]{1,0:T(8,128)(2,1)S(1)}, u32[]{:S(2)}, u32[]{:S(2)}) collective-permute-start(bf16[128,2048]{1,0:T(8,128)(2,1)S(1)} %get-tuple-element.133), channel_id=1, source_target_pairs={{0,16},{16,0},{1,17},{17,1},{2,18},{18,2},{3,19},{19,3},{4,20},{20... | collective-permute-start | bytes 1572872 | tf_op jit(solution)/shard_map/ppermute | solution.py:236
  184.1 25.6 %collective-permute-start.37 = (bf16[128,2048]{1,0:T(8,128)(2,1)S(1)}, bf16[128,2048]{1,0:T(8,128)(2,1)S(1)}, u32[]{:S(2)}, u32[]{:S(2)}) collective-permute-start(bf16[128,2048]{1,0:T(8,128)(2,1)S(1)} %get-tuple-element.137), channel_id=1, source_target_pairs={{0,16},{16,0},{1,17},{17,1},{2,18},{18,2},{3,19},{19,3},{4,20},{20... | collective-permute-start | bytes 1572872 | tf_op jit(solution)/shard_map/ppermute | solution.py:236
  186.1 46.1 %collective-permute-start.36 = (bf16[128,2048]{1,0:T(8,128)(2,1)S(1)}, bf16[128,2048]{1,0:T(8,128)(2,1)S(1)}, u32[]{:S(2)}, u32[]{:S(2)}) collective-permute-start(bf16[128,2048]{1,0:T(8,128)(2,1)S(1)} %get-tuple-element.135), channel_id=1, source_target_pairs={{0,16},{16,0},{1,17},{17,1},{2,18},{18,2},{3,19},{19,3},{4,20},{20... | collective-permute-start | bytes 1572872 | tf_op jit(solution)/shard_map/ppermute | solution.py:236
  187.0 53.1 %collective-permute-start.41 = (bf16[128,2048]{1,0:T(8,128)(2,1)S(1)}, bf16[128,2048]{1,0:T(8,128)(2,1)S(1)}, u32[]{:S(2)}, u32[]{:S(2)}) collective-permute-start(bf16[128,2048]{1,0:T(8,128)(2,1)S(1)} %add_convert_fusion.2), channel_id=1, source_target_pairs={{0,6},{2,0},{4,2},{6,4},{1,7},{3,1},{5,3},{7,5},{8,14},{10,8},{12,... | collective-permute-start | bytes 1572872 | tf_op jit(solution)/shard_map/ppermute | solution.py:241
  193.4 35.4 %collective-permute-start.42 = (bf16[128,2048]{1,0:T(8,128)(2,1)S(1)}, bf16[128,2048]{1,0:T(8,128)(2,1)S(1)}, u32[]{:S(2)}, u32[]{:S(2)}) collective-permute-start(bf16[128,2048]{1,0:T(8,128)(2,1)S(1)} %get-tuple-element.141), channel_id=1, source_target_pairs={{0,16},{16,0},{1,17},{17,1},{2,18},{18,2},{3,19},{19,3},{4,20},{20... | collective-permute-start | bytes 1572872 | tf_op jit(solution)/shard_map/ppermute | solution.py:236
  198.5 41.6 %collective-permute-start.31 = (bf16[128,2048]{1,0:T(8,128)(2,1)S(1)}, bf16[128,2048]{1,0:T(8,128)(2,1)S(1)}, u32[]{:S(2)}, u32[]{:S(2)}) collective-permute-start(bf16[128,2048]{1,0:T(8,128)(2,1)S(1)} %add_convert_fusion.7), channel_id=1, source_target_pairs={{0,16},{16,0},{1,17},{17,1},{2,18},{18,2},{3,19},{19,3},{4,20},{20... | collective-permute-start | bytes 1572872 | tf_op jit(solution)/shard_map/ppermute | solution.py:236
  209.7 20.7 %collective-permute-start.34 = (bf16[128,2048]{1,0:T(8,128)(2,1)S(1)}, bf16[128,2048]{1,0:T(8,128)(2,1)S(1)}, u32[]{:S(2)}, u32[]{:S(2)}) collective-permute-start(bf16[128,2048]{1,0:T(8,128)(2,1)S(1)} %add_convert_fusion.6), channel_id=1, source_target_pairs={{0,2},{2,4},{4,6},{6,0},{1,3},{3,5},{5,7},{7,1},{8,10},{10,12},{12... | collective-permute-start | bytes 1572872 | tf_op jit(solution)/shard_map/ppermute | solution.py:241
  228.8 9.2 %collective-permute-start.38 = (bf16[128,2048]{1,0:T(8,128)(2,1)S(1)}, bf16[128,2048]{1,0:T(8,128)(2,1)S(1)}, u32[]{:S(2)}, u32[]{:S(2)}) collective-permute-start(bf16[128,2048]{1,0:T(8,128)(2,1)S(1)} %add_convert_fusion.4), channel_id=1, source_target_pairs={{0,1},{1,0},{2,3},{3,2},{4,5},{5,4},{6,7},{7,6},{8,9},{9,8},{10,11... | collective-permute-start | bytes 1572872 | tf_op jit(solution)/shard_map/ppermute | solution.py:236
  230.4 11.1 %collective-permute-start.43 = (bf16[128,2048]{1,0:T(8,128)(2,1)S(1)}, bf16[128,2048]{1,0:T(8,128)(2,1)S(1)}, u32[]{:S(2)}, u32[]{:S(2)}) collective-permute-start(bf16[128,2048]{1,0:T(8,128)(2,1)S(1)} %add_convert_fusion.1), channel_id=1, source_target_pairs={{0,2},{2,4},{4,6},{6,0},{1,3},{3,5},{5,7},{7,1},{8,10},{10,12},{12... | collective-permute-start | bytes 1572872 | tf_op jit(solution)/shard_map/ppermute | solution.py:241
  232.3 11.4 %collective-permute-start.35 = (bf16[128,2048]{1,0:T(8,128)(2,1)S(1)}, bf16[128,2048]{1,0:T(8,128)(2,1)S(1)}, u32[]{:S(2)}, u32[]{:S(2)}) collective-permute-start(bf16[128,2048]{1,0:T(8,128)(2,1)S(1)} %add_convert_fusion.5), channel_id=1, source_target_pairs={{0,1},{1,0},{2,3},{3,2},{4,5},{5,4},{6,7},{7,6},{8,9},{9,8},{10,11... | collective-permute-start | bytes 1572872 | tf_op jit(solution)/shard_map/ppermute | solution.py:236
  238.3 16.8 %collective-permute-start.39 = (bf16[128,2048]{1,0:T(8,128)(2,1)S(1)}, bf16[128,2048]{1,0:T(8,128)(2,1)S(1)}, u32[]{:S(2)}, u32[]{:S(2)}) collective-permute-start(bf16[128,2048]{1,0:T(8,128)(2,1)S(1)} %add_convert_fusion.3), channel_id=1, source_target_pairs={{0,4},{2,6},{4,0},{6,2},{1,5},{3,7},{5,1},{7,3},{8,12},{10,14},{12... | collective-permute-start | bytes 1572872 | tf_op jit(solution)/shard_map/ppermute | solution.py:241
  (13 other events, 22.3 us)

commit v8 on v7

--- a/solution.py
+++ b/solution.py
@@ -13,8 +13,8 @@
 TOP = 6
 ALL = ("far", "core", "line", "side")
 GATHER_BUDGET = 40 * 2**20
-ATTEND_VMEM = 24 * 2**20
-EXPERT_VMEM = 36 * 2**20
+ATTEND_VMEM = 52 * 2**20
+EXPERT_VMEM = 40 * 2**20
 
 
 def attend_kernel(count, gain_ref, *refs):
@@ -110,20 +110,25 @@
     rows_refs, refs = refs[:count], refs[count:]
     weight_refs, refs = refs[:4], refs[4:]
     out_refs, refs = refs[:count], refs[count:]
-    picked, scaled, held, arrived = refs[0], refs[1], refs[2:6], refs[6]
+    picked, scaled, held, landed, arrived = refs[0], refs[1], refs[2:6], refs[6], refs[7]
+    loads = [
+        pltpu.make_async_copy(rows_refs[i], landed.at[i], arrived.at[4 + i])
+        for i in range(count)
+    ]
     copies = [
         pltpu.make_async_copy(source, target, arrived.at[i])
         for i, (source, target) in enumerate(zip(weight_refs, held))
     ]
-    for copy in copies:
+    for copy in loads + copies:
         copy.start()
-    rows = rows_refs[0].shape[0]
+    rows = landed.shape[1]
     hidden = held[1].shape[0]
     levels = lax.broadcasted_iota(jnp.int32, (2 * capacity, rows), 0)
     for one in range(count):
         chosen = (levels == slot_ref[one, 0]) | (levels == slot_ref[one, 1])
+        loads[one].wait()
         taken = jnp.dot(
-            chosen.astype(jnp.bfloat16), rows_refs[one][...], preferred_element_type=jnp.float32
+            chosen.astype(jnp.bfloat16), landed[one], preferred_element_type=jnp.float32
         ).astype(jnp.bfloat16)
         picked[0, one * capacity : (one + 1) * capacity, :] = taken[:capacity]
         picked[1, one * capacity : (one + 1) * capacity, :] = taken[capacity:]
@@ -163,7 +168,7 @@
     local = pl.BlockSpec(memory_space=pltpu.VMEM)
     return pl.pallas_call(
         lambda *refs: experts_kernel(capacity, count, *refs),
-        in_specs=[local] * (2 + count) + [pl.BlockSpec(memory_space=pltpu.HBM)] * 4,
+        in_specs=[local] * 2 + [pl.BlockSpec(memory_space=pltpu.HBM)] * (count + 4),
         out_specs=[local] * count,
         out_shape=[jax.ShapeDtypeStruct((rows, width), jnp.bfloat16)] * count,
         scratch_shapes=[
@@ -171,7 +176,10 @@
             pltpu.VMEM((count, 2 * capacity, width), jnp.bfloat16),
         ]
         + [pltpu.VMEM(one.shape, jnp.bfloat16) for one in weights]
-        + [pltpu.SemaphoreType.DMA((4,))],
+        + [
+            pltpu.VMEM((count, rows, width), jnp.bfloat16),
+            pltpu.SemaphoreType.DMA((4 + count,)),
+        ],
         compiler_params=pltpu.CompilerParams(vmem_limit_bytes=EXPERT_VMEM),
         cost_estimate=pl.CostEstimate(
             flops=total * width * hidden * 12,
@@ -272,10 +280,8 @@
             held[back] = shift(held[(back - step) % len(order)], "line", step)
         for back in ready:
             swapped[back] = swap(held[back], "side")
-        if i == 1:
-            tables = [table] + [shift(table, "line", back) for back in range(1, len(order))]
-        moved, crossed, tables, weights = lax.optimization_barrier(
-            ([held[back] for back in fresh], [swapped[back] for back in ready], tables, weights)
+        moved, crossed, table, weights = lax.optimization_barrier(
+            ([held[back] for back in fresh], [swapped[back] for back in ready], table, weights)
         )
         if i == 1:
             others = [swap(one, "core") for one in weights]
@@ -284,13 +290,10 @@
         ready = fresh
     for back in ready:
         swapped[back] = swap(held[back], "side")
-    table = jnp.stack(tables)
-    beside, crossed = lax.optimization_barrier(
-        (swap(table, "side"), [swapped[back] for back in ready])
-    )
+    tables = [table] + [shift(table, "line", back) for back in range(1, len(order))]
+    tables, crossed = lax.optimization_barrier((tables, [swapped[back] for back in ready]))
     swapped.update(zip(ready, crossed))
-    table = jnp.stack([table, beside])
-    return list(held.values()) + list(swapped.values()), table, others
+    return list(held.values()) + list(swapped.values()), jnp.stack(tables), others
 
 
 def relative_slots(table, capacity):
@@ -307,70 +310,42 @@
     return slots, gates
 
 
-def spread(normed):
-    columns = lax.axis_size("line")
-    beside, across = swap(normed, "side"), swap(normed, "far")
-    up, down = shift(normed, "line", 1), shift(normed, "line", -1)
-    planes = {0: [normed, beside, across, swap(beside, "far")]}
-    up, down, beside, across = lax.optimization_barrier((up, down, beside, across))
-    lines = {1: up, columns - 1: down}
-    for back in nearest_first()[3:]:
-        step = 1 if back <= columns // 2 else -1
-        lines[back] = shift(lines[back - step], "line", step)
-        far_block = swap(lines[back], "far")
-        planes[back] = [
-            lines[back],
-            swap(lines[back], "side"),
-            far_block,
-            swap(far_block, "side"),
-        ]
-    across_up, beside_down = shift(across, "line", 1), shift(beside, "line", -1)
-    planes[1] = [up, swap(up, "side"), across_up, swap(across_up, "side")]
-    planes[columns - 1] = [down, beside_down, swap(down, "far"), swap(beside_down, "far")]
-    return planes
+def over_plane(block, axes):
+    first = swap(block, axes[0])
+    second = swap(block, axes[1])
+    corner = swap(first, axes[1])
+    if axes[0] == "side":
+        return [block, first, second, corner]
+    return [block, second, first, corner]
 
 
 def gather_plan(normed, slots, gates, weights, capacity):
-    columns = lax.axis_size("line")
-    distant = nearest_first()[3:]
-    order = [0, 1] + distant + [columns - 1]
-    planes = spread(normed)
-    results, corner_up, previous = {}, None, None
+    order = nearest_first()
+    blocks = along_line(normed)
+    axes = [("side", "far") if i % 2 == 0 else ("far", "side") for i in range(len(order))]
+    results, corner = [], None
+    for i in range(0, len(order), 2):
+        group = order[i : i + 2]
+        planes = []
+        for j, back in enumerate(group):
+            planes = planes + over_plane(blocks[back], axes[i + j])
+        mine = jnp.concatenate([slots[:, back] for back in group])
+        share = jnp.concatenate([gates[:, back] for back in group])
+        if i == 2:
+            corner = swap(results[1][3], axes[1][0])
+        if i > 0:
+            mine, corner, results[-1] = lax.optimization_barrier((mine, corner, results[-1]))
+        outputs = run_experts(planes, mine, share, weights, capacity)
+        for j in range(len(group)):
+            results.append(list(outputs[4 * j : 4 * j + 4]))
+    parts = []
     for i, back in enumerate(order):
-        mine = slots[:, back]
-        if i > 0:
-            mine, previous = lax.optimization_barrier((mine, previous))
-            results[order[i - 1]] = previous
-        if back == 1:
-            mine, planes[columns - 1][:3] = lax.optimization_barrier(
-                (mine, planes[columns - 1][:3])
-            )
-        if i == 2:
-            corner_up = swap(results[1][3], "side")
-            results[0], planes[back][3] = lax.optimization_barrier(
-                (results[0], planes[back][3])
-            )
-        if i == 3:
-            mine, corner_up = lax.optimization_barrier((mine, corner_up))
-        previous = run_experts(planes[back], mine, gates[:, back], weights, capacity)
-    results[order[-1]] = previous
-    parts = []
-    for back in distant:
-        here, beside, across, corner = results[back]
-        side_sum = add(beside, swap(corner, "far"))
-        total = add(here, swap(across, "far"), swap(side_sum, "side"))
-        parts.append(shift(total, "line", -back))
-    here, beside, across, corner = results[1]
-    up = add(here, swap(beside, "side"))
-    across_up = add(across, corner_up)
-    here, beside, across, corner = results[columns - 1]
-    beside_down = add(beside, swap(corner, "far"))
-    down = add(here, swap(across, "far"))
-    here, beside, across, corner = results[0]
-    across = add(across, swap(corner, "side"), shift(across_up, "line", -1))
-    beside = add(beside, shift(beside_down, "line", 1))
-    parts = parts + [shift(up, "line", -1), shift(down, "line", 1)]
-    return add(here, swap(across, "far"), swap(beside, "side"), *parts)
+        here, beside, across, last = results[i]
+        near, rest = (beside, across) if axes[i][0] == "side" else (across, beside)
+        moved = corner if i == 1 else swap(last, axes[i][0])
+        total = add(here, swap(near, axes[i][0]), swap(add(rest, moved), axes[i][1]))
+        parts.append(shift(total, "line", -back) if back else total)
+    return add(*parts)
 
 
 def on_device(
@@ -391,22 +366,22 @@
     devices = lax.axis_size(ALL)
     experts = devices // 2
     capacity = 4 * rows_here * TOP // (3 * experts)
-    gather_fits = (
-        devices * rows_here * width * 2 <= GATHER_BUDGET and lax.axis_size("line") > 2
-    )
+    gather_fits = devices * rows_here * width * 2 <= GATHER_BUDGET
     kv = jnp.concatenate([prefix_keys, prefix_values])
     weights = [gate_up_weight[0], down_weight[0]]
     if gather_fits:
         table = jnp.concatenate([routes.T.astype(jnp.float32), route_weights.T])
         pieces, table, others = prefix_pieces(kv, table, weights)
-        across = swap(table, "far")
+        beside = swap(table, "side")
     else:
         pieces = [lax.all_gather(kv, ("line", "side"), axis=1, tiled=True)]
     attended, normed = attend(
         queries, suffix_keys, suffix_values, pieces, tokens, out_weight, norm_gain
     )
     if gather_fits:
-        normed, others, across = lax.optimization_barrier((normed, others, across))
+        normed, others, beside = lax.optimization_barrier((normed, others, beside))
+        table = jnp.stack([table, beside])
+        across = swap(table, "far")
         slots, gates = relative_slots(jnp.stack([table, across]), capacity)
         routed = gather_plan(normed, slots, gates, weights + others, capacity)
     else:

time: 257 us -> 232 us (0.903)
  local copies, waits for them, and re-layouts: 22.1 us -> 7.16 us
  waiting for transfers between devices: 135 us -> 131 us
  starting transfers between devices: 51.2 us -> 47.7 us
  Pallas kernels: 43.1 us -> 39.8 us
    unnamed x35 -> x13, local copies, waits for them, and re-layouts: 21.1 us -> 6.2 us
    ppermute x16 -> x12, waiting for transfers between devices: 62.8 us -> 54.7 us  [shift(): lax.ppermute(array, axis, [(i, (i + amount) % size) for i in range(size)])]
    ppermute x16 -> x12, starting transfers between devices: 24.6 us -> 16.9 us  [shift(): lax.ppermute(array, axis, [(i, (i + amount) % size) for i in range(size)])]
    pallas_call x4 -> x2, Pallas kernels: 35.9 us -> 30.7 us  [run_experts(): pl.pallas_call(lambda *refs: experts_kernel(capacity, count, *refs), in_s...]
    ppermute x28 -> x32, waiting for transfers between devices: 71.8 us -> 76.4 us  [swap(): return lax.ppermute(array, axis, [(0, 1), (1, 0)])]
    ppermute x28 -> x32, starting transfers between devices: 26.7 us -> 30.8 us  [swap(): return lax.ppermute(array, axis, [(0, 1), (1, 0)])]
  transfers between devices with their start and end apart: 44 -> 44, of which waited for: 23 -> 24; matrix products, arithmetic and copies ran while one was open for 1% -> 2% of each run, Pallas kernels for 17% -> 17%
where the time goes in v8:
time: 232 us
  waiting for transfers between devices  131 us (56%)
  starting transfers between devices  47.7 us (21%)
  Pallas kernels  39.8 us (17%)
  local copies, waits for them, and re-layouts  7.16 us (3%)
  other arithmetic  4.96 us (2%)
    ppermute x32, waiting for transfers between devices, swap(): return lax.ppermute(array, axis, [(0, 1), (1, 0)])  76.4 us
    ppermute x12, waiting for transfers between devices, shift(): lax.ppermute(array, axis, [(i, (i + amount) % size) for i in range(size)])  54.7 us
    ppermute x32, starting transfers between devices, swap(): return lax.ppermute(array, axis, [(0, 1), (1, 0)])  30.8 us
    pallas_call x2, Pallas kernels, run_experts(): pl.pallas_call(lambda *refs: experts_kernel(capacity, count, *refs), in_s...  30.7 us
    ppermute x12, starting transfers between devices, shift(): lax.ppermute(array, axis, [(i, (i + amount) % size) for i in range(size)])  16.9 us
    pallas_call x1, Pallas kernels, attend(): pl.pallas_call(lambda *refs: attend_kernel(len(pieces), *refs), in_specs=...  9.09 us
    unnamed x13, local copies, waits for them, and re-layouts  6.2 us
  transfers between devices with their start and end apart: 44, of which 24 were waited for; matrix products, arithmetic and copies ran while one was open for 2% of the time, Pallas kernels for 17%

profile of v8, /device:TPU:0, one launch (start us, length us, event | category | flops | bytes accessed | tf_op | source)
XLA Modules:
  0.0 231.9 jit_solution(2666323837835891203)
XLA Ops:
  2.5 3.1 %collective-permute-start = (bf16[2,32,2048]{2,1,0:T(8,128)(2,1)S(1)}, bf16[2,32,2048]{2,1,0:T(8,128)(2,1)S(1)}, u32[]{:S(2)}, u32[]{:S(2)}) collective-permute-start(bf16[2,32,2048]{2,1,0:T(8,128)(2,1)S(1)} %constant_dynamic-update-slice_fusion.refs_1_), channel_id=1, source_target_pairs={{0,2},{2,4},{4,6},{6,0},{1,3},{3,5},{5,7},{7,1},{8,10},{10,12},{12... | collective-permute-start | bytes 786440 | tf_op jit(solution)/shard_map/ppermute | solution.py:249
  5.5 2.1 collective-permute-start.1
  7.6 1.7 collective-permute-start.2
  10.7 4.1 %collective-permute-done.refs_2_ = bf16[2,32,2048]{2,1,0:T(8,128)(2,1)S(1)} collective-permute-done((bf16[2,32,2048]{2,1,0:T(8,128)(2,1)S(1)}, bf16[2,32,2048]{2,1,0:T(8,128)(2,1)S(1)}, u32[]{:S(2)}, u32[]{:S(2)}) %collective-permute-start) | collective-permute-done | bytes 262176 | tf_op jit(solution)/shard_map/ppermute | solution.py:249
  14.7 4.2 %collective-permute-done.1.refs_3_ = bf16[2,32,2048]{2,1,0:T(8,128)(2,1)S(1)} collective-permute-done((bf16[2,32,2048]{2,1,0:T(8,128)(2,1)S(1)}, bf16[2,32,2048]{2,1,0:T(8,128)(2,1)S(1)}, u32[]{:S(2)}, u32[]{:S(2)}) %collective-permute-start.1) | collective-permute-done | bytes 262176 | tf_op jit(solution)/shard_map/ppermute | solution.py:249
  19.4 1.1 collective-permute-start.3
  20.6 1.5 collective-permute-start.4
  22.6 6.9 %collective-permute-done.3.refs_4_ = bf16[2,32,2048]{2,1,0:T(8,128)(2,1)S(1)} collective-permute-done((bf16[2,32,2048]{2,1,0:T(8,128)(2,1)S(1)}, bf16[2,32,2048]{2,1,0:T(8,128)(2,1)S(1)}, u32[]{:S(2)}, u32[]{:S(2)}) %collective-permute-start.3) | collective-permute-done | bytes 262176 | tf_op jit(solution)/shard_map/ppermute | solution.py:249
  29.8 4.4 %collective-permute-done.5.refs_7_ = bf16[2,32,2048]{2,1,0:T(8,128)(2,1)S(1)} collective-permute-done((bf16[2,32,2048]{2,1,0:T(8,128)(2,1)S(1)}, bf16[2,32,2048]{2,1,0:T(8,128)(2,1)S(1)}, u32[]{:S(2)}, u32[]{:S(2)}) %collective-permute-start.5) | collective-permute-done | bytes 262176 | tf_op jit(solution)/shard_map/ppermute | solution.py:244
  34.1 1.5 collective-permute-start.9
  36.4 2.5 %collective-permute-start.7 = (f32[12,128]{1,0:T(8,128)S(1)}, f32[12,128]{1,0:T(8,128)S(1)}, u32[]{:S(2)}, u32[]{:S(2)}) collective-permute-start(f32[12,128]{1,0:T(8,128)S(1)} %pad_maximum_fusion.3), channel_id=1, source_target_pairs={{0,4},{2,6},{4,0},{6,2},{1,5},{3,7},{5,1},{7,3},{8,12},{10,14},{12... | collective-permute-start | bytes 18440 | tf_op jit(solution)/shard_map/ppermute | solution.py:249
  38.9 2.2 collective-permute-done.6
  42.0 2.8 %collective-permute-done.8 = f32[12,128]{1,0:T(8,128)S(1)} collective-permute-done((f32[12,128]{1,0:T(8,128)S(1)}, f32[12,128]{1,0:T(8,128)S(1)}, u32[]{:S(2)}, u32[]{:S(2)}) %collective-permute-start.8) | collective-permute-done | bytes 6176 | tf_op jit(solution)/shard_map/ppermute | solution.py:249
  46.2 9.1 %attend_project_norm.1 = (bf16[128,2048]{1,0:T(8,128)(2,1)}, bf16[128,2048]{1,0:T(8,128)(2,1)}) custom-call(f32[1,2048]{1,0:T(1,128)S(1)} %bitcast.46, bf16[2,32,2048]{2,1,0:T(8,128)(2,1)S(1)} %constant_dynamic-update-slice_fusion.refs_1_, bf16[2,32,2048]{2,1,0:T(8,128)(2,1)S(1)} %collective-permute-done.refs_2_, ...), custom_call_target="tpu_custom_call" | custom-call | flops 6442450944 | bytes 1048576 | tf_op jit(solution)/shard_map/attend_project_norm/pallas_call | solution.py:90
  55.3 1.6 copy-done.1
  56.9 1.6 collective-permute-start.13
  58.5 1.4 collective-permute-start.14
  60.4 3.8 %collective-permute-start.28 = (bf16[128,2048]{1,0:T(8,128)(2,1)}, bf16[128,2048]{1,0:T(8,128)(2,1)S(1)}, u32[]{:S(2)}, u32[]{:S(2)}) collective-permute-start(bf16[128,2048]{1,0:T(8,128)(2,1)} %get-tuple-element.62.refs_2_), channel_id=1, source_target_pairs={{0,6},{2,0},{4,2},{6,4},{1,7},{3,1},{5,3},{7,5},{8,14},{10,8},{12,... | collective-permute-start | bytes 1572872 | tf_op jit(solution)/shard_map/ppermute | solution.py:249
  64.2 9.6 %collective-permute-done.17.refs_6_ = bf16[128,2048]{1,0:T(8,128)(2,1)} collective-permute-done((bf16[128,2048]{1,0:T(8,128)(2,1)}, bf16[128,2048]{1,0:T(8,128)(2,1)}, u32[]{:S(2)}, u32[]{:S(2)}) %collective-permute-start.17) | collective-permute-done | bytes 524320 | tf_op jit(solution)/shard_map/ppermute | solution.py:249
  73.9 1.5 collective-permute-start.19
  76.5 1.4 collective-permute-start.18
  78.5 8.8 %collective-permute-done.19.refs_8_ = bf16[128,2048]{1,0:T(8,128)(2,1)} collective-permute-done((bf16[128,2048]{1,0:T(8,128)(2,1)}, bf16[128,2048]{1,0:T(8,128)(2,1)}, u32[]{:S(2)}, u32[]{:S(2)}) %collective-permute-start.19) | collective-permute-done | bytes 524320 | tf_op jit(solution)/shard_map/ppermute | solution.py:244
  88.5 1.2 collective-permute-start.29
  89.7 2.8 %collective-permute-done.32.refs_6_ = bf16[128,2048]{1,0:T(8,128)(2,1)S(1)} collective-permute-done((bf16[128,2048]{1,0:T(8,128)(2,1)}, bf16[128,2048]{1,0:T(8,128)(2,1)S(1)}, u32[]{:S(2)}, u32[]{:S(2)}) %collective-permute-start.32) | collective-permute-done | bytes 524320 | tf_op jit(solution)/shard_map/ppermute | solution.py:249
  93.3 2.9 %collective-permute-done.16.refs_5_ = bf16[128,2048]{1,0:T(8,128)(2,1)S(1)} collective-permute-done((bf16[128,2048]{1,0:T(8,128)(2,1)}, bf16[128,2048]{1,0:T(8,128)(2,1)S(1)}, u32[]{:S(2)}, u32[]{:S(2)}) %collective-permute-start.16) | collective-permute-done | bytes 524320 | tf_op jit(solution)/shard_map/ppermute | solution.py:244
  96.2 5.1 %collective-permute-done.20.refs_9_ = bf16[128,2048]{1,0:T(8,128)(2,1)S(1)} collective-permute-done((bf16[128,2048]{1,0:T(8,128)(2,1)}, bf16[128,2048]{1,0:T(8,128)(2,1)S(1)}, u32[]{:S(2)}, u32[]{:S(2)}) %collective-permute-start.20) | collective-permute-done | bytes 524320 | tf_op jit(solution)/shard_map/ppermute | solution.py:244
  101.4 1.8 copy-done.2
  104.2 15.4 %experts.2 = (bf16[128,2048]{1,0:T(8,128)(2,1)S(1)}, bf16[128,2048]{1,0:T(8,128)(2,1)S(1)}, bf16[128,2048]{1,0:T(8,128)(2,1)S(1)}, bf16[128,2048]{1,0:T(8,128)(2...) custom-call(s32[8,2,1,128]{3,2,1,0:T(1,128)S(1)} %bitcast.42, ...), custom_call_target="tpu_custom_call" | custom-call | flops 17716740096 | bytes 2097152 | tf_op jit(solution)/shard_map/experts/pallas_call | solution.py:169
  120.2 1.5 collective-permute-start.30
  123.2 1.1 collective-permute-start.35
  124.3 7.9 %collective-permute-done.24 = bf16[128,2048]{1,0:T(8,128)(2,1)S(1)} collective-permute-done((bf16[128,2048]{1,0:T(8,128)(2,1)S(1)}, bf16[128,2048]{1,0:T(8,128)(2,1)S(1)}, u32[]{:S(2)}, u32[]{:S(2)}) %collective-permute-start.24) | collective-permute-done | bytes 524320 | tf_op jit(solution)/shard_map/ppermute | solution.py:244
  133.0 4.8 %collective-permute-done.30.refs_4_ = bf16[128,2048]{1,0:T(8,128)(2,1)S(1)} collective-permute-done((bf16[128,2048]{1,0:T(8,128)(2,1)S(1)}, bf16[128,2048]{1,0:T(8,128)(2,1)S(1)}, u32[]{:S(2)}, u32[]{:S(2)}) %collective-permute-start.30) | collective-permute-done | bytes 524320 | tf_op jit(solution)/shard_map/ppermute | solution.py:244
  138.6 4.8 %collective-permute-done.31.refs_5_ = bf16[128,2048]{1,0:T(8,128)(2,1)S(1)} collective-permute-done((bf16[128,2048]{1,0:T(8,128)(2,1)S(1)}, bf16[128,2048]{1,0:T(8,128)(2,1)S(1)}, u32[]{:S(2)}, u32[]{:S(2)}) %collective-permute-start.31) | collective-permute-done | bytes 524320 | tf_op jit(solution)/shard_map/ppermute | solution.py:244
  143.4 1.5 collective-permute-done.35.refs_9_
  144.9 15.3 %experts.3 = (bf16[128,2048]{1,0:T(8,128)(2,1)S(1)}, bf16[128,2048]{1,0:T(8,128)(2,1)S(1)}, bf16[128,2048]{1,0:T(8,128)(2,1)S(1)}, bf16[128,2048]{1,0:T(8,128)(2...) custom-call(s32[8,2,1,128]{3,2,1,0:T(1,128)S(1)} %pad_add_fusion.1.r, ...), custom_call_target="tpu_custom_call" | custom-call | flops 17716740096 | bytes 2097152 | tf_op jit(solution)/shard_map/experts/pallas_call | solution.py:169
  161.2 1.3 collective-permute-start.26
  163.0 1.5 collective-permute-start.41
  164.6 10.9 %collective-permute-done.37 = bf16[128,2048]{1,0:T(8,128)(2,1)S(1)} collective-permute-done((bf16[128,2048]{1,0:T(8,128)(2,1)S(1)}, bf16[128,2048]{1,0:T(8,128)(2,1)S(1)}, u32[]{:S(2)}, u32[]{:S(2)}) %collective-permute-start.37) | collective-permute-done | bytes 524320 | tf_op jit(solution)/shard_map/ppermute | solution.py:244
  176.5 11.0 %collective-permute-done.41 = bf16[128,2048]{1,0:T(8,128)(2,1)S(1)} collective-permute-done((bf16[128,2048]{1,0:T(8,128)(2,1)S(1)}, bf16[128,2048]{1,0:T(8,128)(2,1)S(1)}, u32[]{:S(2)}, u32[]{:S(2)}) %collective-permute-start.41) | collective-permute-done | bytes 524320 | tf_op jit(solution)/shard_map/ppermute | solution.py:244
  188.2 1.6 collective-permute-start.40
  190.7 4.8 %collective-permute-done.36 = bf16[128,2048]{1,0:T(8,128)(2,1)S(1)} collective-permute-done((bf16[128,2048]{1,0:T(8,128)(2,1)S(1)}, bf16[128,2048]{1,0:T(8,128)(2,1)S(1)}, u32[]{:S(2)}, u32[]{:S(2)}) %collective-permute-start.36) | collective-permute-done | bytes 524320 | tf_op jit(solution)/shard_map/ppermute | solution.py:244
  196.0 1.2 collective-permute-done.38
  197.5 5.4 %collective-permute-done.40 = bf16[128,2048]{1,0:T(8,128)(2,1)S(1)} collective-permute-done((bf16[128,2048]{1,0:T(8,128)(2,1)S(1)}, bf16[128,2048]{1,0:T(8,128)(2,1)S(1)}, u32[]{:S(2)}, u32[]{:S(2)}) %collective-permute-start.40) | collective-permute-done | bytes 524320 | tf_op jit(solution)/shard_map/ppermute | solution.py:244
  202.8 2.6 %collective-permute-start.39 = (bf16[128,2048]{1,0:T(8,128)(2,1)S(1)}, bf16[128,2048]{1,0:T(8,128)(2,1)S(1)}, u32[]{:S(2)}, u32[]{:S(2)}) collective-permute-start(bf16[128,2048]{1,0:T(8,128)(2,1)S(1)} %add_convert_fusion.3), channel_id=1, source_target_pairs={{0,2},{2,4},{4,6},{6,0},{1,3},{3,5},{5,7},{7,1},{8,10},{10,12},{12... | collective-permute-start | bytes 1572872 | tf_op jit(solution)/shard_map/ppermute | solution.py:249
  205.8 2.7 %collective-permute-done.23 = bf16[128,2048]{1,0:T(8,128)(2,1)S(1)} collective-permute-done((bf16[128,2048]{1,0:T(8,128)(2,1)S(1)}, bf16[128,2048]{1,0:T(8,128)(2,1)S(1)}, u32[]{:S(2)}, u32[]{:S(2)}) %collective-permute-start.23) | collective-permute-done | bytes 524320 | tf_op jit(solution)/shard_map/ppermute | solution.py:244
  208.4 7.0 %collective-permute-done.27 = bf16[128,2048]{1,0:T(8,128)(2,1)S(1)} collective-permute-done((bf16[128,2048]{1,0:T(8,128)(2,1)S(1)}, bf16[128,2048]{1,0:T(8,128)(2,1)S(1)}, u32[]{:S(2)}, u32[]{:S(2)}) %collective-permute-start.27) | collective-permute-done | bytes 524320 | tf_op jit(solution)/shard_map/ppermute | solution.py:249
  215.5 15.1 %collective-permute-done.43 = bf16[128,2048]{1,0:T(8,128)(2,1)S(1)} collective-permute-done((bf16[128,2048]{1,0:T(8,128)(2,1)S(1)}, bf16[128,2048]{1,0:T(8,128)(2,1)S(1)}, u32[]{:S(2)}, u32[]{:S(2)}) %collective-permute-start.43) | collective-permute-done | bytes 524320 | tf_op jit(solution)/shard_map/ppermute | solution.py:249
  230.6 1.3 add_convert_fusion
  (85 shorter events, 21.8 us)
Async XLA Ops:
  2.5 12.3 %collective-permute-start = (bf16[2,32,2048]{2,1,0:T(8,128)(2,1)S(1)}, bf16[2,32,2048]{2,1,0:T(8,128)(2,1)S(1)}, u32[]{:S(2)}, u32[]{:S(2)}) collective-permute-start(bf16[2,32,2048]{2,1,0:T(8,128)(2,1)S(1)} %constant_dynamic-update-slice_fusion.refs_1_), channel_id=1, source_target_pairs={{0,2},{2,4},{4,6},{6,0},{1,3},{3,5},{5,7},{7,1},{8,10},{10,12},{12... | collective-permute-start | bytes 786440 | tf_op jit(solution)/shard_map/ppermute | solution.py:249
  5.5 13.4 %collective-permute-start.1 = (bf16[2,32,2048]{2,1,0:T(8,128)(2,1)S(1)}, bf16[2,32,2048]{2,1,0:T(8,128)(2,1)S(1)}, u32[]{:S(2)}, u32[]{:S(2)}) collective-permute-start(bf16[2,32,2048]{2,1,0:T(8,128)(2,1)S(1)} %constant_dynamic-update-slice_fusion.refs_1_), channel_id=1, source_target_pairs={{0,6},{2,0},{4,2},{6,4},{1,7},{3,1},{5,3},{7,5},{8,14},{10,8},{12,... | collective-permute-start | bytes 786440 | tf_op jit(solution)/shard_map/ppermute | solution.py:249
  7.6 11.3 %collective-permute-start.2 = (bf16[2,32,2048]{2,1,0:T(8,128)(2,1)S(1)}, bf16[2,32,2048]{2,1,0:T(8,128)(2,1)S(1)}, u32[]{:S(2)}, u32[]{:S(2)}) collective-permute-start(bf16[2,32,2048]{2,1,0:T(8,128)(2,1)S(1)} %constant_dynamic-update-slice_fusion.refs_1_), channel_id=1, source_target_pairs={{0,1},{1,0},{2,3},{3,2},{4,5},{5,4},{6,7},{7,6},{8,9},{9,8},{10,11... | collective-permute-start | bytes 786440 | tf_op jit(solution)/shard_map/ppermute | solution.py:244
  18.9 38.0 %collective-permute-start.10 = (bf16[2048,1408]{1,0:T(8,128)(2,1)}, bf16[2048,1408]{1,0:T(8,128)(2,1)}, u32[]{:S(2)}, u32[]{:S(2)}) collective-permute-start(bf16[2048,1408]{1,0:T(8,128)(2,1)} %bitcast.62), channel_id=1, source_target_pairs={{0,8},{8,0},{1,9},{9,1},{2,10},{10,2},{3,11},{11,3},{4,12},{12,4},... | collective-permute-start | bytes 17301512 | tf_op jit(solution)/shard_map/ppermute | solution.py:244
  18.9 36.3 %collective-permute-start.11 = (bf16[704,2048]{1,0:T(8,128)(2,1)}, bf16[704,2048]{1,0:T(8,128)(2,1)S(1)}, u32[]{:S(2)}, u32[]{:S(2)}) collective-permute-start(bf16[704,2048]{1,0:T(8,128)(2,1)} %bitcast.43), channel_id=1, source_target_pairs={{0,8},{8,0},{1,9},{9,1},{2,10},{10,2},{3,11},{11,3},{4,12},{12,4},... | collective-permute-start | bytes 8650760 | tf_op jit(solution)/shard_map/ppermute | solution.py:244
  19.4 10.0 %collective-permute-start.3 = (bf16[2,32,2048]{2,1,0:T(8,128)(2,1)S(1)}, bf16[2,32,2048]{2,1,0:T(8,128)(2,1)S(1)}, u32[]{:S(2)}, u32[]{:S(2)}) collective-permute-start(bf16[2,32,2048]{2,1,0:T(8,128)(2,1)S(1)} %collective-permute-done.refs_2_), channel_id=1, source_target_pairs={{0,2},{2,4},{4,6},{6,0},{1,3},{3,5},{5,7},{7,1},{8,10},{10,12},{12... | collective-permute-start | bytes 786440 | tf_op jit(solution)/shard_map/ppermute | solution.py:249
  20.6 9.2 %collective-permute-start.4 = (bf16[2,32,2048]{2,1,0:T(8,128)(2,1)S(1)}, bf16[2,32,2048]{2,1,0:T(8,128)(2,1)S(1)}, u32[]{:S(2)}, u32[]{:S(2)}) collective-permute-start(bf16[2,32,2048]{2,1,0:T(8,128)(2,1)S(1)} %collective-permute-done.refs_2_), channel_id=1, source_target_pairs={{0,1},{1,0},{2,3},{3,2},{4,5},{5,4},{6,7},{7,6},{8,9},{9,8},{10,11... | collective-permute-start | bytes 786440 | tf_op jit(solution)/shard_map/ppermute | solution.py:244
  22.1 12.0 %collective-permute-start.5 = (bf16[2,32,2048]{2,1,0:T(8,128)(2,1)S(1)}, bf16[2,32,2048]{2,1,0:T(8,128)(2,1)S(1)}, u32[]{:S(2)}, u32[]{:S(2)}) collective-permute-start(bf16[2,32,2048]{2,1,0:T(8,128)(2,1)S(1)} %collective-permute-done.1.refs_3_), channel_id=1, source_target_pairs={{0,1},{1,0},{2,3},{3,2},{4,5},{5,4},{6,7},{7,6},{8,9},{9,8},{10,11... | collective-permute-start | bytes 786440 | tf_op jit(solution)/shard_map/ppermute | solution.py:244
  34.1 10.6 %collective-permute-start.9 = (bf16[2,32,2048]{2,1,0:T(8,128)(2,1)S(1)}, bf16[2,32,2048]{2,1,0:T(8,128)(2,1)S(1)}, u32[]{:S(2)}, u32[]{:S(2)}) collective-permute-start(bf16[2,32,2048]{2,1,0:T(8,128)(2,1)S(1)} %collective-permute-done.3.refs_4_), channel_id=1, source_target_pairs={{0,1},{1,0},{2,3},{3,2},{4,5},{5,4},{6,7},{7,6},{8,9},{9,8},{10,11... | collective-permute-start | bytes 786440 | tf_op jit(solution)/shard_map/ppermute | solution.py:244
  35.7 5.4 %collective-permute-start.6 = (f32[12,128]{1,0:T(8,128)S(1)}, f32[12,128]{1,0:T(8,128)S(1)}, u32[]{:S(2)}, u32[]{:S(2)}) collective-permute-start(f32[12,128]{1,0:T(8,128)S(1)} %pad_maximum_fusion.3), channel_id=1, source_target_pairs={{0,2},{2,4},{4,6},{6,0},{1,3},{3,5},{5,7},{7,1},{8,10},{10,12},{12... | collective-permute-start | bytes 18440 | tf_op jit(solution)/shard_map/ppermute | solution.py:249
  36.4 5.5 %collective-permute-start.7 = (f32[12,128]{1,0:T(8,128)S(1)}, f32[12,128]{1,0:T(8,128)S(1)}, u32[]{:S(2)}, u32[]{:S(2)}) collective-permute-start(f32[12,128]{1,0:T(8,128)S(1)} %pad_maximum_fusion.3), channel_id=1, source_target_pairs={{0,4},{2,6},{4,0},{6,2},{1,5},{3,7},{5,1},{7,3},{8,12},{10,14},{12... | collective-permute-start | bytes 18440 | tf_op jit(solution)/shard_map/ppermute | solution.py:249
  41.1 3.7 %collective-permute-start.8 = (f32[12,128]{1,0:T(8,128)S(1)}, f32[12,128]{1,0:T(8,128)S(1)}, u32[]{:S(2)}, u32[]{:S(2)}) collective-permute-start(f32[12,128]{1,0:T(8,128)S(1)} %pad_maximum_fusion.3), channel_id=1, source_target_pairs={{0,6},{2,0},{4,2},{6,4},{1,7},{3,1},{5,3},{7,5},{8,14},{10,8},{12,... | collective-permute-start | bytes 18440 | tf_op jit(solution)/shard_map/ppermute | solution.py:249
  44.8 10.5 %collective-permute-start.12 = (f32[4,12,128]{2,1,0:T(8,128)S(1)}, f32[4,12,128]{2,1,0:T(8,128)S(1)}, u32[]{:S(2)}, u32[]{:S(2)}) collective-permute-start(f32[4,12,128]{2,1,0:T(8,128)S(1)} %get-tuple-element.93), channel_id=1, source_target_pairs={{0,1},{1,0},{2,3},{3,2},{4,5},{5,4},{6,7},{7,6},{8,9},{9,8},{10,11... | collective-permute-start | bytes 73736 | tf_op jit(solution)/shard_map/ppermute | solution.py:244
  46.2 55.2 %copy-start = (bf16[1,704,2048]{2,1,0:T(8,128)(2,1)S(1)}, bf16[1,704,2048]{2,1,0:T(8,128)(2,1)}, u32[]{:S(2)}) copy-start(bf16[1,704,2048]{2,1,0:T(8,128)(2,1)} %param.23) | copy-start | bytes 8650756
  55.3 1.6 copy-start.1
  56.9 17.0 %collective-permute-start.17 = (bf16[128,2048]{1,0:T(8,128)(2,1)}, bf16[128,2048]{1,0:T(8,128)(2,1)}, u32[]{:S(2)}, u32[]{:S(2)}) collective-permute-start(bf16[128,2048]{1,0:T(8,128)(2,1)} %get-tuple-element.62.refs_2_), channel_id=1, source_target_pairs={{0,2},{2,4},{4,6},{6,0},{1,3},{3,5},{5,7},{7,1},{8,10},{10,12},{12... | collective-permute-start | bytes 1572872 | tf_op jit(solution)/shard_map/ppermute | solution.py:249
  56.9 18.5 %collective-permute-start.13 = (f32[2,4,12,128]{3,2,1,0:T(8,128)S(1)}, f32[2,4,12,128]{3,2,1,0:T(8,128)}, u32[]{:S(2)}, u32[]{:S(2)}) collective-permute-start(f32[2,4,12,128]{3,2,1,0:T(8,128)S(1)} %get-tuple-element.91), channel_id=1, source_target_pairs={{0,16},{16,0},{1,17},{17,1},{2,18},{18,2},{3,19},{19,3},{4,20},{20... | collective-permute-start | bytes 147464 | tf_op jit(solution)/shard_map/ppermute | solution.py:244
  58.5 19.5 %collective-permute-start.14 = (bf16[128,2048]{1,0:T(8,128)(2,1)}, bf16[128,2048]{1,0:T(8,128)(2,1)}, u32[]{:S(2)}, u32[]{:S(2)}) collective-permute-start(bf16[128,2048]{1,0:T(8,128)(2,1)} %get-tuple-element.62.refs_2_), channel_id=1, source_target_pairs={{0,1},{1,0},{2,3},{3,2},{4,5},{5,4},{6,7},{7,6},{8,9},{9,8},{10,11... | collective-permute-start | bytes 1572872 | tf_op jit(solution)/shard_map/ppermute | solution.py:244
  59.9 18.1 %collective-permute-start.15 = (bf16[128,2048]{1,0:T(8,128)(2,1)}, bf16[128,2048]{1,0:T(8,128)(2,1)}, u32[]{:S(2)}, u32[]{:S(2)}) collective-permute-start(bf16[128,2048]{1,0:T(8,128)(2,1)} %get-tuple-element.62.refs_2_), channel_id=1, source_target_pairs={{0,16},{16,0},{1,17},{17,1},{2,18},{18,2},{3,19},{19,3},{4,20},{20... | collective-permute-start | bytes 1572872 | tf_op jit(solution)/shard_map/ppermute | solution.py:244
  60.4 28.1 %collective-permute-start.28 = (bf16[128,2048]{1,0:T(8,128)(2,1)}, bf16[128,2048]{1,0:T(8,128)(2,1)S(1)}, u32[]{:S(2)}, u32[]{:S(2)}) collective-permute-start(bf16[128,2048]{1,0:T(8,128)(2,1)} %get-tuple-element.62.refs_2_), channel_id=1, source_target_pairs={{0,6},{2,0},{4,2},{6,4},{1,7},{3,1},{5,3},{7,5},{8,14},{10,8},{12,... | collective-permute-start | bytes 1572872 | tf_op jit(solution)/shard_map/ppermute | solution.py:249
  73.9 13.4 %collective-permute-start.19 = (bf16[128,2048]{1,0:T(8,128)(2,1)}, bf16[128,2048]{1,0:T(8,128)(2,1)}, u32[]{:S(2)}, u32[]{:S(2)}) collective-permute-start(bf16[128,2048]{1,0:T(8,128)(2,1)} %collective-permute-done.17.refs_6_), channel_id=1, source_target_pairs={{0,16},{16,0},{1,17},{17,1},{2,18},{18,2},{3,19},{19,3},{4,20},{20... | collective-permute-start | bytes 1572872 | tf_op jit(solution)/shard_map/ppermute | solution.py:244
  76.5 19.7 %collective-permute-start.18 = (bf16[128,2048]{1,0:T(8,128)(2,1)}, bf16[128,2048]{1,0:T(8,128)(2,1)S(1)}, u32[]{:S(2)}, u32[]{:S(2)}) collective-permute-start(bf16[128,2048]{1,0:T(8,128)(2,1)} %collective-permute-done.17.refs_6_), channel_id=1, source_target_pairs={{0,1},{1,0},{2,3},{3,2},{4,5},{5,4},{6,7},{7,6},{8,9},{9,8},{10,11... | collective-permute-start | bytes 1572872 | tf_op jit(solution)/shard_map/ppermute | solution.py:244
  77.9 14.6 %collective-permute-start.32 = (bf16[128,2048]{1,0:T(8,128)(2,1)}, bf16[128,2048]{1,0:T(8,128)(2,1)S(1)}, u32[]{:S(2)}, u32[]{:S(2)}) collective-permute-start(bf16[128,2048]{1,0:T(8,128)(2,1)} %collective-permute-done.17.refs_6_), channel_id=1, source_target_pairs={{0,2},{2,4},{4,6},{6,0},{1,3},{3,5},{5,7},{7,1},{8,10},{10,12},{12... | collective-permute-start | bytes 1572872 | tf_op jit(solution)/shard_map/ppermute | solution.py:249
  77.9 18.3 %collective-permute-start.16 = (bf16[128,2048]{1,0:T(8,128)(2,1)}, bf16[128,2048]{1,0:T(8,128)(2,1)S(1)}, u32[]{:S(2)}, u32[]{:S(2)}) collective-permute-start(bf16[128,2048]{1,0:T(8,128)(2,1)} %collective-permute-done.14.refs_3_), channel_id=1, source_target_pairs={{0,16},{16,0},{1,17},{17,1},{2,18},{18,2},{3,19},{19,3},{4,20},{20... | collective-permute-start | bytes 1572872 | tf_op jit(solution)/shard_map/ppermute | solution.py:244
  87.3 14.0 %collective-permute-start.20 = (bf16[128,2048]{1,0:T(8,128)(2,1)}, bf16[128,2048]{1,0:T(8,128)(2,1)S(1)}, u32[]{:S(2)}, u32[]{:S(2)}) collective-permute-start(bf16[128,2048]{1,0:T(8,128)(2,1)} %collective-permute-done.19.refs_8_), channel_id=1, source_target_pairs={{0,1},{1,0},{2,3},{3,2},{4,5},{5,4},{6,7},{7,6},{8,9},{9,8},{10,11... | collective-permute-start | bytes 1572872 | tf_op jit(solution)/shard_map/ppermute | solution.py:244
  88.5 34.1 %collective-permute-start.29 = (bf16[128,2048]{1,0:T(8,128)(2,1)S(1)}, bf16[128,2048]{1,0:T(8,128)(2,1)S(1)}, u32[]{:S(2)}, u32[]{:S(2)}) collective-permute-start(bf16[128,2048]{1,0:T(8,128)(2,1)S(1)} %collective-permute-done.28.refs_2_), channel_id=1, source_target_pairs={{0,1},{1,0},{2,3},{3,2},{4,5},{5,4},{6,7},{7,6},{8,9},{9,8},{10,11... | collective-permute-start | bytes 1572872 | tf_op jit(solution)/shard_map/ppermute | solution.py:244
  92.5 30.6 %collective-permute-start.34 = (bf16[128,2048]{1,0:T(8,128)(2,1)S(1)}, bf16[128,2048]{1,0:T(8,128)(2,1)S(1)}, u32[]{:S(2)}, u32[]{:S(2)}) collective-permute-start(bf16[128,2048]{1,0:T(8,128)(2,1)S(1)} %collective-permute-done.32.refs_6_), channel_id=1, source_target_pairs={{0,16},{16,0},{1,17},{17,1},{2,18},{18,2},{3,19},{19,3},{4,20},{20... | collective-permute-start | bytes 1572872 | tf_op jit(solution)/shard_map/ppermute | solution.py:244
  101.4 1.8 copy-start.2
  103.2 1.0 copy-start.3
  119.6 12.5 %collective-permute-start.24 = (bf16[128,2048]{1,0:T(8,128)(2,1)S(1)}, bf16[128,2048]{1,0:T(8,128)(2,1)S(1)}, u32[]{:S(2)}, u32[]{:S(2)}) collective-permute-start(bf16[128,2048]{1,0:T(8,128)(2,1)S(1)} %get-tuple-element.69), channel_id=1, source_target_pairs={{0,16},{16,0},{1,17},{17,1},{2,18},{18,2},{3,19},{19,3},{4,20},{20... | collective-permute-start | bytes 1572872 | tf_op jit(solution)/shard_map/ppermute | solution.py:244
  120.2 17.6 %collective-permute-start.30 = (bf16[128,2048]{1,0:T(8,128)(2,1)S(1)}, bf16[128,2048]{1,0:T(8,128)(2,1)S(1)}, u32[]{:S(2)}, u32[]{:S(2)}) collective-permute-start(bf16[128,2048]{1,0:T(8,128)(2,1)S(1)} %collective-permute-done.28.refs_2_), channel_id=1, source_target_pairs={{0,16},{16,0},{1,17},{17,1},{2,18},{18,2},{3,19},{19,3},{4,20},{20... | collective-permute-start | bytes 1572872 | tf_op jit(solution)/shard_map/ppermute | solution.py:244
  121.7 21.7 %collective-permute-start.33 = (bf16[128,2048]{1,0:T(8,128)(2,1)S(1)}, bf16[128,2048]{1,0:T(8,128)(2,1)S(1)}, u32[]{:S(2)}, u32[]{:S(2)}) collective-permute-start(bf16[128,2048]{1,0:T(8,128)(2,1)S(1)} %collective-permute-done.32.refs_6_), channel_id=1, source_target_pairs={{0,1},{1,0},{2,3},{3,2},{4,5},{5,4},{6,7},{7,6},{8,9},{9,8},{10,11... | collective-permute-start | bytes 1572872 | tf_op jit(solution)/shard_map/ppermute | solution.py:244
  122.6 20.8 %collective-permute-start.31 = (bf16[128,2048]{1,0:T(8,128)(2,1)S(1)}, bf16[128,2048]{1,0:T(8,128)(2,1)S(1)}, u32[]{:S(2)}, u32[]{:S(2)}) collective-permute-start(bf16[128,2048]{1,0:T(8,128)(2,1)S(1)} %collective-permute-done.29.refs_3_), channel_id=1, source_target_pairs={{0,16},{16,0},{1,17},{17,1},{2,18},{18,2},{3,19},{19,3},{4,20},{20... | collective-permute-start | bytes 1572872 | tf_op jit(solution)/shard_map/ppermute | solution.py:244
  123.2 21.7 %collective-permute-start.35 = (bf16[128,2048]{1,0:T(8,128)(2,1)S(1)}, bf16[128,2048]{1,0:T(8,128)(2,1)S(1)}, u32[]{:S(2)}, u32[]{:S(2)}) collective-permute-start(bf16[128,2048]{1,0:T(8,128)(2,1)S(1)} %collective-permute-done.34.refs_8_), channel_id=1, source_target_pairs={{0,1},{1,0},{2,3},{3,2},{4,5},{5,4},{6,7},{7,6},{8,9},{9,8},{10,11... | collective-permute-start | bytes 1572872 | tf_op jit(solution)/shard_map/ppermute | solution.py:244
  132.2 30.8 %collective-permute-start.22 = (bf16[128,2048]{1,0:T(8,128)(2,1)S(1)}, bf16[128,2048]{1,0:T(8,128)(2,1)S(1)}, u32[]{:S(2)}, u32[]{:S(2)}) collective-permute-start(bf16[128,2048]{1,0:T(8,128)(2,1)S(1)} %get-tuple-element.68), channel_id=1, source_target_pairs={{0,1},{1,0},{2,3},{3,2},{4,5},{5,4},{6,7},{7,6},{8,9},{9,8},{10,11... | collective-permute-start | bytes 1572872 | tf_op jit(solution)/shard_map/ppermute | solution.py:244
  137.8 68.0 %collective-permute-start.21 = (bf16[128,2048]{1,0:T(8,128)(2,1)S(1)}, bf16[128,2048]{1,0:T(8,128)(2,1)S(1)}, u32[]{:S(2)}, u32[]{:S(2)}) collective-permute-start(bf16[128,2048]{1,0:T(8,128)(2,1)S(1)} %get-tuple-element.66), channel_id=1, source_target_pairs={{0,1},{1,0},{2,3},{3,2},{4,5},{5,4},{6,7},{7,6},{8,9},{9,8},{10,11... | collective-permute-start | bytes 1572872 | tf_op jit(solution)/shard_map/ppermute | solution.py:244
  160.2 15.3 %collective-permute-start.37 = (bf16[128,2048]{1,0:T(8,128)(2,1)S(1)}, bf16[128,2048]{1,0:T(8,128)(2,1)S(1)}, u32[]{:S(2)}, u32[]{:S(2)}) collective-permute-start(bf16[128,2048]{1,0:T(8,128)(2,1)S(1)} %get-tuple-element.81), channel_id=1, source_target_pairs={{0,1},{1,0},{2,3},{3,2},{4,5},{5,4},{6,7},{7,6},{8,9},{9,8},{10,11... | collective-permute-start | bytes 1572872 | tf_op jit(solution)/shard_map/ppermute | solution.py:244
  161.2 27.0 %collective-permute-start.26 = (bf16[128,2048]{1,0:T(8,128)(2,1)S(1)}, bf16[128,2048]{1,0:T(8,128)(2,1)S(1)}, u32[]{:S(2)}, u32[]{:S(2)}) collective-permute-start(bf16[128,2048]{1,0:T(8,128)(2,1)S(1)} %add_convert_fusion.6), channel_id=1, source_target_pairs={{0,1},{1,0},{2,3},{3,2},{4,5},{5,4},{6,7},{7,6},{8,9},{9,8},{10,11... | collective-permute-start | bytes 1572872 | tf_op jit(solution)/shard_map/ppermute | solution.py:244
  162.5 27.3 %collective-permute-start.25 = (bf16[128,2048]{1,0:T(8,128)(2,1)S(1)}, bf16[128,2048]{1,0:T(8,128)(2,1)S(1)}, u32[]{:S(2)}, u32[]{:S(2)}) collective-permute-start(bf16[128,2048]{1,0:T(8,128)(2,1)S(1)} %get-tuple-element.74), channel_id=1, source_target_pairs={{0,16},{16,0},{1,17},{17,1},{2,18},{18,2},{3,19},{19,3},{4,20},{20... | collective-permute-start | bytes 1572872 | tf_op jit(solution)/shard_map/ppermute | solution.py:244
  163.0 24.5 %collective-permute-start.41 = (bf16[128,2048]{1,0:T(8,128)(2,1)S(1)}, bf16[128,2048]{1,0:T(8,128)(2,1)S(1)}, u32[]{:S(2)}, u32[]{:S(2)}) collective-permute-start(bf16[128,2048]{1,0:T(8,128)(2,1)S(1)} %get-tuple-element.85), channel_id=1, source_target_pairs={{0,16},{16,0},{1,17},{17,1},{2,18},{18,2},{3,19},{19,3},{4,20},{20... | collective-permute-start | bytes 1572872 | tf_op jit(solution)/shard_map/ppermute | solution.py:244
  175.5 19.9 %collective-permute-start.36 = (bf16[128,2048]{1,0:T(8,128)(2,1)S(1)}, bf16[128,2048]{1,0:T(8,128)(2,1)S(1)}, u32[]{:S(2)}, u32[]{:S(2)}) collective-permute-start(bf16[128,2048]{1,0:T(8,128)(2,1)S(1)} %get-tuple-element.79), channel_id=1, source_target_pairs={{0,1},{1,0},{2,3},{3,2},{4,5},{5,4},{6,7},{7,6},{8,9},{9,8},{10,11... | collective-permute-start | bytes 1572872 | tf_op jit(solution)/shard_map/ppermute | solution.py:244
  187.5 9.7 %collective-permute-start.38 = (bf16[128,2048]{1,0:T(8,128)(2,1)S(1)}, bf16[128,2048]{1,0:T(8,128)(2,1)S(1)}, u32[]{:S(2)}, u32[]{:S(2)}) collective-permute-start(bf16[128,2048]{1,0:T(8,128)(2,1)S(1)} %add_convert_fusion.4), channel_id=1, source_target_pairs={{0,16},{16,0},{1,17},{17,1},{2,18},{18,2},{3,19},{19,3},{4,20},{20... | collective-permute-start | bytes 1572872 | tf_op jit(solution)/shard_map/ppermute | solution.py:244
  188.2 14.7 %collective-permute-start.40 = (bf16[128,2048]{1,0:T(8,128)(2,1)S(1)}, bf16[128,2048]{1,0:T(8,128)(2,1)S(1)}, u32[]{:S(2)}, u32[]{:S(2)}) collective-permute-start(bf16[128,2048]{1,0:T(8,128)(2,1)S(1)} %get-tuple-element.83), channel_id=1, source_target_pairs={{0,16},{16,0},{1,17},{17,1},{2,18},{18,2},{3,19},{19,3},{4,20},{20... | collective-permute-start | bytes 1572872 | tf_op jit(solution)/shard_map/ppermute | solution.py:244
  189.7 15.7 %collective-permute-start.42 = (bf16[128,2048]{1,0:T(8,128)(2,1)S(1)}, bf16[128,2048]{1,0:T(8,128)(2,1)S(1)}, u32[]{:S(2)}, u32[]{:S(2)}) collective-permute-start(bf16[128,2048]{1,0:T(8,128)(2,1)S(1)} %add_convert_fusion.2), channel_id=1, source_target_pairs={{0,1},{1,0},{2,3},{3,2},{4,5},{5,4},{6,7},{7,6},{8,9},{9,8},{10,11... | collective-permute-start | bytes 1572872 | tf_op jit(solution)/shard_map/ppermute | solution.py:244
  195.4 13.0 %collective-permute-start.23 = (bf16[128,2048]{1,0:T(8,128)(2,1)S(1)}, bf16[128,2048]{1,0:T(8,128)(2,1)S(1)}, u32[]{:S(2)}, u32[]{:S(2)}) collective-permute-start(bf16[128,2048]{1,0:T(8,128)(2,1)S(1)} %add_convert_fusion.8), channel_id=1, source_target_pairs={{0,16},{16,0},{1,17},{17,1},{2,18},{18,2},{3,19},{19,3},{4,20},{20... | collective-permute-start | bytes 1572872 | tf_op jit(solution)/shard_map/ppermute | solution.py:244
  197.2 18.3 %collective-permute-start.27 = (bf16[128,2048]{1,0:T(8,128)(2,1)S(1)}, bf16[128,2048]{1,0:T(8,128)(2,1)S(1)}, u32[]{:S(2)}, u32[]{:S(2)}) collective-permute-start(bf16[128,2048]{1,0:T(8,128)(2,1)S(1)} %add_convert_fusion.5), channel_id=1, source_target_pairs={{0,6},{2,0},{4,2},{6,4},{1,7},{3,1},{5,3},{7,5},{8,14},{10,8},{12,... | collective-permute-start | bytes 1572872 | tf_op jit(solution)/shard_map/ppermute | solution.py:249
  202.8 12.7 %collective-permute-start.39 = (bf16[128,2048]{1,0:T(8,128)(2,1)S(1)}, bf16[128,2048]{1,0:T(8,128)(2,1)S(1)}, u32[]{:S(2)}, u32[]{:S(2)}) collective-permute-start(bf16[128,2048]{1,0:T(8,128)(2,1)S(1)} %add_convert_fusion.3), channel_id=1, source_target_pairs={{0,2},{2,4},{4,6},{6,0},{1,3},{3,5},{5,7},{7,1},{8,10},{10,12},{12... | collective-permute-start | bytes 1572872 | tf_op jit(solution)/shard_map/ppermute | solution.py:249
  205.7 24.9 %collective-permute-start.43 = (bf16[128,2048]{1,0:T(8,128)(2,1)S(1)}, bf16[128,2048]{1,0:T(8,128)(2,1)S(1)}, u32[]{:S(2)}, u32[]{:S(2)}) collective-permute-start(bf16[128,2048]{1,0:T(8,128)(2,1)S(1)} %add_convert_fusion.1), channel_id=1, source_target_pairs={{0,4},{2,6},{4,0},{6,2},{1,5},{3,7},{5,1},{7,3},{8,12},{10,14},{12... | collective-permute-start | bytes 1572872 | tf_op jit(solution)/shard_map/ppermute | solution.py:249
  (2 other events, 1.4 us)

commit v9 on v8

--- a/solution.py
+++ b/solution.py
@@ -319,6 +319,12 @@
     return [block, second, first, corner]
 
 
+def meet_early(results, corner, axes):
+    _, beside, across, _ = results
+    near, rest = (beside, across) if axes[0] == "side" else (across, beside)
+    return swap(near, axes[0]), swap(add(rest, corner), axes[1])
+
+
 def gather_plan(normed, slots, gates, weights, capacity):
     order = nearest_first()
     blocks = along_line(normed)
@@ -335,17 +341,32 @@
             corner = swap(results[1][3], axes[1][0])
         if i > 0:
             mine, corner, results[-1] = lax.optimization_barrier((mine, corner, results[-1]))
+        if i == 2:
+            early = meet_early(results[1], corner, axes[1])
         outputs = run_experts(planes, mine, share, weights, capacity)
+        if i == 2:
+            outputs, early = lax.optimization_barrier((outputs, early))
         for j in range(len(group)):
             results.append(list(outputs[4 * j : 4 * j + 4]))
-    parts = []
-    for i, back in enumerate(order):
+    parts = {}
+    parts[1] = add(results[1][0], *early)
+    for i, back in reversed(list(enumerate(order))):
+        if back == 1:
+            continue
         here, beside, across, last = results[i]
         near, rest = (beside, across) if axes[i][0] == "side" else (across, beside)
-        moved = corner if i == 1 else swap(last, axes[i][0])
-        total = add(here, swap(near, axes[i][0]), swap(add(rest, moved), axes[i][1]))
-        parts.append(shift(total, "line", -back) if back else total)
-    return add(*parts)
+        rest = add(rest, swap(last, axes[i][0]))
+        if back == 0 and len(order) // 2 in parts:
+            rest, parts[len(order) // 2] = lax.optimization_barrier(
+                (rest, parts[len(order) // 2])
+            )
+        parts[back] = add(here, swap(near, axes[i][0]), swap(rest, axes[i][1]))
+    columns = len(order)
+    for back in range(columns // 2, 1, -1):
+        parts[back - 1] = add(parts[back - 1], shift(parts[back], "line", -1))
+    for back in range(columns // 2 + 1, columns - 1):
+        parts[back + 1] = add(parts[back + 1], shift(parts[back], "line", 1))
+    return add(parts[0], shift(parts[1], "line", -1), shift(parts[columns - 1], "line", 1))
 
 
 def on_device(

time: 232 us -> 222 us (0.957)
  waiting for transfers between devices: 131 us -> 118 us
    ppermute x12, waiting for transfers between devices: 54.7 us -> 44.8 us  [shift(): lax.ppermute(array, axis, [(i, (i + amount) % size) for i in range(size)])]
    ppermute x32, waiting for transfers between devices: 76.4 us -> 73.1 us  [swap(): return lax.ppermute(array, axis, [(0, 1), (1, 0)])]
    unnamed x13 -> x15, local copies, waits for them, and re-layouts: 6.2 us -> 6.21 us
  transfers between devices with their start and end apart: 44 -> 44, of which waited for: 24 -> 22; matrix products, arithmetic and copies ran while one was open for 2% -> 2% of each run, Pallas kernels for 17% -> 18%
where the time goes in v9:
time: 222 us; the launch traced here: 220 us
  waiting for transfers between devices  118 us (53%)
  starting transfers between devices  48.5 us (22%)
  Pallas kernels  39.9 us (18%)
  local copies, waits for them, and re-layouts  7.16 us (3%)
  other arithmetic  4.98 us (2%)
    ppermute x32, waiting for transfers between devices, swap(): return lax.ppermute(array, axis, [(0, 1), (1, 0)])  73.1 us
    ppermute x12, waiting for transfers between devices, shift(): lax.ppermute(array, axis, [(i, (i + amount) % size) for i in range(size)])  44.8 us
    pallas_call x2, Pallas kernels, run_experts(): pl.pallas_call(lambda *refs: experts_kernel(capacity, count, *refs), in_s...  30.8 us
    ppermute x32, starting transfers between devices, swap(): return lax.ppermute(array, axis, [(0, 1), (1, 0)])  30.2 us
    ppermute x12, starting transfers between devices, shift(): lax.ppermute(array, axis, [(i, (i + amount) % size) for i in range(size)])  18.3 us
    pallas_call x1, Pallas kernels, attend(): pl.pallas_call(lambda *refs: attend_kernel(len(pieces), *refs), in_specs=...  9.09 us
    unnamed x15, local copies, waits for them, and re-layouts  6.21 us
  transfers between devices with their start and end apart: 44, of which 22 were waited for; matrix products, arithmetic and copies ran while one was open for 2% of the time, Pallas kernels for 18%

profile of v9, /device:TPU:0, one launch (start us, length us, event | category | flops | bytes accessed | tf_op | source)
XLA Modules:
  0.0 219.7 jit_solution(4313248542422125014)
XLA Ops:
  2.5 3.1 %collective-permute-start = (bf16[2,32,2048]{2,1,0:T(8,128)(2,1)S(1)}, bf16[2,32,2048]{2,1,0:T(8,128)(2,1)S(1)}, u32[]{:S(2)}, u32[]{:S(2)}) collective-permute-start(bf16[2,32,2048]{2,1,0:T(8,128)(2,1)S(1)} %constant_dynamic-update-slice_fusion.refs_1_), channel_id=1, source_target_pairs={{0,2},{2,4},{4,6},{6,0},{1,3},{3,5},{5,7},{7,1},{8,10},{10,12},{12... | collective-permute-start | bytes 786440 | tf_op jit(solution)/shard_map/ppermute | solution.py:249
  5.5 2.1 collective-permute-start.1
  7.6 1.7 collective-permute-start.2
  10.7 4.1 %collective-permute-done.refs_2_ = bf16[2,32,2048]{2,1,0:T(8,128)(2,1)S(1)} collective-permute-done((bf16[2,32,2048]{2,1,0:T(8,128)(2,1)S(1)}, bf16[2,32,2048]{2,1,0:T(8,128)(2,1)S(1)}, u32[]{:S(2)}, u32[]{:S(2)}) %collective-permute-start) | collective-permute-done | bytes 262176 | tf_op jit(solution)/shard_map/ppermute | solution.py:249
  14.7 4.2 %collective-permute-done.1.refs_3_ = bf16[2,32,2048]{2,1,0:T(8,128)(2,1)S(1)} collective-permute-done((bf16[2,32,2048]{2,1,0:T(8,128)(2,1)S(1)}, bf16[2,32,2048]{2,1,0:T(8,128)(2,1)S(1)}, u32[]{:S(2)}, u32[]{:S(2)}) %collective-permute-start.1) | collective-permute-done | bytes 262176 | tf_op jit(solution)/shard_map/ppermute | solution.py:249
  19.4 1.1 collective-permute-start.3
  20.6 1.5 collective-permute-start.4
  22.6 6.9 %collective-permute-done.3.refs_4_ = bf16[2,32,2048]{2,1,0:T(8,128)(2,1)S(1)} collective-permute-done((bf16[2,32,2048]{2,1,0:T(8,128)(2,1)S(1)}, bf16[2,32,2048]{2,1,0:T(8,128)(2,1)S(1)}, u32[]{:S(2)}, u32[]{:S(2)}) %collective-permute-start.3) | collective-permute-done | bytes 262176 | tf_op jit(solution)/shard_map/ppermute | solution.py:249
  29.8 4.4 %collective-permute-done.5.refs_7_ = bf16[2,32,2048]{2,1,0:T(8,128)(2,1)S(1)} collective-permute-done((bf16[2,32,2048]{2,1,0:T(8,128)(2,1)S(1)}, bf16[2,32,2048]{2,1,0:T(8,128)(2,1)S(1)}, u32[]{:S(2)}, u32[]{:S(2)}) %collective-permute-start.5) | collective-permute-done | bytes 262176 | tf_op jit(solution)/shard_map/ppermute | solution.py:244
  34.1 1.5 collective-permute-start.9
  36.4 2.5 %collective-permute-start.7 = (f32[12,128]{1,0:T(8,128)S(1)}, f32[12,128]{1,0:T(8,128)S(1)}, u32[]{:S(2)}, u32[]{:S(2)}) collective-permute-start(f32[12,128]{1,0:T(8,128)S(1)} %pad_maximum_fusion.3), channel_id=1, source_target_pairs={{0,4},{2,6},{4,0},{6,2},{1,5},{3,7},{5,1},{7,3},{8,12},{10,14},{12... | collective-permute-start | bytes 18440 | tf_op jit(solution)/shard_map/ppermute | solution.py:249
  38.9 2.2 %collective-permute-done.6 = f32[12,128]{1,0:T(8,128)S(1)} collective-permute-done((f32[12,128]{1,0:T(8,128)S(1)}, f32[12,128]{1,0:T(8,128)S(1)}, u32[]{:S(2)}, u32[]{:S(2)}) %collective-permute-start.6) | collective-permute-done | bytes 6176 | tf_op jit(solution)/shard_map/ppermute | solution.py:249
  42.0 2.8 %collective-permute-done.8 = f32[12,128]{1,0:T(8,128)S(1)} collective-permute-done((f32[12,128]{1,0:T(8,128)S(1)}, f32[12,128]{1,0:T(8,128)S(1)}, u32[]{:S(2)}, u32[]{:S(2)}) %collective-permute-start.8) | collective-permute-done | bytes 6176 | tf_op jit(solution)/shard_map/ppermute | solution.py:249
  46.2 9.1 %attend_project_norm.1 = (bf16[128,2048]{1,0:T(8,128)(2,1)}, bf16[128,2048]{1,0:T(8,128)(2,1)}) custom-call(f32[1,2048]{1,0:T(1,128)S(1)} %bitcast.46, bf16[2,32,2048]{2,1,0:T(8,128)(2,1)S(1)} %constant_dynamic-update-slice_fusion.refs_1_, bf16[2,32,2048]{2,1,0:T(8,128)(2,1)S(1)} %collective-permute-done.refs_2_, ...), custom_call_target="tpu_custom_call" | custom-call | flops 6442450944 | bytes 1048576 | tf_op jit(solution)/shard_map/attend_project_norm/pallas_call | solution.py:90
  55.3 1.6 copy-done.1
  56.9 1.6 collective-permute-start.13
  58.5 1.4 collective-permute-start.14
  60.4 3.8 %collective-permute-start.24 = (bf16[128,2048]{1,0:T(8,128)(2,1)}, bf16[128,2048]{1,0:T(8,128)(2,1)S(1)}, u32[]{:S(2)}, u32[]{:S(2)}) collective-permute-start(bf16[128,2048]{1,0:T(8,128)(2,1)} %get-tuple-element.74.refs_2_), channel_id=1, source_target_pairs={{0,6},{2,0},{4,2},{6,4},{1,7},{3,1},{5,3},{7,5},{8,14},{10,8},{12,... | collective-permute-start | bytes 1572872 | tf_op jit(solution)/shard_map/ppermute | solution.py:249
  64.2 9.6 %collective-permute-done.17.refs_6_ = bf16[128,2048]{1,0:T(8,128)(2,1)} collective-permute-done((bf16[128,2048]{1,0:T(8,128)(2,1)}, bf16[128,2048]{1,0:T(8,128)(2,1)}, u32[]{:S(2)}, u32[]{:S(2)}) %collective-permute-start.17) | collective-permute-done | bytes 524320 | tf_op jit(solution)/shard_map/ppermute | solution.py:249
  73.9 1.5 collective-permute-start.19
  76.5 1.4 collective-permute-start.18
  78.5 8.8 %collective-permute-done.19.refs_8_ = bf16[128,2048]{1,0:T(8,128)(2,1)} collective-permute-done((bf16[128,2048]{1,0:T(8,128)(2,1)}, bf16[128,2048]{1,0:T(8,128)(2,1)}, u32[]{:S(2)}, u32[]{:S(2)}) %collective-permute-start.19) | collective-permute-done | bytes 524320 | tf_op jit(solution)/shard_map/ppermute | solution.py:244
  88.5 1.2 collective-permute-start.25
  89.7 2.8 %collective-permute-done.28.refs_6_ = bf16[128,2048]{1,0:T(8,128)(2,1)S(1)} collective-permute-done((bf16[128,2048]{1,0:T(8,128)(2,1)}, bf16[128,2048]{1,0:T(8,128)(2,1)S(1)}, u32[]{:S(2)}, u32[]{:S(2)}) %collective-permute-start.28) | collective-permute-done | bytes 524320 | tf_op jit(solution)/shard_map/ppermute | solution.py:249
  93.3 2.9 %collective-permute-done.16.refs_5_ = bf16[128,2048]{1,0:T(8,128)(2,1)S(1)} collective-permute-done((bf16[128,2048]{1,0:T(8,128)(2,1)}, bf16[128,2048]{1,0:T(8,128)(2,1)S(1)}, u32[]{:S(2)}, u32[]{:S(2)}) %collective-permute-start.16) | collective-permute-done | bytes 524320 | tf_op jit(solution)/shard_map/ppermute | solution.py:244
  96.2 5.1 %collective-permute-done.20.refs_9_ = bf16[128,2048]{1,0:T(8,128)(2,1)S(1)} collective-permute-done((bf16[128,2048]{1,0:T(8,128)(2,1)}, bf16[128,2048]{1,0:T(8,128)(2,1)S(1)}, u32[]{:S(2)}, u32[]{:S(2)}) %collective-permute-start.20) | collective-permute-done | bytes 524320 | tf_op jit(solution)/shard_map/ppermute | solution.py:244
  101.4 1.8 copy-done.2
  103.2 1.0 copy-done.4
  104.2 15.5 %experts.2 = (bf16[128,2048]{1,0:T(8,128)(2,1)S(1)}, bf16[128,2048]{1,0:T(8,128)(2,1)S(1)}, bf16[128,2048]{1,0:T(8,128)(2,1)S(1)}, bf16[128,2048]{1,0:T(8,128)(2...) custom-call(s32[8,2,1,128]{3,2,1,0:T(1,128)S(1)} %bitcast.42, ...), custom_call_target="tpu_custom_call" | custom-call | flops 17716740096 | bytes 2097152 | tf_op jit(solution)/shard_map/experts/pallas_call | solution.py:169
  120.3 1.5 collective-permute-start.26
  123.3 1.1 collective-permute-start.31
  124.4 10.3 %collective-permute-done.23 = bf16[128,2048]{1,0:T(8,128)(2,1)S(1)} collective-permute-done((bf16[128,2048]{1,0:T(8,128)(2,1)S(1)}, bf16[128,2048]{1,0:T(8,128)(2,1)S(1)}, u32[]{:S(2)}, u32[]{:S(2)}) %collective-permute-start.23) | collective-permute-done | bytes 524320 | tf_op jit(solution)/shard_map/ppermute | solution.py:244
  135.8 7.8 %collective-permute-done.26.refs_4_ = bf16[128,2048]{1,0:T(8,128)(2,1)S(1)} collective-permute-done((bf16[128,2048]{1,0:T(8,128)(2,1)S(1)}, bf16[128,2048]{1,0:T(8,128)(2,1)S(1)}, u32[]{:S(2)}, u32[]{:S(2)}) %collective-permute-start.26) | collective-permute-done | bytes 524320 | tf_op jit(solution)/shard_map/ppermute | solution.py:244
  144.0 6.1 %collective-permute-done.27.refs_5_ = bf16[128,2048]{1,0:T(8,128)(2,1)S(1)} collective-permute-done((bf16[128,2048]{1,0:T(8,128)(2,1)S(1)}, bf16[128,2048]{1,0:T(8,128)(2,1)S(1)}, u32[]{:S(2)}, u32[]{:S(2)}) %collective-permute-start.27) | collective-permute-done | bytes 524320 | tf_op jit(solution)/shard_map/ppermute | solution.py:244
  150.2 15.3 %experts.3 = (bf16[128,2048]{1,0:T(8,128)(2,1)S(1)}, bf16[128,2048]{1,0:T(8,128)(2,1)S(1)}, bf16[128,2048]{1,0:T(8,128)(2,1)S(1)}, bf16[128,2048]{1,0:T(8,128)(2...) custom-call(s32[8,2,1,128]{3,2,1,0:T(1,128)S(1)} %pad_add_fusion.1.r, ...), custom_call_target="tpu_custom_call" | custom-call | flops 17716740096 | bytes 2097152 | tf_op jit(solution)/shard_map/experts/pallas_call | solution.py:169
  166.8 1.7 collective-permute-start.34
  168.5 1.1 collective-permute-start.41
  169.7 10.8 %collective-permute-done.35 = bf16[128,2048]{1,0:T(8,128)(2,1)S(1)} collective-permute-done((bf16[128,2048]{1,0:T(8,128)(2,1)S(1)}, bf16[128,2048]{1,0:T(8,128)(2,1)S(1)}, u32[]{:S(2)}, u32[]{:S(2)}) %collective-permute-start.35) | collective-permute-done | bytes 524320 | tf_op jit(solution)/shard_map/ppermute | solution.py:244
  181.7 1.2 collective-permute-start.40
  182.9 7.4 %collective-permute-done.41 = bf16[128,2048]{1,0:T(8,128)(2,1)S(1)} collective-permute-done((bf16[128,2048]{1,0:T(8,128)(2,1)S(1)}, bf16[128,2048]{1,0:T(8,128)(2,1)S(1)}, u32[]{:S(2)}, u32[]{:S(2)}) %collective-permute-start.41) | collective-permute-done | bytes 524320 | tf_op jit(solution)/shard_map/ppermute | solution.py:244
  191.1 4.9 %collective-permute-done.36 = bf16[128,2048]{1,0:T(8,128)(2,1)S(1)} collective-permute-done((bf16[128,2048]{1,0:T(8,128)(2,1)S(1)}, bf16[128,2048]{1,0:T(8,128)(2,1)S(1)}, u32[]{:S(2)}, u32[]{:S(2)}) %collective-permute-start.36) | collective-permute-done | bytes 524320 | tf_op jit(solution)/shard_map/ppermute | solution.py:244
  197.3 4.3 %collective-permute-done.40 = bf16[128,2048]{1,0:T(8,128)(2,1)S(1)} collective-permute-done((bf16[128,2048]{1,0:T(8,128)(2,1)S(1)}, bf16[128,2048]{1,0:T(8,128)(2,1)S(1)}, u32[]{:S(2)}, u32[]{:S(2)}) %collective-permute-start.40) | collective-permute-done | bytes 524320 | tf_op jit(solution)/shard_map/ppermute | solution.py:244
  201.8 2.2 collective-permute-start.43
  204.0 1.5 collective-permute-done.38
  205.9 1.9 collective-permute-start.39
  207.7 5.3 %collective-permute-done.43 = bf16[128,2048]{1,0:T(8,128)(2,1)S(1)} collective-permute-done((bf16[128,2048]{1,0:T(8,128)(2,1)S(1)}, bf16[128,2048]{1,0:T(8,128)(2,1)S(1)}, u32[]{:S(2)}, u32[]{:S(2)}) %collective-permute-start.43) | collective-permute-done | bytes 524320 | tf_op jit(solution)/shard_map/ppermute | solution.py:249
  213.0 5.5 %collective-permute-done.39 = bf16[128,2048]{1,0:T(8,128)(2,1)S(1)} collective-permute-done((bf16[128,2048]{1,0:T(8,128)(2,1)S(1)}, bf16[128,2048]{1,0:T(8,128)(2,1)S(1)}, u32[]{:S(2)}, u32[]{:S(2)}) %collective-permute-start.39) | collective-permute-done | bytes 524320 | tf_op jit(solution)/shard_map/ppermute | solution.py:249
  218.5 1.2 add_convert_fusion
  (87 shorter events, 20.6 us)
Async XLA Ops:
  2.5 12.3 %collective-permute-start = (bf16[2,32,2048]{2,1,0:T(8,128)(2,1)S(1)}, bf16[2,32,2048]{2,1,0:T(8,128)(2,1)S(1)}, u32[]{:S(2)}, u32[]{:S(2)}) collective-permute-start(bf16[2,32,2048]{2,1,0:T(8,128)(2,1)S(1)} %constant_dynamic-update-slice_fusion.refs_1_), channel_id=1, source_target_pairs={{0,2},{2,4},{4,6},{6,0},{1,3},{3,5},{5,7},{7,1},{8,10},{10,12},{12... | collective-permute-start | bytes 786440 | tf_op jit(solution)/shard_map/ppermute | solution.py:249
  5.5 13.4 %collective-permute-start.1 = (bf16[2,32,2048]{2,1,0:T(8,128)(2,1)S(1)}, bf16[2,32,2048]{2,1,0:T(8,128)(2,1)S(1)}, u32[]{:S(2)}, u32[]{:S(2)}) collective-permute-start(bf16[2,32,2048]{2,1,0:T(8,128)(2,1)S(1)} %constant_dynamic-update-slice_fusion.refs_1_), channel_id=1, source_target_pairs={{0,6},{2,0},{4,2},{6,4},{1,7},{3,1},{5,3},{7,5},{8,14},{10,8},{12,... | collective-permute-start | bytes 786440 | tf_op jit(solution)/shard_map/ppermute | solution.py:249
  7.6 11.3 %collective-permute-start.2 = (bf16[2,32,2048]{2,1,0:T(8,128)(2,1)S(1)}, bf16[2,32,2048]{2,1,0:T(8,128)(2,1)S(1)}, u32[]{:S(2)}, u32[]{:S(2)}) collective-permute-start(bf16[2,32,2048]{2,1,0:T(8,128)(2,1)S(1)} %constant_dynamic-update-slice_fusion.refs_1_), channel_id=1, source_target_pairs={{0,1},{1,0},{2,3},{3,2},{4,5},{5,4},{6,7},{7,6},{8,9},{9,8},{10,11... | collective-permute-start | bytes 786440 | tf_op jit(solution)/shard_map/ppermute | solution.py:244
  18.9 38.0 %collective-permute-start.10 = (bf16[2048,1408]{1,0:T(8,128)(2,1)}, bf16[2048,1408]{1,0:T(8,128)(2,1)}, u32[]{:S(2)}, u32[]{:S(2)}) collective-permute-start(bf16[2048,1408]{1,0:T(8,128)(2,1)} %bitcast.62), channel_id=1, source_target_pairs={{0,8},{8,0},{1,9},{9,1},{2,10},{10,2},{3,11},{11,3},{4,12},{12,4},... | collective-permute-start | bytes 17301512 | tf_op jit(solution)/shard_map/ppermute | solution.py:244
  18.9 36.3 %collective-permute-start.11 = (bf16[704,2048]{1,0:T(8,128)(2,1)}, bf16[704,2048]{1,0:T(8,128)(2,1)S(1)}, u32[]{:S(2)}, u32[]{:S(2)}) collective-permute-start(bf16[704,2048]{1,0:T(8,128)(2,1)} %bitcast.43), channel_id=1, source_target_pairs={{0,8},{8,0},{1,9},{9,1},{2,10},{10,2},{3,11},{11,3},{4,12},{12,4},... | collective-permute-start | bytes 8650760 | tf_op jit(solution)/shard_map/ppermute | solution.py:244
  19.4 10.0 %collective-permute-start.3 = (bf16[2,32,2048]{2,1,0:T(8,128)(2,1)S(1)}, bf16[2,32,2048]{2,1,0:T(8,128)(2,1)S(1)}, u32[]{:S(2)}, u32[]{:S(2)}) collective-permute-start(bf16[2,32,2048]{2,1,0:T(8,128)(2,1)S(1)} %collective-permute-done.refs_2_), channel_id=1, source_target_pairs={{0,2},{2,4},{4,6},{6,0},{1,3},{3,5},{5,7},{7,1},{8,10},{10,12},{12... | collective-permute-start | bytes 786440 | tf_op jit(solution)/shard_map/ppermute | solution.py:249
  20.6 9.2 %collective-permute-start.4 = (bf16[2,32,2048]{2,1,0:T(8,128)(2,1)S(1)}, bf16[2,32,2048]{2,1,0:T(8,128)(2,1)S(1)}, u32[]{:S(2)}, u32[]{:S(2)}) collective-permute-start(bf16[2,32,2048]{2,1,0:T(8,128)(2,1)S(1)} %collective-permute-done.refs_2_), channel_id=1, source_target_pairs={{0,1},{1,0},{2,3},{3,2},{4,5},{5,4},{6,7},{7,6},{8,9},{9,8},{10,11... | collective-permute-start | bytes 786440 | tf_op jit(solution)/shard_map/ppermute | solution.py:244
  22.1 12.0 %collective-permute-start.5 = (bf16[2,32,2048]{2,1,0:T(8,128)(2,1)S(1)}, bf16[2,32,2048]{2,1,0:T(8,128)(2,1)S(1)}, u32[]{:S(2)}, u32[]{:S(2)}) collective-permute-start(bf16[2,32,2048]{2,1,0:T(8,128)(2,1)S(1)} %collective-permute-done.1.refs_3_), channel_id=1, source_target_pairs={{0,1},{1,0},{2,3},{3,2},{4,5},{5,4},{6,7},{7,6},{8,9},{9,8},{10,11... | collective-permute-start | bytes 786440 | tf_op jit(solution)/shard_map/ppermute | solution.py:244
  34.1 10.6 %collective-permute-start.9 = (bf16[2,32,2048]{2,1,0:T(8,128)(2,1)S(1)}, bf16[2,32,2048]{2,1,0:T(8,128)(2,1)S(1)}, u32[]{:S(2)}, u32[]{:S(2)}) collective-permute-start(bf16[2,32,2048]{2,1,0:T(8,128)(2,1)S(1)} %collective-permute-done.3.refs_4_), channel_id=1, source_target_pairs={{0,1},{1,0},{2,3},{3,2},{4,5},{5,4},{6,7},{7,6},{8,9},{9,8},{10,11... | collective-permute-start | bytes 786440 | tf_op jit(solution)/shard_map/ppermute | solution.py:244
  35.7 5.4 %collective-permute-start.6 = (f32[12,128]{1,0:T(8,128)S(1)}, f32[12,128]{1,0:T(8,128)S(1)}, u32[]{:S(2)}, u32[]{:S(2)}) collective-permute-start(f32[12,128]{1,0:T(8,128)S(1)} %pad_maximum_fusion.3), channel_id=1, source_target_pairs={{0,2},{2,4},{4,6},{6,0},{1,3},{3,5},{5,7},{7,1},{8,10},{10,12},{12... | collective-permute-start | bytes 18440 | tf_op jit(solution)/shard_map/ppermute | solution.py:249
  36.4 5.5 %collective-permute-start.7 = (f32[12,128]{1,0:T(8,128)S(1)}, f32[12,128]{1,0:T(8,128)S(1)}, u32[]{:S(2)}, u32[]{:S(2)}) collective-permute-start(f32[12,128]{1,0:T(8,128)S(1)} %pad_maximum_fusion.3), channel_id=1, source_target_pairs={{0,4},{2,6},{4,0},{6,2},{1,5},{3,7},{5,1},{7,3},{8,12},{10,14},{12... | collective-permute-start | bytes 18440 | tf_op jit(solution)/shard_map/ppermute | solution.py:249
  41.1 3.7 %collective-permute-start.8 = (f32[12,128]{1,0:T(8,128)S(1)}, f32[12,128]{1,0:T(8,128)S(1)}, u32[]{:S(2)}, u32[]{:S(2)}) collective-permute-start(f32[12,128]{1,0:T(8,128)S(1)} %pad_maximum_fusion.3), channel_id=1, source_target_pairs={{0,6},{2,0},{4,2},{6,4},{1,7},{3,1},{5,3},{7,5},{8,14},{10,8},{12,... | collective-permute-start | bytes 18440 | tf_op jit(solution)/shard_map/ppermute | solution.py:249
  44.8 10.5 %collective-permute-start.12 = (f32[4,12,128]{2,1,0:T(8,128)S(1)}, f32[4,12,128]{2,1,0:T(8,128)S(1)}, u32[]{:S(2)}, u32[]{:S(2)}) collective-permute-start(f32[4,12,128]{2,1,0:T(8,128)S(1)} %get-tuple-element.117), channel_id=1, source_target_pairs={{0,1},{1,0},{2,3},{3,2},{4,5},{5,4},{6,7},{7,6},{8,9},{9,8},{10,11... | collective-permute-start | bytes 73736 | tf_op jit(solution)/shard_map/ppermute | solution.py:244
  46.2 55.2 %copy-start = (bf16[1,704,2048]{2,1,0:T(8,128)(2,1)S(1)}, bf16[1,704,2048]{2,1,0:T(8,128)(2,1)}, u32[]{:S(2)}) copy-start(bf16[1,704,2048]{2,1,0:T(8,128)(2,1)} %param.23) | copy-start | bytes 8650756
  55.3 1.6 copy-start.1
  56.9 17.0 %collective-permute-start.17 = (bf16[128,2048]{1,0:T(8,128)(2,1)}, bf16[128,2048]{1,0:T(8,128)(2,1)}, u32[]{:S(2)}, u32[]{:S(2)}) collective-permute-start(bf16[128,2048]{1,0:T(8,128)(2,1)} %get-tuple-element.74.refs_2_), channel_id=1, source_target_pairs={{0,2},{2,4},{4,6},{6,0},{1,3},{3,5},{5,7},{7,1},{8,10},{10,12},{12... | collective-permute-start | bytes 1572872 | tf_op jit(solution)/shard_map/ppermute | solution.py:249
  56.9 18.5 %collective-permute-start.13 = (f32[2,4,12,128]{3,2,1,0:T(8,128)S(1)}, f32[2,4,12,128]{3,2,1,0:T(8,128)}, u32[]{:S(2)}, u32[]{:S(2)}) collective-permute-start(f32[2,4,12,128]{3,2,1,0:T(8,128)S(1)} %get-tuple-element.115), channel_id=1, source_target_pairs={{0,16},{16,0},{1,17},{17,1},{2,18},{18,2},{3,19},{19,3},{4,20},{20... | collective-permute-start | bytes 147464 | tf_op jit(solution)/shard_map/ppermute | solution.py:244
  58.5 19.5 %collective-permute-start.14 = (bf16[128,2048]{1,0:T(8,128)(2,1)}, bf16[128,2048]{1,0:T(8,128)(2,1)}, u32[]{:S(2)}, u32[]{:S(2)}) collective-permute-start(bf16[128,2048]{1,0:T(8,128)(2,1)} %get-tuple-element.74.refs_2_), channel_id=1, source_target_pairs={{0,1},{1,0},{2,3},{3,2},{4,5},{5,4},{6,7},{7,6},{8,9},{9,8},{10,11... | collective-permute-start | bytes 1572872 | tf_op jit(solution)/shard_map/ppermute | solution.py:244
  59.9 18.1 %collective-permute-start.15 = (bf16[128,2048]{1,0:T(8,128)(2,1)}, bf16[128,2048]{1,0:T(8,128)(2,1)}, u32[]{:S(2)}, u32[]{:S(2)}) collective-permute-start(bf16[128,2048]{1,0:T(8,128)(2,1)} %get-tuple-element.74.refs_2_), channel_id=1, source_target_pairs={{0,16},{16,0},{1,17},{17,1},{2,18},{18,2},{3,19},{19,3},{4,20},{20... | collective-permute-start | bytes 1572872 | tf_op jit(solution)/shard_map/ppermute | solution.py:244
  60.4 28.1 %collective-permute-start.24 = (bf16[128,2048]{1,0:T(8,128)(2,1)}, bf16[128,2048]{1,0:T(8,128)(2,1)S(1)}, u32[]{:S(2)}, u32[]{:S(2)}) collective-permute-start(bf16[128,2048]{1,0:T(8,128)(2,1)} %get-tuple-element.74.refs_2_), channel_id=1, source_target_pairs={{0,6},{2,0},{4,2},{6,4},{1,7},{3,1},{5,3},{7,5},{8,14},{10,8},{12,... | collective-permute-start | bytes 1572872 | tf_op jit(solution)/shard_map/ppermute | solution.py:249
  73.9 13.4 %collective-permute-start.19 = (bf16[128,2048]{1,0:T(8,128)(2,1)}, bf16[128,2048]{1,0:T(8,128)(2,1)}, u32[]{:S(2)}, u32[]{:S(2)}) collective-permute-start(bf16[128,2048]{1,0:T(8,128)(2,1)} %collective-permute-done.17.refs_6_), channel_id=1, source_target_pairs={{0,16},{16,0},{1,17},{17,1},{2,18},{18,2},{3,19},{19,3},{4,20},{20... | collective-permute-start | bytes 1572872 | tf_op jit(solution)/shard_map/ppermute | solution.py:244
  76.5 19.7 %collective-permute-start.18 = (bf16[128,2048]{1,0:T(8,128)(2,1)}, bf16[128,2048]{1,0:T(8,128)(2,1)S(1)}, u32[]{:S(2)}, u32[]{:S(2)}) collective-permute-start(bf16[128,2048]{1,0:T(8,128)(2,1)} %collective-permute-done.17.refs_6_), channel_id=1, source_target_pairs={{0,1},{1,0},{2,3},{3,2},{4,5},{5,4},{6,7},{7,6},{8,9},{9,8},{10,11... | collective-permute-start | bytes 1572872 | tf_op jit(solution)/shard_map/ppermute | solution.py:244
  77.9 14.6 %collective-permute-start.28 = (bf16[128,2048]{1,0:T(8,128)(2,1)}, bf16[128,2048]{1,0:T(8,128)(2,1)S(1)}, u32[]{:S(2)}, u32[]{:S(2)}) collective-permute-start(bf16[128,2048]{1,0:T(8,128)(2,1)} %collective-permute-done.17.refs_6_), channel_id=1, source_target_pairs={{0,2},{2,4},{4,6},{6,0},{1,3},{3,5},{5,7},{7,1},{8,10},{10,12},{12... | collective-permute-start | bytes 1572872 | tf_op jit(solution)/shard_map/ppermute | solution.py:249
  77.9 18.3 %collective-permute-start.16 = (bf16[128,2048]{1,0:T(8,128)(2,1)}, bf16[128,2048]{1,0:T(8,128)(2,1)S(1)}, u32[]{:S(2)}, u32[]{:S(2)}) collective-permute-start(bf16[128,2048]{1,0:T(8,128)(2,1)} %collective-permute-done.14.refs_3_), channel_id=1, source_target_pairs={{0,16},{16,0},{1,17},{17,1},{2,18},{18,2},{3,19},{19,3},{4,20},{20... | collective-permute-start | bytes 1572872 | tf_op jit(solution)/shard_map/ppermute | solution.py:244
  87.3 14.0 %collective-permute-start.20 = (bf16[128,2048]{1,0:T(8,128)(2,1)}, bf16[128,2048]{1,0:T(8,128)(2,1)S(1)}, u32[]{:S(2)}, u32[]{:S(2)}) collective-permute-start(bf16[128,2048]{1,0:T(8,128)(2,1)} %collective-permute-done.19.refs_8_), channel_id=1, source_target_pairs={{0,1},{1,0},{2,3},{3,2},{4,5},{5,4},{6,7},{7,6},{8,9},{9,8},{10,11... | collective-permute-start | bytes 1572872 | tf_op jit(solution)/shard_map/ppermute | solution.py:244
  88.5 34.2 %collective-permute-start.25 = (bf16[128,2048]{1,0:T(8,128)(2,1)S(1)}, bf16[128,2048]{1,0:T(8,128)(2,1)S(1)}, u32[]{:S(2)}, u32[]{:S(2)}) collective-permute-start(bf16[128,2048]{1,0:T(8,128)(2,1)S(1)} %collective-permute-done.24.refs_2_), channel_id=1, source_target_pairs={{0,1},{1,0},{2,3},{3,2},{4,5},{5,4},{6,7},{7,6},{8,9},{9,8},{10,11... | collective-permute-start | bytes 1572872 | tf_op jit(solution)/shard_map/ppermute | solution.py:244
  92.5 30.8 %collective-permute-start.30 = (bf16[128,2048]{1,0:T(8,128)(2,1)S(1)}, bf16[128,2048]{1,0:T(8,128)(2,1)S(1)}, u32[]{:S(2)}, u32[]{:S(2)}) collective-permute-start(bf16[128,2048]{1,0:T(8,128)(2,1)S(1)} %collective-permute-done.28.refs_6_), channel_id=1, source_target_pairs={{0,16},{16,0},{1,17},{17,1},{2,18},{18,2},{3,19},{19,3},{4,20},{20... | collective-permute-start | bytes 1572872 | tf_op jit(solution)/shard_map/ppermute | solution.py:244
  101.4 1.8 copy-start.2
  104.2 46.0 %copy-start.3 = (bf16[704,2048]{1,0:T(8,128)(2,1)S(1)}, bf16[704,2048]{1,0:T(8,128)(2,1)}, u32[]{:S(2)}) copy-start(bf16[704,2048]{1,0:T(8,128)(2,1)} %copy-done.1) | copy-start | bytes 8650756
  119.7 14.9 %collective-permute-start.23 = (bf16[128,2048]{1,0:T(8,128)(2,1)S(1)}, bf16[128,2048]{1,0:T(8,128)(2,1)S(1)}, u32[]{:S(2)}, u32[]{:S(2)}) collective-permute-start(bf16[128,2048]{1,0:T(8,128)(2,1)S(1)} %get-tuple-element.81), channel_id=1, source_target_pairs={{0,16},{16,0},{1,17},{17,1},{2,18},{18,2},{3,19},{19,3},{4,20},{20... | collective-permute-start | bytes 1572872 | tf_op jit(solution)/shard_map/ppermute | solution.py:244
  120.3 23.2 %collective-permute-start.26 = (bf16[128,2048]{1,0:T(8,128)(2,1)S(1)}, bf16[128,2048]{1,0:T(8,128)(2,1)S(1)}, u32[]{:S(2)}, u32[]{:S(2)}) collective-permute-start(bf16[128,2048]{1,0:T(8,128)(2,1)S(1)} %collective-permute-done.24.refs_2_), channel_id=1, source_target_pairs={{0,16},{16,0},{1,17},{17,1},{2,18},{18,2},{3,19},{19,3},{4,20},{20... | collective-permute-start | bytes 1572872 | tf_op jit(solution)/shard_map/ppermute | solution.py:244
  121.8 28.3 %collective-permute-start.29 = (bf16[128,2048]{1,0:T(8,128)(2,1)S(1)}, bf16[128,2048]{1,0:T(8,128)(2,1)S(1)}, u32[]{:S(2)}, u32[]{:S(2)}) collective-permute-start(bf16[128,2048]{1,0:T(8,128)(2,1)S(1)} %collective-permute-done.28.refs_6_), channel_id=1, source_target_pairs={{0,1},{1,0},{2,3},{3,2},{4,5},{5,4},{6,7},{7,6},{8,9},{9,8},{10,11... | collective-permute-start | bytes 1572872 | tf_op jit(solution)/shard_map/ppermute | solution.py:244
  122.7 27.4 %collective-permute-start.27 = (bf16[128,2048]{1,0:T(8,128)(2,1)S(1)}, bf16[128,2048]{1,0:T(8,128)(2,1)S(1)}, u32[]{:S(2)}, u32[]{:S(2)}) collective-permute-start(bf16[128,2048]{1,0:T(8,128)(2,1)S(1)} %collective-permute-done.25.refs_3_), channel_id=1, source_target_pairs={{0,16},{16,0},{1,17},{17,1},{2,18},{18,2},{3,19},{19,3},{4,20},{20... | collective-permute-start | bytes 1572872 | tf_op jit(solution)/shard_map/ppermute | solution.py:244
  123.3 26.9 %collective-permute-start.31 = (bf16[128,2048]{1,0:T(8,128)(2,1)S(1)}, bf16[128,2048]{1,0:T(8,128)(2,1)S(1)}, u32[]{:S(2)}, u32[]{:S(2)}) collective-permute-start(bf16[128,2048]{1,0:T(8,128)(2,1)S(1)} %collective-permute-done.30.refs_8_), channel_id=1, source_target_pairs={{0,1},{1,0},{2,3},{3,2},{4,5},{5,4},{6,7},{7,6},{8,9},{9,8},{10,11... | collective-permute-start | bytes 1572872 | tf_op jit(solution)/shard_map/ppermute | solution.py:244
  134.8 30.7 %collective-permute-start.33 = (bf16[128,2048]{1,0:T(8,128)(2,1)S(1)}, bf16[128,2048]{1,0:T(8,128)(2,1)S(1)}, u32[]{:S(2)}, u32[]{:S(2)}) collective-permute-start(bf16[128,2048]{1,0:T(8,128)(2,1)S(1)} %add_convert_fusion.8), channel_id=1, source_target_pairs={{0,1},{1,0},{2,3},{3,2},{4,5},{5,4},{6,7},{7,6},{8,9},{9,8},{10,11... | collective-permute-start | bytes 1572872 | tf_op jit(solution)/shard_map/ppermute | solution.py:244
  143.5 22.0 %collective-permute-start.32 = (bf16[128,2048]{1,0:T(8,128)(2,1)S(1)}, bf16[128,2048]{1,0:T(8,128)(2,1)S(1)}, u32[]{:S(2)}, u32[]{:S(2)}) collective-permute-start(bf16[128,2048]{1,0:T(8,128)(2,1)S(1)} %get-tuple-element.94), channel_id=1, source_target_pairs={{0,16},{16,0},{1,17},{17,1},{2,18},{18,2},{3,19},{19,3},{4,20},{20... | collective-permute-start | bytes 1572872 | tf_op jit(solution)/shard_map/ppermute | solution.py:244
  165.5 14.9 %collective-permute-start.35 = (bf16[128,2048]{1,0:T(8,128)(2,1)S(1)}, bf16[128,2048]{1,0:T(8,128)(2,1)S(1)}, u32[]{:S(2)}, u32[]{:S(2)}) collective-permute-start(bf16[128,2048]{1,0:T(8,128)(2,1)S(1)} %get-tuple-element.100), channel_id=1, source_target_pairs={{0,16},{16,0},{1,17},{17,1},{2,18},{18,2},{3,19},{19,3},{4,20},{20... | collective-permute-start | bytes 1572872 | tf_op jit(solution)/shard_map/ppermute | solution.py:244
  166.1 15.4 %collective-permute-start.22 = (bf16[128,2048]{1,0:T(8,128)(2,1)S(1)}, bf16[128,2048]{1,0:T(8,128)(2,1)S(1)}, u32[]{:S(2)}, u32[]{:S(2)}) collective-permute-start(bf16[128,2048]{1,0:T(8,128)(2,1)S(1)} %get-tuple-element.80), channel_id=1, source_target_pairs={{0,1},{1,0},{2,3},{3,2},{4,5},{5,4},{6,7},{7,6},{8,9},{9,8},{10,11... | collective-permute-start | bytes 1572872 | tf_op jit(solution)/shard_map/ppermute | solution.py:244
  166.8 24.3 %collective-permute-start.34 = (bf16[128,2048]{1,0:T(8,128)(2,1)S(1)}, bf16[128,2048]{1,0:T(8,128)(2,1)S(1)}, u32[]{:S(2)}, u32[]{:S(2)}) collective-permute-start(bf16[128,2048]{1,0:T(8,128)(2,1)S(1)} %get-tuple-element.98), channel_id=1, source_target_pairs={{0,16},{16,0},{1,17},{17,1},{2,18},{18,2},{3,19},{19,3},{4,20},{20... | collective-permute-start | bytes 1572872 | tf_op jit(solution)/shard_map/ppermute | solution.py:244
  168.5 21.8 %collective-permute-start.41 = (bf16[128,2048]{1,0:T(8,128)(2,1)S(1)}, bf16[128,2048]{1,0:T(8,128)(2,1)S(1)}, u32[]{:S(2)}, u32[]{:S(2)}) collective-permute-start(bf16[128,2048]{1,0:T(8,128)(2,1)S(1)} %get-tuple-element.109), channel_id=1, source_target_pairs={{0,1},{1,0},{2,3},{3,2},{4,5},{5,4},{6,7},{7,6},{8,9},{9,8},{10,11... | collective-permute-start | bytes 1572872 | tf_op jit(solution)/shard_map/ppermute | solution.py:244
  180.6 15.4 %collective-permute-start.36 = (bf16[128,2048]{1,0:T(8,128)(2,1)S(1)}, bf16[128,2048]{1,0:T(8,128)(2,1)S(1)}, u32[]{:S(2)}, u32[]{:S(2)}) collective-permute-start(bf16[128,2048]{1,0:T(8,128)(2,1)S(1)} %add_convert_fusion.7), channel_id=1, source_target_pairs={{0,1},{1,0},{2,3},{3,2},{4,5},{5,4},{6,7},{7,6},{8,9},{9,8},{10,11... | collective-permute-start | bytes 1572872 | tf_op jit(solution)/shard_map/ppermute | solution.py:244
  181.7 19.9 %collective-permute-start.40 = (bf16[128,2048]{1,0:T(8,128)(2,1)S(1)}, bf16[128,2048]{1,0:T(8,128)(2,1)S(1)}, u32[]{:S(2)}, u32[]{:S(2)}) collective-permute-start(bf16[128,2048]{1,0:T(8,128)(2,1)S(1)} %get-tuple-element.107), channel_id=1, source_target_pairs={{0,1},{1,0},{2,3},{3,2},{4,5},{5,4},{6,7},{7,6},{8,9},{9,8},{10,11... | collective-permute-start | bytes 1572872 | tf_op jit(solution)/shard_map/ppermute | solution.py:244
  190.5 11.1 %collective-permute-start.42 = (bf16[128,2048]{1,0:T(8,128)(2,1)S(1)}, bf16[128,2048]{1,0:T(8,128)(2,1)S(1)}, u32[]{:S(2)}, u32[]{:S(2)}) collective-permute-start(bf16[128,2048]{1,0:T(8,128)(2,1)S(1)} %add_convert_fusion.2), channel_id=1, source_target_pairs={{0,16},{16,0},{1,17},{17,1},{2,18},{18,2},{3,19},{19,3},{4,20},{20... | collective-permute-start | bytes 1572872 | tf_op jit(solution)/shard_map/ppermute | solution.py:244
  196.2 9.3 %collective-permute-start.38 = (bf16[128,2048]{1,0:T(8,128)(2,1)S(1)}, bf16[128,2048]{1,0:T(8,128)(2,1)S(1)}, u32[]{:S(2)}, u32[]{:S(2)}) collective-permute-start(bf16[128,2048]{1,0:T(8,128)(2,1)S(1)} %add_convert_fusion.6), channel_id=1, source_target_pairs={{0,6},{2,0},{4,2},{6,4},{1,7},{3,1},{5,3},{7,5},{8,14},{10,8},{12,... | collective-permute-start | bytes 1572872 | tf_op jit(solution)/shard_map/ppermute | solution.py:249
  196.3 11.5 %collective-permute-start.21 = (bf16[128,2048]{1,0:T(8,128)(2,1)S(1)}, bf16[128,2048]{1,0:T(8,128)(2,1)S(1)}, u32[]{:S(2)}, u32[]{:S(2)}) collective-permute-start(bf16[128,2048]{1,0:T(8,128)(2,1)S(1)} %get-tuple-element.78), channel_id=1, source_target_pairs={{0,1},{1,0},{2,3},{3,2},{4,5},{5,4},{6,7},{7,6},{8,9},{9,8},{10,11... | collective-permute-start | bytes 1572872 | tf_op jit(solution)/shard_map/ppermute | solution.py:244
  197.0 10.7 %collective-permute-start.37 = (bf16[128,2048]{1,0:T(8,128)(2,1)S(1)}, bf16[128,2048]{1,0:T(8,128)(2,1)S(1)}, u32[]{:S(2)}, u32[]{:S(2)}) collective-permute-start(bf16[128,2048]{1,0:T(8,128)(2,1)S(1)} %add_convert_fusion.9), channel_id=1, source_target_pairs={{0,16},{16,0},{1,17},{17,1},{2,18},{18,2},{3,19},{19,3},{4,20},{20... | collective-permute-start | bytes 1572872 | tf_op jit(solution)/shard_map/ppermute | solution.py:244
  201.8 11.2 %collective-permute-start.43 = (bf16[128,2048]{1,0:T(8,128)(2,1)S(1)}, bf16[128,2048]{1,0:T(8,128)(2,1)S(1)}, u32[]{:S(2)}, u32[]{:S(2)}) collective-permute-start(bf16[128,2048]{1,0:T(8,128)(2,1)S(1)} %add_convert_fusion.1), channel_id=1, source_target_pairs={{0,2},{2,4},{4,6},{6,0},{1,3},{3,5},{5,7},{7,1},{8,10},{10,12},{12... | collective-permute-start | bytes 1572872 | tf_op jit(solution)/shard_map/ppermute | solution.py:249
  205.9 12.6 %collective-permute-start.39 = (bf16[128,2048]{1,0:T(8,128)(2,1)S(1)}, bf16[128,2048]{1,0:T(8,128)(2,1)S(1)}, u32[]{:S(2)}, u32[]{:S(2)}) collective-permute-start(bf16[128,2048]{1,0:T(8,128)(2,1)S(1)} %add_convert_fusion.3), channel_id=1, source_target_pairs={{0,6},{2,0},{4,2},{6,4},{1,7},{3,1},{5,3},{7,5},{8,14},{10,8},{12,... | collective-permute-start | bytes 1572872 | tf_op jit(solution)/shard_map/ppermute | solution.py:249
  (3 other events, 2.4 us)

commit v10 on v9

--- a/solution.py
+++ b/solution.py
@@ -319,48 +319,44 @@
     return [block, second, first, corner]
 
 
-def meet_early(results, corner, axes):
-    _, beside, across, _ = results
-    near, rest = (beside, across) if axes[0] == "side" else (across, beside)
-    return swap(near, axes[0]), swap(add(rest, corner), axes[1])
+def first_two(results, axes):
+    _, beside, across, last = results
+    near = beside if axes[0] == "side" else across
+    return swap(near, axes[0]), swap(last, axes[0])
 
 
 def gather_plan(normed, slots, gates, weights, capacity):
     order = nearest_first()
     blocks = along_line(normed)
     axes = [("side", "far") if i % 2 == 0 else ("far", "side") for i in range(len(order))]
-    results, corner = [], None
+    results, early = [], []
     for i in range(0, len(order), 2):
         group = order[i : i + 2]
-        planes = []
-        for j, back in enumerate(group):
-            planes = planes + over_plane(blocks[back], axes[i + j])
+        planes = [over_plane(blocks[back], axes[i + j]) for j, back in enumerate(group)]
         mine = jnp.concatenate([slots[:, back] for back in group])
         share = jnp.concatenate([gates[:, back] for back in group])
-        if i == 2:
-            corner = swap(results[1][3], axes[1][0])
         if i > 0:
-            mine, corner, results[-1] = lax.optimization_barrier((mine, corner, results[-1]))
-        if i == 2:
-            early = meet_early(results[1], corner, axes[1])
-        outputs = run_experts(planes, mine, share, weights, capacity)
-        if i == 2:
+            direct = [one[1:3] for one in planes]
+            results, direct = lax.optimization_barrier((results, direct))
+            planes = [one[:1] + two + one[3:] for one, two in zip(planes, direct)]
+            results, planes, mine = lax.optimization_barrier((results, planes, mine))
+            early = early + [first_two(results[j], axes[j]) for j in range(i - 2, i)]
+        outputs = run_experts(sum(planes, []), mine, share, weights, capacity)
+        if i > 0:
             outputs, early = lax.optimization_barrier((outputs, early))
         for j in range(len(group)):
             results.append(list(outputs[4 * j : 4 * j + 4]))
     parts = {}
-    parts[1] = add(results[1][0], *early)
     for i, back in reversed(list(enumerate(order))):
-        if back == 1:
-            continue
-        here, beside, across, last = results[i]
-        near, rest = (beside, across) if axes[i][0] == "side" else (across, beside)
-        rest = add(rest, swap(last, axes[i][0]))
+        here, beside, across, _ = results[i]
+        rest = across if axes[i][0] == "side" else beside
+        near, moved = early[i] if i < len(early) else first_two(results[i], axes[i])
+        rest = add(rest, moved)
         if back == 0 and len(order) // 2 in parts:
             rest, parts[len(order) // 2] = lax.optimization_barrier(
                 (rest, parts[len(order) // 2])
             )
-        parts[back] = add(here, swap(near, axes[i][0]), swap(rest, axes[i][1]))
+        parts[back] = add(here, near, swap(rest, axes[i][1]))
     columns = len(order)
     for back in range(columns // 2, 1, -1):
         parts[back - 1] = add(parts[back - 1], shift(parts[back], "line", -1))

time: 222 us -> 239 us (1.077)
  waiting for transfers between devices: 118 us -> 133 us
  starting transfers between devices: 48.5 us -> 51.7 us
    ppermute x12, waiting for transfers between devices: 44.8 us -> 67.8 us  [shift(): lax.ppermute(array, axis, [(i, (i + amount) % size) for i in range(size)])]
    ppermute x32, waiting for transfers between devices: 73.1 us -> 65.7 us  [swap(): return lax.ppermute(array, axis, [(0, 1), (1, 0)])]
    ppermute x32, starting transfers between devices: 30.2 us -> 32.9 us  [swap(): return lax.ppermute(array, axis, [(0, 1), (1, 0)])]
    unnamed x15 -> x13, local copies, waits for them, and re-layouts: 6.21 us -> 6.2 us
  transfers between devices with their start and end apart: 44 -> 44, of which waited for: 22 -> 24; matrix products, arithmetic and copies ran while one was open for 2% -> 2% of each run, Pallas kernels for 18% -> 17%
where the time goes in v10:
time: 239 us; the launch traced here: 238 us
  waiting for transfers between devices  133 us (56%)
  starting transfers between devices  51.7 us (22%)
  Pallas kernels  39.8 us (17%)
  local copies, waits for them, and re-layouts  7.16 us (3%)
  other arithmetic  4.97 us (2%)
    ppermute x12, waiting for transfers between devices, shift(): lax.ppermute(array, axis, [(i, (i + amount) % size) for i in range(size)])  67.8 us
    ppermute x32, waiting for transfers between devices, swap(): return lax.ppermute(array, axis, [(0, 1), (1, 0)])  65.7 us
    ppermute x32, starting transfers between devices, swap(): return lax.ppermute(array, axis, [(0, 1), (1, 0)])  32.9 us
    pallas_call x2, Pallas kernels, run_experts(): pl.pallas_call(lambda *refs: experts_kernel(capacity, count, *refs), in_s...  30.7 us
    ppermute x12, starting transfers between devices, shift(): lax.ppermute(array, axis, [(i, (i + amount) % size) for i in range(size)])  18.8 us
    pallas_call x1, Pallas kernels, attend(): pl.pallas_call(lambda *refs: attend_kernel(len(pieces), *refs), in_specs=...  9.09 us
    unnamed x13, local copies, waits for them, and re-layouts  6.2 us
  transfers between devices with their start and end apart: 44, of which 24 were waited for; matrix products, arithmetic and copies ran while one was open for 2% of the time, Pallas kernels for 17%

profile of v10, /device:TPU:0, one launch (start us, length us, event | category | flops | bytes accessed | tf_op | source)
XLA Modules:
  0.0 238.3 jit_solution(7512007553508968024)
XLA Ops:
  2.5 3.1 %collective-permute-start = (bf16[2,32,2048]{2,1,0:T(8,128)(2,1)S(1)}, bf16[2,32,2048]{2,1,0:T(8,128)(2,1)S(1)}, u32[]{:S(2)}, u32[]{:S(2)}) collective-permute-start(bf16[2,32,2048]{2,1,0:T(8,128)(2,1)S(1)} %constant_dynamic-update-slice_fusion.refs_1_), channel_id=1, source_target_pairs={{0,2},{2,4},{4,6},{6,0},{1,3},{3,5},{5,7},{7,1},{8,10},{10,12},{12... | collective-permute-start | bytes 786440 | tf_op jit(solution)/shard_map/ppermute | solution.py:249
  5.5 2.1 collective-permute-start.1
  7.6 1.7 collective-permute-start.2
  10.7 4.1 %collective-permute-done.refs_2_ = bf16[2,32,2048]{2,1,0:T(8,128)(2,1)S(1)} collective-permute-done((bf16[2,32,2048]{2,1,0:T(8,128)(2,1)S(1)}, bf16[2,32,2048]{2,1,0:T(8,128)(2,1)S(1)}, u32[]{:S(2)}, u32[]{:S(2)}) %collective-permute-start) | collective-permute-done | bytes 262176 | tf_op jit(solution)/shard_map/ppermute | solution.py:249
  14.7 4.2 %collective-permute-done.1.refs_3_ = bf16[2,32,2048]{2,1,0:T(8,128)(2,1)S(1)} collective-permute-done((bf16[2,32,2048]{2,1,0:T(8,128)(2,1)S(1)}, bf16[2,32,2048]{2,1,0:T(8,128)(2,1)S(1)}, u32[]{:S(2)}, u32[]{:S(2)}) %collective-permute-start.1) | collective-permute-done | bytes 262176 | tf_op jit(solution)/shard_map/ppermute | solution.py:249
  20.6 1.5 collective-permute-start.4
  22.6 6.9 %collective-permute-done.3.refs_4_ = bf16[2,32,2048]{2,1,0:T(8,128)(2,1)S(1)} collective-permute-done((bf16[2,32,2048]{2,1,0:T(8,128)(2,1)S(1)}, bf16[2,32,2048]{2,1,0:T(8,128)(2,1)S(1)}, u32[]{:S(2)}, u32[]{:S(2)}) %collective-permute-start.3) | collective-permute-done | bytes 262176 | tf_op jit(solution)/shard_map/ppermute | solution.py:249
  29.8 4.4 %collective-permute-done.5.refs_7_ = bf16[2,32,2048]{2,1,0:T(8,128)(2,1)S(1)} collective-permute-done((bf16[2,32,2048]{2,1,0:T(8,128)(2,1)S(1)}, bf16[2,32,2048]{2,1,0:T(8,128)(2,1)S(1)}, u32[]{:S(2)}, u32[]{:S(2)}) %collective-permute-start.5) | collective-permute-done | bytes 262176 | tf_op jit(solution)/shard_map/ppermute | solution.py:244
  34.1 1.5 collective-permute-start.9
  36.4 2.5 %collective-permute-start.7 = (f32[12,128]{1,0:T(8,128)S(1)}, f32[12,128]{1,0:T(8,128)S(1)}, u32[]{:S(2)}, u32[]{:S(2)}) collective-permute-start(f32[12,128]{1,0:T(8,128)S(1)} %pad_maximum_fusion.3), channel_id=1, source_target_pairs={{0,4},{2,6},{4,0},{6,2},{1,5},{3,7},{5,1},{7,3},{8,12},{10,14},{12... | collective-permute-start | bytes 18440 | tf_op jit(solution)/shard_map/ppermute | solution.py:249
  38.9 2.2 collective-permute-done.6
  42.0 2.8 %collective-permute-done.8 = f32[12,128]{1,0:T(8,128)S(1)} collective-permute-done((f32[12,128]{1,0:T(8,128)S(1)}, f32[12,128]{1,0:T(8,128)S(1)}, u32[]{:S(2)}, u32[]{:S(2)}) %collective-permute-start.8) | collective-permute-done | bytes 6176 | tf_op jit(solution)/shard_map/ppermute | solution.py:249
  46.2 9.1 %attend_project_norm.1 = (bf16[128,2048]{1,0:T(8,128)(2,1)}, bf16[128,2048]{1,0:T(8,128)(2,1)}) custom-call(f32[1,2048]{1,0:T(1,128)S(1)} %bitcast.46, bf16[2,32,2048]{2,1,0:T(8,128)(2,1)S(1)} %constant_dynamic-update-slice_fusion.refs_1_, bf16[2,32,2048]{2,1,0:T(8,128)(2,1)S(1)} %collective-permute-done.refs_2_, ...), custom_call_target="tpu_custom_call" | custom-call | flops 6442450944 | bytes 1048576 | tf_op jit(solution)/shard_map/attend_project_norm/pallas_call | solution.py:90
  55.3 1.6 copy-done.1
  56.9 1.6 collective-permute-start.13
  60.4 3.8 %collective-permute-start.21 = (bf16[128,2048]{1,0:T(8,128)(2,1)}, bf16[128,2048]{1,0:T(8,128)(2,1)}, u32[]{:S(2)}, u32[]{:S(2)}) collective-permute-start(bf16[128,2048]{1,0:T(8,128)(2,1)} %get-tuple-element.100.refs_2_), channel_id=1, source_target_pairs={{0,6},{2,0},{4,2},{6,4},{1,7},{3,1},{5,3},{7,5},{8,14},{10,8},{12,... | collective-permute-start | bytes 1572872 | tf_op jit(solution)/shard_map/ppermute | solution.py:249
  65.2 8.6 %collective-permute-done.17.refs_6_ = bf16[128,2048]{1,0:T(8,128)(2,1)S(1)} collective-permute-done((bf16[128,2048]{1,0:T(8,128)(2,1)}, bf16[128,2048]{1,0:T(8,128)(2,1)S(1)}, u32[]{:S(2)}, u32[]{:S(2)}) %collective-permute-start.17) | collective-permute-done | bytes 524320 | tf_op jit(solution)/shard_map/ppermute | solution.py:249
  73.8 1.5 collective-permute-start.19
  75.3 2.3 collective-permute-start.24
  78.9 6.1 %collective-permute-done.21.refs_2_ = bf16[128,2048]{1,0:T(8,128)(2,1)} collective-permute-done((bf16[128,2048]{1,0:T(8,128)(2,1)}, bf16[128,2048]{1,0:T(8,128)(2,1)}, u32[]{:S(2)}, u32[]{:S(2)}) %collective-permute-start.21) | collective-permute-done | bytes 524320 | tf_op jit(solution)/shard_map/ppermute | solution.py:249
  85.0 1.4 collective-permute-start.22
  88.2 3.8 %collective-permute-done.24.refs_6_ = bf16[128,2048]{1,0:T(8,128)(2,1)} collective-permute-done((bf16[128,2048]{1,0:T(8,128)(2,1)S(1)}, bf16[128,2048]{1,0:T(8,128)(2,1)}, u32[]{:S(2)}, u32[]{:S(2)}) %collective-permute-start.24) | collective-permute-done | bytes 524320 | tf_op jit(solution)/shard_map/ppermute | solution.py:249
  92.0 1.4 collective-permute-start.26
  93.5 2.0 collective-permute-done.16.refs_5_
  96.4 3.7 %collective-permute-done.22.refs_3_ = bf16[128,2048]{1,0:T(8,128)(2,1)S(1)} collective-permute-done((bf16[128,2048]{1,0:T(8,128)(2,1)}, bf16[128,2048]{1,0:T(8,128)(2,1)S(1)}, u32[]{:S(2)}, u32[]{:S(2)}) %collective-permute-start.22) | collective-permute-done | bytes 524320 | tf_op jit(solution)/shard_map/ppermute | solution.py:244
  100.1 1.5 collective-permute-start.27
  101.6 5.5 %collective-permute-done.26.refs_8_ = bf16[128,2048]{1,0:T(8,128)(2,1)S(1)} collective-permute-done((bf16[128,2048]{1,0:T(8,128)(2,1)}, bf16[128,2048]{1,0:T(8,128)(2,1)S(1)}, u32[]{:S(2)}, u32[]{:S(2)}) %collective-permute-start.26) | collective-permute-done | bytes 524320 | tf_op jit(solution)/shard_map/ppermute | solution.py:244
  107.1 1.4 collective-permute-start.28
  108.5 2.8 %collective-permute-done.20.refs_9_ = bf16[128,2048]{1,0:T(8,128)(2,1)S(1)} collective-permute-done((bf16[128,2048]{1,0:T(8,128)(2,1)}, bf16[128,2048]{1,0:T(8,128)(2,1)S(1)}, u32[]{:S(2)}, u32[]{:S(2)}) %collective-permute-start.20) | collective-permute-done | bytes 524320 | tf_op jit(solution)/shard_map/ppermute | solution.py:244
  111.3 1.8 copy-done.2
  114.2 15.3 %experts.2 = (bf16[128,2048]{1,0:T(8,128)(2,1)S(1)}, bf16[128,2048]{1,0:T(8,128)(2,1)S(1)}, bf16[128,2048]{1,0:T(8,128)(2,1)S(1)}, bf16[128,2048]{1,0:T(8,128)(2...) custom-call(s32[8,2,1,128]{3,2,1,0:T(1,128)S(1)} %bitcast.41, ...), custom_call_target="tpu_custom_call" | custom-call | flops 17716740096 | bytes 2097152 | tf_op jit(solution)/shard_map/experts/pallas_call | solution.py:169
  129.5 3.1 %collective-permute-done.28.refs_9_ = bf16[128,2048]{1,0:T(8,128)(2,1)S(1)} collective-permute-done((bf16[128,2048]{1,0:T(8,128)(2,1)S(1)}, bf16[128,2048]{1,0:T(8,128)(2,1)S(1)}, u32[]{:S(2)}, u32[]{:S(2)}) %collective-permute-start.28) | collective-permute-done | bytes 524320 | tf_op jit(solution)/shard_map/ppermute | solution.py:244
  134.6 1.5 collective-permute-start.31
  136.6 15.4 %experts.3 = (bf16[128,2048]{1,0:T(8,128)(2,1)S(1)}, bf16[128,2048]{1,0:T(8,128)(2,1)S(1)}, bf16[128,2048]{1,0:T(8,128)(2,1)S(1)}, bf16[128,2048]{1,0:T(8,128)(2...) custom-call(s32[8,2,1,128]{3,2,1,0:T(1,128)S(1)} %pad_add_fusion.1.r, ...), custom_call_target="tpu_custom_call" | custom-call | flops 17716740096 | bytes 2097152 | tf_op jit(solution)/shard_map/experts/pallas_call | solution.py:169
  152.1 4.5 %collective-permute-done.30 = bf16[128,2048]{1,0:T(8,128)(2,1)S(1)} collective-permute-done((bf16[128,2048]{1,0:T(8,128)(2,1)S(1)}, bf16[128,2048]{1,0:T(8,128)(2,1)S(1)}, u32[]{:S(2)}, u32[]{:S(2)}) %collective-permute-start.30) | collective-permute-done | bytes 524320 | tf_op jit(solution)/shard_map/ppermute | solution.py:244
  156.6 1.5 collective-permute-done.32
  158.0 1.5 collective-permute-start.34
  159.5 1.4 collective-permute-start.41
  162.2 1.5 collective-permute-start.37
  163.7 9.2 %collective-permute-done.34 = bf16[128,2048]{1,0:T(8,128)(2,1)S(1)} collective-permute-done((bf16[128,2048]{1,0:T(8,128)(2,1)S(1)}, bf16[128,2048]{1,0:T(8,128)(2,1)S(1)}, u32[]{:S(2)}, u32[]{:S(2)}) %collective-permute-start.34) | collective-permute-done | bytes 524320 | tf_op jit(solution)/shard_map/ppermute | solution.py:244
  173.0 1.5 collective-permute-start.35
  174.8 1.6 collective-permute-start.42
  176.4 7.8 %collective-permute-done.33 = bf16[128,2048]{1,0:T(8,128)(2,1)S(1)} collective-permute-done((bf16[128,2048]{1,0:T(8,128)(2,1)S(1)}, bf16[128,2048]{1,0:T(8,128)(2,1)S(1)}, u32[]{:S(2)}, u32[]{:S(2)}) %collective-permute-start.33) | collective-permute-done | bytes 524320 | tf_op jit(solution)/shard_map/ppermute | solution.py:244
  184.1 20.1 %collective-permute-done.35 = bf16[128,2048]{1,0:T(8,128)(2,1)S(1)} collective-permute-done((bf16[128,2048]{1,0:T(8,128)(2,1)S(1)}, bf16[128,2048]{1,0:T(8,128)(2,1)S(1)}, u32[]{:S(2)}, u32[]{:S(2)}) %collective-permute-start.35) | collective-permute-done | bytes 524320 | tf_op jit(solution)/shard_map/ppermute | solution.py:244
  204.8 2.1 collective-permute-start.43
  207.4 14.6 %collective-permute-done.38 = bf16[128,2048]{1,0:T(8,128)(2,1)S(1)} collective-permute-done((bf16[128,2048]{1,0:T(8,128)(2,1)S(1)}, bf16[128,2048]{1,0:T(8,128)(2,1)S(1)}, u32[]{:S(2)}, u32[]{:S(2)}) %collective-permute-start.38) | collective-permute-done | bytes 524320 | tf_op jit(solution)/shard_map/ppermute | solution.py:249
  222.4 5.7 %collective-permute-done.43 = bf16[128,2048]{1,0:T(8,128)(2,1)S(1)} collective-permute-done((bf16[128,2048]{1,0:T(8,128)(2,1)S(1)}, bf16[128,2048]{1,0:T(8,128)(2,1)S(1)}, u32[]{:S(2)}, u32[]{:S(2)}) %collective-permute-start.43) | collective-permute-done | bytes 524320 | tf_op jit(solution)/shard_map/ppermute | solution.py:249
  228.2 8.9 %collective-permute-done.39 = bf16[128,2048]{1,0:T(8,128)(2,1)S(1)} collective-permute-done((bf16[128,2048]{1,0:T(8,128)(2,1)S(1)}, bf16[128,2048]{1,0:T(8,128)(2,1)S(1)}, u32[]{:S(2)}, u32[]{:S(2)}) %collective-permute-start.39) | collective-permute-done | bytes 524320 | tf_op jit(solution)/shard_map/ppermute | solution.py:249
  (85 shorter events, 23.6 us)
Async XLA Ops:
  2.5 12.3 %collective-permute-start = (bf16[2,32,2048]{2,1,0:T(8,128)(2,1)S(1)}, bf16[2,32,2048]{2,1,0:T(8,128)(2,1)S(1)}, u32[]{:S(2)}, u32[]{:S(2)}) collective-permute-start(bf16[2,32,2048]{2,1,0:T(8,128)(2,1)S(1)} %constant_dynamic-update-slice_fusion.refs_1_), channel_id=1, source_target_pairs={{0,2},{2,4},{4,6},{6,0},{1,3},{3,5},{5,7},{7,1},{8,10},{10,12},{12... | collective-permute-start | bytes 786440 | tf_op jit(solution)/shard_map/ppermute | solution.py:249
  5.5 13.4 %collective-permute-start.1 = (bf16[2,32,2048]{2,1,0:T(8,128)(2,1)S(1)}, bf16[2,32,2048]{2,1,0:T(8,128)(2,1)S(1)}, u32[]{:S(2)}, u32[]{:S(2)}) collective-permute-start(bf16[2,32,2048]{2,1,0:T(8,128)(2,1)S(1)} %constant_dynamic-update-slice_fusion.refs_1_), channel_id=1, source_target_pairs={{0,6},{2,0},{4,2},{6,4},{1,7},{3,1},{5,3},{7,5},{8,14},{10,8},{12,... | collective-permute-start | bytes 786440 | tf_op jit(solution)/shard_map/ppermute | solution.py:249
  7.6 11.3 %collective-permute-start.2 = (bf16[2,32,2048]{2,1,0:T(8,128)(2,1)S(1)}, bf16[2,32,2048]{2,1,0:T(8,128)(2,1)S(1)}, u32[]{:S(2)}, u32[]{:S(2)}) collective-permute-start(bf16[2,32,2048]{2,1,0:T(8,128)(2,1)S(1)} %constant_dynamic-update-slice_fusion.refs_1_), channel_id=1, source_target_pairs={{0,1},{1,0},{2,3},{3,2},{4,5},{5,4},{6,7},{7,6},{8,9},{9,8},{10,11... | collective-permute-start | bytes 786440 | tf_op jit(solution)/shard_map/ppermute | solution.py:244
  18.9 38.0 %collective-permute-start.10 = (bf16[2048,1408]{1,0:T(8,128)(2,1)}, bf16[2048,1408]{1,0:T(8,128)(2,1)}, u32[]{:S(2)}, u32[]{:S(2)}) collective-permute-start(bf16[2048,1408]{1,0:T(8,128)(2,1)} %bitcast.62), channel_id=1, source_target_pairs={{0,8},{8,0},{1,9},{9,1},{2,10},{10,2},{3,11},{11,3},{4,12},{12,4},... | collective-permute-start | bytes 17301512 | tf_op jit(solution)/shard_map/ppermute | solution.py:244
  18.9 36.3 %collective-permute-start.11 = (bf16[704,2048]{1,0:T(8,128)(2,1)}, bf16[704,2048]{1,0:T(8,128)(2,1)S(1)}, u32[]{:S(2)}, u32[]{:S(2)}) collective-permute-start(bf16[704,2048]{1,0:T(8,128)(2,1)} %bitcast.43), channel_id=1, source_target_pairs={{0,8},{8,0},{1,9},{9,1},{2,10},{10,2},{3,11},{11,3},{4,12},{12,4},... | collective-permute-start | bytes 8650760 | tf_op jit(solution)/shard_map/ppermute | solution.py:244
  19.4 10.0 %collective-permute-start.3 = (bf16[2,32,2048]{2,1,0:T(8,128)(2,1)S(1)}, bf16[2,32,2048]{2,1,0:T(8,128)(2,1)S(1)}, u32[]{:S(2)}, u32[]{:S(2)}) collective-permute-start(bf16[2,32,2048]{2,1,0:T(8,128)(2,1)S(1)} %collective-permute-done.refs_2_), channel_id=1, source_target_pairs={{0,2},{2,4},{4,6},{6,0},{1,3},{3,5},{5,7},{7,1},{8,10},{10,12},{12... | collective-permute-start | bytes 786440 | tf_op jit(solution)/shard_map/ppermute | solution.py:249
  20.6 9.2 %collective-permute-start.4 = (bf16[2,32,2048]{2,1,0:T(8,128)(2,1)S(1)}, bf16[2,32,2048]{2,1,0:T(8,128)(2,1)S(1)}, u32[]{:S(2)}, u32[]{:S(2)}) collective-permute-start(bf16[2,32,2048]{2,1,0:T(8,128)(2,1)S(1)} %collective-permute-done.refs_2_), channel_id=1, source_target_pairs={{0,1},{1,0},{2,3},{3,2},{4,5},{5,4},{6,7},{7,6},{8,9},{9,8},{10,11... | collective-permute-start | bytes 786440 | tf_op jit(solution)/shard_map/ppermute | solution.py:244
  22.1 12.0 %collective-permute-start.5 = (bf16[2,32,2048]{2,1,0:T(8,128)(2,1)S(1)}, bf16[2,32,2048]{2,1,0:T(8,128)(2,1)S(1)}, u32[]{:S(2)}, u32[]{:S(2)}) collective-permute-start(bf16[2,32,2048]{2,1,0:T(8,128)(2,1)S(1)} %collective-permute-done.1.refs_3_), channel_id=1, source_target_pairs={{0,1},{1,0},{2,3},{3,2},{4,5},{5,4},{6,7},{7,6},{8,9},{9,8},{10,11... | collective-permute-start | bytes 786440 | tf_op jit(solution)/shard_map/ppermute | solution.py:244
  34.1 10.6 %collective-permute-start.9 = (bf16[2,32,2048]{2,1,0:T(8,128)(2,1)S(1)}, bf16[2,32,2048]{2,1,0:T(8,128)(2,1)S(1)}, u32[]{:S(2)}, u32[]{:S(2)}) collective-permute-start(bf16[2,32,2048]{2,1,0:T(8,128)(2,1)S(1)} %collective-permute-done.3.refs_4_), channel_id=1, source_target_pairs={{0,1},{1,0},{2,3},{3,2},{4,5},{5,4},{6,7},{7,6},{8,9},{9,8},{10,11... | collective-permute-start | bytes 786440 | tf_op jit(solution)/shard_map/ppermute | solution.py:244
  35.7 5.4 %collective-permute-start.6 = (f32[12,128]{1,0:T(8,128)S(1)}, f32[12,128]{1,0:T(8,128)S(1)}, u32[]{:S(2)}, u32[]{:S(2)}) collective-permute-start(f32[12,128]{1,0:T(8,128)S(1)} %pad_maximum_fusion.3), channel_id=1, source_target_pairs={{0,2},{2,4},{4,6},{6,0},{1,3},{3,5},{5,7},{7,1},{8,10},{10,12},{12... | collective-permute-start | bytes 18440 | tf_op jit(solution)/shard_map/ppermute | solution.py:249
  36.4 5.5 %collective-permute-start.7 = (f32[12,128]{1,0:T(8,128)S(1)}, f32[12,128]{1,0:T(8,128)S(1)}, u32[]{:S(2)}, u32[]{:S(2)}) collective-permute-start(f32[12,128]{1,0:T(8,128)S(1)} %pad_maximum_fusion.3), channel_id=1, source_target_pairs={{0,4},{2,6},{4,0},{6,2},{1,5},{3,7},{5,1},{7,3},{8,12},{10,14},{12... | collective-permute-start | bytes 18440 | tf_op jit(solution)/shard_map/ppermute | solution.py:249
  41.1 3.7 %collective-permute-start.8 = (f32[12,128]{1,0:T(8,128)S(1)}, f32[12,128]{1,0:T(8,128)S(1)}, u32[]{:S(2)}, u32[]{:S(2)}) collective-permute-start(f32[12,128]{1,0:T(8,128)S(1)} %pad_maximum_fusion.3), channel_id=1, source_target_pairs={{0,6},{2,0},{4,2},{6,4},{1,7},{3,1},{5,3},{7,5},{8,14},{10,8},{12,... | collective-permute-start | bytes 18440 | tf_op jit(solution)/shard_map/ppermute | solution.py:249
  44.8 10.5 %collective-permute-start.12 = (f32[4,12,128]{2,1,0:T(8,128)S(1)}, f32[4,12,128]{2,1,0:T(8,128)S(1)}, u32[]{:S(2)}, u32[]{:S(2)}) collective-permute-start(f32[4,12,128]{2,1,0:T(8,128)S(1)} %get-tuple-element.169), channel_id=1, source_target_pairs={{0,1},{1,0},{2,3},{3,2},{4,5},{5,4},{6,7},{7,6},{8,9},{9,8},{10,11... | collective-permute-start | bytes 73736 | tf_op jit(solution)/shard_map/ppermute | solution.py:244
  46.2 65.1 %copy-start = (bf16[1,704,2048]{2,1,0:T(8,128)(2,1)S(1)}, bf16[1,704,2048]{2,1,0:T(8,128)(2,1)}, u32[]{:S(2)}) copy-start(bf16[1,704,2048]{2,1,0:T(8,128)(2,1)} %param.23) | copy-start | bytes 8650756
  55.3 1.6 copy-start.1
  56.9 16.9 %collective-permute-start.17 = (bf16[128,2048]{1,0:T(8,128)(2,1)}, bf16[128,2048]{1,0:T(8,128)(2,1)S(1)}, u32[]{:S(2)}, u32[]{:S(2)}) collective-permute-start(bf16[128,2048]{1,0:T(8,128)(2,1)} %get-tuple-element.100.refs_2_), channel_id=1, source_target_pairs={{0,2},{2,4},{4,6},{6,0},{1,3},{3,5},{5,7},{7,1},{8,10},{10,12},{12... | collective-permute-start | bytes 1572872 | tf_op jit(solution)/shard_map/ppermute | solution.py:249
  56.9 7.3 %collective-permute-start.13 = (f32[2,4,12,128]{3,2,1,0:T(8,128)S(1)}, f32[2,4,12,128]{3,2,1,0:T(8,128)}, u32[]{:S(2)}, u32[]{:S(2)}) collective-permute-start(f32[2,4,12,128]{3,2,1,0:T(8,128)S(1)} %get-tuple-element.167), channel_id=1, source_target_pairs={{0,16},{16,0},{1,17},{17,1},{2,18},{18,2},{3,19},{19,3},{4,20},{20... | collective-permute-start | bytes 147464 | tf_op jit(solution)/shard_map/ppermute | solution.py:244
  58.5 19.5 %collective-permute-start.14 = (bf16[128,2048]{1,0:T(8,128)(2,1)}, bf16[128,2048]{1,0:T(8,128)(2,1)}, u32[]{:S(2)}, u32[]{:S(2)}) collective-permute-start(bf16[128,2048]{1,0:T(8,128)(2,1)} %get-tuple-element.100.refs_2_), channel_id=1, source_target_pairs={{0,1},{1,0},{2,3},{3,2},{4,5},{5,4},{6,7},{7,6},{8,9},{9,8},{10,11... | collective-permute-start | bytes 1572872 | tf_op jit(solution)/shard_map/ppermute | solution.py:244
  59.9 19.0 %collective-permute-start.15 = (bf16[128,2048]{1,0:T(8,128)(2,1)}, bf16[128,2048]{1,0:T(8,128)(2,1)}, u32[]{:S(2)}, u32[]{:S(2)}) collective-permute-start(bf16[128,2048]{1,0:T(8,128)(2,1)} %get-tuple-element.100.refs_2_), channel_id=1, source_target_pairs={{0,16},{16,0},{1,17},{17,1},{2,18},{18,2},{3,19},{19,3},{4,20},{20... | collective-permute-start | bytes 1572872 | tf_op jit(solution)/shard_map/ppermute | solution.py:244
  60.4 24.6 %collective-permute-start.21 = (bf16[128,2048]{1,0:T(8,128)(2,1)}, bf16[128,2048]{1,0:T(8,128)(2,1)}, u32[]{:S(2)}, u32[]{:S(2)}) collective-permute-start(bf16[128,2048]{1,0:T(8,128)(2,1)} %get-tuple-element.100.refs_2_), channel_id=1, source_target_pairs={{0,6},{2,0},{4,2},{6,4},{1,7},{3,1},{5,3},{7,5},{8,14},{10,8},{12,... | collective-permute-start | bytes 1572872 | tf_op jit(solution)/shard_map/ppermute | solution.py:249
  73.8 13.5 %collective-permute-start.19 = (bf16[128,2048]{1,0:T(8,128)(2,1)S(1)}, bf16[128,2048]{1,0:T(8,128)(2,1)}, u32[]{:S(2)}, u32[]{:S(2)}) collective-permute-start(bf16[128,2048]{1,0:T(8,128)(2,1)S(1)} %collective-permute-done.17.refs_6_), channel_id=1, source_target_pairs={{0,16},{16,0},{1,17},{17,1},{2,18},{18,2},{3,19},{19,3},{4,20},{20... | collective-permute-start | bytes 1572872 | tf_op jit(solution)/shard_map/ppermute | solution.py:244
  75.3 16.7 %collective-permute-start.24 = (bf16[128,2048]{1,0:T(8,128)(2,1)S(1)}, bf16[128,2048]{1,0:T(8,128)(2,1)}, u32[]{:S(2)}, u32[]{:S(2)}) collective-permute-start(bf16[128,2048]{1,0:T(8,128)(2,1)S(1)} %collective-permute-done.17.refs_6_), channel_id=1, source_target_pairs={{0,2},{2,4},{4,6},{6,0},{1,3},{3,5},{5,7},{7,1},{8,10},{10,12},{12... | collective-permute-start | bytes 1572872 | tf_op jit(solution)/shard_map/ppermute | solution.py:249
  78.0 17.4 %collective-permute-start.18 = (bf16[128,2048]{1,0:T(8,128)(2,1)S(1)}, bf16[128,2048]{1,0:T(8,128)(2,1)S(1)}, u32[]{:S(2)}, u32[]{:S(2)}) collective-permute-start(bf16[128,2048]{1,0:T(8,128)(2,1)S(1)} %collective-permute-done.17.refs_6_), channel_id=1, source_target_pairs={{0,1},{1,0},{2,3},{3,2},{4,5},{5,4},{6,7},{7,6},{8,9},{9,8},{10,11... | collective-permute-start | bytes 1572872 | tf_op jit(solution)/shard_map/ppermute | solution.py:244
  78.9 16.5 %collective-permute-start.16 = (bf16[128,2048]{1,0:T(8,128)(2,1)}, bf16[128,2048]{1,0:T(8,128)(2,1)S(1)}, u32[]{:S(2)}, u32[]{:S(2)}) collective-permute-start(bf16[128,2048]{1,0:T(8,128)(2,1)} %collective-permute-done.14.refs_3_), channel_id=1, source_target_pairs={{0,16},{16,0},{1,17},{17,1},{2,18},{18,2},{3,19},{19,3},{4,20},{20... | collective-permute-start | bytes 1572872 | tf_op jit(solution)/shard_map/ppermute | solution.py:244
  85.0 15.0 %collective-permute-start.22 = (bf16[128,2048]{1,0:T(8,128)(2,1)}, bf16[128,2048]{1,0:T(8,128)(2,1)S(1)}, u32[]{:S(2)}, u32[]{:S(2)}) collective-permute-start(bf16[128,2048]{1,0:T(8,128)(2,1)} %collective-permute-done.21.refs_2_), channel_id=1, source_target_pairs={{0,1},{1,0},{2,3},{3,2},{4,5},{5,4},{6,7},{7,6},{8,9},{9,8},{10,11... | collective-permute-start | bytes 1572872 | tf_op jit(solution)/shard_map/ppermute | solution.py:244
  87.3 24.0 %collective-permute-start.20 = (bf16[128,2048]{1,0:T(8,128)(2,1)}, bf16[128,2048]{1,0:T(8,128)(2,1)S(1)}, u32[]{:S(2)}, u32[]{:S(2)}) collective-permute-start(bf16[128,2048]{1,0:T(8,128)(2,1)} %collective-permute-done.19.refs_8_), channel_id=1, source_target_pairs={{0,1},{1,0},{2,3},{3,2},{4,5},{5,4},{6,7},{7,6},{8,9},{9,8},{10,11... | collective-permute-start | bytes 1572872 | tf_op jit(solution)/shard_map/ppermute | solution.py:244
  92.0 15.1 %collective-permute-start.26 = (bf16[128,2048]{1,0:T(8,128)(2,1)}, bf16[128,2048]{1,0:T(8,128)(2,1)S(1)}, u32[]{:S(2)}, u32[]{:S(2)}) collective-permute-start(bf16[128,2048]{1,0:T(8,128)(2,1)} %collective-permute-done.24.refs_6_), channel_id=1, source_target_pairs={{0,16},{16,0},{1,17},{17,1},{2,18},{18,2},{3,19},{19,3},{4,20},{20... | collective-permute-start | bytes 1572872 | tf_op jit(solution)/shard_map/ppermute | solution.py:244
  95.4 34.0 %collective-permute-start.23 = (bf16[128,2048]{1,0:T(8,128)(2,1)}, bf16[128,2048]{1,0:T(8,128)(2,1)S(1)}, u32[]{:S(2)}, u32[]{:S(2)}) collective-permute-start(bf16[128,2048]{1,0:T(8,128)(2,1)} %collective-permute-done.21.refs_2_), channel_id=1, source_target_pairs={{0,16},{16,0},{1,17},{17,1},{2,18},{18,2},{3,19},{19,3},{4,20},{20... | collective-permute-start | bytes 1572872 | tf_op jit(solution)/shard_map/ppermute | solution.py:244
  95.4 34.0 %collective-permute-start.25 = (bf16[128,2048]{1,0:T(8,128)(2,1)}, bf16[128,2048]{1,0:T(8,128)(2,1)S(1)}, u32[]{:S(2)}, u32[]{:S(2)}) collective-permute-start(bf16[128,2048]{1,0:T(8,128)(2,1)} %collective-permute-done.24.refs_6_), channel_id=1, source_target_pairs={{0,1},{1,0},{2,3},{3,2},{4,5},{5,4},{6,7},{7,6},{8,9},{9,8},{10,11... | collective-permute-start | bytes 1572872 | tf_op jit(solution)/shard_map/ppermute | solution.py:244
  100.1 29.4 %collective-permute-start.27 = (bf16[128,2048]{1,0:T(8,128)(2,1)S(1)}, bf16[128,2048]{1,0:T(8,128)(2,1)S(1)}, u32[]{:S(2)}, u32[]{:S(2)}) collective-permute-start(bf16[128,2048]{1,0:T(8,128)(2,1)S(1)} %collective-permute-done.22.refs_3_), channel_id=1, source_target_pairs={{0,16},{16,0},{1,17},{17,1},{2,18},{18,2},{3,19},{19,3},{4,20},{20... | collective-permute-start | bytes 1572872 | tf_op jit(solution)/shard_map/ppermute | solution.py:244
  107.1 25.5 %collective-permute-start.28 = (bf16[128,2048]{1,0:T(8,128)(2,1)S(1)}, bf16[128,2048]{1,0:T(8,128)(2,1)S(1)}, u32[]{:S(2)}, u32[]{:S(2)}) collective-permute-start(bf16[128,2048]{1,0:T(8,128)(2,1)S(1)} %collective-permute-done.26.refs_8_), channel_id=1, source_target_pairs={{0,1},{1,0},{2,3},{3,2},{4,5},{5,4},{6,7},{7,6},{8,9},{9,8},{10,11... | collective-permute-start | bytes 1572872 | tf_op jit(solution)/shard_map/ppermute | solution.py:244
  111.3 1.8 copy-start.2
  113.1 1.0 copy-start.3
  132.6 19.5 %collective-permute-start.29 = (bf16[128,2048]{1,0:T(8,128)(2,1)S(1)}, bf16[128,2048]{1,0:T(8,128)(2,1)S(1)}, u32[]{:S(2)}, u32[]{:S(2)}) collective-permute-start(bf16[128,2048]{1,0:T(8,128)(2,1)S(1)} %get-tuple-element.141), channel_id=1, source_target_pairs={{0,1},{1,0},{2,3},{3,2},{4,5},{5,4},{6,7},{7,6},{8,9},{9,8},{10,11... | collective-permute-start | bytes 1572872 | tf_op jit(solution)/shard_map/ppermute | solution.py:244
  134.0 22.6 %collective-permute-start.30 = (bf16[128,2048]{1,0:T(8,128)(2,1)S(1)}, bf16[128,2048]{1,0:T(8,128)(2,1)S(1)}, u32[]{:S(2)}, u32[]{:S(2)}) collective-permute-start(bf16[128,2048]{1,0:T(8,128)(2,1)S(1)} %get-tuple-element.142), channel_id=1, source_target_pairs={{0,1},{1,0},{2,3},{3,2},{4,5},{5,4},{6,7},{7,6},{8,9},{9,8},{10,11... | collective-permute-start | bytes 1572872 | tf_op jit(solution)/shard_map/ppermute | solution.py:244
  134.6 22.0 %collective-permute-start.31 = (bf16[128,2048]{1,0:T(8,128)(2,1)S(1)}, bf16[128,2048]{1,0:T(8,128)(2,1)S(1)}, u32[]{:S(2)}, u32[]{:S(2)}) collective-permute-start(bf16[128,2048]{1,0:T(8,128)(2,1)S(1)} %get-tuple-element.143), channel_id=1, source_target_pairs={{0,16},{16,0},{1,17},{17,1},{2,18},{18,2},{3,19},{19,3},{4,20},{20... | collective-permute-start | bytes 1572872 | tf_op jit(solution)/shard_map/ppermute | solution.py:244
  136.1 21.9 %collective-permute-start.32 = (bf16[128,2048]{1,0:T(8,128)(2,1)S(1)}, bf16[128,2048]{1,0:T(8,128)(2,1)S(1)}, u32[]{:S(2)}, u32[]{:S(2)}) collective-permute-start(bf16[128,2048]{1,0:T(8,128)(2,1)S(1)} %get-tuple-element.144), channel_id=1, source_target_pairs={{0,16},{16,0},{1,17},{17,1},{2,18},{18,2},{3,19},{19,3},{4,20},{20... | collective-permute-start | bytes 1572872 | tf_op jit(solution)/shard_map/ppermute | solution.py:244
  158.0 14.9 %collective-permute-start.34 = (bf16[128,2048]{1,0:T(8,128)(2,1)S(1)}, bf16[128,2048]{1,0:T(8,128)(2,1)S(1)}, u32[]{:S(2)}, u32[]{:S(2)}) collective-permute-start(bf16[128,2048]{1,0:T(8,128)(2,1)S(1)} %get-tuple-element.151), channel_id=1, source_target_pairs={{0,16},{16,0},{1,17},{17,1},{2,18},{18,2},{3,19},{19,3},{4,20},{20... | collective-permute-start | bytes 1572872 | tf_op jit(solution)/shard_map/ppermute | solution.py:244
  159.5 15.1 %collective-permute-start.41 = (bf16[128,2048]{1,0:T(8,128)(2,1)S(1)}, bf16[128,2048]{1,0:T(8,128)(2,1)S(1)}, u32[]{:S(2)}, u32[]{:S(2)}) collective-permute-start(bf16[128,2048]{1,0:T(8,128)(2,1)S(1)} %get-tuple-element.161), channel_id=1, source_target_pairs={{0,1},{1,0},{2,3},{3,2},{4,5},{5,4},{6,7},{7,6},{8,9},{9,8},{10,11... | collective-permute-start | bytes 1572872 | tf_op jit(solution)/shard_map/ppermute | solution.py:244
  161.0 43.6 %collective-permute-start.40 = (bf16[128,2048]{1,0:T(8,128)(2,1)S(1)}, bf16[128,2048]{1,0:T(8,128)(2,1)S(1)}, u32[]{:S(2)}, u32[]{:S(2)}) collective-permute-start(bf16[128,2048]{1,0:T(8,128)(2,1)S(1)} %get-tuple-element.159), channel_id=1, source_target_pairs={{0,1},{1,0},{2,3},{3,2},{4,5},{5,4},{6,7},{7,6},{8,9},{9,8},{10,11... | collective-permute-start | bytes 1572872 | tf_op jit(solution)/shard_map/ppermute | solution.py:244
  161.6 22.6 %collective-permute-start.33 = (bf16[128,2048]{1,0:T(8,128)(2,1)S(1)}, bf16[128,2048]{1,0:T(8,128)(2,1)S(1)}, u32[]{:S(2)}, u32[]{:S(2)}) collective-permute-start(bf16[128,2048]{1,0:T(8,128)(2,1)S(1)} %get-tuple-element.149), channel_id=1, source_target_pairs={{0,16},{16,0},{1,17},{17,1},{2,18},{18,2},{3,19},{19,3},{4,20},{20... | collective-permute-start | bytes 1572872 | tf_op jit(solution)/shard_map/ppermute | solution.py:244
  162.2 45.2 %collective-permute-start.37 = (bf16[128,2048]{1,0:T(8,128)(2,1)S(1)}, bf16[128,2048]{1,0:T(8,128)(2,1)S(1)}, u32[]{:S(2)}, u32[]{:S(2)}) collective-permute-start(bf16[128,2048]{1,0:T(8,128)(2,1)S(1)} %add_convert_fusion.5), channel_id=1, source_target_pairs={{0,1},{1,0},{2,3},{3,2},{4,5},{5,4},{6,7},{7,6},{8,9},{9,8},{10,11... | collective-permute-start | bytes 1572872 | tf_op jit(solution)/shard_map/ppermute | solution.py:244
  173.0 31.2 %collective-permute-start.35 = (bf16[128,2048]{1,0:T(8,128)(2,1)S(1)}, bf16[128,2048]{1,0:T(8,128)(2,1)S(1)}, u32[]{:S(2)}, u32[]{:S(2)}) collective-permute-start(bf16[128,2048]{1,0:T(8,128)(2,1)S(1)} %add_convert_fusion.8), channel_id=1, source_target_pairs={{0,1},{1,0},{2,3},{3,2},{4,5},{5,4},{6,7},{7,6},{8,9},{9,8},{10,11... | collective-permute-start | bytes 1572872 | tf_op jit(solution)/shard_map/ppermute | solution.py:244
  174.8 29.8 %collective-permute-start.42 = (bf16[128,2048]{1,0:T(8,128)(2,1)S(1)}, bf16[128,2048]{1,0:T(8,128)(2,1)S(1)}, u32[]{:S(2)}, u32[]{:S(2)}) collective-permute-start(bf16[128,2048]{1,0:T(8,128)(2,1)S(1)} %add_convert_fusion.2), channel_id=1, source_target_pairs={{0,16},{16,0},{1,17},{17,1},{2,18},{18,2},{3,19},{19,3},{4,20},{20... | collective-permute-start | bytes 1572872 | tf_op jit(solution)/shard_map/ppermute | solution.py:244
  204.5 17.6 %collective-permute-start.38 = (bf16[128,2048]{1,0:T(8,128)(2,1)S(1)}, bf16[128,2048]{1,0:T(8,128)(2,1)S(1)}, u32[]{:S(2)}, u32[]{:S(2)}) collective-permute-start(bf16[128,2048]{1,0:T(8,128)(2,1)S(1)} %add_convert_fusion.7), channel_id=1, source_target_pairs={{0,6},{2,0},{4,2},{6,4},{1,7},{3,1},{5,3},{7,5},{8,14},{10,8},{12,... | collective-permute-start | bytes 1572872 | tf_op jit(solution)/shard_map/ppermute | solution.py:249
  204.8 23.4 %collective-permute-start.43 = (bf16[128,2048]{1,0:T(8,128)(2,1)S(1)}, bf16[128,2048]{1,0:T(8,128)(2,1)S(1)}, u32[]{:S(2)}, u32[]{:S(2)}) collective-permute-start(bf16[128,2048]{1,0:T(8,128)(2,1)S(1)} %add_convert_fusion.1), channel_id=1, source_target_pairs={{0,2},{2,4},{4,6},{6,0},{1,3},{3,5},{5,7},{7,1},{8,10},{10,12},{12... | collective-permute-start | bytes 1572872 | tf_op jit(solution)/shard_map/ppermute | solution.py:249
  206.9 21.3 %collective-permute-start.36 = (bf16[128,2048]{1,0:T(8,128)(2,1)S(1)}, bf16[128,2048]{1,0:T(8,128)(2,1)S(1)}, u32[]{:S(2)}, u32[]{:S(2)}) collective-permute-start(bf16[128,2048]{1,0:T(8,128)(2,1)S(1)} %add_convert_fusion.9), channel_id=1, source_target_pairs={{0,16},{16,0},{1,17},{17,1},{2,18},{18,2},{3,19},{19,3},{4,20},{20... | collective-permute-start | bytes 1572872 | tf_op jit(solution)/shard_map/ppermute | solution.py:244
  222.4 14.7 %collective-permute-start.39 = (bf16[128,2048]{1,0:T(8,128)(2,1)S(1)}, bf16[128,2048]{1,0:T(8,128)(2,1)S(1)}, u32[]{:S(2)}, u32[]{:S(2)}) collective-permute-start(bf16[128,2048]{1,0:T(8,128)(2,1)S(1)} %add_convert_fusion.3), channel_id=1, source_target_pairs={{0,6},{2,0},{4,2},{6,4},{1,7},{3,1},{5,3},{7,5},{8,14},{10,8},{12,... | collective-permute-start | bytes 1572872 | tf_op jit(solution)/shard_map/ppermute | solution.py:249
  (2 other events, 1.4 us)
